TPU v7x, 32 devices: a whole 2x2x4 slice. The times are simulated.
32 devices in a mesh: dp: 8 (over z, x), expert: 4 (over y, core).
Axes of the slice: x: 2, y: 2, z: 4, core: 2. Of those that a mesh axis runs over, the one named last changes fastest.
Arguments:
- inputs: bfloat16 [32768, 512], P(('dp', 'expert')), may hold values from -12 to 12
- embedding: bfloat16 [32768, 512], P(('dp', 'expert')), may hold values from -6 to 6
- cotangent: bfloat16 [32768, 512], P(('dp', 'expert')), may hold values from -6 to 6
- first_routes: int32 [32768, 1], P(('dp', 'expert')), may hold values from 0 to 3; in each aligned block of 1024 rows (0 to 1023, 1024 to 2047, ...) at most 272 rows name the same one
- second_routes: int32 [32768, 1], P(('dp', 'expert')), may hold values from 0 to 3; in each aligned block of 1024 rows (0 to 1023, 1024 to 2047, ...) at most 272 rows name the same one
- segment_starts: int32 [32, 5], P(('dp', 'expert')), may hold values from 0 to 1024, as said below
- norm_gains: bfloat16 [5, 512], P(None, ('dp', 'expert')), may hold values from 0.099609375 to 1.8984375
- first_router: bfloat16 [1024, 4], P(('dp', 'expert')), may hold values from -0.119628906 to 0.119628906
- second_router: bfloat16 [1024, 4], P(('dp', 'expert')), may hold values from -0.119628906 to 0.119628906
- first_in: bfloat16 [4, 512, 2048], P('expert', 'dp'), may hold values from -0.25 to 0.25
- first_out: bfloat16 [4, 2048, 512], P('expert', 'dp'), may hold values from -2 to 2
- second_in: bfloat16 [4, 512, 2048], P('expert', 'dp'), may hold values from -0.25 to 0.25
- second_out: bfloat16 [4, 2048, 512], P('expert', 'dp'), may hold values from -2 to 2
- attention_in: bfloat16 [512, 1536], P(('dp', 'expert')), may hold values from -0.25 to 0.25
- position_weight: bfloat16 [512, 512], P(('dp', 'expert')), may hold values from -0.25 to 0.25
- position_bias: bfloat16 [2, 512], P(None, ('dp', 'expert')), may hold values from -3 to 3
- attention_out: bfloat16 [512, 512], P(('dp', 'expert')), may hold values from -0.75 to 0.75
- pointwise_in: bfloat16 [512, 1024], P(('dp', 'expert')), may hold values from -0.25 to 0.25
- depthwise_kernel: bfloat16 [15, 512], P(None, ('dp', 'expert')), may hold values from -1.5 to 1.5
- batch_gain: bfloat16 [512], P(('dp', 'expert')), may hold values from 0.099609375 to 1.8984375
- batch_bias: bfloat16 [512], P(('dp', 'expert')), may hold values from -1.796875 to 1.796875
- pointwise_out: bfloat16 [512, 512], P(('dp', 'expert')), may hold values from -0.25 to 0.25
Outputs:
- output: bfloat16 [32768, 512], P(('dp', 'expert'))
- inputs_gradient: float32 [32768, 512], P(('dp', 'expert'))
- embedding_gradient: float32 [32768, 512], P(('dp', 'expert'))
- norm_gains_gradient: float32 [5, 512], P(None, ('dp', 'expert'))
- first_router_gradient: float32 [1024, 4], P(('dp', 'expert'))
- second_router_gradient: float32 [1024, 4], P(('dp', 'expert'))
- first_in_gradient: float32 [4, 512, 2048], P('expert', 'dp')
- first_out_gradient: float32 [4, 2048, 512], P('expert', 'dp')
- second_in_gradient: float32 [4, 512, 2048], P('expert', 'dp')
- second_out_gradient: float32 [4, 2048, 512], P('expert', 'dp')
- attention_in_gradient: float32 [512, 1536], P(('dp', 'expert'))
- position_weight_gradient: float32 [512, 512], P(('dp', 'expert'))
- position_bias_gradient: float32 [2, 512], P(None, ('dp', 'expert'))
- attention_out_gradient: float32 [512, 512], P(('dp', 'expert'))
- pointwise_in_gradient: float32 [512, 1024], P(('dp', 'expert'))
- depthwise_kernel_gradient: float32 [15, 512], P(None, ('dp', 'expert'))
- batch_gain_gradient: float32 [512], P(('dp', 'expert'))
- batch_bias_gradient: float32 [512], P(('dp', 'expert'))
- pointwise_out_gradient: float32 [512, 512], P(('dp', 'expert'))
Inputs may be any that keep to these rules, and one draw needn't show every extreme that they name: `first_routes`: at most 272 frames of one row name the same expert. `second_routes`: at most 272 frames of one row name the same expert. `segment_starts`: each row starts with 0 and rises; consecutive entries differ by 128 to 256; the last entry is the row's count of valid frames, and some row has 1024.
All inputs are finite; a program needn't handle non-finite values.
Results may differ from a plain program's by a relative error of at most 0.025.
Values may be sent and summed in bfloat16 or wider, within the bound.
No kernel may reach another device: no remote copies, remote signals or barrier semaphores. Data moves between devices by JAX's collectives and lax.ppermute only.
A program may use at most 384 MiB of HBM per device.

v0:
```python
import math

import jax
import jax.numpy as jnp
from jax import lax
from jax.sharding import PartitionSpec as P

H = 8


epsilon = 1e-05
masked_score = -1e30


def plain_product(left, right):
    return jnp.dot(left, right, preferred_element_type=jnp.float32)


def rows_product(left, right):
    return lax.dot_general(
        left, right, (((0,), (0,)), ((), ())), preferred_element_type=jnp.float32
    )


def columns_product(left, right):
    return lax.dot_general(
        left, right, (((1,), (1,)), ((), ())), preferred_element_type=jnp.float32
    )


def norm_scale(values, gain):
    center = values - jnp.mean(values, axis=-1, keepdims=True)
    spread = jnp.mean(center * center, axis=-1, keepdims=True)
    return center * lax.rsqrt(spread + epsilon) * gain


def norm_backward(values, gain, upstream):
    unused, pull = jax.vjp(norm_scale, values, gain.astype(jnp.float32))
    return pull(upstream)


def segment_numbers(starts, length):
    frames = jnp.arange(length, dtype=jnp.int32)
    numbers = jnp.sum((starts[1:][None, :] <= frames[:, None]).astype(jnp.int32), axis=1)
    return (numbers, frames < starts[-1])


def sinus_table(length, width):
    distance = (length - 1 - jnp.arange(2 * length - 1, dtype=jnp.int32)).astype(jnp.float32)
    rates = jnp.exp(
        jnp.arange(width // 2, dtype=jnp.int32).astype(jnp.float32)
        * (-2.0 * math.log(10000.0) / width)
    )
    angles = distance[:, None] * rates[None, :]
    return jnp.concatenate([jnp.sin(angles), jnp.cos(angles)], axis=1)


def relative_shift(flipped, length):
    heads, rows, span = flipped.shape
    flat = flipped.reshape(heads, rows * span)
    flat = flat[:, rows - 1 : rows - 1 + rows * (span - 1)]
    return flat.reshape(heads, rows, span - 1)[:, :, :length]


def shift_transpose(gradient, span, length):
    heads, rows, unused = gradient.shape

    def shifted(flipped):
        return relative_shift(flipped, length)

    result, pull = jax.vjp(shifted, jnp.zeros((heads, rows, span), jnp.float32))
    return pull(gradient)[0]


def depthwise(gates_in, kernel, numbers):
    length, double = gates_in.shape
    width = double // 2
    linear = gates_in[:, :width] * jax.nn.sigmoid(gates_in[:, width:])
    reach = kernel.shape[0] // 2
    padded = jnp.pad(linear, ((reach, reach), (0, 0)))
    padded_numbers = jnp.pad(numbers, (reach, reach), constant_values=-1)
    total = jnp.zeros_like(linear)
    for offset in range(kernel.shape[0]):
        same = (padded_numbers[offset : offset + length] == numbers)[:, None]
        total = total + jnp.where(same, padded[offset : offset + length], 0.0) * kernel[offset]
    return total


def load_experts(weight_in, weight_out):
    return (
        lax.all_gather(weight_in, "dp", axis=1, tiled=True),
        lax.all_gather(weight_out, "dp", axis=1, tiled=True),
    )


def reload_experts(weight_in, weight_out):
    return (
        lax.all_gather(weight_in, "dp", axis=1, tiled=True),
        lax.all_gather(weight_out, "dp", axis=1, tiled=True),
    )


def sum_experts(grad_in, grad_out):
    return (
        lax.psum_scatter(
            grad_in.astype(jnp.bfloat16), "dp", scatter_dimension=1, tiled=True
        ).astype(jnp.float32),
        lax.psum_scatter(
            grad_out.astype(jnp.bfloat16), "dp", scatter_dimension=1, tiled=True
        ).astype(jnp.float32),
    )


def route_slots(chosen, experts, capacity, length):
    onehot = chosen[:, None] == jnp.arange(experts, dtype=jnp.int32)[None, :]
    counts = jnp.cumsum(onehot.astype(jnp.int32), axis=0) - 1
    rank = jnp.sum(jnp.where(onehot, counts, 0), axis=1)
    slot = chosen * capacity + rank
    owner = (
        jnp.full((experts * capacity,), length, jnp.int32)
        .at[slot]
        .set(jnp.arange(length, dtype=jnp.int32))
    )
    return (onehot, slot, owner)


def expert_apply(weight_in, weight_out, received):
    local = weight_in.shape[0]
    groups, count, width = received.shape
    grouped = received.reshape(groups // local, local, count, width)
    inner = jnp.einsum("sgcd,gdf->sgcf", grouped, weight_in, preferred_element_type=jnp.float32)
    activated = jax.nn.silu(inner).astype(jnp.bfloat16)
    result = jnp.einsum("sgcf,gfd->sgcd", activated, weight_out, preferred_element_type=jnp.float32)
    result = result.astype(jnp.bfloat16).reshape(groups, count, width)
    returned = lax.all_to_all(result, "expert", split_axis=0, concat_axis=0, tiled=True)
    return (returned, received, inner.reshape(groups, count, -1))


def expert_forward(hidden_in, embedding, gain, router, pair, chosen):
    length, width = hidden_in.shape
    experts = router.shape[1]
    capacity = 17 * length // (16 * experts)
    normed_low = norm_scale(hidden_in, gain.astype(jnp.float32)).astype(jnp.bfloat16)
    joined = jnp.concatenate([normed_low, embedding], axis=1)
    probs = jax.nn.softmax(plain_product(joined, router), axis=-1)
    onehot, slot, owner = route_slots(chosen, experts, capacity, length)
    gate = jnp.sum(jnp.where(onehot, probs, 0.0), axis=1)
    padded = jnp.concatenate([normed_low, jnp.zeros((1, width), jnp.bfloat16)], axis=0)
    outgoing = padded[owner].reshape(experts, capacity, width)
    returned, received, inner = expert_apply(
        pair[0],
        pair[1],
        lax.all_to_all(outgoing, "expert", split_axis=0, concat_axis=0, tiled=True),
    )
    picked = returned.reshape(experts * capacity, width)[slot].astype(jnp.float32)
    mixed = hidden_in + 0.5 * gate[:, None] * picked
    return (mixed, (joined, probs, onehot, gate, slot, owner, picked, received, inner))


def expert_backward(upstream, hidden_in, saved, gain, router, pair):
    joined, probs, onehot, gate, slot, owner, picked, received, inner = saved
    weight_in, weight_out = pair
    length, width = upstream.shape
    experts = probs.shape[1]
    local = weight_in.shape[0]
    groups = received.shape[0]
    count = received.shape[1]
    d_gate = 0.5 * jnp.sum(upstream * picked, axis=1)
    d_rows = (0.5 * gate[:, None] * upstream).astype(jnp.bfloat16)
    padded = jnp.concatenate([d_rows, jnp.zeros((1, width), jnp.bfloat16)], axis=0)
    d_outgoing = padded[owner].reshape(experts, -1, width)
    d_result = lax.all_to_all(d_outgoing, "expert", split_axis=0, concat_axis=0, tiled=True)
    four_shape = (groups // local, local, count, width)
    d_four = d_result.reshape(four_shape)
    inner_four = inner.reshape(groups // local, local, count, -1)
    d_activated = jnp.einsum(
        "sgcd,gfd->sgcf", d_four, weight_out, preferred_element_type=jnp.float32
    )
    unused, silu_pull = jax.vjp(jax.nn.silu, inner_four)
    d_inner = silu_pull(d_activated)[0].astype(jnp.bfloat16)
    activated = jax.nn.silu(inner_four).astype(jnp.bfloat16)
    d_weight_out = jnp.einsum(
        "sgcf,sgcd->gfd", activated, d_four, preferred_element_type=jnp.float32
    )
    d_weight_in = jnp.einsum(
        "sgcd,sgcf->gdf", received.reshape(four_shape), d_inner, preferred_element_type=jnp.float32
    )
    d_received = jnp.einsum(
        "sgcf,gdf->sgcd", d_inner, weight_in, preferred_element_type=jnp.float32
    )
    d_received = d_received.astype(jnp.bfloat16).reshape(groups, count, width)
    d_sent = lax.all_to_all(d_received, "expert", split_axis=0, concat_axis=0, tiled=True)
    d_normed = d_sent.reshape(-1, width)[slot].astype(jnp.float32)
    d_logits = d_gate[:, None] * gate[:, None] * (onehot.astype(jnp.float32) - probs)
    d_router = jnp.dot(
        joined.T, d_logits, precision=lax.Precision.HIGHEST, preferred_element_type=jnp.float32
    )
    d_joined = jnp.dot(
        d_logits, router.T, precision=lax.Precision.HIGHEST, preferred_element_type=jnp.float32
    )
    d_normed = d_normed + d_joined[:, :width]
    d_input, d_gain = norm_backward(hidden_in, gain, d_normed)
    return (upstream + d_input, d_gain, d_router, d_joined[:, width:], d_weight_in, d_weight_out)


def block_scores(query_u, query_v, keys, table, numbers, start_row, block):
    length, heads, size = keys.shape
    span = length + block - 1
    offset_row = length - start_row - block
    content = jnp.einsum(
        "qhd,khd->hqk",
        query_u[start_row : start_row + block],
        keys,
        preferred_element_type=jnp.float32,
    )
    flipped = jnp.einsum(
        "qhd,whd->hqw",
        query_v[start_row : start_row + block],
        table[offset_row : offset_row + span],
        preferred_element_type=jnp.float32,
    )
    scores = (content + relative_shift(flipped, length)) * (1.0 / math.sqrt(size))
    same = numbers[start_row : start_row + block][:, None] == numbers[None, :]
    return jnp.where(same[None], scores, masked_score)


def attention_forward(normed_low, weights, numbers, sinus_low):
    mixing_in, table_weight, bias_pair, mixing_out = weights
    length, width = normed_low.shape
    size = width // H
    mixed = plain_product(normed_low, mixing_in)
    queries = mixed[:, :width]
    biases = bias_pair.astype(jnp.float32)
    query_u = (queries + biases[0]).astype(jnp.bfloat16).reshape(length, H, size)
    query_v = (queries + biases[1]).astype(jnp.bfloat16).reshape(length, H, size)
    keys = mixed[:, width : 2 * width].astype(jnp.bfloat16).reshape(length, H, size)
    values = mixed[:, 2 * width :].astype(jnp.bfloat16).reshape(length, H, size)
    table = (
        plain_product(sinus_low, table_weight).astype(jnp.bfloat16).reshape(2 * length - 1, H, size)
    )
    block = min(512, length)
    contexts = []
    logsums = []
    for index in range(length // block):
        scores = block_scores(query_u, query_v, keys, table, numbers, index * block, block)
        peak = jnp.max(scores, axis=-1, keepdims=True)
        raised = jnp.exp(scores - peak)
        total = jnp.sum(raised, axis=-1, keepdims=True)
        probs_low = (raised / total).astype(jnp.bfloat16)
        contexts.append(
            jnp.einsum("hqk,khd->qhd", probs_low, values, preferred_element_type=jnp.float32)
        )
        logsums.append(peak + jnp.log(total))
    context = jnp.concatenate(contexts, axis=0).reshape(length, width).astype(jnp.bfloat16)
    return (
        plain_product(context, mixing_out),
        (query_u, query_v, keys, values, table, context, logsums),
    )


def attention_backward(upstream, normed_low, weights, numbers, sinus_low, saved):
    mixing_in, table_weight, bias_pair, mixing_out = weights
    query_u, query_v, keys, values, table, context, logsums = saved
    length, width = upstream.shape
    heads = keys.shape[1]
    size = keys.shape[2]
    scale = 1.0 / math.sqrt(size)
    block = min(512, length)
    span = length + block - 1
    d_output = upstream.astype(jnp.bfloat16)
    d_mixing_out = rows_product(context, d_output)
    d_context = (
        columns_product(d_output, mixing_out).astype(jnp.bfloat16).reshape(length, heads, size)
    )
    d_keys = jnp.zeros((length, heads, size), jnp.float32)
    d_values = jnp.zeros((length, heads, size), jnp.float32)
    d_table = jnp.zeros((2 * length - 1, heads, size), jnp.float32)
    parts_u = []
    parts_v = []
    for index in range(length // block):
        start_row = index * block
        offset_row = length - start_row - block
        scores = block_scores(query_u, query_v, keys, table, numbers, start_row, block)
        probs = jnp.exp(scores - logsums[index])
        block_context = d_context[start_row : start_row + block]
        d_probs = jnp.einsum(
            "qhd,khd->hqk", block_context, values, preferred_element_type=jnp.float32
        )
        d_values = d_values + jnp.einsum(
            "hqk,qhd->khd",
            probs.astype(jnp.bfloat16),
            block_context,
            preferred_element_type=jnp.float32,
        )
        d_scores = (probs * (d_probs - jnp.sum(probs * d_probs, axis=-1, keepdims=True))).astype(
            jnp.bfloat16
        )
        parts_u.append(
            jnp.einsum("hqk,khd->qhd", d_scores, keys, preferred_element_type=jnp.float32) * scale
        )
        d_keys = (
            d_keys
            + jnp.einsum(
                "hqk,qhd->khd",
                d_scores,
                query_u[start_row : start_row + block],
                preferred_element_type=jnp.float32,
            )
            * scale
        )
        d_flipped = shift_transpose(d_scores.astype(jnp.float32), span, length).astype(jnp.bfloat16)
        window = table[offset_row : offset_row + span]
        parts_v.append(
            jnp.einsum("hqw,whd->qhd", d_flipped, window, preferred_element_type=jnp.float32)
            * scale
        )
        d_window = (
            jnp.einsum(
                "hqw,qhd->whd",
                d_flipped,
                query_v[start_row : start_row + block],
                preferred_element_type=jnp.float32,
            )
            * scale
        )
        d_table = d_table.at[offset_row : offset_row + span].add(d_window)
    d_query_u = jnp.concatenate(parts_u, axis=0).reshape(length, width)
    d_query_v = jnp.concatenate(parts_v, axis=0).reshape(length, width)
    d_bias = jnp.stack([jnp.sum(d_query_u, axis=0), jnp.sum(d_query_v, axis=0)])
    d_mixed = jnp.concatenate(
        [d_query_u + d_query_v, d_keys.reshape(length, width), d_values.reshape(length, width)],
        axis=1,
    ).astype(jnp.bfloat16)
    d_mixing_in = rows_product(normed_low, d_mixed)
    d_normed = columns_product(d_mixed, mixing_in)
    d_table_weight = rows_product(
        sinus_low, d_table.reshape(2 * length - 1, width).astype(jnp.bfloat16)
    )
    return (d_normed, (d_mixing_in, d_table_weight, d_bias, d_mixing_out))


def body(
    inputs,
    embedding,
    cotangent,
    first_routes,
    second_routes,
    segment_starts,
    norm_gains,
    first_router,
    second_router,
    first_in,
    first_out,
    second_in,
    second_out,
    attention_in,
    position_weight,
    position_bias,
    attention_out,
    pointwise_in,
    depthwise_kernel,
    batch_gain,
    batch_bias,
    pointwise_out,
):
    dense = (
        norm_gains,
        first_router,
        second_router,
        attention_in,
        position_weight,
        position_bias,
        attention_out,
        pointwise_in,
        depthwise_kernel,
        batch_gain,
        batch_bias,
        pointwise_out,
    )
    forward_set = (
        lax.all_gather(dense[0], ("dp", "expert"), axis=1, tiled=True),
        lax.all_gather(dense[1], ("dp", "expert"), axis=0, tiled=True),
        lax.all_gather(dense[2], ("dp", "expert"), axis=0, tiled=True),
        lax.all_gather(dense[3], ("dp", "expert"), axis=0, tiled=True),
        lax.all_gather(dense[4], ("dp", "expert"), axis=0, tiled=True),
        lax.all_gather(dense[5], ("dp", "expert"), axis=1, tiled=True),
        lax.all_gather(dense[6], ("dp", "expert"), axis=0, tiled=True),
        lax.all_gather(dense[7], ("dp", "expert"), axis=0, tiled=True),
        lax.all_gather(dense[8], ("dp", "expert"), axis=1, tiled=True),
        lax.all_gather(dense[9], ("dp", "expert"), axis=0, tiled=True),
        lax.all_gather(dense[10], ("dp", "expert"), axis=0, tiled=True),
        lax.all_gather(dense[11], ("dp", "expert"), axis=0, tiled=True),
    )
    first_pair = load_experts(first_in, first_out)
    second_pair = load_experts(second_in, second_out)
    length, width = inputs.shape
    numbers, valid = segment_numbers(segment_starts[0], length)
    mask = valid.astype(jnp.float32)[:, None]
    sinus_low = sinus_table(length, width).astype(jnp.bfloat16)
    start_rows = inputs.astype(jnp.float32)
    mixed_one, first_saved = expert_forward(
        start_rows, embedding, forward_set[0][0], forward_set[1], first_pair, first_routes[:, 0]
    )
    normed_two = norm_scale(mixed_one, forward_set[0][1].astype(jnp.float32)).astype(jnp.bfloat16)
    attended, attention_saved = attention_forward(
        normed_two,
        (forward_set[3], forward_set[4], forward_set[5], forward_set[6]),
        numbers,
        sinus_low,
    )
    mixed_two = mixed_one + attended
    normed_three = norm_scale(mixed_two, forward_set[0][2].astype(jnp.float32)).astype(jnp.bfloat16)
    gates_in = plain_product(normed_three, forward_set[7])
    kernel_values = forward_set[8].astype(jnp.float32)
    convolved = depthwise(gates_in, kernel_values, numbers)
    totals = lax.psum(
        (
            jnp.sum(mask * convolved, axis=0),
            jnp.sum(mask * convolved * convolved, axis=0),
            jnp.sum(mask),
        ),
        ("dp", "expert"),
    )
    count = totals[2]
    mean = totals[0] / count
    variance = totals[1] / count - mean * mean
    inverse = lax.rsqrt(variance + epsilon)
    centred = convolved - mean
    standard = centred * inverse
    batched = standard * forward_set[9].astype(jnp.float32) + forward_set[10].astype(jnp.float32)
    active_low = jax.nn.silu(batched).astype(jnp.bfloat16)
    mixed_three = mixed_two + plain_product(active_low, forward_set[11])
    mixed_four, second_saved = expert_forward(
        mixed_three, embedding, forward_set[0][3], forward_set[2], second_pair, second_routes[:, 0]
    )
    output = norm_scale(mixed_four, forward_set[0][4].astype(jnp.float32)).astype(jnp.bfloat16)
    back_set = (
        lax.all_gather(dense[0], ("dp", "expert"), axis=1, tiled=True),
        lax.all_gather(dense[1], ("dp", "expert"), axis=0, tiled=True),
        lax.all_gather(dense[2], ("dp", "expert"), axis=0, tiled=True),
        lax.all_gather(dense[3], ("dp", "expert"), axis=0, tiled=True),
        lax.all_gather(dense[4], ("dp", "expert"), axis=0, tiled=True),
        lax.all_gather(dense[5], ("dp", "expert"), axis=1, tiled=True),
        lax.all_gather(dense[6], ("dp", "expert"), axis=0, tiled=True),
        lax.all_gather(dense[7], ("dp", "expert"), axis=0, tiled=True),
        lax.all_gather(dense[8], ("dp", "expert"), axis=1, tiled=True),
        lax.all_gather(dense[9], ("dp", "expert"), axis=0, tiled=True),
        lax.all_gather(dense[10], ("dp", "expert"), axis=0, tiled=True),
        lax.all_gather(dense[11], ("dp", "expert"), axis=0, tiled=True),
    )
    first_back = reload_experts(first_in, first_out)
    second_back = reload_experts(second_in, second_out)
    d_four, d_gain_five = norm_backward(mixed_four, back_set[0][4], cotangent.astype(jnp.float32))
    d_three, d_gain_four, d_router_two, d_embed_two, d_second_in_part, d_second_out_part = (
        expert_backward(d_four, mixed_three, second_saved, back_set[0][3], back_set[2], second_back)
    )
    second_sums = sum_experts(d_second_in_part, d_second_out_part)
    d_branch = d_three.astype(jnp.bfloat16)
    d_pointwise_out = rows_product(active_low, d_branch)
    d_active = columns_product(d_branch, back_set[11])
    unused, silu_pull = jax.vjp(jax.nn.silu, batched)
    d_batched = silu_pull(d_active)[0]
    d_batch_gain = jnp.sum(d_batched * standard, axis=0)
    d_batch_bias = jnp.sum(d_batched, axis=0)
    d_standard = d_batched * back_set[9].astype(jnp.float32)
    sums = lax.psum(
        (jnp.sum(d_standard, axis=0), jnp.sum(d_standard * centred, axis=0)), ("dp", "expert")
    )
    d_variance = -0.5 * inverse * inverse * inverse * sums[1]
    d_convolved = (
        inverse * d_standard + mask * (2.0 * d_variance * centred - inverse * sums[0]) / count
    )

    def convolve_only(gates_value, kernel_value):
        return depthwise(gates_value, kernel_value, numbers)

    unused_conv, conv_pull = jax.vjp(convolve_only, gates_in, kernel_values)
    d_gates, d_kernel = conv_pull(d_convolved)
    d_gates_low = d_gates.astype(jnp.bfloat16)
    d_pointwise_in = rows_product(normed_three, d_gates_low)
    d_normed_three = columns_product(d_gates_low, back_set[7])
    d_from_three, d_gain_three = norm_backward(mixed_two, back_set[0][2], d_normed_three)
    d_two = d_three + d_from_three
    d_normed_two, attention_grads = attention_backward(
        d_two,
        normed_two,
        (back_set[3], back_set[4], back_set[5], back_set[6]),
        numbers,
        sinus_low,
        attention_saved,
    )
    d_from_two, d_gain_two = norm_backward(mixed_one, back_set[0][1], d_normed_two)
    d_one = d_two + d_from_two
    d_start, d_gain_one, d_router_one, d_embed_one, d_first_in_part, d_first_out_part = (
        expert_backward(d_one, start_rows, first_saved, back_set[0][0], back_set[1], first_back)
    )
    first_sums = sum_experts(d_first_in_part, d_first_out_part)
    d_first_in, d_first_out = (first_sums[0], first_sums[1])
    d_second_in, d_second_out = (second_sums[0], second_sums[1])
    d_gains = jnp.stack([d_gain_one, d_gain_two, d_gain_three, d_gain_four, d_gain_five])
    dense_grads = (
        d_gains,
        d_router_one,
        d_router_two,
        attention_grads[0],
        attention_grads[1],
        attention_grads[2],
        attention_grads[3],
        d_pointwise_in,
        d_kernel,
        d_batch_gain,
        d_batch_bias,
        d_pointwise_out,
    )
    shards = (
        lax.psum_scatter(dense_grads[0], ("dp", "expert"), scatter_dimension=1, tiled=True),
        lax.psum_scatter(dense_grads[1], ("dp", "expert"), scatter_dimension=0, tiled=True),
        lax.psum_scatter(dense_grads[2], ("dp", "expert"), scatter_dimension=0, tiled=True),
        lax.psum_scatter(dense_grads[3], ("dp", "expert"), scatter_dimension=0, tiled=True),
        lax.psum_scatter(dense_grads[4], ("dp", "expert"), scatter_dimension=0, tiled=True),
        lax.psum_scatter(dense_grads[5], ("dp", "expert"), scatter_dimension=1, tiled=True),
        lax.psum_scatter(dense_grads[6], ("dp", "expert"), scatter_dimension=0, tiled=True),
        lax.psum_scatter(dense_grads[7], ("dp", "expert"), scatter_dimension=0, tiled=True),
        lax.psum_scatter(dense_grads[8], ("dp", "expert"), scatter_dimension=1, tiled=True),
        lax.psum_scatter(dense_grads[9], ("dp", "expert"), scatter_dimension=0, tiled=True),
        lax.psum_scatter(dense_grads[10], ("dp", "expert"), scatter_dimension=0, tiled=True),
        lax.psum_scatter(dense_grads[11], ("dp", "expert"), scatter_dimension=0, tiled=True),
    )
    return (
        output,
        d_start,
        d_embed_one + d_embed_two,
        shards[0],
        shards[1],
        shards[2],
        d_first_in,
        d_first_out,
        d_second_in,
        d_second_out,
        shards[3],
        shards[4],
        shards[5],
        shards[6],
        shards[7],
        shards[8],
        shards[9],
        shards[10],
        shards[11],
    )


def solution(mesh):
    in_specs = (
        P(("dp", "expert"), None),
        P(("dp", "expert"), None),
        P(("dp", "expert"), None),
        P(("dp", "expert"), None),
        P(("dp", "expert"), None),
        P(("dp", "expert"), None),
        P(None, ("dp", "expert")),
        P(("dp", "expert"), None),
        P(("dp", "expert"), None),
        P("expert", "dp", None),
        P("expert", "dp", None),
        P("expert", "dp", None),
        P("expert", "dp", None),
        P(("dp", "expert"), None),
        P(("dp", "expert"), None),
        P(None, ("dp", "expert")),
        P(("dp", "expert"), None),
        P(("dp", "expert"), None),
        P(None, ("dp", "expert")),
        P(("dp", "expert")),
        P(("dp", "expert")),
        P(("dp", "expert"), None),
    )
    out_specs = (
        P(("dp", "expert"), None),
        P(("dp", "expert"), None),
        P(("dp", "expert"), None),
        P(None, ("dp", "expert")),
        P(("dp", "expert"), None),
        P(("dp", "expert"), None),
        P("expert", "dp", None),
        P("expert", "dp", None),
        P("expert", "dp", None),
        P("expert", "dp", None),
        P(("dp", "expert"), None),
        P(("dp", "expert"), None),
        P(None, ("dp", "expert")),
        P(("dp", "expert"), None),
        P(("dp", "expert"), None),
        P(None, ("dp", "expert")),
        P(("dp", "expert")),
        P(("dp", "expert")),
        P(("dp", "expert"), None),
    )
    return jax.shard_map(body, mesh=mesh, in_specs=in_specs, out_specs=out_specs, check_vma=False)
```

profile of v0, /device:TPU:0, one launch (start us, length us, event | category | flops | bytes accessed | tf_op | source)
XLA Modules:
  0.0 3000.8 jit_solution(17095037624002832506)
XLA Ops:
  12.8 44.0 %all-gather = bf16[32,16,5]{1,2,0:T(8,128)(2,1)S(1)} all-gather(bf16[1,16,5]{1,2,0:T(8,128)(2,1)} %bitcast.479), channel_id=1, replica_groups=mesh['dp'=8,'expert'=4] {'dp','expert'}, dimensions={0}, use_global_device_ids=true | all-gather | bytes 5280 | tf_op jit(solution)/shard_map/all_gather | solution.py:381
  74.7 43.3 %all-gather.2 = bf16[32,16,2]{1,2,0:T(2,128)(2,1)S(1)} all-gather(bf16[1,16,2]{1,2,0:T(2,128)(2,1)S(1)} %bitcast.483), channel_id=1, replica_groups=mesh['dp'=8,'expert'=4] {'dp','expert'}, dimensions={0}, use_global_device_ids=true | all-gather | bytes 2112 | tf_op jit(solution)/shard_map/all_gather | solution.py:386
  125.0 37.9 %all-gather.1 = bf16[32,32,4]{1,2,0:T(4,128)(2,1)S(1)} all-gather(bf16[1,32,4]{1,2,0:T(4,128)(2,1)S(1)} %bitcast.481), channel_id=1, replica_groups=mesh['dp'=8,'expert'=4] {'dp','expert'}, dimensions={0}, use_global_device_ids=true | all-gather | bytes 8448 | tf_op jit(solution)/shard_map/all_gather | solution.py:382
  163.0 37.2 %all_gather.69 = bf16[15,512]{0,1:T(8,128)(2,1)S(1)} all-gather(bf16[15,16]{0,1:T(8,128)(2,1)S(1)} %copy.120), channel_id=1, replica_groups=mesh['dp'=8,'expert'=4] {'dp','expert'}, dimensions={1}, use_global_device_ids=true | all-gather | bytes 15840 | tf_op jit(solution)/shard_map/all_gather | solution.py:389
  202.9 42.4 %all_gather.67 = bf16[512,512]{1,0:T(8,128)(2,1)} all-gather(bf16[16,512]{1,0:T(8,128)(2,1)S(1)} %copy-done.138), channel_id=1, replica_groups=mesh['dp'=8,'expert'=4] {'dp','expert'}, dimensions={0}, use_global_device_ids=true | all-gather | bytes 540672 | tf_op jit(solution)/shard_map/all_gather | solution.py:387
  245.4 42.3 %all_gather.72 = bf16[512,512]{1,0:T(8,128)(2,1)} all-gather(bf16[16,512]{1,0:T(8,128)(2,1)S(1)} %copy-done.139), channel_id=1, replica_groups=mesh['dp'=8,'expert'=4] {'dp','expert'}, dimensions={0}, use_global_device_ids=true | all-gather | bytes 540672 | tf_op jit(solution)/shard_map/all_gather | solution.py:392
  287.6 40.6 %all_gather.66 = bf16[512,512]{1,0:T(8,128)(2,1)S(1)} all-gather(bf16[16,512]{1,0:T(8,128)(2,1)S(1)} %copy-done.140), channel_id=1, replica_groups=mesh['dp'=8,'expert'=4] {'dp','expert'}, dimensions={0}, use_global_device_ids=true | all-gather | bytes 540672 | tf_op jit(solution)/shard_map/all_gather | solution.py:385
  366.3 43.5 %all-reduce.49 = (bf16[512]{0:T(512)(128)(2,1)S(1)}, bf16[512]{0:T(512)(128)(2,1)S(1)}) all-reduce(bf16[512]{0:T(512)(128)(2,1)S(1)} %dynamic-update-slice.7, bf16[512]{0:T(512)(128)(2,1)S(1)} %dynamic-update-slice.6), channel_id=1, replica_groups=mesh['dp'=8,'expert'=4] {'dp','expert'}, use_global_device_ids=true, to_apply=%add.44 | all-reduce | flops 1024 | bytes 4096
  446.0 38.0 %reshape.883 = f32[6287360]{0:T(1024)} reshape(f32[8,512,1535]{2,1,0:T(8,128)} %fusion.253) | data formatting | bytes 50298880
  547.1 24.2 reshape.699
  581.6 37.5 %reshape.879 = f32[6287360]{0:T(1024)} reshape(f32[8,512,1535]{2,1,0:T(8,128)} %fusion.254) | data formatting | bytes 50298880
  682.7 24.2 reshape.701
  774.6 39.8 %all-reduce.48 = (f32[512]{0:T(512)S(1)}, f32[]{:T(128)}, f32[512]{0:T(512)S(1)}) all-reduce(f32[512]{0:T(512)S(1)} %get-tuple-element.71, f32[]{:T(128)} %fusion.206, f32[512]{0:T(512)S(1)} %get-tuple-element.70), channel_id=1, replica_groups=mesh['dp'=8,'expert'=4] {'dp','expert'}, use_global_device_ids=true, to_apply=%region_23.24 | all-reduce | flops 1025 | bytes 8200 | tf_op jit(solution)/shard_map/psum | solution.py:416
  863.6 47.2 %all-gather.3 = bf16[32,32,4]{1,2,0:T(4,128)(2,1)S(1)} all-gather(bf16[1,32,4]{1,2,0:T(4,128)(2,1)S(1)} %bitcast.482), channel_id=1, replica_groups=mesh['dp'=8,'expert'=4] {'dp','expert'}, dimensions={0}, use_global_device_ids=true | all-gather | bytes 8448 | tf_op jit(solution)/shard_map/all_gather | solution.py:383
  996.6 37.1 %all-reduce.47 = (f32[512]{0:T(512)S(1)}, f32[512]{0:T(512)S(1)}, f32[512]{0:T(512)}, f32[512]{0:T(512)}) all-reduce(f32[512]{0:T(512)S(1)} %get-tuple-element.72, f32[512]{0:T(512)S(1)} %get-tuple-element.52, f32[512]{0:T(512)S(1)} %get-tuple-element.51, ...), channel_id=1, replica_groups=mesh['dp'=8,'expert'=4] {'dp','expert'}, use_global_device_ids=true, to_apply=%region_43.44 | all-reduce | flops 2048 | bytes 16384 | tf_op jit(solution)/shard_map/psum | solution.py:466
  1188.0 28.1 reshape.893
  1216.1 24.1 convert_element_type.297
  1322.4 27.8 reshape.889
  1350.2 24.2 convert_element_type.298
  1557.5 117.8 %reduce-scatter.49.cloned.1.call-done = f32[16,2]{1,0:T(8,128)} async-done(((f32[512,2]{1,0:T(8,128)}), f32[16,2]{1,0:T(8,128)}) %reduce-scatter.49.cloned.1.call-update) | async-done | bytes 144
  1676.6 131.4 %reduce-scatter.45.cloned.1.call-done = f32[32,4]{1,0:T(8,128)} async-done(((f32[1024,4]{1,0:T(8,128)}), f32[32,4]{1,0:T(8,128)}) %reduce-scatter.45.cloned.1.call-update) | async-done | bytes 528
  1809.4 130.2 %reduce-scatter.51.cloned.1.call-done = f32[16,15]{1,0:T(8,128)} async-done(((f32[512,15]{1,0:T(8,128)}), f32[16,15]{1,0:T(8,128)}) %reduce-scatter.51.cloned.1.call-update) | async-done | bytes 976
  1945.0 126.7 %reduce-scatter.43.cloned.1.call-done = f32[16,5]{1,0:T(8,128)} async-done(((f32[512,5]{1,0:T(8,128)}), f32[16,5]{1,0:T(8,128)}) %reduce-scatter.43.cloned.1.call-update) | async-done | bytes 336
  2073.1 66.0 %reduce-scatter.31.cloned.1.call-done = bf16[1,256,512]{2,1,0:T(8,128)(2,1)} async-done(((bf16[1,2048,512]{2,1,0:T(8,128)(2,1)}), bf16[1,256,512]{2,1,0:T(8,128)(2,1)}) %reduce-scatter.31.cloned.1.call-update) | async-done | bytes 262160 | tf_op jit(solution)/shard_map/reduce_scatter | solution.py:108
  2140.9 68.7 %reduce-scatter.29.cloned.1.call-done = bf16[1,64,2048]{2,1,0:T(8,128)(2,1)} async-done(((bf16[1,512,2048]{2,1,0:T(8,128)(2,1)}), bf16[1,64,2048]{2,1,0:T(8,128)(2,1)}) %reduce-scatter.29.cloned.1.call-update) | async-done | bytes 262160 | tf_op jit(solution)/shard_map/reduce_scatter | solution.py:105
  2211.4 68.8 %reduce-scatter.27.cloned.1.call-done = bf16[1,256,512]{2,1,0:T(8,128)(2,1)} async-done(((bf16[1,2048,512]{2,1,0:T(8,128)(2,1)}), bf16[1,256,512]{2,1,0:T(8,128)(2,1)}) %reduce-scatter.27.cloned.1.call-update) | async-done | bytes 262160 | tf_op jit(solution)/shard_map/reduce_scatter | solution.py:108
  2282.0 68.7 %reduce-scatter.25.cloned.1.call-done = bf16[1,64,2048]{2,1,0:T(8,128)(2,1)} async-done(((bf16[1,512,2048]{2,1,0:T(8,128)(2,1)}), bf16[1,64,2048]{2,1,0:T(8,128)(2,1)}) %reduce-scatter.25.cloned.1.call-update) | async-done | bytes 262160 | tf_op jit(solution)/shard_map/reduce_scatter | solution.py:105
  2352.4 134.7 %reduce-scatter.41.cloned.1.call-done = f32[16,512]{1,0:T(8,128)} async-done(((f32[512,512]{1,0:T(8,128)}), f32[16,512]{1,0:T(8,128)}) %reduce-scatter.41.cloned.1.call-update) | async-done | bytes 32784 | tf_op jit(solution)/shard_map/reduce_scatter | solution.py:527
  2487.2 133.4 %reduce-scatter.37.cloned.1.call-done = f32[16,512]{1,0:T(8,128)} async-done(((f32[512,512]{1,0:T(8,128)}), f32[16,512]{1,0:T(8,128)}) %reduce-scatter.37.cloned.1.call-update) | async-done | bytes 32784 | tf_op jit(solution)/shard_map/reduce_scatter | solution.py:522
  2620.6 133.4 %reduce-scatter.35.cloned.1.call-done = f32[16,512]{1,0:T(8,128)} async-done(((f32[512,512]{1,0:T(8,128)}), f32[16,512]{1,0:T(8,128)}) %reduce-scatter.35.cloned.1.call-update) | async-done | bytes 32784 | tf_op jit(solution)/shard_map/reduce_scatter | solution.py:520
  2754.0 135.5 %reduce-scatter.39.cloned.1.call-done = f32[16,1024]{1,0:T(8,128)} async-done(((f32[512,1024]{1,0:T(8,128)}), f32[16,1024]{1,0:T(8,128)}) %reduce-scatter.39.cloned.1.call-update) | async-done | bytes 65552 | tf_op jit(solution)/shard_map/reduce_scatter | solution.py:523
  2889.5 104.2 %reduce-scatter.33.cloned.1.call-done = f32[16,1536]{1,0:T(8,128)} async-done(((f32[512,1536]{1,0:T(8,128)}), f32[16,1536]{1,0:T(8,128)}) %reduce-scatter.33.cloned.1.call-update) | async-done | bytes 98320 | tf_op jit(solution)/shard_map/reduce_scatter | solution.py:519
  (720 shorter events, 880.4 us)
Async XLA Ops:
  7.2 336.9 %all-gather.11.cloned.1.call-start = ((), (), s32[]{:S(2)}) async-start(), calls=%async_computation.22 | async-start | bytes 2359296 | tf_op jit(solution)/shard_map/all_gather | solution.py:91
  7.9 344.1 %all-gather.13.cloned.1.call-start = ((), (), s32[]{:S(2)}) async-start(), calls=%async_computation.23 | async-start | bytes 2359296 | tf_op jit(solution)/shard_map/all_gather | solution.py:92
  8.7 412.2 %all-gather.15.cloned.1.call-start = ((), (), s32[]{:S(2)}) async-start(), calls=%async_computation.24 | async-start | bytes 1622016 | tf_op jit(solution)/shard_map/all_gather | solution.py:384
  9.4 752.1 %all-gather.17.cloned.1.call-start = ((), (), s32[]{:S(2)}) async-start(), calls=%async_computation.25 | async-start | bytes 1081344 | tf_op jit(solution)/shard_map/all_gather | solution.py:388
  10.0 819.2 %all-gather.19.cloned.1.call-start = ((), (), s32[]{:S(2)}) async-start(), calls=%async_computation.26 | async-start | bytes 2359296 | tf_op jit(solution)/shard_map/all_gather | solution.py:91
  59.6 361.3 %copy-start.95 = (f32[1,512]{1,0:T(1,128)}, f32[1,512]{1,0:T(1,128)S(1)}, u32[]{:S(2)}) copy-start(f32[1,512]{1,0:T(1,128)S(1)} %get-tuple-element.154) | copy-start | bytes 6148
  69.4 274.7 %all-to-all-start = ((bf16[4,272,512]{2,1,0:T(8,128)(2,1)}), bf16[4,272,512]{2,1,0:T(8,128)(2,1)}, u32[]{:S(2)}, u32[]{:S(2)}) async-start(bf16[4,272,512]{2,1,0:T(8,128)(2,1)} %bitcast.10), calls=%async_computation | async-start | bytes 2228224 | tf_op jit(solution)/shard_map/all_to_all | solution.py:153
  73.9 778.4 %all-gather.21.cloned.1.call-start = ((), (), s32[]{:S(2)}) async-start(), calls=%async_computation.27 | async-start | bytes 2359296 | tf_op jit(solution)/shard_map/all_gather | solution.py:92
  74.5 340.9 %copy-start.97 = (s32[1024]{0:T(1024)}, s32[1024]{0:T(1024)S(1)}, u32[]{:S(2)}) copy-start(s32[1024]{0:T(1024)S(1)} %broadcast_clamp_fusion.1) | copy-start | bytes 12292
  359.7 55.7 %all-to-all-start.1 = ((bf16[4,272,512]{2,1,0:T(8,128)(2,1)}), bf16[4,272,512]{2,1,0:T(8,128)(2,1)S(1)}, u32[]{:S(2)}, u32[]{:S(2)}) async-start(bf16[4,272,512]{2,1,0:T(8,128)(2,1)} %fusion.108), calls=%async_computation.1 | async-start | bytes 2228224 | tf_op jit(solution)/shard_map/all_to_all | solution.py:135
  761.0 302.4 %copy-start.106 = (f32[1024]{0:T(1024)}, f32[1024]{0:T(1024)S(1)}, u32[]{:S(2)}) copy-start(f32[1024]{0:T(1024)S(1)} %broadcast_multiply_fusion.5) | copy-start | bytes 12292
  825.2 19.1 all-to-all-start.2
  859.9 53.4 %all-to-all-start.3 = ((bf16[4,272,512]{2,1,0:T(8,128)(2,1)}), bf16[4,272,512]{2,1,0:T(8,128)(2,1)S(1)}, u32[]{:S(2)}, u32[]{:S(2)}) async-start(bf16[4,272,512]{2,1,0:T(8,128)(2,1)} %fusion.113), calls=%async_computation.3 | async-start | bytes 2228224 | tf_op jit(solution)/shard_map/all_to_all | solution.py:135
  962.8 18.7 all-to-all-start.5
  1397.6 19.7 all-to-all-start.6
  1402.0 151.6 %reduce-scatter.47.cloned.1.call-start = ((), (), s32[]{:S(2)}) async-start(), calls=%async_computation.39 | async-start | bytes 540672
  1406.4 268.9 %reduce-scatter.49.cloned.1.call-start = ((), (), s32[]{:S(2)}) async-start(), calls=%async_computation.40 | async-start | bytes 270336
  1431.9 19.2 all-to-all-start.7
  1435.6 372.4 %reduce-scatter.45.cloned.1.call-start = ((), (), s32[]{:S(2)}) async-start(), calls=%async_computation.38 | async-start | bytes 540672
  1440.5 499.1 %reduce-scatter.51.cloned.1.call-start = ((), (), s32[]{:S(2)}) async-start(), calls=%async_computation.41 | async-start | bytes 270336
  1441.6 630.1 %reduce-scatter.43.cloned.1.call-start = ((), (), s32[]{:S(2)}) async-start(), calls=%async_computation.37 | async-start | bytes 270336
  1462.0 677.1 %reduce-scatter.31.cloned.1.call-start = ((), (), s32[]{:S(2)}) async-start(), calls=%async_computation.31 | async-start | bytes 2359296 | tf_op jit(solution)/shard_map/reduce_scatter | solution.py:108
  1470.1 739.5 %reduce-scatter.29.cloned.1.call-start = ((), (), s32[]{:S(2)}) async-start(), calls=%async_computation.30 | async-start | bytes 2359296 | tf_op jit(solution)/shard_map/reduce_scatter | solution.py:105
  1477.8 802.4 %reduce-scatter.27.cloned.1.call-start = ((), (), s32[]{:S(2)}) async-start(), calls=%async_computation.29 | async-start | bytes 2359296 | tf_op jit(solution)/shard_map/reduce_scatter | solution.py:108
  1486.1 864.5 %reduce-scatter.25.cloned.1.call-start = ((), (), s32[]{:S(2)}) async-start(), calls=%async_computation.28 | async-start | bytes 2359296 | tf_op jit(solution)/shard_map/reduce_scatter | solution.py:105
  1493.3 993.9 %reduce-scatter.41.cloned.1.call-start = ((), (), s32[]{:S(2)}) async-start(), calls=%async_computation.36 | async-start | bytes 1081344 | tf_op jit(solution)/shard_map/reduce_scatter | solution.py:527
  1498.3 1122.3 %reduce-scatter.37.cloned.1.call-start = ((), (), s32[]{:S(2)}) async-start(), calls=%async_computation.34 | async-start | bytes 1081344 | tf_op jit(solution)/shard_map/reduce_scatter | solution.py:522
  1502.0 1252.0 %reduce-scatter.35.cloned.1.call-start = ((), (), s32[]{:S(2)}) async-start(), calls=%async_computation.33 | async-start | bytes 1081344 | tf_op jit(solution)/shard_map/reduce_scatter | solution.py:520
  1541.1 1348.4 %reduce-scatter.39.cloned.1.call-start = ((), (), s32[]{:S(2)}) async-start(), calls=%async_computation.35 | async-start | bytes 2162688 | tf_op jit(solution)/shard_map/reduce_scatter | solution.py:523
  1546.8 1446.9 %reduce-scatter.33.cloned.1.call-start = ((), (), s32[]{:S(2)}) async-start(), calls=%async_computation.32 | async-start | bytes 3244032 | tf_op jit(solution)/shard_map/reduce_scatter | solution.py:519
  1553.5 387.4 %copy-start.101 = (f32[1024]{0:T(1024)S(1)}, f32[1024]{0:T(1024)}, u32[]{:S(2)}) copy-start(f32[1024]{0:T(1024)} %copy-done.100) | copy-start | bytes 12292
  1553.6 387.4 %copy-start.28 = (bf16[1024,512]{1,0:T(8,128)(2,1)S(1)}, bf16[1024,512]{1,0:T(8,128)(2,1)}, u32[]{:S(2)}) copy-start(bf16[1024,512]{1,0:T(8,128)(2,1)} %gather_fusion.7) | copy-start | bytes 3145732
  (205 other events, 3137.3 us)
Sparse Core Ops, SparseCore 0:
  10.2 52.1 all-gather.10
  64.5 47.8 all-gather.12
  115.3 53.6 all-gather.14
  171.7 52.6 all-gather.16
  226.4 49.4 all-gather.18
  277.9 49.1 all-gather.20
  1406.5 136.0 reduce-scatter.46
  1545.5 129.7 reduce-scatter.48
  1678.1 129.8 reduce-scatter.44
  1810.2 129.3 reduce-scatter.50
  1942.3 129.3 reduce-scatter.42
  2075.5 63.5 reduce-scatter.30
  2143.0 66.5 reduce-scatter.28
  2213.4 66.7 reduce-scatter.26
  2283.9 66.6 reduce-scatter.24
  2353.4 133.7 reduce-scatter.40
  2489.8 130.6 reduce-scatter.36
  2623.3 130.6 reduce-scatter.34
  2756.8 132.6 reduce-scatter.38
  2896.2 97.4 reduce-scatter.32
where the time goes:
time: 3010 us; the launch traced here: 3000 us
  waiting for transfers between devices  1460 us (49%)
  local copies, waits for them, and re-layouts  592 us (20%)
  blocking collectives  475 us (16%)
  matrix products  286 us (10%)
  other arithmetic  140 us (5%)
    unnamed x25, waiting for transfers between devices  510 us
    unnamed x446, local copies, waits for them, and re-layouts  258 us
    reduce_scatter x2, waiting for transfers between devices, sum_experts(): lax.psum_scatter(grad_in.astype(jnp.bfloat16), 'dp', scatter_dimension=1,...  137 us
    reduce_scatter x1, waiting for transfers between devices, body(): lax.psum_scatter(dense_grads[7], ('dp', 'expert'), scatter_dimension=0, t...  136 us
    reduce_scatter x2, waiting for transfers between devices, sum_experts(): lax.psum_scatter(grad_out.astype(jnp.bfloat16), 'dp', scatter_dimension=1...  135 us
    reduce_scatter x1, waiting for transfers between devices, body(): lax.psum_scatter(dense_grads[11], ('dp', 'expert'), scatter_dimension=0,...  135 us
    reduce_scatter x1, waiting for transfers between devices, body(): lax.psum_scatter(dense_grads[4], ('dp', 'expert'), scatter_dimension=0, t...  133 us
    reduce_scatter x1, waiting for transfers between devices, body(): lax.psum_scatter(dense_grads[6], ('dp', 'expert'), scatter_dimension=0, t...  133 us
  transfers between devices with their start and end apart: 27, of which 17 were waited for; matrix products, arithmetic and copies ran while one was open for 19% of the time, Pallas kernels for 0%

commit v1 on v0

v1 whole, which is shorter than its diff:
```python
import functools
import math

import jax
import jax.numpy as jnp
import numpy as np
from jax import lax
from jax.experimental import pallas as pl
from jax.experimental.pallas import tpu as pltpu
from jax.sharding import PartitionSpec as P

H = 8
TILE = 128
epsilon = 1e-05
masked_score = -1e30
BOTH = ("dp", "expert")
f32 = jnp.float32
bf16 = jnp.bfloat16

VMEM = pl.BlockSpec(memory_space=pltpu.VMEM)
SMEM = pl.BlockSpec(memory_space=pltpu.SMEM)


def shape_of(dims, kind):
    return jax.ShapeDtypeStruct(dims, kind)


def run(kernel, args, in_specs, outs, scratch=(), flops=0, name=None):
    moved = sum(math.prod(a.shape) * a.dtype.itemsize for a in list(args) + list(outs))
    return pl.pallas_call(
        kernel,
        out_shape=outs,
        in_specs=in_specs,
        out_specs=[VMEM] * len(outs),
        scratch_shapes=list(scratch),
        compiler_params=pltpu.CompilerParams(vmem_limit_bytes=56 * 2**20),
        cost_estimate=pl.CostEstimate(flops=flops, bytes_accessed=moved, transcendentals=0),
        name=name,
    )(*args)


def dot(left, right):
    return lax.dot_general(left, right, (((1,), (0,)), ((), ())), preferred_element_type=f32)


def dot_t(left, right):
    return lax.dot_general(left, right, (((1,), (1,)), ((), ())), preferred_element_type=f32)


def t_dot(left, right):
    return lax.dot_general(left, right, (((0,), (0,)), ((), ())), preferred_element_type=f32)


def iota(dims, axis):
    return lax.broadcasted_iota(jnp.int32, dims, axis)


def normalize(values):
    center = values - jnp.mean(values, axis=-1, keepdims=True)
    spread = jnp.mean(center * center, axis=-1, keepdims=True)
    inverse = lax.rsqrt(spread + epsilon)
    return center * inverse, inverse


def normalize_back(standard, inverse, gain, upstream):
    scaled = upstream * gain
    first = jnp.mean(scaled, axis=-1, keepdims=True)
    second = jnp.mean(scaled * standard, axis=-1, keepdims=True)
    return inverse * (scaled - first - standard * second)


def column_sum(values):
    return jnp.sum(values, axis=0, keepdims=True)


def sigmoid(values):
    return 1.0 / (1.0 + jnp.exp(-values))


def loop(count, body):
    def step(index, carry):
        body(index)
        return carry

    lax.fori_loop(0, count, step, 0)


def rows_at(index, size):
    return pl.ds(pl.multiple_of(index * size, size), size)


def slots_kernel(experts, capacity, rows_ref, cols_ref, slot_row_ref, slot_one_ref, slot_two_ref):
    length = rows_ref.shape[1]
    block = 256
    slot_row_ref[...] = jnp.zeros_like(slot_row_ref)
    for half, out_ref in enumerate((slot_one_ref, slot_two_ref)):
        chosen = rows_ref[half : half + 1, :]
        onehot = jnp.where(iota((8, length), 0) == chosen, 1.0, 0.0)
        onehot_low = onehot.astype(bf16)
        for index in range(length // block):
            earlier = iota((length, block), 0) < iota((length, block), 1) + index * block
            counts = dot(onehot_low, jnp.where(earlier, 1.0, 0.0).astype(bf16))
            span = slice(index * block, (index + 1) * block)
            rank = column_sum(onehot[:, span] * counts).astype(jnp.int32)
            slot_row_ref[half : half + 1, span] = chosen[:, span] * capacity + rank
        picks = cols_ref[:, half : half + 1]
        wide = jnp.where(iota((length, TILE), 1) == picks, 1.0, 0.0)
        wide_low = wide.astype(bf16)
        for index in range(length // block):
            earlier = iota((block, length), 1) < iota((block, length), 0) + index * block
            counts = dot(jnp.where(earlier, 1.0, 0.0).astype(bf16), wide_low)
            span = slice(index * block, (index + 1) * block)
            rank = jnp.sum(wide[span] * counts, axis=1, keepdims=True).astype(jnp.int32)
            out_ref[span, :] = picks[span] * capacity + rank


def find_slots(routes_one, routes_two, experts, capacity):
    length = routes_one.shape[0]
    rows = jnp.concatenate([routes_one.reshape(1, length), routes_two.reshape(1, length)], axis=0)
    cols = jnp.concatenate([routes_one, routes_two], axis=1)
    return run(
        functools.partial(slots_kernel, experts, capacity),
        (rows, cols),
        [VMEM, VMEM],
        [
            shape_of((8, length), jnp.int32),
            shape_of((length, 1), jnp.int32),
            shape_of((length, 1), jnp.int32),
        ],
        flops=8 * length * length * 128,
        name="slots",
    )


def dispatch(low_ref, slot_row, out_ref):
    slots, width = out_ref.shape
    length = low_ref.shape[0]
    block = slots // 4

    def step(index):
        ids = iota((block, length), 0) + index * block
        onehot = jnp.where(ids == slot_row, 1.0, 0.0).astype(bf16)
        out_ref[rows_at(index, block), :] = dot(onehot, low_ref[...]).astype(bf16)

    loop(4, step)


def collect(slot_col, table_ref):
    rows = slot_col.shape[0]
    slots = table_ref.shape[0]
    onehot = jnp.where(iota((rows, slots), 1) == slot_col, 1.0, 0.0).astype(bf16)
    return dot(onehot, table_ref[...])


def route_block(low, embed, router_ref, picks, experts):
    width = low.shape[1]
    logits = dot(low, router_ref[:width, :]) + dot(embed, router_ref[width:, :])
    lanes = iota(logits.shape, 1)
    inside = lanes < experts
    logits = jnp.where(inside, logits, masked_score)
    raised = jnp.where(inside, jnp.exp(logits - jnp.max(logits, axis=1, keepdims=True)), 0.0)
    probs = raised / jnp.sum(raised, axis=1, keepdims=True)
    gate = jnp.sum(jnp.where(lanes == picks, probs, 0.0), axis=1, keepdims=True)
    return probs, gate


BLOCK = 256


def front_kernel(
    experts, hidden_ref, embed_ref, gain_ref, router_ref, picks_ref, slot_row_ref,
    out_ref, probs_ref, gate_ref, low_ref,
):
    length = hidden_ref.shape[0]

    def step(index):
        at = rows_at(index, BLOCK)
        standard, unused = normalize(hidden_ref[at, :].astype(f32))
        low = (standard * gain_ref[0:1, :]).astype(bf16)
        low_ref[at, :] = low
        probs, gate = route_block(low, embed_ref[at, :], router_ref, picks_ref[at, :], experts)
        probs_ref[at, :] = probs
        gate_ref[at, :] = gate

    loop(length // BLOCK, step)
    dispatch(low_ref, slot_row_ref[0:1, :], out_ref)


def expert_forward_kernel(x_ref, in_ref, out_ref, y_ref):
    slots = x_ref.shape[0]
    block = slots // 4

    def step(index):
        at = rows_at(index, block)
        inner = dot(x_ref[at, :], in_ref[...])
        hidden = (inner * sigmoid(inner)).astype(bf16)
        y_ref[at, :] = dot(hidden, out_ref[...]).astype(bf16)

    loop(4, step)


def expert_forward(received, weight_in, weight_out):
    slots, width = received.shape
    return run(
        expert_forward_kernel,
        (received, weight_in, weight_out),
        [VMEM] * 3,
        [shape_of((slots, width), bf16)],
        flops=4 * slots * width * weight_in.shape[1],
        name="experts",
    )[0]


def expert_backward_kernel(x_ref, dy_ref, in_ref, out_ref, dx_ref, hidden_ref, dinner_ref):
    slots = x_ref.shape[0]
    block = slots // 4

    def step(index):
        at = rows_at(index, block)
        inner = dot(x_ref[at, :], in_ref[...])
        gates = sigmoid(inner)
        hidden = inner * gates
        hidden_ref[at, :] = hidden.astype(bf16)
        d_hidden = dot_t(dy_ref[at, :], out_ref[...])
        d_inner = (d_hidden * (gates + hidden * (1.0 - gates))).astype(bf16)
        dinner_ref[at, :] = d_inner
        dx_ref[at, :] = dot_t(d_inner, in_ref[...]).astype(bf16)

    loop(4, step)


def expert_backward(received, d_result, weight_in, weight_out):
    slots, width = received.shape
    inner = weight_in.shape[1]
    return run(
        expert_backward_kernel,
        (received, d_result, weight_in, weight_out),
        [VMEM] * 4,
        [
            shape_of((slots, width), bf16),
            shape_of((slots, inner), bf16),
            shape_of((slots, inner), bf16),
        ],
        flops=6 * slots * width * inner,
        name="experts_back",
    )


def tile_window(starts_ref, first, length):
    count = starts_ref.shape[1]
    low = jnp.int32(0)
    high = jnp.int32(length)
    for k in range(1, count):
        low = jnp.where(starts_ref[0, k] <= first, starts_ref[0, k], low)
    for k in range(count - 1, 0, -1):
        high = jnp.where(starts_ref[0, k] > first + (TILE - 1), starts_ref[0, k], high)
    return low // TILE, (high + (TILE - 1)) // TILE


def numbers_at(starts_ref, positions):
    total = jnp.zeros(positions.shape, jnp.int32)
    for k in range(1, starts_ref.shape[1]):
        total = total + jnp.where(positions >= starts_ref[0, k], 1, 0)
    return total


def same_tile(starts_ref, first_query, first_key):
    rows = numbers_at(starts_ref, iota((TILE, TILE), 0) + first_query)
    cols = numbers_at(starts_ref, iota((TILE, TILE), 1) + first_key)
    return rows == cols


def chunk_rows(query_tile, key_tile, extra, length, mirrored=False):
    tiles = length // TILE
    index = tiles - 1 - query_tile + key_tile + extra - tiles // 2
    index = jnp.clip(index, 0, tiles - 1)
    if mirrored:
        index = tiles - 1 - index
    return pl.ds(pl.multiple_of(index * TILE, TILE), TILE)


def halves(values):
    left = iota(values.shape, 1) < TILE // 2
    zero = jnp.zeros_like(values)
    return jnp.concatenate(
        [jnp.where(left, values, zero), jnp.where(left, zero, values)], axis=0
    )


def skew(values):
    return jnp.concatenate(
        [
            pltpu.roll(values[:TILE], 1, 1, stride=1, stride_axis=0),
            pltpu.roll(values[TILE:], 1, 1, stride=1, stride_axis=0),
        ],
        axis=0,
    )


def mirror(values):
    flip = iota((TILE, TILE), 0) + iota((TILE, TILE), 1) == TILE - 1
    return dot(values, jnp.where(flip, 1.0, 0.0).astype(bf16))


def twice(values):
    return jnp.concatenate([values, values], axis=0)


PAIRS = H // 2


def attend_forward(
    starts_ref, qu_ref, qv_ref, k_ref, v_ref, t_ref, context_ref, logs_ref,
    qum, qvm, scores, rolled, peaks, sums, mixed,
):
    length = qu_ref.shape[0]
    tiles = length // TILE

    def query_step(tile):
        first = tile * TILE
        at = rows_at(tile, TILE)
        low, high = tile_window(starts_ref, first, length)
        chunk = chunk_rows(tile, low, 0, length)
        for p in range(PAIRS):
            lanes = slice(p * TILE, (p + 1) * TILE)
            qum[p] = halves(qu_ref[at, lanes])
            qvm[p] = halves(qv_ref[at, lanes])
            rolled[p] = skew(dot_t(qvm[p], t_ref[chunk, lanes]))
            peaks[p] = jnp.full((2 * TILE, TILE), masked_score, f32)
            sums[p] = jnp.zeros((2 * TILE, TILE), f32)
            mixed[p] = jnp.zeros((2 * TILE, TILE), f32)
        lower = twice(iota((TILE, TILE), 1) <= iota((TILE, TILE), 0))

        def score_step(key, carry):
            keys = rows_at(key, TILE)
            same = twice(same_tile(starts_ref, first, key * TILE))
            chunk = chunk_rows(tile, key, 1, length)
            for p in range(PAIRS):
                lanes = slice(p * TILE, (p + 1) * TILE)
                content = dot_t(qum[p], k_ref[keys, lanes])
                fresh = skew(dot_t(qvm[p], t_ref[chunk, lanes]))
                value = content + jnp.where(lower, rolled[p], fresh)
                value = jnp.where(same, value, masked_score)
                rolled[p] = fresh
                scores[key, p] = value
                peaks[p] = jnp.maximum(peaks[p], value)
            return carry

        lax.fori_loop(low, high, score_step, 0)
        for p in range(PAIRS):
            peaks[p] = jnp.broadcast_to(
                jnp.max(peaks[p], axis=1, keepdims=True), (2 * TILE, TILE)
            )

        def value_step(key, carry):
            keys = rows_at(key, TILE)
            for p in range(PAIRS):
                lanes = slice(p * TILE, (p + 1) * TILE)
                raised = jnp.exp(scores[key, p] - peaks[p])
                sums[p] = sums[p] + raised
                mixed[p] = mixed[p] + dot(raised.astype(bf16), v_ref[keys, lanes])
            return carry

        lax.fori_loop(low, high, value_step, 0)
        left = iota((TILE, TILE), 1) < TILE // 2
        logs = jnp.zeros((TILE, TILE), f32)
        lane = iota((TILE, TILE), 1)
        for p in range(PAIRS):
            lanes = slice(p * TILE, (p + 1) * TILE)
            total = jnp.sum(sums[p], axis=1, keepdims=True)
            result = mixed[p] * (1.0 / total)
            context_ref[at, lanes] = jnp.where(left, result[:TILE], result[TILE:]).astype(bf16)
            logsum = peaks[p] + jnp.log(total)
            logs = jnp.where(lane == 2 * p, logsum[:TILE], logs)
            logs = jnp.where(lane == 2 * p + 1, logsum[TILE:], logs)
        logs_ref[at, :] = logs

    loop(tiles, query_step)


def attend_scratch(length):
    pair = (PAIRS, 2 * TILE, TILE)
    return [
        pltpu.VMEM(pair, bf16),
        pltpu.VMEM(pair, bf16),
        pltpu.VMEM((length // TILE,) + pair, f32),
        pltpu.VMEM(pair, f32),
        pltpu.VMEM(pair, f32),
        pltpu.VMEM(pair, f32),
        pltpu.VMEM(pair, f32),
    ]


def attend_backward(
    starts_ref, qu_ref, qv_ref, k_ref, v_ref, t_ref, mirrored_ref, context_ref, logs_ref, dcontext_ref,
    dm_ref, dk_ref, dv_ref, dt_ref, dbias_ref,
    qum, qvm, dcm, logs, deltas, rolled, unrolled, dqu, dqv,
):
    length, width = qu_ref.shape
    tiles = length // TILE
    scale = 1.0 / math.sqrt(width // H)
    dk_ref[...] = jnp.zeros_like(dk_ref)
    dv_ref[...] = jnp.zeros_like(dv_ref)
    dt_ref[...] = jnp.zeros_like(dt_ref)
    dbias_ref[...] = jnp.zeros_like(dbias_ref)

    def query_step(tile):
        first = tile * TILE
        at = rows_at(tile, TILE)
        low, high = tile_window(starts_ref, first, length)
        chunk = chunk_rows(tile, low, 0, length)
        lanes_all = iota((TILE, TILE), 1)
        logs_tile = logs_ref[at, :]
        for p in range(PAIRS):
            lanes = slice(p * TILE, (p + 1) * TILE)
            qum[p] = halves(qu_ref[at, lanes])
            qvm[p] = halves(qv_ref[at, lanes])
            upstream = halves(dcontext_ref[at, lanes])
            dcm[p] = upstream
            delta = jnp.sum(
                upstream.astype(f32) * twice(context_ref[at, lanes].astype(f32)),
                axis=1,
                keepdims=True,
            )
            deltas[p] = jnp.broadcast_to(delta, (2 * TILE, TILE))
            logs[p, :TILE] = jnp.broadcast_to(logs_tile[:, 2 * p : 2 * p + 1], (TILE, TILE))
            logs[p, TILE:] = jnp.broadcast_to(logs_tile[:, 2 * p + 1 : 2 * p + 2], (TILE, TILE))
            rolled[p] = skew(dot_t(qvm[p], t_ref[chunk, lanes]))
            unrolled[p] = jnp.zeros((2 * TILE, TILE), f32)
            dqu[p] = jnp.zeros((2 * TILE, TILE), f32)
            dqv[p] = jnp.zeros((2 * TILE, TILE), f32)
        lower = twice(iota((TILE, TILE), 1) <= iota((TILE, TILE), 0))

        def step(key, carry):
            keys = rows_at(key, TILE)
            same = twice(same_tile(starts_ref, first, key * TILE))
            before = chunk_rows(tile, key, 0, length, True)
            after = chunk_rows(tile, key, 1, length)
            for p in range(PAIRS):
                lanes = slice(p * TILE, (p + 1) * TILE)
                content = dot_t(qum[p], k_ref[keys, lanes])
                fresh = skew(dot_t(qvm[p], t_ref[after, lanes]))
                value = content + jnp.where(lower, rolled[p], fresh)
                rolled[p] = fresh
                probs = jnp.where(same, jnp.exp(value - logs[p]), 0.0)
                dprobs = dot_t(dcm[p], v_ref[keys, lanes])
                dscores = probs * (dprobs - deltas[p])
                dlow = dscores.astype(bf16)
                dv_ref[keys, lanes] += t_dot(probs.astype(bf16), dcm[p])
                dk_ref[keys, lanes] += t_dot(dlow, qum[p])
                dqu[p] += dot(dlow, k_ref[keys, lanes])
                turned = skew(mirror(dlow))
                moved = jnp.where(lower, turned, unrolled[p]).astype(bf16)
                unrolled[p] = turned
                dqv[p] += dot(moved, mirrored_ref[before, lanes])
                dt_ref[before, lanes] += t_dot(moved, qvm[p])
            return carry

        lax.fori_loop(low, high, step, 0)
        last = chunk_rows(tile, high, 0, length, True)
        left = iota((TILE, TILE), 1) < TILE // 2
        for p in range(PAIRS):
            lanes = slice(p * TILE, (p + 1) * TILE)
            moved = jnp.where(lower, 0.0, unrolled[p]).astype(bf16)
            dq = dqv[p] + dot(moved, mirrored_ref[last, lanes])
            dt_ref[last, lanes] += t_dot(moved, qvm[p])
            part_u = jnp.where(left, dqu[p, :TILE], dqu[p, TILE:]) * scale
            part_v = jnp.where(left, dq[:TILE], dq[TILE:]) * scale
            dbias_ref[0:1, lanes] += column_sum(part_u)
            dbias_ref[1:2, lanes] += column_sum(part_v)
            dm_ref[at, lanes] = (part_u + part_v).astype(bf16)

    loop(tiles, query_step)

    def finish(index):
        at = rows_at(index, BLOCK)
        dm_ref[at, width : 2 * width] = dk_ref[at, :].astype(bf16)
        dm_ref[at, 2 * width : 3 * width] = dv_ref[at, :].astype(bf16)

    loop(length // BLOCK, finish)


def attend_back_scratch():
    pair = (PAIRS, 2 * TILE, TILE)
    return [pltpu.VMEM(pair, bf16) for unused in range(3)] + [
        pltpu.VMEM(pair, f32) for unused in range(6)
    ]


def dense_parts(dense_ref):
    width = dense_ref.shape[0]
    cuts = (0, 3, 4, 5, 6, 8)
    return [
        dense_ref.at[:, pl.ds(start * width, (stop - start) * width)]
        for start, stop in zip(cuts[:-1], cuts[1:])
    ]


EDGE = 16


def middle_kernel(
    starts_ref, hidden_ref, returned_ref, slot_ref, gate_ref, gains_ref, dense_ref, bias_ref,
    taps_ref, sinus_ref,
    h1_ref, h2_ref, qu_ref, qv_ref, k_ref, v_ref, t_ref, context_ref, logs_ref, conv_ref, sums_ref,
    padded, *attend,
):
    length, width = h1_ref.shape
    scale = 1.0 / math.sqrt(width // H)
    in_ref, place_ref, mix_ref, unused, point_ref = dense_parts(dense_ref)

    def queries_step(index):
        at = rows_at(index, BLOCK)
        picked = collect(slot_ref[at, :], returned_ref)
        h1 = hidden_ref[at, :].astype(f32) + 0.5 * gate_ref[at, :] * picked
        h1_ref[at, :] = h1
        standard, unused = normalize(h1)
        low = (standard * gains_ref[1:2, :]).astype(bf16)
        queries = dot(low, in_ref[:, :width])
        qu_ref[at, :] = ((queries + bias_ref[0:1, :]).astype(bf16).astype(f32) * scale).astype(bf16)
        qv_ref[at, :] = ((queries + bias_ref[1:2, :]).astype(bf16).astype(f32) * scale).astype(bf16)
        k_ref[at, :] = dot(low, in_ref[:, width : 2 * width]).astype(bf16)
        v_ref[at, :] = dot(low, in_ref[:, 2 * width :]).astype(bf16)
        t_ref[at, :] = dot(sinus_ref[at, :], place_ref[...]).astype(bf16)

    loop(length // BLOCK, queries_step)
    attend_forward(
        starts_ref, qu_ref, qv_ref, k_ref, v_ref, t_ref, context_ref, logs_ref, *attend
    )
    padded[:EDGE, :] = jnp.zeros((EDGE, width), f32)
    padded[EDGE + length :, :] = jnp.zeros((EDGE, width), f32)

    def gates_step(index):
        at = rows_at(index, BLOCK)
        h2 = h1_ref[at, :] + dot(context_ref[at, :], mix_ref[...])
        h2_ref[at, :] = h2
        standard, unused = normalize(h2)
        low = (standard * gains_ref[2:3, :]).astype(bf16)
        value = dot(low, point_ref[:, :width])
        gates = dot(low, point_ref[:, width:])
        padded[pl.ds(pl.multiple_of(index * BLOCK + EDGE, EDGE), BLOCK), :] = value * sigmoid(gates)

    loop(length // BLOCK, gates_step)
    sums_ref[...] = jnp.zeros_like(sums_ref)
    taps = taps_ref.shape[0] - 1
    reach = taps // 2
    frames = starts_ref[0, starts_ref.shape[1] - 1]

    def conv_step(index):
        first = index * TILE
        place = iota((TILE, TILE), 0) + first
        here = numbers_at(starts_ref, place)
        valid = place < frames
        totals = [jnp.zeros((TILE, TILE), f32) for unused in range(width // TILE)]
        around = pl.ds(pl.multiple_of(first, TILE), TILE + 2 * EDGE)
        for tap in range(taps):
            same = numbers_at(starts_ref, place + (tap - reach)) == here
            for part in range(width // TILE):
                lanes = slice(part * TILE, (part + 1) * TILE)
                near = padded[around, lanes][EDGE + tap - reach : EDGE + tap - reach + TILE]
                totals[part] = totals[part] + jnp.where(same, near, 0.0) * taps_ref[tap : tap + 1, lanes]
        for part in range(width // TILE):
            lanes = slice(part * TILE, (part + 1) * TILE)
            conv_ref[rows_at(index, TILE), lanes] = totals[part]
            kept = jnp.where(valid, totals[part], 0.0)
            sums_ref[0:1, lanes] += column_sum(kept)
            sums_ref[1:2, lanes] += column_sum(kept * kept)

    loop(length // TILE, conv_step)
    sums_ref[2:3, :] = jnp.zeros((1, width), f32) + frames.astype(f32)


def batch_block(conv, totals_ref, back_ref):
    count = totals_ref[2:3, :]
    mean = totals_ref[0:1, :] / count
    variance = totals_ref[1:2, :] / count - mean * mean
    inverse = lax.rsqrt(variance + epsilon)
    centred = conv - mean
    standard = centred * inverse
    batched = standard * back_ref[0:1, :] + back_ref[1:2, :]
    return centred, standard, inverse, batched


def second_kernel(
    experts, h2_ref, conv_ref, totals_ref, batch_ref, point_ref, embed_ref, gains_ref, router_ref,
    picks_ref, slot_row_ref,
    h3_ref, active_ref, out_ref, probs_ref, gate_ref, low_ref,
):
    length = h2_ref.shape[0]

    def step(index):
        at = rows_at(index, BLOCK)
        unused, unused, unused, batched = batch_block(conv_ref[at, :], totals_ref, batch_ref)
        active = (batched * sigmoid(batched)).astype(bf16)
        active_ref[at, :] = active
        h3 = h2_ref[at, :] + dot(active, point_ref[...])
        h3_ref[at, :] = h3
        standard, unused = normalize(h3)
        low = (standard * gains_ref[3:4, :]).astype(bf16)
        low_ref[at, :] = low
        probs, gate = route_block(low, embed_ref[at, :], router_ref, picks_ref[at, :], experts)
        probs_ref[at, :] = probs
        gate_ref[at, :] = gate

    loop(length // BLOCK, step)
    dispatch(low_ref, slot_row_ref[1:2, :], out_ref)


def gate_back(upstream, picked, gate, probs, picks):
    d_gate = 0.5 * jnp.sum(upstream * picked, axis=1, keepdims=True)
    onehot = jnp.where(iota(probs.shape, 1) == picks, 1.0, 0.0)
    return (d_gate * gate) * (onehot - probs)


def turn_kernel(
    h3_ref, returned_ref, slot_ref, gate_ref, probs_ref, picks_ref, slot_row_ref, gains_ref,
    cotangent_ref,
    output_ref, d4_ref, out_ref, dlogits_ref, dgain_ref, low_ref,
):
    length = h3_ref.shape[0]
    dgain_ref[...] = jnp.zeros_like(dgain_ref)

    def step(index):
        at = rows_at(index, BLOCK)
        picked = collect(slot_ref[at, :], returned_ref)
        gate = gate_ref[at, :]
        h4 = h3_ref[at, :] + 0.5 * gate * picked
        standard, inverse = normalize(h4)
        gain = gains_ref[4:5, :]
        output_ref[at, :] = (standard * gain).astype(bf16)
        upstream = cotangent_ref[at, :].astype(f32)
        dgain_ref[0:1, :] += column_sum(upstream * standard)
        d4 = normalize_back(standard, inverse, gain, upstream)
        d4_ref[at, :] = d4
        dlogits_ref[at, :] = gate_back(d4, picked, gate, probs_ref[at, :], picks_ref[at, :])
        low_ref[at, :] = (0.5 * gate * d4).astype(bf16)

    loop(length // BLOCK, step)
    dispatch(low_ref, slot_row_ref[1:2, :], out_ref)


def router_back(dlogits, low, embed, router_ref, drouter_ref):
    width = low.shape[1]
    high = dlogits.astype(bf16)
    rest = (dlogits - high.astype(f32)).astype(bf16)
    d_low = dot_t(high, router_ref[:width, :]) + dot_t(rest, router_ref[:width, :])
    d_embed = dot_t(high, router_ref[width:, :]) + dot_t(rest, router_ref[width:, :])
    turned = jnp.transpose(dlogits)[:8, :]
    turned_high = turned.astype(bf16)
    turned_rest = (turned - turned_high.astype(f32)).astype(bf16)
    drouter_ref[:, :width] += dot(turned_high, low) + dot(turned_rest, low)
    drouter_ref[:, width:] += dot(turned_high, embed) + dot(turned_rest, embed)
    return d_low, d_embed


def second_back_kernel(
    dsent_ref, slot_ref, dlogits_ref, h3_ref, d4_ref, embed_ref, router_ref, gains_ref,
    conv_ref, totals_ref, batch_ref, point_ref,
    d3_ref, dlow_ref, dz_ref, dembed_ref, drouter_ref, small_ref, sums_ref,
):
    length = h3_ref.shape[0]
    drouter_ref[...] = jnp.zeros_like(drouter_ref)
    small_ref[...] = jnp.zeros_like(small_ref)
    sums_ref[...] = jnp.zeros_like(sums_ref)

    def step(index):
        at = rows_at(index, BLOCK)
        standard, inverse = normalize(h3_ref[at, :])
        gain = gains_ref[3:4, :]
        low = (standard * gain).astype(bf16)
        d_low, d_embed = router_back(
            dlogits_ref[at, :], low, embed_ref[at, :], router_ref, drouter_ref
        )
        dembed_ref[at, :] = d_embed
        d_norm = collect(slot_ref[at, :], dsent_ref) + d_low
        small_ref[0:1, :] += column_sum(d_norm * standard)
        d3 = d4_ref[at, :] + normalize_back(standard, inverse, gain, d_norm)
        d3_ref[at, :] = d3
        d3_low = d3.astype(bf16)
        dlow_ref[at, :] = d3_low
        centred, normed, unused, batched = batch_block(conv_ref[at, :], totals_ref, batch_ref)
        gates = sigmoid(batched)
        d_batched = dot_t(d3_low, point_ref[...]) * (gates + batched * gates * (1.0 - gates))
        small_ref[1:2, :] += column_sum(d_batched * normed)
        small_ref[2:3, :] += column_sum(d_batched)
        d_z = d_batched * batch_ref[0:1, :]
        dz_ref[at, :] = d_z
        sums_ref[0:1, :] += column_sum(d_z)
        sums_ref[1:2, :] += column_sum(d_z * centred)

    loop(length // BLOCK, step)


def middle_back_kernel(
    starts_ref, conv_ref, dz_ref, totals_ref, dsums_ref, batch_ref, d3_ref, h1_ref, h2_ref, gains_ref,
    dense_ref, taps_ref, sinus_ref, qu_ref, qv_ref, k_ref, v_ref, t_ref, context_ref, logs_ref,
    returned_ref, slot_ref, gate_ref, probs_ref, picks_ref, slot_row_ref,
    d1_ref, out_ref, dlogits_ref, n2_ref, n3_ref, dg_ref, d2low_ref, dm_ref, dtable_ref, small_ref,
    dtaps_ref,
    padded, linear, dcontext_ref, low_ref, mirrored_ref, *attend,
):
    length, width = h1_ref.shape
    d2_ref = d1_ref
    dt_ref = padded.at[pl.ds(0, length)]
    dk_ref = linear.at[:, pl.ds(0, width)]
    dv_ref = linear.at[:, pl.ds(width, width)]
    in_ref, place_ref, mix_ref, unused, point_ref = dense_parts(dense_ref)
    taps = taps_ref.shape[0] - 1
    reach = taps // 2
    frames = starts_ref[0, starts_ref.shape[1] - 1]
    small_ref[...] = jnp.zeros_like(small_ref)
    dtaps_ref[...] = jnp.zeros_like(dtaps_ref)
    padded[:EDGE, :] = jnp.zeros((EDGE, width), f32)
    padded[EDGE + length :, :] = jnp.zeros((EDGE, width), f32)

    def conv_step(index):
        at = rows_at(index, BLOCK)
        centred, unused, inverse, unused = batch_block(conv_ref[at, :], totals_ref, batch_ref)
        count = totals_ref[2:3, :]
        d_variance = -0.5 * inverse * inverse * inverse * dsums_ref[1:2, :]
        inside = (iota((BLOCK, 1), 0) + index * BLOCK) < frames
        shared = (2.0 * d_variance * centred - inverse * dsums_ref[0:1, :]) / count
        d_conv = inverse * dz_ref[at, :] + jnp.where(inside, shared, 0.0)
        padded[pl.ds(pl.multiple_of(index * BLOCK + EDGE, EDGE), BLOCK), :] = d_conv
        standard, unused = normalize(h2_ref[at, :])
        low = (standard * gains_ref[2:3, :]).astype(bf16)
        n3_ref[at, :] = low
        value = dot(low, point_ref[:, :width])
        linear[at, :width] = value
        linear[at, width:] = sigmoid(dot(low, point_ref[:, width:]))

    loop(length // BLOCK, conv_step)

    def turn_step(index):
        first = index * TILE
        at = rows_at(index, TILE)
        place = iota((TILE, TILE), 0) + first
        here = numbers_at(starts_ref, place)
        parts = width // TILE
        totals = [jnp.zeros((TILE, TILE), f32) for unused in range(parts)]
        values = [linear[at, part * TILE : (part + 1) * TILE] for part in range(parts)]
        gates = [linear[at, width + part * TILE : width + (part + 1) * TILE] for part in range(parts)]
        around = pl.ds(pl.multiple_of(first, TILE), TILE + 2 * EDGE)
        for tap in range(taps):
            same = numbers_at(starts_ref, place - (tap - reach)) == here
            for part in range(parts):
                lanes = slice(part * TILE, (part + 1) * TILE)
                near = padded[around, lanes][EDGE - tap + reach : EDGE - tap + reach + TILE]
                near = jnp.where(same, near, 0.0)
                totals[part] = totals[part] + near * taps_ref[tap : tap + 1, lanes]
                dtaps_ref[tap : tap + 1, lanes] += column_sum(near * (values[part] * gates[part]))
        for part in range(parts):
            lanes = slice(part * TILE, (part + 1) * TILE)
            other = slice(width + part * TILE, width + (part + 1) * TILE)
            gate = gates[part]
            dg_ref[at, lanes] = (totals[part] * gate).astype(bf16)
            dg_ref[at, other] = (totals[part] * values[part] * gate * (1.0 - gate)).astype(bf16)

    loop(length // TILE, turn_step)

    def gates_step(index):
        at = rows_at(index, BLOCK)
        d_norm = dot_t(dg_ref[at, :], point_ref[...])
        standard, inverse = normalize(h2_ref[at, :])
        small_ref[0:1, :] += column_sum(d_norm * standard)
        d2 = d3_ref[at, :] + normalize_back(standard, inverse, gains_ref[2:3, :], d_norm)
        d2_ref[at, :] = d2
        low = d2.astype(bf16)
        d2low_ref[at, :] = low
        dcontext_ref[at, :] = dot_t(low, mix_ref[...]).astype(bf16)
        mirrored_ref[at, :] = dot(sinus_ref[at, :], place_ref[...]).astype(bf16)

    loop(length // BLOCK, gates_step)
    attend_backward(
        starts_ref, qu_ref, qv_ref, k_ref, v_ref, t_ref, mirrored_ref, context_ref, logs_ref, dcontext_ref,
        dm_ref, dk_ref, dv_ref, dt_ref, small_ref.at[pl.ds(8, 8)], *attend
    )

    def queries_step(index):
        at = rows_at(index, BLOCK)
        dtable_ref[at, :] = dt_ref[at, :].astype(bf16)
        d_norm = dot_t(dm_ref[at, :], in_ref[...])
        standard, inverse = normalize(h1_ref[at, :])
        gain = gains_ref[1:2, :]
        n2_ref[at, :] = (standard * gain).astype(bf16)
        small_ref[1:2, :] += column_sum(d_norm * standard)
        d1 = d2_ref[at, :] + normalize_back(standard, inverse, gain, d_norm)
        d1_ref[at, :] = d1
        picked = collect(slot_ref[at, :], returned_ref)
        gate = gate_ref[at, :]
        dlogits_ref[at, :] = gate_back(d1, picked, gate, probs_ref[at, :], picks_ref[at, :])
        low_ref[at, :] = (0.5 * gate * d1).astype(bf16)

    loop(length // BLOCK, queries_step)
    dispatch(low_ref, slot_row_ref[0:1, :], out_ref)


def last_kernel(
    dsent_ref, slot_ref, dlogits_ref, hidden_ref, d1_ref, embed_ref, router_ref, gains_ref, dembed_two_ref,
    d0_ref, dembed_ref, drouter_ref, small_ref,
):
    length = hidden_ref.shape[0]
    drouter_ref[...] = jnp.zeros_like(drouter_ref)
    small_ref[...] = jnp.zeros_like(small_ref)

    def step(index):
        at = rows_at(index, BLOCK)
        standard, inverse = normalize(hidden_ref[at, :].astype(f32))
        gain = gains_ref[0:1, :]
        low = (standard * gain).astype(bf16)
        d_low, d_embed = router_back(
            dlogits_ref[at, :], low, embed_ref[at, :], router_ref, drouter_ref
        )
        dembed_ref[at, :] = d_embed + dembed_two_ref[at, :]
        d_norm = collect(slot_ref[at, :], dsent_ref) + d_low
        small_ref[0:1, :] += column_sum(d_norm * standard)
        d0_ref[at, :] = d1_ref[at, :] + normalize_back(standard, inverse, gain, d_norm)

    loop(length // BLOCK, step)


def gather_small(values, devices):
    spread = jnp.broadcast_to(values[None], (devices,) + values.shape)
    return lax.all_to_all(spread, BOTH, split_axis=0, concat_axis=0, tiled=True)


def sum_small(values, devices):
    return jnp.sum(gather_small(values, devices), axis=0)


def exchange(values, experts):
    slots, width = values.shape
    parted = values.reshape(experts, slots // experts, width)
    moved = lax.all_to_all(parted, "expert", split_axis=0, concat_axis=0, tiled=True)
    return moved.reshape(slots, width)


def rows_product(left, right):
    return lax.dot_general(left, right, (((0,), (0,)), ((), ())), preferred_element_type=f32)


def expert_sums(received, d_result, hidden, d_inner):
    grad_out = rows_product(hidden, d_result).astype(bf16)
    grad_in = rows_product(received, d_inner).astype(bf16)
    return (
        lax.psum_scatter(grad_in, "dp", scatter_dimension=0, tiled=True).astype(f32)[None],
        lax.psum_scatter(grad_out, "dp", scatter_dimension=0, tiled=True).astype(f32)[None],
    )


def sinus_rows(length, width, upward):
    distance = (length // 2 - 1 - np.arange(length)).astype(np.float32)
    distance = distance[::-1] if upward else distance
    rates = np.exp(
        np.arange(width // 2).astype(np.float32) * np.float32(-2.0 * math.log(10000.0) / width)
    ).astype(np.float32)
    angles = (distance[:, None] * rates[None, :]).astype(np.float64)
    table = np.concatenate([np.sin(angles), np.cos(angles)], axis=1)
    return jnp.asarray(table.astype(np.float32)).astype(bf16)


def body(
    devices,
    inputs,
    embedding,
    cotangent,
    first_routes,
    second_routes,
    segment_starts,
    norm_gains,
    first_router,
    second_router,
    first_in,
    first_out,
    second_in,
    second_out,
    attention_in,
    position_weight,
    position_bias,
    attention_out,
    pointwise_in,
    depthwise_kernel,
    batch_gain,
    batch_bias,
    pointwise_out,
):
    length, width = inputs.shape
    experts = first_router.shape[1]
    capacity = 17 * length // (16 * experts)
    slots = experts * capacity
    inner = first_in.shape[2]
    share = norm_gains.shape[1]
    taps = depthwise_kernel.shape[0]
    feats = first_router.shape[0]

    rows = jnp.concatenate(
        [norm_gains, position_bias, depthwise_kernel, batch_gain[None], batch_bias[None]], axis=0
    )
    count = rows.shape[0]
    flat = jnp.concatenate(
        [rows.reshape(-1), first_router.T.reshape(-1), second_router.T.reshape(-1)]
    ).astype(f32)
    small = gather_small(flat, devices)
    rows_all = small[:, : count * share].reshape(devices, count, share)
    rows_all = rows_all.transpose(1, 0, 2).reshape(count, devices * share)
    routers = small[:, count * share :].reshape(devices, 2, experts, feats)
    routers = routers.transpose(1, 2, 0, 3).reshape(2, experts, devices * feats)
    routers = jnp.pad(routers, ((0, 0), (0, TILE - experts), (0, 0)))
    routers = routers.transpose(0, 2, 1).astype(bf16)
    gains = jnp.pad(rows_all[0:5], ((0, 3), (0, 0)))
    bias = jnp.pad(rows_all[5:7], ((0, 6), (0, 0)))
    kernel_taps = jnp.pad(rows_all[7 : 7 + taps], ((0, 1), (0, 0)))
    batch = jnp.pad(rows_all[7 + taps : 9 + taps], ((0, 6), (0, 0)))

    packed = jnp.concatenate(
        [attention_in, position_weight, attention_out, pointwise_out, pointwise_in], axis=1
    )
    dense = lax.all_gather(packed, BOTH, axis=0, tiled=True)
    point_out = dense[:, 5 * width : 6 * width]

    first_pair = (
        lax.all_gather(first_in[0], "dp", axis=0, tiled=True),
        lax.all_gather(first_out[0], "dp", axis=0, tiled=True),
    )
    second_pair = (
        lax.all_gather(second_in[0], "dp", axis=0, tiled=True),
        lax.all_gather(second_out[0], "dp", axis=0, tiled=True),
    )

    slot_rows, slot_one, slot_two = find_slots(first_routes, second_routes, experts, capacity)
    sinus = sinus_rows(length, width, False)
    mirrored = sinus_rows(length, width, True)
    row_low = shape_of((length, width), bf16)
    row_full = shape_of((length, width), f32)
    lane_full = shape_of((length, TILE), f32)
    slot_low = shape_of((slots, width), bf16)
    column = shape_of((length, 1), f32)
    eight = shape_of((8, width), f32)
    low_scratch = pltpu.VMEM((length, width), bf16)

    sent_one, probs_one, gate_one = run(
        functools.partial(front_kernel, experts),
        (inputs, embedding, gains, routers[0], first_routes, slot_rows),
        [VMEM] * 6,
        [slot_low, lane_full, column],
        [low_scratch],
        flops=4 * slots * length * width,
        name="front",
    )
    received_one = exchange(sent_one, experts)
    result_one = expert_forward(received_one, *first_pair)
    returned_one = exchange(result_one, experts)

    edge_scratch = pltpu.VMEM((length + 2 * EDGE, width), f32)
    (
        h1, h2, query_u, query_v, keys, values, table, context, logs, convolved, sums,
    ) = run(
        middle_kernel,
        (
            segment_starts, inputs, returned_one, slot_one, gate_one, gains, dense, bias, kernel_taps, sinus,
        ),
        [SMEM] + [VMEM] * 9,
        [row_full, row_full] + [row_low] * 6 + [lane_full, row_full, eight],
        [edge_scratch] + attend_scratch(length),
        flops=16 * length * length * width,
        name="middle",
    )
    totals = sum_small(sums, devices)

    h3, active, sent_two, probs_two, gate_two = run(
        functools.partial(second_kernel, experts),
        (
            h2, convolved, totals, batch, point_out, embedding, gains, routers[1], second_routes, slot_rows,
        ),
        [VMEM] * 10,
        [row_full, row_low, slot_low, lane_full, column],
        [low_scratch],
        flops=4 * slots * length * width,
        name="second",
    )
    received_two = exchange(sent_two, experts)
    result_two = expert_forward(received_two, *second_pair)
    returned_two = exchange(result_two, experts)

    output, d4, d_sent_two, dlogits_two, dgain_five = run(
        turn_kernel,
        (
            h3, returned_two, slot_two, gate_two, probs_two, second_routes, slot_rows, gains, cotangent,
        ),
        [VMEM] * 9,
        [row_low, row_full, slot_low, lane_full, eight],
        [low_scratch],
        flops=4 * slots * length * width,
        name="turn",
    )
    d_result_two = exchange(d_sent_two, experts)
    d_received_two, hidden_two, d_inner_two = expert_backward(
        received_two, d_result_two, *second_pair
    )
    d_back_two = exchange(d_received_two, experts)
    d_second_in, d_second_out = expert_sums(received_two, d_result_two, hidden_two, d_inner_two)

    router_shape = shape_of((8, 2 * width), f32)
    d3, d3_low, d_z, dembed_two, drouter_two, small_two, dsums_part = run(
        second_back_kernel,
        (
            d_back_two, slot_two, dlogits_two, h3, d4, embedding, routers[1], gains, convolved, totals,
            batch, point_out,
        ),
        [VMEM] * 12,
        [row_full, row_low, row_full, row_full, router_shape, eight, eight],
        flops=4 * slots * length * width,
        name="second_back",
    )
    dsums = sum_small(dsums_part, devices)
    d_pointwise_out = rows_product(active, d3_low)

    (
        d1, d_sent_one, dlogits_one, normed_two, normed_three, d_gates, d2_low, d_mixed, d_table, small_mid,
        d_taps,
    ) = run(
        middle_back_kernel,
        (
            segment_starts, convolved, d_z, totals, dsums, batch, d3, h1, h2, gains, dense, kernel_taps, mirrored, query_u, query_v, keys, values, table, context, logs, returned_one, slot_one, gate_one,
            probs_one, first_routes, slot_rows,
        ),
        [SMEM] + [VMEM] * 25,
        [
            row_full, slot_low, lane_full, row_low, row_low, shape_of((length, 2 * width), bf16), row_low,
            shape_of((length, 3 * width), bf16), row_low, shape_of((16, width), f32),
            shape_of((16, width), f32),
        ],
        [
            edge_scratch, pltpu.VMEM((length, 2 * width), f32), low_scratch, low_scratch, low_scratch,
        ]
        + attend_back_scratch(),
        flops=32 * length * length * width,
        name="middle_back",
    )
    d_result_one = exchange(d_sent_one, experts)
    d_received_one, hidden_one, d_inner_one = expert_backward(received_one, d_result_one, *first_pair)
    d_back_one = exchange(d_received_one, experts)
    d_first_in, d_first_out = expert_sums(received_one, d_result_one, hidden_one, d_inner_one)

    d_start, d_embed, drouter_one, small_one = run(
        last_kernel,
        (
            d_back_one, slot_one, dlogits_one, inputs, d1, embedding, routers[0], gains, dembed_two,
        ),
        [VMEM] * 9,
        [row_full, row_full, router_shape, eight],
        flops=4 * slots * length * width,
        name="last",
    )

    dense_grad = jnp.concatenate(
        [
            rows_product(normed_two, d_mixed),
            rows_product(mirrored, d_table),
            rows_product(context, d2_low),
            d_pointwise_out,
            rows_product(normed_three, d_gates),
        ],
        axis=1,
    ).astype(bf16)
    dense_share = lax.psum_scatter(dense_grad, BOTH, scatter_dimension=0, tiled=True).astype(f32)

    rows_grad = jnp.concatenate(
        [
            small_one[0:1], small_mid[1:2], small_mid[0:1], small_two[0:1], dgain_five[0:1],
            small_mid[8:10], d_taps[:taps], small_two[1:3],
        ],
        axis=0,
    )
    rows_grad = rows_grad.reshape(count, devices, share).transpose(1, 0, 2).reshape(devices, -1)
    routers_grad = jnp.stack([drouter_one[:experts], drouter_two[:experts]])
    routers_grad = routers_grad.reshape(2 * experts, devices, feats).transpose(1, 0, 2).reshape(devices, -1)
    small_grad = jnp.concatenate([rows_grad, routers_grad], axis=1)
    small_share = jnp.sum(
        lax.all_to_all(small_grad, BOTH, split_axis=0, concat_axis=0, tiled=True), axis=0
    )
    rows_share = small_share[: count * share].reshape(count, share)
    routers_share = small_share[count * share :].reshape(2, experts, feats).transpose(0, 2, 1)

    return (
        output,
        d_start,
        d_embed,
        rows_share[0:5],
        routers_share[0],
        routers_share[1],
        d_first_in,
        d_first_out,
        d_second_in,
        d_second_out,
        dense_share[:, : 3 * width],
        dense_share[:, 3 * width : 4 * width],
        rows_share[5:7],
        dense_share[:, 4 * width : 5 * width],
        dense_share[:, 6 * width : 8 * width],
        rows_share[7 : 7 + taps],
        rows_share[7 + taps],
        rows_share[8 + taps],
        dense_share[:, 5 * width : 6 * width],
    )


def solution(mesh):
    split = P(BOTH, None)
    wide = P(None, BOTH)
    bank = P("expert", "dp", None)
    line = P(BOTH)
    in_specs = (
        (split,) * 6
        + (wide, split, split)
        + (bank,) * 4
        + (split, split, wide, split, split, wide, line, line, split)
    )
    out_specs = (
        (split,) * 3
        + (wide, split, split)
        + (bank,) * 4
        + (split, split, wide, split, split, wide, line, line, split)
    )
    return jax.shard_map(
        functools.partial(body, mesh.size),
        mesh=mesh,
        in_specs=in_specs,
        out_specs=out_specs,
        check_vma=False,
    )
```

time: 3010 us -> 876 us (0.29)
  waiting for transfers between devices: 1460 us -> 365 us
  local copies, waits for them, and re-layouts: 592 us -> 42.3 us
  blocking collectives: 475 us -> 107 us
  Pallas kernels: 0 us -> 262 us
  matrix products: 286 us -> 38 us
  other arithmetic: 140 us -> 9.88 us
    reduce_scatter x9 -> x5, waiting for transfers between devices: 914 us -> 207 us  [the longest x1 141 us: body(): lax.psum_scatter(dense_grad, BOTH, scatter_dimension=0, tiled=True)]
    unnamed x25 -> x10, waiting for transfers between devices: 510 us -> 2.53 us
    all_gather x8 -> x0, blocking collectives: 335 us -> none  [the longest x1 47.2 us: body(): lax.all_gather(dense[2], ('dp', 'expert'), axis=0, tiled=True)]
    pallas_call x0 -> x12, Pallas kernels: none -> 262 us  [run(): pl.pallas_call(kernel, out_shape=outs, in_specs=in_specs, out_specs=[VMEM...]
    dot_general x43 -> x0, matrix products: 254 us -> none  [the longest x2 22.3 us: block_scores(): jnp.einsum('qhd,khd->hqk', query_u[start_row:start_row + block], keys, pr...]
    unnamed x446 -> x50, local copies, waits for them, and re-layouts: 258 us -> 12.3 us
    reshape x6 -> x7, local copies, waits for them, and re-layouts: 125 us -> 0.72 us  [the longest x3 0.28 us: body(): routers_grad.reshape(2 * experts, devices, feats).transpose(1, 0, 2)]
    all_gather x6 -> x5, waiting for transfers between devices: 0.07 us -> 101 us  [the longest x1 50.2 us: body(): lax.all_gather(first_out[0], 'dp', axis=0, tiled=True)]
  transfers between devices with their start and end apart: 27 -> 16, of which waited for: 17 -> 12; matrix products, arithmetic and copies ran while one was open for 19% -> 8% of each run, Pallas kernels for 0% -> 26%
where the time goes in v1:
time: 876 us; the launch traced here: 863 us
  waiting for transfers between devices  365 us (42%)
  Pallas kernels  262 us (30%)
  blocking collectives  107 us (12%)
  local copies, waits for them, and re-layouts  42.3 us (5%)
  matrix products  38 us (4%)
  starting transfers between devices  24.7 us (3%)
  between operations  14.9 us (2%)
  other arithmetic  9.88 us (1%)
    pallas_call x12, Pallas kernels, run(): pl.pallas_call(kernel, out_shape=outs, in_specs=in_specs, out_specs=[VMEM...  262 us
    reduce_scatter x1, waiting for transfers between devices, body(): lax.psum_scatter(dense_grad, BOTH, scatter_dimension=0, tiled=True)  141 us
    all_to_all x5, blocking collectives, exchange(): lax.all_to_all(parted, 'expert', split_axis=0, concat_axis=0, tiled=True)  96.3 us
    reduce_scatter x2, waiting for transfers between devices, expert_sums(): lax.psum_scatter(grad_in, 'dp', scatter_dimension=0, tiled=True).astype(f32)  65.3 us
    all_gather x1, waiting for transfers between devices, body(): lax.all_gather(first_out[0], 'dp', axis=0, tiled=True)  50.2 us
    dot_general x9, matrix products, rows_product(): lax.dot_general(left, right, (((0,), (0,)), ((), ())), preferred_element_...  38 us
    all_gather x1, waiting for transfers between devices, body(): dense = lax.all_gather(packed, BOTH, axis=0, tiled=True)  37.1 us
    all_to_all x3, waiting for transfers between devices, gather_small(): return lax.all_to_all(spread, BOTH, split_axis=0, concat_axis=0, tiled=True)  28.5 us
  transfers between devices with their start and end apart: 16, of which 12 were waited for; matrix products, arithmetic and copies ran while one was open for 8% of the time, Pallas kernels for 26%

profile of v1, /device:TPU:0, one launch (start us, length us, event | category | flops | bytes accessed | tf_op | source)
XLA Modules:
  0.0 863.4 jit_solution(11554404343443266538)
XLA Ops:
  18.2 7.3 all-to-all-start
  36.3 7.5 front.1
  43.8 19.5 %all_to_all.68 = bf16[4,272,512]{2,1,0:T(8,128)(2,1)} all-to-all(bf16[4,272,512]{2,1,0:T(8,128)(2,1)} %bitcast.110), channel_id=1, replica_groups=mesh['dp'=8,'expert'=4] {'expert'}, dimensions={0} | all-to-all | bytes 2228224 | tf_op jit(solution)/shard_map/all_to_all | solution.py:834
  63.9 50.2 %all-gather.14.cloned.1.call-done = bf16[1,2048,512]{2,1,0:T(8,128)(2,1)} async-done(((bf16[1,256,512]{2,1,0:T(8,128)(2,1)}), bf16[1,2048,512]{2,1,0:T(8,128)(2,1)}) %all-gather.14.cloned.1.call-update) | async-done | bytes 2097168 | tf_op jit(solution)/shard_map/all_gather | solution.py:923
  114.1 8.9 %experts.2 = bf16[1088,512]{1,0:T(8,128)(2,1)} custom-call(bf16[1088,512]{1,0:T(8,128)(2,1)} %bitcast.92, bf16[512,2048]{1,0:T(8,128)(2,1)} %bitcast.127, bf16[2048,512]{1,0:T(8,128)(2,1)} %bitcast.129), custom_call_target="tpu_custom_call" | custom-call | flops 4563402752 | bytes 6422528 | tf_op jit(solution)/shard_map/experts/pallas_call | solution.py:30
  128.8 12.8 %all-to-all-done.2 = bf16[4,272,512]{2,1,0:T(8,128)(2,1)S(1)} async-done(((bf16[4,272,512]{2,1,0:T(8,128)(2,1)}), bf16[4,272,512]{2,1,0:T(8,128)(2,1)S(1)}, u32[]{:S(2)}, u32[]{:S(2)}) %all-to-all-start.2) | async-done | bytes 1114144 | tf_op jit(solution)/shard_map/all_to_all | solution.py:834
  141.7 37.1 %all-gather.10.cloned.1.call-done.dense_ref = bf16[512,4096]{1,0:T(8,128)(2,1)} async-done(((bf16[16,4096]{1,0:T(8,128)(2,1)}), bf16[512,4096]{1,0:T(8,128)(2,1)}) %all-gather.10.cloned.1.call-update) | async-done | bytes 4194320 | tf_op jit(solution)/shard_map/all_gather | solution.py:918
  178.8 49.1 %middle.1 = (f32[1024,512]{1,0:T(8,128)}, f32[1024,512]{1,0:T(8,128)}, bf16[1024,512]{1,0:T(8,128)(2,1)}, bf16[1024,512]{1,0:T(8,128)(2,1)}, bf16[1024,512]{1,0:...) custom-call(s32[1,5]{1,0:T(1,128)} %starts_ref.3, ...), custom_call_target="tpu_custom_call" | custom-call | flops 8589934592 | bytes 20602900 | tf_op jit(solution)/shard_map/middle/pallas_call | solution.py:30
  236.5 19.3 %all-to-all-done.3 = f32[32,8,512]{2,1,0:T(8,128)S(1)} async-done(((f32[32,8,512]{2,1,0:T(8,128)}), f32[32,8,512]{2,1,0:T(8,128)S(1)}, u32[]{:S(2)}, u32[]{:S(2)}) %all-to-all-start.3) | async-done | bytes 524320 | tf_op jit(solution)/shard_map/all_to_all | solution.py:824
  256.4 10.5 %second.1 = (f32[1024,512]{1,0:T(8,128)}, bf16[1024,512]{1,0:T(8,128)(2,1)}, bf16[1088,512]{1,0:T(8,128)(2,1)}, f32[1024,128]{1,0:T(8,128)}, f32[1024,1]{1,0:T(8,128)}) custom-call(f32[1024,512]{1,0:T(8,128)} %get-tuple-element.78.h2_ref, f32[1024,512]{1,0:T(8,128)} %get-tuple-element.79.conv_ref, f32[8,512]{1,0:T(8,128)} %reduce_sum.27.totals_ref, ...), custom_call_target="tpu_custom_call" | custom-call | flops 2281701376 | bytes 10903552 | tf_op jit(solution)/shard_map/second/pallas_call | solution.py:30
  270.6 13.3 %all-gather.18.cloned.1.call-done = bf16[1,2048,512]{2,1,0:T(8,128)(2,1)} async-done(((bf16[1,256,512]{2,1,0:T(8,128)(2,1)}), bf16[1,2048,512]{2,1,0:T(8,128)(2,1)}) %all-gather.18.cloned.1.call-update) | async-done | bytes 2097168 | tf_op jit(solution)/shard_map/all_gather | solution.py:927
  286.7 8.9 %experts.3 = bf16[1088,512]{1,0:T(8,128)(2,1)} custom-call(bf16[1088,512]{1,0:T(8,128)(2,1)} %bitcast.97, bf16[512,2048]{1,0:T(8,128)(2,1)} %bitcast.131, bf16[2048,512]{1,0:T(8,128)(2,1)} %bitcast.133), custom_call_target="tpu_custom_call" | custom-call | flops 4563402752 | bytes 6422528 | tf_op jit(solution)/shard_map/experts/pallas_call | solution.py:30
  295.6 19.5 %all_to_all.69 = bf16[4,272,512]{2,1,0:T(8,128)(2,1)} all-to-all(bf16[4,272,512]{2,1,0:T(8,128)(2,1)} %bitcast.111), channel_id=1, replica_groups=mesh['dp'=8,'expert'=4] {'expert'}, dimensions={0} | all-to-all | bytes 2228224 | tf_op jit(solution)/shard_map/all_to_all | solution.py:834
  315.0 10.8 %turn.1 = (bf16[1024,512]{1,0:T(8,128)(2,1)}, f32[1024,512]{1,0:T(8,128)}, bf16[1088,512]{1,0:T(8,128)(2,1)}, f32[1024,128]{1,0:T(8,128)}, f32[8,512]{1,0:T(8,128)}) custom-call(f32[1024,512]{1,0:T(8,128)} %get-tuple-element.81.h3_ref, bf16[1088,512]{1,0:T(8,128)(2,1)} %bitcast.104, s32[1024,1]{1,0:T(8,128)} %get-tuple-element.83.slot_ref, ...), custom_call_target="tpu_custom_call" | custom-call | flops 2281701376 | bytes 9646080 | tf_op jit(solution)/shard_map/turn/pallas_call | solution.py:30
  325.9 19.5 %all_to_all.70 = bf16[4,272,512]{2,1,0:T(8,128)(2,1)} all-to-all(bf16[4,272,512]{2,1,0:T(8,128)(2,1)} %bitcast.105), channel_id=1, replica_groups=mesh['dp'=8,'expert'=4] {'expert'}, dimensions={0} | all-to-all | bytes 2228224 | tf_op jit(solution)/shard_map/all_to_all | solution.py:834
  345.4 14.3 %experts_back.2 = (bf16[1088,512]{1,0:T(8,128)(2,1)}, bf16[1088,2048]{1,0:T(8,128)(2,1)}, bf16[1088,2048]{1,0:T(8,128)(2,1)}) custom-call(bf16[1088,512]{1,0:T(8,128)(2,1)} %bitcast.98, bf16[1088,512]{1,0:T(8,128)(2,1)} %bitcast.106, bf16[512,2048]{1,0:T(8,128)(2,1)} %bitcast.132, bf16[2048,512]{1,0:T(8,128)(2,1)} %bitcast.134), custom_call_target="tpu_custom_call" | custom-call | flops 6845104128 | bytes 16449536 | tf_op jit(solution)/shard_map/experts_back/pallas_call | solution.py:30
  359.6 6.5 convolution_convert_fusion.1
  367.4 18.3 %all_to_all.71 = bf16[4,272,512]{2,1,0:T(8,128)(2,1)} all-to-all(bf16[4,272,512]{2,1,0:T(8,128)(2,1)S(1)} %bitcast.103), channel_id=1, replica_groups=mesh['dp'=8,'expert'=4] {'expert'}, dimensions={0} | all-to-all | bytes 2228224 | tf_op jit(solution)/shard_map/all_to_all | solution.py:834
  385.7 12.4 %second_back.1 = (f32[1024,512]{1,0:T(8,128)}, bf16[1024,512]{1,0:T(8,128)(2,1)}, f32[1024,512]{1,0:T(8,128)}, f32[1024,512]{1,0:T(8,128)}, f32[8,1024]{1,0:T(8,...) custom-call(bf16[1088,512]{1,0:T(8,128)(2,1)} %bitcast.89, s32[1024,1]{1,0:T(8,128)} %get-tuple-element.83.slot_ref, ...), custom_call_target="tpu_custom_call" | custom-call | flops 2281701376 | bytes 17223680 | tf_op jit(solution)/shard_map/second_back/pallas_call | solution.py:30
  402.3 6.4 convolution_convert_fusion.2
  409.0 8.8 %all-to-all-done.8 = f32[32,8,512]{2,1,0:T(8,128)S(1)} async-done(((f32[32,8,512]{2,1,0:T(8,128)}), f32[32,8,512]{2,1,0:T(8,128)S(1)}, u32[]{:S(2)}, u32[]{:S(2)}) %all-to-all-start.8) | async-done | bytes 524320 | tf_op jit(solution)/shard_map/all_to_all | solution.py:824
  418.4 112.4 %middle_back.1 = (f32[1024,512]{1,0:T(8,128)}, bf16[1088,512]{1,0:T(8,128)(2,1)}, f32[1024,128]{1,0:T(8,128)}, bf16[1024,512]{1,0:T(8,128)(2,1)}, bf16[1024,512]...) custom-call(s32[1,5]{1,0:T(1,128)} %starts_ref.3, ...), custom_call_target="tpu_custom_call" | custom-call | flops 17179869184 | bytes 37564436 | tf_op jit(solution)/shard_map/middle_back/pallas_call | solution.py:30
  530.8 19.5 %all_to_all.72 = bf16[4,272,512]{2,1,0:T(8,128)(2,1)} all-to-all(bf16[4,272,512]{2,1,0:T(8,128)(2,1)} %bitcast.100), channel_id=1, replica_groups=mesh['dp'=8,'expert'=4] {'expert'}, dimensions={0} | all-to-all | bytes 2228224 | tf_op jit(solution)/shard_map/all_to_all | solution.py:834
  550.3 14.3 %experts_back.3 = (bf16[1088,512]{1,0:T(8,128)(2,1)}, bf16[1088,2048]{1,0:T(8,128)(2,1)}, bf16[1088,2048]{1,0:T(8,128)(2,1)}) custom-call(bf16[1088,512]{1,0:T(8,128)(2,1)} %bitcast.93, bf16[1088,512]{1,0:T(8,128)(2,1)} %bitcast.108, bf16[512,2048]{1,0:T(8,128)(2,1)} %bitcast.128, bf16[2048,512]{1,0:T(8,128)(2,1)} %bitcast.130), custom_call_target="tpu_custom_call" | custom-call | flops 6845104128 | bytes 16449536 | tf_op jit(solution)/shard_map/experts_back/pallas_call | solution.py:30
  564.6 6.5 convolution_convert_fusion.3
  572.3 6.4 convolution_convert_fusion.4
  579.9 5.0 fusion
  599.9 11.4 %all-to-all-done.10 = bf16[4,272,512]{2,1,0:T(8,128)(2,1)S(1)} async-done(((bf16[4,272,512]{2,1,0:T(8,128)(2,1)}), bf16[4,272,512]{2,1,0:T(8,128)(2,1)S(1)}, u32[]{:S(2)}, u32[]{:S(2)}) %all-to-all-start.10) | async-done | bytes 1114144 | tf_op jit(solution)/shard_map/all_to_all | solution.py:834
  612.4 9.4 %last.1 = (f32[1024,512]{1,0:T(8,128)}, f32[1024,512]{1,0:T(8,128)}, f32[8,1024]{1,0:T(8,128)}, f32[8,512]{1,0:T(8,128)}) custom-call(bf16[1088,512]{1,0:T(8,128)(2,1)} %bitcast.88, s32[1024,1]{1,0:T(8,128)} %get-tuple-element.76.slot_ref, f32[1024,128]{1,0:T(8,128)} %get-tuple-element.105.dlogits_ref, bf16[1024,512]{1,0:T(8,128)(2,1)} %hidden_ref.5, ...), custom_call_target="tpu_custom_call" | custom-call | flops 2281701376 | bytes 12455936 | tf_op jit(solution)/shard_map/last/pallas_call | solution.py:30
  624.3 10.4 %all_to_all.73 = f32[32,1,640]{2,1,0:T(1,128)S(1)} all-to-all(f32[32,1,640]{2,1,0:T(1,128)S(1)} %all_to_all.54), channel_id=1, replica_groups=mesh['dp'=8,'expert'=4] {'dp','expert'}, dimensions={0} | all-to-all | bytes 163840 | tf_op jit(solution)/shard_map/all_to_all | solution.py:1080
  643.6 65.3 %reduce-scatter.6.cloned.1.call-done = bf16[64,2048]{1,0:T(8,128)(2,1)} async-done(((bf16[512,2048]{1,0:T(8,128)(2,1)}), bf16[64,2048]{1,0:T(8,128)(2,1)}) %reduce-scatter.6.cloned.1.call-update) | async-done | bytes 262160 | tf_op jit(solution)/shard_map/reduce_scatter | solution.py:846
  710.7 141.2 %reduce-scatter.14.cloned.1.call-done = bf16[16,4096]{1,0:T(8,128)(2,1)} async-done(((bf16[512,4096]{1,0:T(8,128)(2,1)}), bf16[16,4096]{1,0:T(8,128)(2,1)}) %reduce-scatter.14.cloned.1.call-update) | async-done | bytes 131088 | tf_op jit(solution)/shard_map/reduce_scatter | solution.py:1066
  (160 shorter events, 85.7 us)
Async XLA Ops:
  7.2 21.8 %copy-start.11 = (s32[1024,1]{0,1:T(1,128)S(1)}, s32[1024,1]{0,1:T(1,128)}, u32[]{:S(2)}) copy-start(s32[1024,1]{0,1:T(1,128)} %param.27) | copy-start | bytes 12292
  7.2 21.8 %copy-start.12 = (s32[1024,1]{0,1:T(1,128)S(1)}, s32[1024,1]{0,1:T(1,128)}, u32[]{:S(2)}) copy-start(s32[1024,1]{0,1:T(1,128)} %param.28) | copy-start | bytes 12292
  7.2 56.7 %all-gather.12.cloned.1.call-start = ((), (), s32[]{:S(2)}) async-start(), calls=%async_computation.23 | async-start | bytes 2359296 | tf_op jit(solution)/shard_map/all_gather | solution.py:922
  7.9 106.2 %all-gather.14.cloned.1.call-start = ((), (), s32[]{:S(2)}) async-start(), calls=%async_computation.24 | async-start | bytes 2359296 | tf_op jit(solution)/shard_map/all_gather | solution.py:923
  8.7 170.1 %all-gather.10.cloned.1.call-start = ((), (), s32[]{:S(2)}) async-start(), calls=%async_computation.17 | async-start | bytes 4325376 | tf_op jit(solution)/shard_map/all_gather | solution.py:918
  13.1 257.4 %all-gather.16.cloned.1.call-start = ((), (), s32[]{:S(2)}) async-start(), calls=%async_computation.25 | async-start | bytes 2359296 | tf_op jit(solution)/shard_map/all_gather | solution.py:926
  18.2 15.5 %all-to-all-start = ((f32[32,1,640]{2,1,0:T(1,128)}), f32[32,1,640]{2,1,0:T(1,128)S(1)}, u32[]{:S(2)}, u32[]{:S(2)}) async-start(f32[32,1,640]{2,1,0:T(1,128)} %broadcast_in_dim.50), calls=%async_computation | async-start | bytes 163840 | tf_op jit(solution)/shard_map/all_to_all | solution.py:824
  123.0 18.7 %all-to-all-start.2 = ((bf16[4,272,512]{2,1,0:T(8,128)(2,1)}), bf16[4,272,512]{2,1,0:T(8,128)(2,1)S(1)}, u32[]{:S(2)}, u32[]{:S(2)}) async-start(bf16[4,272,512]{2,1,0:T(8,128)(2,1)} %bitcast.101), calls=%async_computation.2 | async-start | bytes 2228224 | tf_op jit(solution)/shard_map/all_to_all | solution.py:834
  126.5 157.4 %all-gather.18.cloned.1.call-start = ((), (), s32[]{:S(2)}) async-start(), calls=%async_computation.26 | async-start | bytes 2359296 | tf_op jit(solution)/shard_map/all_gather | solution.py:927
  141.7 37.1 %copy-start.3 = (bf16[4,272,512]{2,1,0:T(8,128)(2,1)}, bf16[4,272,512]{2,1,0:T(8,128)(2,1)S(1)}, u32[]{:S(2)}) copy-start(bf16[4,272,512]{2,1,0:T(8,128)(2,1)S(1)} %all-to-all-done.2) | copy-start | bytes 3342340
  229.5 26.3 %all-to-all-start.3 = ((f32[32,8,512]{2,1,0:T(8,128)}), f32[32,8,512]{2,1,0:T(8,128)S(1)}, u32[]{:S(2)}, u32[]{:S(2)}) async-start(f32[32,8,512]{2,1,0:T(8,128)} %broadcast_in_dim.51), calls=%async_computation.3 | async-start | bytes 1048576 | tf_op jit(solution)/shard_map/all_to_all | solution.py:824
  267.0 18.7 %all-to-all-start.4 = ((bf16[4,272,512]{2,1,0:T(8,128)(2,1)}), bf16[4,272,512]{2,1,0:T(8,128)(2,1)S(1)}, u32[]{:S(2)}, u32[]{:S(2)}) async-start(bf16[4,272,512]{2,1,0:T(8,128)(2,1)} %bitcast.102), calls=%async_computation.4 | async-start | bytes 2228224 | tf_op jit(solution)/shard_map/all_to_all | solution.py:834
  270.5 367.7 %reduce-scatter.12.cloned.1.call-start = ((), (), s32[]{:S(2)}) async-start(), calls=%async_computation.21 | async-start | bytes 2359296 | tf_op jit(solution)/shard_map/reduce_scatter | solution.py:847
  345.4 14.3 %copy-start.7 = (bf16[4,272,512]{2,1,0:T(8,128)(2,1)S(1)}, bf16[4,272,512]{2,1,0:T(8,128)(2,1)}, u32[]{:S(2)}) copy-start(bf16[4,272,512]{2,1,0:T(8,128)(2,1)} %all_to_all.70) | copy-start | bytes 3342340
  385.7 16.6 %copy-start.5 = (bf16[4,272,512]{2,1,0:T(8,128)(2,1)S(1)}, bf16[4,272,512]{2,1,0:T(8,128)(2,1)}, u32[]{:S(2)}) copy-start(bf16[4,272,512]{2,1,0:T(8,128)(2,1)} %copy-done.4) | copy-start | bytes 3342340
  399.6 18.2 %all-to-all-start.8 = ((f32[32,8,512]{2,1,0:T(8,128)}), f32[32,8,512]{2,1,0:T(8,128)S(1)}, u32[]{:S(2)}, u32[]{:S(2)}) async-start(f32[32,8,512]{2,1,0:T(8,128)} %broadcast_in_dim.52), calls=%async_computation.8 | async-start | bytes 1048576 | tf_op jit(solution)/shard_map/all_to_all | solution.py:824
  402.2 237.8 %reduce-scatter.10.cloned.1.call-start = ((), (), s32[]{:S(2)}) async-start(), calls=%async_computation.20 | async-start | bytes 2359296 | tf_op jit(solution)/shard_map/reduce_scatter | solution.py:846
  408.7 233.0 %reduce-scatter.8.cloned.1.call-start = ((), (), s32[]{:S(2)}) async-start(), calls=%async_computation.19 | async-start | bytes 2359296 | tf_op jit(solution)/shard_map/reduce_scatter | solution.py:847
  550.3 14.3 %copy-start.8 = (bf16[4,272,512]{2,1,0:T(8,128)(2,1)S(1)}, bf16[4,272,512]{2,1,0:T(8,128)(2,1)}, u32[]{:S(2)}) copy-start(bf16[4,272,512]{2,1,0:T(8,128)(2,1)} %all_to_all.72) | copy-start | bytes 3342340
  571.1 137.8 %reduce-scatter.6.cloned.1.call-start = ((), (), s32[]{:S(2)}) async-start(), calls=%async_computation.18 | async-start | bytes 2359296 | tf_op jit(solution)/shard_map/reduce_scatter | solution.py:846
  578.7 273.2 %reduce-scatter.14.cloned.1.call-start = ((), (), s32[]{:S(2)}) async-start(), calls=%async_computation.22 | async-start | bytes 4325376 | tf_op jit(solution)/shard_map/reduce_scatter | solution.py:1066
  579.9 5.1 copy-start.16
  579.9 5.1 copy-start.18
  585.0 1.6 copy-start.20
  585.0 1.6 copy-start.21
  586.6 1.6 copy-start.15
  586.6 1.6 copy-start.19
  588.2 1.6 copy-start.1
  588.2 2.1 copy-start.9
  592.7 5.7 copy-start.14
  592.7 18.7 %all-to-all-start.10 = ((bf16[4,272,512]{2,1,0:T(8,128)(2,1)}), bf16[4,272,512]{2,1,0:T(8,128)(2,1)S(1)}, u32[]{:S(2)}, u32[]{:S(2)}) async-start(bf16[4,272,512]{2,1,0:T(8,128)(2,1)} %bitcast.34), calls=%async_computation.10 | async-start | bytes 2228224 | tf_op jit(solution)/shard_map/all_to_all | solution.py:834
  612.4 11.2 %copy-start.13 = (f32[16,512]{1,0:T(8,128)S(1)}, f32[16,512]{1,0:T(8,128)}, u32[]{:S(2)}) copy-start(f32[16,512]{1,0:T(8,128)} %get-tuple-element.114) | copy-start | bytes 98308
  (6 other events, 6.4 us)
Sparse Core Ops, SparseCore 0:
  10.2 53.6 all-gather.11
  66.0 48.0 all-gather.13
  117.6 61.1 all-gather.9
  180.8 47.8 all-gather.15
  230.6 53.2 all-gather.17
  366.3 68.9 reduce-scatter.11
  438.8 66.7 reduce-scatter.9
  571.2 66.3 reduce-scatter.7
  641.2 67.6 reduce-scatter.5
  711.0 140.8 reduce-scatter.13

commit v2 on v1

--- a/solution.py
+++ b/solution.py
@@ -25,18 +25,19 @@
     return jax.ShapeDtypeStruct(dims, kind)
 
 
-def run(kernel, args, in_specs, outs, scratch=(), flops=0, name=None):
+def run(kernel, args, in_specs, outs, scratch=(), flops=0, name=None, limit=56):
     moved = sum(math.prod(a.shape) * a.dtype.itemsize for a in list(args) + list(outs))
-    return pl.pallas_call(
+    results = pl.pallas_call(
         kernel,
         out_shape=outs,
         in_specs=in_specs,
         out_specs=[VMEM] * len(outs),
         scratch_shapes=list(scratch),
-        compiler_params=pltpu.CompilerParams(vmem_limit_bytes=56 * 2**20),
+        compiler_params=pltpu.CompilerParams(vmem_limit_bytes=limit * 2**20),
         cost_estimate=pl.CostEstimate(flops=flops, bytes_accessed=moved, transcendentals=0),
         name=name,
     )(*args)
+    return list(results)
 
 
 def dot(left, right):
@@ -132,17 +133,22 @@
     )
 
 
-def dispatch(low_ref, slot_row, out_ref):
-    slots, width = out_ref.shape
+PARTS = 4
+
+
+def dispatch(low_ref, slot_row, out_refs):
+    block = out_refs[0].shape[0]
     length = low_ref.shape[0]
-    block = slots // 4
-
-    def step(index):
+    for index, out_ref in enumerate(out_refs):
         ids = iota((block, length), 0) + index * block
         onehot = jnp.where(ids == slot_row, 1.0, 0.0).astype(bf16)
-        out_ref[rows_at(index, block), :] = dot(onehot, low_ref[...]).astype(bf16)
-
-    loop(4, step)
+        out_ref[...] = dot(onehot, low_ref[...]).astype(bf16)
+
+
+def join_blocks(block_refs, whole_ref):
+    block = block_refs[0].shape[0]
+    for index, block_ref in enumerate(block_refs):
+        whole_ref[index * block : (index + 1) * block, :] = block_ref[...]
 
 
 def collect(slot_col, table_ref):
@@ -168,9 +174,9 @@
 
 
 def front_kernel(
-    experts, hidden_ref, embed_ref, gain_ref, router_ref, picks_ref, slot_row_ref,
-    out_ref, probs_ref, gate_ref, low_ref,
+    experts, hidden_ref, embed_ref, gain_ref, router_ref, picks_ref, slot_row_ref, *refs,
 ):
+    out_refs, (probs_ref, gate_ref, low_ref) = refs[:PARTS], refs[PARTS:]
     length = hidden_ref.shape[0]
 
     def step(index):
@@ -183,67 +189,60 @@
         gate_ref[at, :] = gate
 
     loop(length // BLOCK, step)
-    dispatch(low_ref, slot_row_ref[0:1, :], out_ref)
-
-
-def expert_forward_kernel(x_ref, in_ref, out_ref, y_ref):
-    slots = x_ref.shape[0]
-    block = slots // 4
-
-    def step(index):
-        at = rows_at(index, block)
-        inner = dot(x_ref[at, :], in_ref[...])
+    dispatch(low_ref, slot_row_ref[0:1, :], out_refs)
+
+
+def expert_forward_kernel(count, in_ref, out_ref, *refs):
+    for x_ref, y_ref in zip(refs[:count], refs[count:]):
+        inner = dot(x_ref[...], in_ref[...])
         hidden = (inner * sigmoid(inner)).astype(bf16)
-        y_ref[at, :] = dot(hidden, out_ref[...]).astype(bf16)
-
-    loop(4, step)
+        y_ref[...] = dot(hidden, out_ref[...]).astype(bf16)
 
 
 def expert_forward(received, weight_in, weight_out):
-    slots, width = received.shape
+    block, width = received[0].shape
+    count = len(received)
     return run(
-        expert_forward_kernel,
-        (received, weight_in, weight_out),
-        [VMEM] * 3,
-        [shape_of((slots, width), bf16)],
-        flops=4 * slots * width * weight_in.shape[1],
+        functools.partial(expert_forward_kernel, count),
+        (weight_in, weight_out) + tuple(received),
+        [VMEM] * (2 + count),
+        [shape_of((block, width), bf16)] * count,
+        flops=4 * count * block * width * weight_in.shape[1],
         name="experts",
-    )[0]
-
-
-def expert_backward_kernel(x_ref, dy_ref, in_ref, out_ref, dx_ref, hidden_ref, dinner_ref):
-    slots = x_ref.shape[0]
-    block = slots // 4
-
-    def step(index):
-        at = rows_at(index, block)
-        inner = dot(x_ref[at, :], in_ref[...])
+        limit=32,
+    )
+
+
+def expert_backward_kernel(count, in_ref, out_ref, *refs):
+    x_refs, dy_refs, dx_refs = refs[:count], refs[count : 2 * count], refs[2 * count : 3 * count]
+    hidden_refs, dinner_refs = refs[3 * count : 4 * count], refs[4 * count :]
+    for x_ref, dy_ref, dx_ref, hidden_ref, dinner_ref in zip(
+        x_refs, dy_refs, dx_refs, hidden_refs, dinner_refs
+    ):
+        inner = dot(x_ref[...], in_ref[...])
         gates = sigmoid(inner)
         hidden = inner * gates
-        hidden_ref[at, :] = hidden.astype(bf16)
-        d_hidden = dot_t(dy_ref[at, :], out_ref[...])
+        hidden_ref[...] = hidden.astype(bf16)
+        d_hidden = dot_t(dy_ref[...], out_ref[...])
         d_inner = (d_hidden * (gates + hidden * (1.0 - gates))).astype(bf16)
-        dinner_ref[at, :] = d_inner
-        dx_ref[at, :] = dot_t(d_inner, in_ref[...]).astype(bf16)
-
-    loop(4, step)
+        dinner_ref[...] = d_inner
+        dx_ref[...] = dot_t(d_inner, in_ref[...]).astype(bf16)
 
 
 def expert_backward(received, d_result, weight_in, weight_out):
-    slots, width = received.shape
+    block, width = received[0].shape
     inner = weight_in.shape[1]
-    return run(
-        expert_backward_kernel,
-        (received, d_result, weight_in, weight_out),
-        [VMEM] * 4,
-        [
-            shape_of((slots, width), bf16),
-            shape_of((slots, inner), bf16),
-            shape_of((slots, inner), bf16),
-        ],
-        flops=6 * slots * width * inner,
+    count = len(received)
+    outs = run(
+        functools.partial(expert_backward_kernel, count),
+        (weight_in, weight_out) + tuple(received) + tuple(d_result),
+        [VMEM] * (2 + 2 * count),
+        [shape_of((block, width), bf16)] * count + [shape_of((block, inner), bf16)] * (2 * count),
+        flops=6 * count * block * width * inner,
         name="experts_back",
-    )
+        limit=40,
+    )
+    return outs[:count], outs[count : 2 * count], outs[2 * count :]
 
 
 def tile_window(starts_ref, first, length):
@@ -500,11 +499,14 @@
 
 
 def middle_kernel(
-    starts_ref, hidden_ref, returned_ref, slot_ref, gate_ref, gains_ref, dense_ref, bias_ref,
-    taps_ref, sinus_ref,
-    h1_ref, h2_ref, qu_ref, qv_ref, k_ref, v_ref, t_ref, context_ref, logs_ref, conv_ref, sums_ref,
-    padded, *attend,
+    starts_ref, hidden_ref, slot_ref, gate_ref, gains_ref, dense_ref, bias_ref, taps_ref, sinus_ref,
+    *refs,
 ):
+    returned_refs, refs = refs[:PARTS], refs[PARTS:]
+    h1_ref, h2_ref, qu_ref, qv_ref, k_ref, v_ref, t_ref, context_ref, logs_ref = refs[:9]
+    conv_ref, sums_ref, padded, sums, returned_ref = refs[9:14]
+    attend = refs[14:]
+    join_blocks(returned_refs, returned_ref)
     length, width = h1_ref.shape
     scale = 1.0 / math.sqrt(width // H)
     in_ref, place_ref, mix_ref, unused, point_ref = dense_parts(dense_ref)
@@ -541,7 +543,7 @@
         padded[pl.ds(pl.multiple_of(index * BLOCK + EDGE, EDGE), BLOCK), :] = value * sigmoid(gates)
 
     loop(length // BLOCK, gates_step)
-    sums_ref[...] = jnp.zeros_like(sums_ref)
+    sums[...] = jnp.zeros_like(sums)
     taps = taps_ref.shape[0] - 1
     reach = taps // 2
     frames = starts_ref[0, starts_ref.shape[1] - 1]
@@ -563,34 +565,46 @@
             lanes = slice(part * TILE, (part + 1) * TILE)
             conv_ref[rows_at(index, TILE), lanes] = totals[part]
             kept = jnp.where(valid, totals[part], 0.0)
-            sums_ref[0:1, lanes] += column_sum(kept)
-            sums_ref[1:2, lanes] += column_sum(kept * kept)
+            sums[0:1, lanes] += column_sum(kept)
+            sums[1:2, lanes] += column_sum(kept * kept)
 
     loop(length // TILE, conv_step)
-    sums_ref[2:3, :] = jnp.zeros((1, width), f32) + frames.astype(f32)
-
-
-def batch_block(conv, totals_ref, back_ref):
-    count = totals_ref[2:3, :]
-    mean = totals_ref[0:1, :] / count
-    variance = totals_ref[1:2, :] / count - mean * mean
-    inverse = lax.rsqrt(variance + epsilon)
+    copies = sums_ref.shape[0]
+    sums_ref[:, :width] = jnp.broadcast_to(sums[0:1, :], (copies, width))
+    sums_ref[:, width : 2 * width] = jnp.broadcast_to(sums[1:2, :], (copies, width))
+    sums_ref[:, 2 * width :] = jnp.zeros((copies, width), f32) + frames.astype(f32)
+
+
+def batch_totals(totals_ref, width):
+    totals = column_sum(totals_ref[...])
+    count = totals[:, 2 * width :]
+    mean = totals[:, :width] / count
+    variance = totals[:, width : 2 * width] / count - mean * mean
+    return mean, lax.rsqrt(variance + epsilon), count
+
+
+def batch_block(conv, mean, inverse, batch_ref):
     centred = conv - mean
     standard = centred * inverse
-    batched = standard * back_ref[0:1, :] + back_ref[1:2, :]
-    return centred, standard, inverse, batched
+    batched = standard * batch_ref[0:1, :] + batch_ref[1:2, :]
+    return centred, standard, batched
 
 
 def second_kernel(
     experts, h2_ref, conv_ref, totals_ref, batch_ref, point_ref, embed_ref, gains_ref, router_ref,
-    picks_ref, slot_row_ref,
-    h3_ref, active_ref, out_ref, probs_ref, gate_ref, low_ref,
+    picks_ref, slot_row_ref, *refs,
 ):
-    length = h2_ref.shape[0]
+    out_refs, refs = refs[:PARTS], refs[PARTS:]
+    h3_ref, active_ref, probs_ref, gate_ref, stats_ref, low_ref = refs
+    length, width = h2_ref.shape
+    mean, inverse, count = batch_totals(totals_ref, width)
+    stats_ref[0:1, :] = mean
+    stats_ref[1:2, :] = inverse
+    stats_ref[2:3, :] = count
 
     def step(index):
         at = rows_at(index, BLOCK)
-        unused, unused, unused, batched = batch_block(conv_ref[at, :], totals_ref, batch_ref)
+        unused, unused, batched = batch_block(conv_ref[at, :], mean, inverse, batch_ref)
         active = (batched * sigmoid(batched)).astype(bf16)
         active_ref[at, :] = active
         h3 = h2_ref[at, :] + dot(active, point_ref[...])
@@ -603,7 +617,7 @@
         gate_ref[at, :] = gate
 
     loop(length // BLOCK, step)
-    dispatch(low_ref, slot_row_ref[1:2, :], out_ref)
+    dispatch(low_ref, slot_row_ref[1:2, :], out_refs)
 
 
 def gate_back(upstream, picked, gate, probs, picks):
@@ -613,11 +627,12 @@
 
 
 def turn_kernel(
-    h3_ref, returned_ref, slot_ref, gate_ref, probs_ref, picks_ref, slot_row_ref, gains_ref,
-    cotangent_ref,
-    output_ref, d4_ref, out_ref, dlogits_ref, dgain_ref, low_ref,
+    h3_ref, slot_ref, gate_ref, probs_ref, picks_ref, slot_row_ref, gains_ref, cotangent_ref, *refs,
 ):
+    returned_refs, out_refs, refs = refs[:PARTS], refs[PARTS : 2 * PARTS], refs[2 * PARTS :]
+    output_ref, d4_ref, dlogits_ref, dgain_ref, low_ref, returned_ref = refs
     length = h3_ref.shape[0]
+    join_blocks(returned_refs, returned_ref)
     dgain_ref[...] = jnp.zeros_like(dgain_ref)
 
     def step(index):
@@ -636,7 +651,7 @@
         low_ref[at, :] = (0.5 * gate * d4).astype(bf16)
 
     loop(length // BLOCK, step)
-    dispatch(low_ref, slot_row_ref[1:2, :], out_ref)
+    dispatch(low_ref, slot_row_ref[1:2, :], out_refs)
 
 
 def router_back(dlogits, low, embed, router_ref, drouter_ref):
@@ -654,14 +669,17 @@
 
 
 def second_back_kernel(
-    dsent_ref, slot_ref, dlogits_ref, h3_ref, d4_ref, embed_ref, router_ref, gains_ref,
-    conv_ref, totals_ref, batch_ref, point_ref,
-    d3_ref, dlow_ref, dz_ref, dembed_ref, drouter_ref, small_ref, sums_ref,
+    slot_ref, dlogits_ref, h3_ref, d4_ref, embed_ref, router_ref, gains_ref, conv_ref, stats_ref,
+    batch_ref, point_ref, *refs,
 ):
-    length = h3_ref.shape[0]
+    dsent_refs, refs = refs[:PARTS], refs[PARTS:]
+    d3_ref, dlow_ref, dz_ref, dembed_ref, drouter_ref, small_ref, sums_ref, sums, dsent_ref = refs
+    length, width = h3_ref.shape
     drouter_ref[...] = jnp.zeros_like(drouter_ref)
     small_ref[...] = jnp.zeros_like(small_ref)
-    sums_ref[...] = jnp.zeros_like(sums_ref)
+    sums[...] = jnp.zeros_like(sums)
+    join_blocks(dsent_refs, dsent_ref)
+    mean, batch_inverse = stats_ref[0:1, :], stats_ref[1:2, :]
 
     def step(index):
         at = rows_at(index, BLOCK)
@@ -678,27 +696,31 @@
         d3_ref[at, :] = d3
         d3_low = d3.astype(bf16)
         dlow_ref[at, :] = d3_low
-        centred, normed, unused, batched = batch_block(conv_ref[at, :], totals_ref, batch_ref)
+        centred, normed, batched = batch_block(conv_ref[at, :], mean, batch_inverse, batch_ref)
         gates = sigmoid(batched)
         d_batched = dot_t(d3_low, point_ref[...]) * (gates + batched * gates * (1.0 - gates))
         small_ref[1:2, :] += column_sum(d_batched * normed)
         small_ref[2:3, :] += column_sum(d_batched)
         d_z = d_batched * batch_ref[0:1, :]
         dz_ref[at, :] = d_z
-        sums_ref[0:1, :] += column_sum(d_z)
-        sums_ref[1:2, :] += column_sum(d_z * centred)
+        sums[0:1, :] += column_sum(d_z)
+        sums[1:2, :] += column_sum(d_z * centred)
 
     loop(length // BLOCK, step)
+    copies = sums_ref.shape[0]
+    sums_ref[:, :width] = jnp.broadcast_to(sums[0:1, :], (copies, width))
+    sums_ref[:, width:] = jnp.broadcast_to(sums[1:2, :], (copies, width))
 
 
 def middle_back_kernel(
-    starts_ref, conv_ref, dz_ref, totals_ref, dsums_ref, batch_ref, d3_ref, h1_ref, h2_ref, gains_ref,
+    starts_ref, conv_ref, dz_ref, stats_ref, dsums_ref, batch_ref, d3_ref, h1_ref, h2_ref, gains_ref,
     dense_ref, taps_ref, sinus_ref, qu_ref, qv_ref, k_ref, v_ref, t_ref, context_ref, logs_ref,
-    returned_ref, slot_ref, gate_ref, probs_ref, picks_ref, slot_row_ref,
-    d1_ref, out_ref, dlogits_ref, n2_ref, n3_ref, dg_ref, d2low_ref, dm_ref, dtable_ref, small_ref,
-    dtaps_ref,
-    padded, linear, dcontext_ref, low_ref, mirrored_ref, *attend,
+    slot_ref, gate_ref, probs_ref, picks_ref, slot_row_ref, *refs,
 ):
+    returned_refs, out_refs, refs = refs[:PARTS], refs[PARTS : 2 * PARTS], refs[2 * PARTS :]
+    d1_ref, dlogits_ref, n2_ref, n3_ref, dg_ref, d2low_ref, dm_ref, dtable_ref = refs[:8]
+    small_ref, dtaps_ref, padded, linear, dcontext_ref, low_ref, mirrored_ref, returned_ref = refs[8:16]
+    attend = refs[16:]
     length, width = h1_ref.shape
     d2_ref = d1_ref
     dt_ref = padded.at[pl.ds(0, length)]
@@ -710,17 +732,19 @@
     frames = starts_ref[0, starts_ref.shape[1] - 1]
     small_ref[...] = jnp.zeros_like(small_ref)
     dtaps_ref[...] = jnp.zeros_like(dtaps_ref)
+    join_blocks(returned_refs, returned_ref)
+    mean, batch_inverse, count = stats_ref[0:1, :], stats_ref[1:2, :], stats_ref[2:3, :]
+    dsums = column_sum(dsums_ref[...])
+    d_variance = -0.5 * batch_inverse * batch_inverse * batch_inverse * dsums[:, width:]
     padded[:EDGE, :] = jnp.zeros((EDGE, width), f32)
     padded[EDGE + length :, :] = jnp.zeros((EDGE, width), f32)
 
     def conv_step(index):
         at = rows_at(index, BLOCK)
-        centred, unused, inverse, unused = batch_block(conv_ref[at, :], totals_ref, batch_ref)
-        count = totals_ref[2:3, :]
-        d_variance = -0.5 * inverse * inverse * inverse * dsums_ref[1:2, :]
+        centred = conv_ref[at, :] - mean
         inside = (iota((BLOCK, 1), 0) + index * BLOCK) < frames
-        shared = (2.0 * d_variance * centred - inverse * dsums_ref[0:1, :]) / count
-        d_conv = inverse * dz_ref[at, :] + jnp.where(inside, shared, 0.0)
+        shared = (2.0 * d_variance * centred - batch_inverse * dsums[:, :width]) / count
+        d_conv = batch_inverse * dz_ref[at, :] + jnp.where(inside, shared, 0.0)
         padded[pl.ds(pl.multiple_of(index * BLOCK + EDGE, EDGE), BLOCK), :] = d_conv
         standard, unused = normalize(h2_ref[at, :])
         low = (standard * gains_ref[2:3, :]).astype(bf16)
@@ -792,14 +816,16 @@
         low_ref[at, :] = (0.5 * gate * d1).astype(bf16)
 
     loop(length // BLOCK, queries_step)
-    dispatch(low_ref, slot_row_ref[0:1, :], out_ref)
+    dispatch(low_ref, slot_row_ref[0:1, :], out_refs)
 
 
 def last_kernel(
-    dsent_ref, slot_ref, dlogits_ref, hidden_ref, d1_ref, embed_ref, router_ref, gains_ref, dembed_two_ref,
-    d0_ref, dembed_ref, drouter_ref, small_ref,
+    slot_ref, dlogits_ref, hidden_ref, d1_ref, embed_ref, router_ref, gains_ref, dembed_two_ref, *refs,
 ):
+    dsent_refs, refs = refs[:PARTS], refs[PARTS:]
+    d0_ref, dembed_ref, drouter_ref, small_ref, dsent_ref = refs
     length = hidden_ref.shape[0]
+    join_blocks(dsent_refs, dsent_ref)
     drouter_ref[...] = jnp.zeros_like(drouter_ref)
     small_ref[...] = jnp.zeros_like(small_ref)
 
@@ -819,32 +845,168 @@
     loop(length // BLOCK, step)
 
 
-def gather_small(values, devices):
-    spread = jnp.broadcast_to(values[None], (devices,) + values.shape)
-    return lax.all_to_all(spread, BOTH, split_axis=0, concat_axis=0, tiled=True)
-
-
-def sum_small(values, devices):
-    return jnp.sum(gather_small(values, devices), axis=0)
-
-
-def exchange(values, experts):
-    slots, width = values.shape
-    parted = values.reshape(experts, slots // experts, width)
-    moved = lax.all_to_all(parted, "expert", split_axis=0, concat_axis=0, tiled=True)
-    return moved.reshape(slots, width)
+def backward_parts(received, d_result, pair):
+    parts = [
+        expert_backward(received[start:stop], d_result[start:stop], *pair)
+        for start, stop in ((0, 2), (2, 3), (3, PARTS))
+    ]
+    return [sum((part[k] for part in parts), []) for k in range(3)]
+
+
+def gather_small(values):
+    return lax.all_to_all(values, BOTH, split_axis=0, concat_axis=0, tiled=True)
+
+
+def across(values, axis, size, offset):
+    return lax.ppermute(values, axis, [(i, i ^ offset) for i in range(size)])
+
+
+def exchange(blocks, experts):
+    per = experts // PARTS
+    moved = []
+    for index, block in enumerate(blocks):
+        rows = block.shape[0] // per
+        pieces = []
+        for k in range(index * per, (index + 1) * per):
+            piece = block[(k - index * per) * rows : (k - index * per + 1) * rows]
+            pieces.append(across(piece, "expert", experts, k) if k else piece)
+        moved.append(pieces[0] if per == 1 else jnp.concatenate(pieces, axis=0))
+    return moved
+
+
+def ring_place(index, size):
+    return jnp.where(index % 2 == 0, index // 2, size - 1 - index // 2)
+
+
+def ring_member(place, size):
+    place = (place + 2 * size) % size
+    return jnp.where(place < size // 2, 2 * place, 2 * (size - 1 - place) + 1)
+
+
+def ring_pairs(size, forward):
+    order = list(range(0, size, 2)) + list(range(size - 1, 0, -2))
+    step = 1 if forward else -1
+    return [(order[k], order[(k + step) % size]) for k in range(size)]
+
+
+def ring_gather(shards, size):
+    found = []
+    for number, shard in enumerate(shards):
+        ahead = size // 2 if number % 2 == 0 else (size - 1) // 2
+        pieces = [None] * size
+        pieces[0] = shard
+        found.append((pieces, ahead))
+    for step in range(1, size // 2 + 1):
+        for pieces, ahead in found:
+            if step <= ahead:
+                pieces[step] = lax.ppermute(pieces[step - 1], "dp", ring_pairs(size, False))
+            if step <= size - 1 - ahead:
+                pieces[-step] = lax.ppermute(pieces[-step + 1 or 0], "dp", ring_pairs(size, True))
+    return [pieces for pieces, unused in found]
+
+
+def assemble_kernel(count, order_ref, *refs):
+    size = (len(refs) - 1 - count) // count
+    sems = refs[-1]
+    copies = []
+    for number in range(count):
+        target = refs[count * size + number]
+        for offset in range(size):
+            piece = refs[number * size + offset]
+            rows = piece.shape[0]
+            start = pl.multiple_of(order_ref[offset] * rows, 16)
+            copies.append(
+                pltpu.make_async_copy(
+                    piece, target.at[pl.ds(start, rows)], sems.at[number * size + offset]
+                )
+            )
+    for copy in copies:
+        copy.start()
+    for copy in copies:
+        copy.wait()
+
+
+def assemble(shards, size):
+    place = ring_place(lax.axis_index("dp"), size)
+    order = ring_member(place + jnp.arange(size, dtype=jnp.int32), size).astype(jnp.int32)
+    groups = ring_gather(shards, size)
+    count = len(groups)
+    anywhere = pl.BlockSpec(memory_space=pl.ANY)
+    return pl.pallas_call(
+        functools.partial(assemble_kernel, count),
+        out_shape=[
+            shape_of((size * shard.shape[0],) + shard.shape[1:], shard.dtype) for shard in shards
+        ],
+        in_specs=[SMEM] + [anywhere] * (count * size),
+        out_specs=[VMEM] * count,
+        scratch_shapes=[pltpu.SemaphoreType.DMA((count * size,))],
+        name="assemble",
+    )(order, *[piece for pieces in groups for piece in pieces])
+
+
+def keep_half(values, axis, bit, size, offset, mesh_axis):
+    mine = lax.dynamic_index_in_dim(values, bit, axis, keepdims=False)
+    theirs = lax.dynamic_index_in_dim(values, 1 - bit, axis, keepdims=False)
+    arrived = across(theirs, mesh_axis, size, offset)
+    return (mine.astype(f32) + arrived.astype(f32)).astype(bf16)
+
+
+def keep_one(values, place, size, stride, mesh_axis):
+    total = lax.dynamic_index_in_dim(values, place, 0, keepdims=False).astype(f32)
+    for k in range(1, values.shape[0]):
+        theirs = lax.dynamic_index_in_dim(values, place ^ k, 0, keepdims=False)
+        total = total + across(theirs, mesh_axis, size, k * stride).astype(f32)
+    return total
+
+
+def scatter_groups(values, size):
+    me = lax.axis_index("dp")
+    rows, width = values.shape
+    values = values.reshape(size // 2, 2, rows // size, width)
+    values = keep_half(values, 1, me % 2, size, 1, "dp")
+    return keep_one(values, me // 2, size, 2, "dp")
+
+
+def scatter_dense(grad, groups, experts):
+    rows, width = grad.shape
+    me, group = lax.axis_index("expert"), lax.axis_index("dp")
+    rows = rows // (groups * experts)
+    values = grad.reshape(groups // 2, 2, experts // 2, 2, rows, width)
+    values = keep_half(values, 3, me % 2, experts, 1, "expert")
+    values = keep_half(values, 1, group % 2, groups, 1, "dp")
+    values = keep_one(values, group // 2, groups, 2, "dp").astype(bf16)
+    return keep_one(values, me // 2, experts, 2, "expert")
 
 
 def rows_product(left, right):
     return lax.dot_general(left, right, (((0,), (0,)), ((), ())), preferred_element_type=f32)
 
 
-def expert_sums(received, d_result, hidden, d_inner):
-    grad_out = rows_product(hidden, d_result).astype(bf16)
-    grad_in = rows_product(received, d_inner).astype(bf16)
+def expert_grads(received, d_result, hidden, d_inner):
+    received, d_result, hidden, d_inner = (
+        jnp.concatenate(blocks, axis=0) for blocks in (received, d_result, hidden, d_inner)
+    )
+    return rows_product(received, d_inner).astype(bf16), rows_product(hidden, d_result).astype(bf16)
+
+
+def scatter_offloaded(grad_in, grad_out):
     return (
         lax.psum_scatter(grad_in, "dp", scatter_dimension=0, tiled=True).astype(f32)[None],
         lax.psum_scatter(grad_out, "dp", scatter_dimension=0, tiled=True).astype(f32)[None],
+    )
+
+
+def scatter_direct(grad_in, grad_out, size):
+    half_in, half_out = grad_in.shape[1] // 2, grad_out.shape[1] // 2
+    sums = [
+        scatter_groups(part, size)
+        for part in (
+            grad_out[:, :half_out], grad_out[:, half_out:], grad_in[:, :half_in], grad_in[:, half_in:],
+        )
+    ]
+    return (
+        jnp.concatenate(sums[2:], axis=1)[None],
+        jnp.concatenate(sums[:2], axis=1)[None],
     )
 
 
@@ -860,7 +1022,7 @@
 
 
 def body(
-    devices,
+    groups,
     inputs,
     embedding,
     cotangent,
@@ -886,6 +1048,7 @@
 ):
     length, width = inputs.shape
     experts = first_router.shape[1]
+    devices = groups * experts
     capacity = 17 * length // (16 * experts)
     slots = experts * capacity
     inner = first_in.shape[2]
@@ -900,7 +1063,7 @@
     flat = jnp.concatenate(
         [rows.reshape(-1), first_router.T.reshape(-1), second_router.T.reshape(-1)]
     ).astype(f32)
-    small = gather_small(flat, devices)
+    small = gather_small(jnp.broadcast_to(flat[None], (devices,) + flat.shape))
     rows_all = small[:, : count * share].reshape(devices, count, share)
     rows_all = rows_all.transpose(1, 0, 2).reshape(count, devices * share)
     routers = small[:, count * share :].reshape(devices, 2, experts, feats)
@@ -918,37 +1081,43 @@
     dense = lax.all_gather(packed, BOTH, axis=0, tiled=True)
     point_out = dense[:, 5 * width : 6 * width]
 
-    first_pair = (
-        lax.all_gather(first_in[0], "dp", axis=0, tiled=True),
-        lax.all_gather(first_out[0], "dp", axis=0, tiled=True),
-    )
+    first_pair = assemble((first_in[0], first_out[0]), groups)
     second_pair = (
         lax.all_gather(second_in[0], "dp", axis=0, tiled=True),
         lax.all_gather(second_out[0], "dp", axis=0, tiled=True),
     )
 
-    slot_rows, slot_one, slot_two = find_slots(first_routes, second_routes, experts, capacity)
+    me = lax.axis_index("expert")
+    slot_rows, slot_one, slot_two = find_slots(
+        first_routes ^ me, second_routes ^ me, experts, capacity
+    )
     sinus = sinus_rows(length, width, False)
     mirrored = sinus_rows(length, width, True)
     row_low = shape_of((length, width), bf16)
     row_full = shape_of((length, width), f32)
     lane_full = shape_of((length, TILE), f32)
-    slot_low = shape_of((slots, width), bf16)
+    block_low = shape_of((slots // PARTS, width), bf16)
+    slots_scratch = pltpu.VMEM((slots, width), bf16)
+    sums_scratch = pltpu.VMEM((8, width), f32)
     column = shape_of((length, 1), f32)
     eight = shape_of((8, width), f32)
     low_scratch = pltpu.VMEM((length, width), bf16)
 
-    sent_one, probs_one, gate_one = run(
+    *sent_one, probs_one, gate_one = run(
         functools.partial(front_kernel, experts),
         (inputs, embedding, gains, routers[0], first_routes, slot_rows),
         [VMEM] * 6,
-        [slot_low, lane_full, column],
+        [block_low] * PARTS + [lane_full, column],
         [low_scratch],
         flops=4 * slots * length * width,
         name="front",
     )
     received_one = exchange(sent_one, experts)
-    result_one = expert_forward(received_one, *first_pair)
+    result_one = (
+        expert_forward(received_one[:2], *first_pair)
+        + expert_forward(received_one[2:3], *first_pair)
+        + expert_forward(received_one[3:], *first_pair)
+    )
     returned_one = exchange(result_one, experts)
 
     edge_scratch = pltpu.VMEM((length + 2 * EDGE, width), f32)
@@ -957,98 +1126,109 @@
     ) = run(
         middle_kernel,
         (
-            segment_starts, inputs, returned_one, slot_one, gate_one, gains, dense, bias, kernel_taps, sinus,
+            segment_starts, inputs, slot_one, gate_one, gains, dense, bias, kernel_taps, sinus,
+            *returned_one,
         ),
-        [SMEM] + [VMEM] * 9,
-        [row_full, row_full] + [row_low] * 6 + [lane_full, row_full, eight],
-        [edge_scratch] + attend_scratch(length),
+        [SMEM] + [VMEM] * (8 + PARTS),
+        [row_full, row_full] + [row_low] * 6 + [lane_full, row_full, shape_of((devices, 3 * width), f32)],
+        [edge_scratch, sums_scratch, slots_scratch] + attend_scratch(length),
         flops=16 * length * length * width,
         name="middle",
     )
-    totals = sum_small(sums, devices)
-
-    h3, active, sent_two, probs_two, gate_two = run(
+    totals = gather_small(sums)
+
+    *sent_two, h3, active, probs_two, gate_two, stats = run(
         functools.partial(second_kernel, experts),
         (
             h2, convolved, totals, batch, point_out, embedding, gains, routers[1], second_routes, slot_rows,
         ),
         [VMEM] * 10,
-        [row_full, row_low, slot_low, lane_full, column],
+        [block_low] * PARTS + [row_full, row_low, lane_full, column, eight],
         [low_scratch],
         flops=4 * slots * length * width,
         name="second",
     )
     received_two = exchange(sent_two, experts)
-    result_two = expert_forward(received_two, *second_pair)
+    result_two = (
+        expert_forward(received_two[:2], *second_pair)
+        + expert_forward(received_two[2:3], *second_pair)
+        + expert_forward(received_two[3:], *second_pair)
+    )
     returned_two = exchange(result_two, experts)
 
-    output, d4, d_sent_two, dlogits_two, dgain_five = run(
+    *d_sent_two, output, d4, dlogits_two, dgain_five = run(
         turn_kernel,
         (
-            h3, returned_two, slot_two, gate_two, probs_two, second_routes, slot_rows, gains, cotangent,
+            h3, slot_two, gate_two, probs_two, second_routes, slot_rows, gains, cotangent, *returned_two,
         ),
-        [VMEM] * 9,
-        [row_low, row_full, slot_low, lane_full, eight],
-        [low_scratch],
+        [VMEM] * (8 + PARTS),
+        [block_low] * PARTS + [row_low, row_full, lane_full, eight],
+        [low_scratch, slots_scratch],
         flops=4 * slots * length * width,
         name="turn",
     )
     d_result_two = exchange(d_sent_two, experts)
-    d_received_two, hidden_two, d_inner_two = expert_backward(
-        received_two, d_result_two, *second_pair
-    )
+    d_received_two, hidden_two, d_inner_two = backward_parts(received_two, d_result_two, second_pair)
     d_back_two = exchange(d_received_two, experts)
-    d_second_in, d_second_out = expert_sums(received_two, d_result_two, hidden_two, d_inner_two)
+    d_second_in, d_second_out = scatter_offloaded(
+        *expert_grads(received_two, d_result_two, hidden_two, d_inner_two)
+    )
 
     router_shape = shape_of((8, 2 * width), f32)
     d3, d3_low, d_z, dembed_two, drouter_two, small_two, dsums_part = run(
         second_back_kernel,
         (
-            d_back_two, slot_two, dlogits_two, h3, d4, embedding, routers[1], gains, convolved, totals,
-            batch, point_out,
+            slot_two, dlogits_two, h3, d4, embedding, routers[1], gains, convolved, stats, batch, point_out,
+            *d_back_two,
         ),
-        [VMEM] * 12,
-        [row_full, row_low, row_full, row_full, router_shape, eight, eight],
+        [VMEM] * (11 + PARTS),
+        [row_full, row_low, row_full, row_full, router_shape, eight, shape_of((devices, 2 * width), f32)],
+        [sums_scratch, slots_scratch],
         flops=4 * slots * length * width,
         name="second_back",
     )
-    dsums = sum_small(dsums_part, devices)
+    dsums = gather_small(dsums_part)
     d_pointwise_out = rows_product(active, d3_low)
 
     (
-        d1, d_sent_one, dlogits_one, normed_two, normed_three, d_gates, d2_low, d_mixed, d_table, small_mid,
+        *d_sent_one, d1, dlogits_one, normed_two, normed_three, d_gates, d2_low, d_mixed, d_table, small_mid,
         d_taps,
     ) = run(
         middle_back_kernel,
         (
-            segment_starts, convolved, d_z, totals, dsums, batch, d3, h1, h2, gains, dense, kernel_taps, mirrored, query_u, query_v, keys, values, table, context, logs, returned_one, slot_one, gate_one,
-            probs_one, first_routes, slot_rows,
+            segment_starts, convolved, d_z, stats, dsums, batch, d3, h1, h2, gains, dense, kernel_taps, mirrored, query_u, query_v, keys, values, table, context, logs, slot_one, gate_one, probs_one,
+            first_routes, slot_rows, *returned_one,
         ),
-        [SMEM] + [VMEM] * 25,
-        [
-            row_full, slot_low, lane_full, row_low, row_low, shape_of((length, 2 * width), bf16), row_low,
+        [SMEM] + [VMEM] * (24 + PARTS),
+        [block_low] * PARTS
+        + [
+            row_full, lane_full, row_low, row_low, shape_of((length, 2 * width), bf16), row_low,
             shape_of((length, 3 * width), bf16), row_low, shape_of((16, width), f32),
             shape_of((16, width), f32),
         ],
         [
             edge_scratch, pltpu.VMEM((length, 2 * width), f32), low_scratch, low_scratch, low_scratch,
+            slots_scratch,
         ]
         + attend_back_scratch(),
         flops=32 * length * length * width,
         name="middle_back",
     )
     d_result_one = exchange(d_sent_one, experts)
-    d_received_one, hidden_one, d_inner_one = expert_backward(received_one, d_result_one, *first_pair)
+    d_received_one, hidden_one, d_inner_one = backward_parts(received_one, d_result_one, first_pair)
     d_back_one = exchange(d_received_one, experts)
-    d_first_in, d_first_out = expert_sums(received_one, d_result_one, hidden_one, d_inner_one)
+    d_first_in, d_first_out = scatter_direct(
+        *expert_grads(received_one, d_result_one, hidden_one, d_inner_one), groups
+    )
 
     d_start, d_embed, drouter_one, small_one = run(
         last_kernel,
         (
-            d_back_one, slot_one, dlogits_one, inputs, d1, embedding, routers[0], gains, dembed_two,
+            slot_one, dlogits_one, inputs, d1, embedding, routers[0], gains, dembed_two, *d_back_one,
         ),
-        [VMEM] * 9,
+        [VMEM] * (8 + PARTS),
         [row_full, row_full, router_shape, eight],
+        [slots_scratch],
         flops=4 * slots * length * width,
         name="last",
     )
@@ -1063,7 +1243,7 @@
         ],
         axis=1,
     ).astype(bf16)
-    dense_share = lax.psum_scatter(dense_grad, BOTH, scatter_dimension=0, tiled=True).astype(f32)
+    dense_share = scatter_dense(dense_grad, groups, experts)
 
     rows_grad = jnp.concatenate(
         [
@@ -1123,7 +1303,7 @@
         + (split, split, wide, split, split, wide, line, line, split)
     )
     return jax.shard_map(
-        functools.partial(body, mesh.size),
+        functools.partial(body, mesh.shape["dp"]),
         mesh=mesh,
         in_specs=in_specs,
         out_specs=out_specs,

time: 876 us -> 593 us (0.68)
  waiting for transfers between devices: 365 us -> 114 us
  blocking collectives: 107 us -> 0 us
  starting transfers between devices: 24.7 us -> 98.7 us
  local copies, waits for them, and re-layouts: 42.3 us -> 72.3 us
  Pallas kernels: 262 us -> 246 us
  matrix products: 38 us -> 25.1 us
    reduce_scatter x5 -> x2, waiting for transfers between devices: 207 us -> 0.01 us  [the longest x1 0.01 us: scatter_offloaded(): lax.psum_scatter(grad_out, 'dp', scatter_dimension=0, tiled=True)]
    all_to_all x6 -> x0, blocking collectives: 107 us -> none  [the longest x5 96.3 us: exchange(): lax.all_to_all(parted, 'expert', split_axis=0, concat_axis=0, tiled=True)]
    ppermute x0 -> x60, waiting for transfers between devices: none -> 96.3 us  [the longest x46 77.4 us: across(): return lax.ppermute(values, axis, [(i, i ^ offset) for i in range(size)])]
    ppermute x0 -> x60, starting transfers between devices: none -> 75.5 us  [the longest x46 60.2 us: across(): return lax.ppermute(values, axis, [(i, i ^ offset) for i in range(size)])]
    all_gather x2 -> x0, waiting for transfers between devices: 50.9 us -> none  [the longest x1 50.2 us: body(): lax.all_gather(first_out[0], 'dp', axis=0, tiled=True)]
    all_to_all x6 -> x4, waiting for transfers between devices: 54.5 us -> 9.99 us  [the longest x3 9.17 us: gather_small(): return lax.all_to_all(values, BOTH, split_axis=0, concat_axis=0, tiled=True)]
    all_gather x1, waiting for transfers between devices: 37.1 us -> 0.01 us  [body(): dense = lax.all_gather(packed, BOTH, axis=0, tiled=True)]
    pallas_call x12 -> x20, Pallas kernels: 262 us -> 241 us  [run(): pl.pallas_call(kernel, out_shape=outs, in_specs=in_specs, out_specs=[VMEM...]
  transfers between devices with their start and end apart: 16 -> 69, of which waited for: 12 -> 28; matrix products, arithmetic and copies ran while one was open for 8% -> 13% of each run, Pallas kernels for 26% -> 39%
where the time goes in v2:
time: 593 us; the launch traced here: 586 us
  Pallas kernels  246 us (41%)
  waiting for transfers between devices  114 us (19%)
  starting transfers between devices  98.7 us (17%)
  local copies, waits for them, and re-layouts  72.3 us (12%)
  matrix products  25.1 us (4%)
  between operations  15.2 us (3%)
  other arithmetic  14.4 us (2%)
    pallas_call x20, Pallas kernels, run(): pl.pallas_call(kernel, out_shape=outs, in_specs=in_specs, out_specs=[VMEM...  241 us
    ppermute x46, waiting for transfers between devices, across(): return lax.ppermute(values, axis, [(i, i ^ offset) for i in range(size)])  77.4 us
    ppermute x46, starting transfers between devices, across(): return lax.ppermute(values, axis, [(i, i ^ offset) for i in range(size)])  60.2 us
    unnamed x141, local copies, waits for them, and re-layouts  32.5 us
    dot_general x9, matrix products, rows_product(): lax.dot_general(left, right, (((0,), (0,)), ((), ())), preferred_element_...  25.1 us
    all_to_all x3, starting transfers between devices, gather_small(): return lax.all_to_all(values, BOTH, split_axis=0, concat_axis=0, tiled=True)  16.3 us
    ppermute x7, waiting for transfers between devices, ring_gather(): pieces[step] = lax.ppermute(pieces[step - 1], 'dp', ring_pairs(size, False))  12.8 us
  transfers between devices with their start and end apart: 69, of which 28 were waited for; matrix products, arithmetic and copies ran while one was open for 13% of the time, Pallas kernels for 39%

profile of v2, /device:TPU:0, one launch (start us, length us, event | category | flops | bytes accessed | tf_op | source)
XLA Modules:
  0.0 585.5 jit_solution(15117112792763355838)
XLA Ops:
  22.0 6.3 %all-to-all-start = ((f32[32,1,640]{2,1,0:T(1,128)}), f32[32,1,640]{2,1,0:T(1,128)S(1)}, u32[]{:S(2)}, u32[]{:S(2)}) async-start(f32[32,1,640]{2,1,0:T(1,128)} %broadcast_in_dim.32), calls=%async_computation | async-start | bytes 163840 | tf_op jit(solution)/shard_map/all_to_all | solution.py:857
  35.2 3.7 slots.1
  45.7 6.1 %collective-permute-done.5.refs_6_ = bf16[64,2048]{1,0:T(8,128)(2,1)S(1)} collective-permute-done((bf16[64,2048]{1,0:T(8,128)(2,1)S(1)}, bf16[64,2048]{1,0:T(8,128)(2,1)S(1)}, u32[]{:S(2)}, u32[]{:S(2)}) %collective-permute-start.5) | collective-permute-done | bytes 262176 | tf_op jit(solution)/shard_map/ppermute | solution.py:904
  55.2 6.8 %front.1 = (bf16[272,512]{1,0:T(8,128)(2,1)}, bf16[272,512]{1,0:T(8,128)(2,1)}, bf16[272,512]{1,0:T(8,128)(2,1)}, bf16[272,512]{1,0:T(8,128)(2,1)}, f32[1024,128]{1,0:T(8,128)}, /*index=5*/f32[1024,1]{1,0:T(8,128)}) custom-call(bf16[1024,512]{1,0:T(8,128)(2,1)} %hidden_ref.5, bf16[1024,512]{1,0:T(8,128)(2,1)} %embed_ref.7, f32[8,512]{1,0:T(8,128)} %pad.20.gain_ref.gains_ref, ...), custom_call_target="tpu_custom_call" | custom-call | flops 2281701376 | bytes 4055040 | tf_op jit(solution)/shard_map/front/pallas_call | solution.py:30
  66.0 4.9 collective-permute-done.9.refs_11_
  71.5 6.1 %collective-permute-done.3.refs_4_ = bf16[64,2048]{1,0:T(8,128)(2,1)S(1)} collective-permute-done((bf16[64,2048]{1,0:T(8,128)(2,1)S(1)}, bf16[64,2048]{1,0:T(8,128)(2,1)S(1)}, u32[]{:S(2)}, u32[]{:S(2)}) %collective-permute-start.3) | collective-permute-done | bytes 262176 | tf_op jit(solution)/shard_map/ppermute | solution.py:902
  79.0 5.0 assemble.1
  101.5 49.2 %middle.1 = (f32[1024,512]{1,0:T(8,128)}, f32[1024,512]{1,0:T(8,128)}, bf16[1024,512]{1,0:T(8,128)(2,1)}, bf16[1024,512]{1,0:T(8,128)(2,1)}, bf16[1024,512]{1,0:...) custom-call(s32[1,5]{1,0:T(1,128)} %starts_ref.3, ...), custom_call_target="tpu_custom_call" | custom-call | flops 8589934592 | bytes 20783124 | tf_op jit(solution)/shard_map/middle/pallas_call | solution.py:30
  152.5 6.4 %all-to-all-start.1 = ((f32[32,1,1536]{2,1,0:T(1,128)}), f32[32,1,1536]{2,1,0:T(1,128)S(1)}, u32[]{:S(2)}, u32[]{:S(2)}) async-start(f32[32,1,1536]{2,1,0:T(1,128)} %copy.90), calls=%async_computation.1 | async-start | bytes 393216 | tf_op jit(solution)/shard_map/all_to_all | solution.py:857
  163.2 4.7 all-to-all-done.1
  168.6 9.6 %second.1 = (bf16[272,512]{1,0:T(8,128)(2,1)}, bf16[272,512]{1,0:T(8,128)(2,1)}, bf16[272,512]{1,0:T(8,128)(2,1)}, bf16[272,512]{1,0:T(8,128)(2,1)}, f32[1024,51...) custom-call(f32[1024,512]{1,0:T(8,128)} %get-tuple-element.122.h2_ref, ...), custom_call_target="tpu_custom_call" | custom-call | flops 2281701376 | bytes 11100160 | tf_op jit(solution)/shard_map/second/pallas_call | solution.py:30
  180.4 6.0 %all-gather.10.cloned.1.call-done = bf16[1,2048,512]{2,1,0:T(8,128)(2,1)} async-done(((bf16[1,256,512]{2,1,0:T(8,128)(2,1)}), bf16[1,2048,512]{2,1,0:T(8,128)(2,1)}) %all-gather.10.cloned.1.call-update) | async-done | bytes 2097168 | tf_op jit(solution)/shard_map/all_gather | solution.py:1087
  205.4 9.9 %turn.1 = (bf16[272,512]{1,0:T(8,128)(2,1)}, bf16[272,512]{1,0:T(8,128)(2,1)}, bf16[272,512]{1,0:T(8,128)(2,1)}, bf16[272,512]{1,0:T(8,128)(2,1)}, bf16[1024,512...) custom-call(f32[1024,512]{1,0:T(8,128)} %get-tuple-element.125.h3_ref, ...), custom_call_target="tpu_custom_call" | custom-call | flops 2281701376 | bytes 9646080 | tf_op jit(solution)/shard_map/turn/pallas_call | solution.py:30
  218.5 5.6 collective-permute-done.30.refs_1_
  234.3 5.1 experts_back.6
  242.9 4.2 fusion.33
  250.3 6.7 %fusion.36 = bf16[512,2048]{1,0:T(8,128)(2,1)} fusion(bf16[272,2048]{1,0:T(8,128)(2,1)} %copy-done.13, bf16[272,2048]{1,0:T(8,128)(2,1)} %copy-done.14, bf16[272,2048]{1,0:T(8,128)(2,1)} %copy-done.20, bf16[272,2048]{1,0:T(8,128)(2,1)} %copy-done.19, bf16[272,512]{1,0:T(8,128)(2,1)S(1)} %collective-permute-done.24.refs_0_, ...), kind=kOutput, calls=%fused_computation.35 | convolution fusion | flops 2305032192 | bytes 7667712 | tf_op jit(solution)/shard_map/dot_general | solution.py:982
  257.7 6.0 %collective-permute-done.29.refs_2_ = bf16[272,512]{1,0:T(8,128)(2,1)} collective-permute-done((bf16[272,512]{1,0:T(8,128)(2,1)}, bf16[272,512]{1,0:T(8,128)(2,1)}, u32[]{:S(2)}, u32[]{:S(2)}) %collective-permute-start.29) | collective-permute-done | bytes 278560 | tf_op jit(solution)/shard_map/ppermute | solution.py:861
  263.7 12.3 %second_back.1 = (f32[1024,512]{1,0:T(8,128)}, bf16[1024,512]{1,0:T(8,128)(2,1)}, f32[1024,512]{1,0:T(8,128)}, f32[1024,512]{1,0:T(8,128)}, f32[8,1024]{1,0:T(8,...) custom-call(s32[1024,1]{1,0:T(8,128)} %get-tuple-element.126.slot_ref, f32[1024,128]{1,0:T(8,128)} %get-tuple-element.136.dlogits_ref, ...), custom_call_target="tpu_custom_call" | custom-call | flops 2281701376 | bytes 17338368 | tf_op jit(solution)/shard_map/second_back/pallas_call | solution.py:30
  285.1 4.5 all-to-all-done.2
  291.2 110.2 %middle_back.1 = (bf16[272,512]{1,0:T(8,128)(2,1)}, bf16[272,512]{1,0:T(8,128)(2,1)}, bf16[272,512]{1,0:T(8,128)(2,1)}, bf16[272,512]{1,0:T(8,128)(2,1)}, f32[10...) custom-call(s32[1,5]{1,0:T(1,128)} %starts_ref.3, ...), custom_call_target="tpu_custom_call" | custom-call | flops 17179869184 | bytes 37679124 | tf_op jit(solution)/shard_map/middle_back/pallas_call | solution.py:30
  425.2 4.4 experts_back.9
  439.4 9.3 %last.1 = (f32[1024,512]{1,0:T(8,128)}, f32[1024,512]{1,0:T(8,128)}, f32[8,1024]{1,0:T(8,128)}, f32[8,512]{1,0:T(8,128)}) custom-call(s32[1024,1]{1,0:T(8,128)} %get-tuple-element.111.slot_ref, f32[1024,128]{1,0:T(8,128)} %get-tuple-element.159.dlogits_ref, bf16[1024,512]{1,0:T(8,128)(2,1)} %hidden_ref.5, f32[1024,512]{1,0:T(8,128)} %get-tuple-element.160.d1_ref, ...), custom_call_target="tpu_custom_call" | custom-call | flops 2281701376 | bytes 12455936 | tf_op jit(solution)/shard_map/last/pallas_call | solution.py:30
  451.9 5.7 all-to-all-start.3
  468.6 6.1 %collective-permute-done.38 = bf16[4,64,1024]{2,1,0:T(8,128)(2,1)} collective-permute-done((bf16[4,64,1024]{2,1,0:T(8,128)(2,1)}, bf16[4,64,1024]{2,1,0:T(8,128)(2,1)}, u32[]{:S(2)}, u32[]{:S(2)}) %collective-permute-start.38) | collective-permute-done | bytes 524320 | tf_op jit(solution)/shard_map/ppermute | solution.py:861
  477.9 8.0 %collective-permute-done.42 = bf16[4,64,1024]{2,1,0:T(8,128)(2,1)} collective-permute-done((bf16[4,64,1024]{2,1,0:T(8,128)(2,1)}, bf16[4,64,1024]{2,1,0:T(8,128)(2,1)}, u32[]{:S(2)}, u32[]{:S(2)}) %collective-permute-start.42) | collective-permute-done | bytes 524320 | tf_op jit(solution)/shard_map/ppermute | solution.py:861
  490.8 6.2 %collective-permute-done.46 = bf16[4,256,256]{2,1,0:T(8,128)(2,1)S(1)} collective-permute-done((bf16[4,256,256]{2,1,0:T(8,128)(2,1)}, bf16[4,256,256]{2,1,0:T(8,128)(2,1)S(1)}, u32[]{:S(2)}, u32[]{:S(2)}) %collective-permute-start.46) | collective-permute-done | bytes 524320 | tf_op jit(solution)/shard_map/ppermute | solution.py:861
  514.7 6.9 %collective-permute-start.49 = (bf16[256,256]{1,0:T(8,128)(2,1)S(1)}, bf16[256,256]{1,0:T(8,128)(2,1)S(1)}, u32[]{:S(2)}, u32[]{:S(2)}) collective-permute-start(bf16[256,256]{1,0:T(8,128)(2,1)S(1)} %get-tuple-element.213), channel_id=1, source_target_pairs={{0,24},{4,28},{8,16},{12,20},{16,8},{20,12},{24,0},{28,4},{1,25},{... | collective-permute-start | bytes 393224 | tf_op jit(solution)/shard_map/ppermute | solution.py:861
  524.8 5.4 collective-permute-done.44
  536.6 6.8 %collective-permute-start.58 = (bf16[2,16,4096]{2,1,0:T(8,128)(2,1)S(1)}, bf16[2,16,4096]{2,1,0:T(8,128)(2,1)S(1)}, u32[]{:S(2)}, u32[]{:S(2)}) collective-permute-start(bf16[2,16,4096]{2,1,0:T(8,128)(2,1)S(1)} %get-tuple-element.210), channel_id=1, source_target_pairs={{0,24},{4,28},{8,16},{12,20},{16,8},{20,12},{24,0},{28,4},{1,25},{... | collective-permute-start | bytes 786440 | tf_op jit(solution)/shard_map/ppermute | solution.py:861
  543.5 4.4 collective-permute-done.52
  554.4 13.6 %collective-permute-done.57 = bf16[2,16,4096]{2,1,0:T(8,128)(2,1)S(1)} collective-permute-done((bf16[2,16,4096]{2,1,0:T(8,128)(2,1)S(1)}, bf16[2,16,4096]{2,1,0:T(8,128)(2,1)S(1)}, u32[]{:S(2)}, u32[]{:S(2)}) %collective-permute-start.57) | collective-permute-done | bytes 262176 | tf_op jit(solution)/shard_map/ppermute | solution.py:861
  (382 shorter events, 214.1 us)
Async XLA Ops:
  7.2 94.4 %all-gather.6.cloned.1.call-start = ((), (), s32[]{:S(2)}) async-start(), calls=%async_computation.6 | async-start | bytes 4325376 | tf_op jit(solution)/shard_map/all_gather | solution.py:1081
  11.6 168.8 %all-gather.8.cloned.1.call-start = ((), (), s32[]{:S(2)}) async-start(), calls=%async_computation.9 | async-start | bytes 2359296 | tf_op jit(solution)/shard_map/all_gather | solution.py:1086
  12.4 27.4 %collective-permute-start.4 = (bf16[64,2048]{1,0:T(8,128)(2,1)}, bf16[64,2048]{1,0:T(8,128)(2,1)S(1)}, u32[]{:S(2)}, u32[]{:S(2)}) collective-permute-start(bf16[64,2048]{1,0:T(8,128)(2,1)} %bitcast.202), channel_id=1, source_target_pairs={{0,8},{8,16},{16,24},{24,28},{28,20},{20,12},{12,4},{4,0},{1,9},{9... | collective-permute-start | bytes 786440 | tf_op jit(solution)/shard_map/ppermute | solution.py:904
  15.4 16.1 %collective-permute-start.10 = (bf16[256,512]{1,0:T(8,128)(2,1)}, bf16[256,512]{1,0:T(8,128)(2,1)S(1)}, u32[]{:S(2)}, u32[]{:S(2)}) collective-permute-start(bf16[256,512]{1,0:T(8,128)(2,1)} %bitcast.205), channel_id=1, source_target_pairs={{0,8},{8,16},{16,24},{24,28},{28,20},{20,12},{12,4},{4,0},{1,9},{9... | collective-permute-start | bytes 786440 | tf_op jit(solution)/shard_map/ppermute | solution.py:904
  17.5 24.1 %collective-permute-start.7 = (bf16[256,512]{1,0:T(8,128)(2,1)}, bf16[256,512]{1,0:T(8,128)(2,1)S(1)}, u32[]{:S(2)}, u32[]{:S(2)}) collective-permute-start(bf16[256,512]{1,0:T(8,128)(2,1)} %bitcast.206), channel_id=1, source_target_pairs={{0,4},{8,0},{16,8},{24,16},{28,24},{20,28},{12,20},{4,12},{1,5},{9... | collective-permute-start | bytes 786440 | tf_op jit(solution)/shard_map/ppermute | solution.py:902
  22.0 17.0 %all-to-all-start = ((f32[32,1,640]{2,1,0:T(1,128)}), f32[32,1,640]{2,1,0:T(1,128)S(1)}, u32[]{:S(2)}, u32[]{:S(2)}) async-start(f32[32,1,640]{2,1,0:T(1,128)} %broadcast_in_dim.32), calls=%async_computation | async-start | bytes 163840 | tf_op jit(solution)/shard_map/all_to_all | solution.py:857
  28.3 158.1 %all-gather.10.cloned.1.call-start = ((), (), s32[]{:S(2)}) async-start(), calls=%async_computation.10 | async-start | bytes 2359296 | tf_op jit(solution)/shard_map/all_gather | solution.py:1087
  42.0 21.6 %collective-permute-start.2 = (bf16[64,2048]{1,0:T(8,128)(2,1)S(1)}, bf16[64,2048]{1,0:T(8,128)(2,1)S(1)}, u32[]{:S(2)}, u32[]{:S(2)}) collective-permute-start(bf16[64,2048]{1,0:T(8,128)(2,1)S(1)} %collective-permute-done.1.refs_2_), channel_id=1, source_target_pairs={{0,4},{8,0},{16,8},{24,16},{28,24},{20,28},{12,20},{4,12},{1,5},{9... | collective-permute-start | bytes 786440 | tf_op jit(solution)/shard_map/ppermute | solution.py:902
  43.8 21.8 %collective-permute-start.12 = (bf16[256,512]{1,0:T(8,128)(2,1)S(1)}, bf16[256,512]{1,0:T(8,128)(2,1)S(1)}, u32[]{:S(2)}, u32[]{:S(2)}) collective-permute-start(bf16[256,512]{1,0:T(8,128)(2,1)S(1)} %collective-permute-done.11.refs_14_), channel_id=1, source_target_pairs={{0,8},{8,16},{16,24},{24,28},{28,20},{20,12},{12,4},{4,0},{1,9},{9... | collective-permute-start | bytes 786440 | tf_op jit(solution)/shard_map/ppermute | solution.py:904
  54.4 16.5 %collective-permute-start.9 = (bf16[256,512]{1,0:T(8,128)(2,1)S(1)}, bf16[256,512]{1,0:T(8,128)(2,1)S(1)}, u32[]{:S(2)}, u32[]{:S(2)}) collective-permute-start(bf16[256,512]{1,0:T(8,128)(2,1)S(1)} %collective-permute-done.8.refs_10_), channel_id=1, source_target_pairs={{0,4},{8,0},{16,8},{24,16},{28,24},{20,28},{12,20},{4,12},{1,5},{9... | collective-permute-start | bytes 786440 | tf_op jit(solution)/shard_map/ppermute | solution.py:902
  62.1 21.9 %collective-permute-start.16 = (bf16[272,512]{1,0:T(8,128)(2,1)}, bf16[272,512]{1,0:T(8,128)(2,1)S(1)}, u32[]{:S(2)}, u32[]{:S(2)}) collective-permute-start(bf16[272,512]{1,0:T(8,128)(2,1)} %get-tuple-element.120), channel_id=1, source_target_pairs={{0,2},{1,3},{2,0},{3,1},{4,6},{5,7},{6,4},{7,5},{8,10},{9,11},{10,... | collective-permute-start | bytes 835592 | tf_op jit(solution)/shard_map/ppermute | solution.py:861
  65.9 24.6 %collective-permute-start.18 = (bf16[272,512]{1,0:T(8,128)(2,1)}, bf16[272,512]{1,0:T(8,128)(2,1)S(1)}, u32[]{:S(2)}, u32[]{:S(2)}) collective-permute-start(bf16[272,512]{1,0:T(8,128)(2,1)} %get-tuple-element.121), channel_id=1, source_target_pairs={{0,3},{1,2},{2,1},{3,0},{4,7},{5,6},{6,5},{7,4},{8,11},{9,10},{10,... | collective-permute-start | bytes 835592 | tf_op jit(solution)/shard_map/ppermute | solution.py:861
  70.9 21.1 %collective-permute-start.14 = (bf16[272,512]{1,0:T(8,128)(2,1)}, bf16[272,512]{1,0:T(8,128)(2,1)S(1)}, u32[]{:S(2)}, u32[]{:S(2)}) collective-permute-start(bf16[272,512]{1,0:T(8,128)(2,1)} %get-tuple-element.117), channel_id=1, source_target_pairs={{0,1},{1,0},{2,3},{3,2},{4,5},{5,4},{6,7},{7,6},{8,9},{9,8},{10,11... | collective-permute-start | bytes 835592 | tf_op jit(solution)/shard_map/ppermute | solution.py:861
  158.9 416.2 %reduce-scatter.5.cloned.1.call-start = ((), (), s32[]{:S(2)}) async-start(), calls=%async_computation.8 | async-start | bytes 2359296 | tf_op jit(solution)/shard_map/reduce_scatter | solution.py:995
  218.5 15.7 %collective-permute-start.26 = (bf16[272,512]{1,0:T(8,128)(2,1)}, bf16[272,512]{1,0:T(8,128)(2,1)S(1)}, u32[]{:S(2)}, u32[]{:S(2)}) collective-permute-start(bf16[272,512]{1,0:T(8,128)(2,1)} %get-tuple-element.140), channel_id=1, source_target_pairs={{0,1},{1,0},{2,3},{3,2},{4,5},{5,4},{6,7},{7,6},{8,9},{9,8},{10,11... | collective-permute-start | bytes 835592 | tf_op jit(solution)/shard_map/ppermute | solution.py:861
  247.2 329.8 %reduce-scatter.3.cloned.1.call-start = ((), (), s32[]{:S(2)}) async-start(), calls=%async_computation.7 | async-start | bytes 2359296 | tf_op jit(solution)/shard_map/reduce_scatter | solution.py:994
  404.3 20.8 %collective-permute-start.32 = (bf16[272,512]{1,0:T(8,128)(2,1)S(1)}, bf16[272,512]{1,0:T(8,128)(2,1)S(1)}, u32[]{:S(2)}, u32[]{:S(2)}) collective-permute-start(bf16[272,512]{1,0:T(8,128)(2,1)S(1)} %copy-done.53), channel_id=1, source_target_pairs={{0,1},{1,0},{2,3},{3,2},{4,5},{5,4},{6,7},{7,6},{8,9},{9,8},{10,11... | collective-permute-start | bytes 835592 | tf_op jit(solution)/shard_map/ppermute | solution.py:861
  404.3 17.1 %collective-permute-start.34 = (bf16[272,512]{1,0:T(8,128)(2,1)S(1)}, bf16[272,512]{1,0:T(8,128)(2,1)S(1)}, u32[]{:S(2)}, u32[]{:S(2)}) collective-permute-start(bf16[272,512]{1,0:T(8,128)(2,1)S(1)} %copy-done.54), channel_id=1, source_target_pairs={{0,2},{1,3},{2,0},{3,1},{4,6},{5,7},{6,4},{7,5},{8,10},{9,11},{10,... | collective-permute-start | bytes 835592 | tf_op jit(solution)/shard_map/ppermute | solution.py:861
  417.1 84.5 %collective-permute-start.54 = (bf16[4,2,2,16,4096]{4,3,2,0,1:T(8,128)(2,1)}, bf16[4,2,2,16,4096]{4,3,2,0,1:T(8,128)(2,1)}, u32[]{:S(2)}, u32[]{:S(2)}) collective-permute-start(bf16[4,2,2,16,4096]{4,3,2,0,1:T(8,128)(2,1)} %bitcast.163), channel_id=1, source_target_pairs={{0,1},{1,0},{2,3},{3,2},{4,5},{5,4},{6,7},{7,6},{8,9},{9,8},{10,11... | collective-permute-start | bytes 6291464 | tf_op jit(solution)/shard_map/ppermute | solution.py:861
  421.0 17.6 %collective-permute-start.37 = (bf16[272,512]{1,0:T(8,128)(2,1)S(1)}, bf16[272,512]{1,0:T(8,128)(2,1)S(1)}, u32[]{:S(2)}, u32[]{:S(2)}) collective-permute-start(bf16[272,512]{1,0:T(8,128)(2,1)S(1)} %get-tuple-element.169), channel_id=1, source_target_pairs={{0,3},{1,2},{2,1},{3,0},{4,7},{5,6},{6,5},{7,4},{8,11},{9,10},{10,... | collective-permute-start | bytes 835592 | tf_op jit(solution)/shard_map/ppermute | solution.py:861
  461.3 24.6 %collective-permute-start.42 = (bf16[4,64,1024]{2,1,0:T(8,128)(2,1)}, bf16[4,64,1024]{2,1,0:T(8,128)(2,1)}, u32[]{:S(2)}, u32[]{:S(2)}) collective-permute-start(bf16[4,64,1024]{2,1,0:T(8,128)(2,1)} %dynamic-slice_bitcast_fusion.3), channel_id=1, source_target_pairs={{0,4},{4,0},{8,12},{12,8},{16,20},{20,16},{24,28},{28,24},{1,5},{5... | collective-permute-start | bytes 1572872 | tf_op jit(solution)/shard_map/ppermute | solution.py:861
  461.4 35.6 %collective-permute-start.46 = (bf16[4,256,256]{2,1,0:T(8,128)(2,1)}, bf16[4,256,256]{2,1,0:T(8,128)(2,1)S(1)}, u32[]{:S(2)}, u32[]{:S(2)}) collective-permute-start(bf16[4,256,256]{2,1,0:T(8,128)(2,1)} %dynamic-slice_bitcast_fusion.2), channel_id=1, source_target_pairs={{0,4},{4,0},{8,12},{12,8},{16,20},{20,16},{24,28},{28,24},{1,5},{5... | collective-permute-start | bytes 1572872 | tf_op jit(solution)/shard_map/ppermute | solution.py:861
  464.1 44.2 %collective-permute-start.50 = (bf16[4,256,256]{2,1,0:T(8,128)(2,1)}, bf16[4,256,256]{2,1,0:T(8,128)(2,1)S(1)}, u32[]{:S(2)}, u32[]{:S(2)}) collective-permute-start(bf16[4,256,256]{2,1,0:T(8,128)(2,1)} %dynamic-slice_bitcast_fusion.1), channel_id=1, source_target_pairs={{0,4},{4,0},{8,12},{12,8},{16,20},{20,16},{24,28},{28,24},{1,5},{5... | collective-permute-start | bytes 1572872 | tf_op jit(solution)/shard_map/ppermute | solution.py:861
  476.1 34.0 %collective-permute-start.39 = (bf16[64,1024]{1,0:T(8,128)(2,1)S(1)}, bf16[64,1024]{1,0:T(8,128)(2,1)S(1)}, u32[]{:S(2)}, u32[]{:S(2)}) collective-permute-start(bf16[64,1024]{1,0:T(8,128)(2,1)S(1)} %get-tuple-element.218), channel_id=1, source_target_pairs={{0,8},{4,12},{8,0},{12,4},{16,24},{20,28},{24,16},{28,20},{1,9},{5... | collective-permute-start | bytes 393224 | tf_op jit(solution)/shard_map/ppermute | solution.py:861
  485.9 26.7 %collective-permute-start.41 = (bf16[64,1024]{1,0:T(8,128)(2,1)S(1)}, bf16[64,1024]{1,0:T(8,128)(2,1)S(1)}, u32[]{:S(2)}, u32[]{:S(2)}) collective-permute-start(bf16[64,1024]{1,0:T(8,128)(2,1)S(1)} %get-tuple-element.219), channel_id=1, source_target_pairs={{0,24},{4,28},{8,16},{12,20},{16,8},{20,12},{24,0},{28,4},{1,25},{... | collective-permute-start | bytes 393224 | tf_op jit(solution)/shard_map/ppermute | solution.py:861
  504.1 26.2 %collective-permute-start.55 = (bf16[4,2,16,4096]{3,2,1,0:T(8,128)(2,1)S(1)}, bf16[4,2,16,4096]{3,2,1,0:T(8,128)(2,1)S(1)}, u32[]{:S(2)}, u32[]{:S(2)}) collective-permute-start(bf16[4,2,16,4096]{3,2,1,0:T(8,128)(2,1)S(1)} %dynamic-slice_bitcast_fusion), channel_id=1, source_target_pairs={{0,4},{4,0},{8,12},{12,8},{16,20},{20,16},{24,28},{28,24},{1,5},{5... | collective-permute-start | bytes 3145736 | tf_op jit(solution)/shard_map/ppermute | solution.py:861
  512.6 17.5 %collective-permute-start.44 = (bf16[64,1024]{1,0:T(8,128)(2,1)S(1)}, bf16[64,1024]{1,0:T(8,128)(2,1)S(1)}, u32[]{:S(2)}, u32[]{:S(2)}) collective-permute-start(bf16[64,1024]{1,0:T(8,128)(2,1)S(1)} %get-tuple-element.223), channel_id=1, source_target_pairs={{0,16},{4,20},{8,24},{12,28},{16,0},{20,4},{24,8},{28,12},{1,17},{... | collective-permute-start | bytes 393224 | tf_op jit(solution)/shard_map/ppermute | solution.py:861
  512.8 21.1 %collective-permute-start.47 = (bf16[256,256]{1,0:T(8,128)(2,1)S(1)}, bf16[256,256]{1,0:T(8,128)(2,1)S(1)}, u32[]{:S(2)}, u32[]{:S(2)}) collective-permute-start(bf16[256,256]{1,0:T(8,128)(2,1)S(1)} %get-tuple-element.212), channel_id=1, source_target_pairs={{0,8},{4,12},{8,0},{12,4},{16,24},{20,28},{24,16},{28,20},{1,9},{5... | collective-permute-start | bytes 393224 | tf_op jit(solution)/shard_map/ppermute | solution.py:861
  514.7 19.5 %collective-permute-start.49 = (bf16[256,256]{1,0:T(8,128)(2,1)S(1)}, bf16[256,256]{1,0:T(8,128)(2,1)S(1)}, u32[]{:S(2)}, u32[]{:S(2)}) collective-permute-start(bf16[256,256]{1,0:T(8,128)(2,1)S(1)} %get-tuple-element.213), channel_id=1, source_target_pairs={{0,24},{4,28},{8,16},{12,20},{16,8},{20,12},{24,0},{28,4},{1,25},{... | collective-permute-start | bytes 393224 | tf_op jit(solution)/shard_map/ppermute | solution.py:861
  534.2 17.0 %collective-permute-start.56 = (bf16[2,16,4096]{2,1,0:T(8,128)(2,1)S(1)}, bf16[2,16,4096]{2,1,0:T(8,128)(2,1)S(1)}, u32[]{:S(2)}, u32[]{:S(2)}) collective-permute-start(bf16[2,16,4096]{2,1,0:T(8,128)(2,1)S(1)} %get-tuple-element.209), channel_id=1, source_target_pairs={{0,8},{4,12},{8,0},{12,4},{16,24},{20,28},{24,16},{28,20},{1,9},{5... | collective-permute-start | bytes 786440 | tf_op jit(solution)/shard_map/ppermute | solution.py:861
  536.6 17.8 %collective-permute-start.58 = (bf16[2,16,4096]{2,1,0:T(8,128)(2,1)S(1)}, bf16[2,16,4096]{2,1,0:T(8,128)(2,1)S(1)}, u32[]{:S(2)}, u32[]{:S(2)}) collective-permute-start(bf16[2,16,4096]{2,1,0:T(8,128)(2,1)S(1)} %get-tuple-element.210), channel_id=1, source_target_pairs={{0,24},{4,28},{8,16},{12,20},{16,8},{20,12},{24,0},{28,4},{1,25},{... | collective-permute-start | bytes 786440 | tf_op jit(solution)/shard_map/ppermute | solution.py:861
  543.4 24.7 %collective-permute-start.57 = (bf16[2,16,4096]{2,1,0:T(8,128)(2,1)S(1)}, bf16[2,16,4096]{2,1,0:T(8,128)(2,1)S(1)}, u32[]{:S(2)}, u32[]{:S(2)}) collective-permute-start(bf16[2,16,4096]{2,1,0:T(8,128)(2,1)S(1)} %get-tuple-element.211), channel_id=1, source_target_pairs={{0,16},{4,20},{8,24},{12,28},{16,0},{20,4},{24,8},{28,12},{1,17},{... | collective-permute-start | bytes 786440 | tf_op jit(solution)/shard_map/ppermute | solution.py:861
  (101 other events, 938.9 us)
Sparse Core Ops, SparseCore 0:
  11.7 74.1 all-gather.5
  88.0 48.1 all-gather.7
  138.3 48.0 all-gather.9
  247.3 66.7 reduce-scatter.4
  317.5 66.9 reduce-scatter.2

commit v3 on v2

--- a/solution.py
+++ b/solution.py
@@ -90,44 +90,36 @@
     return pl.ds(pl.multiple_of(index * size, size), size)
 
 
-def slots_kernel(experts, capacity, rows_ref, cols_ref, slot_row_ref, slot_one_ref, slot_two_ref):
+def slots_kernel(capacity, offset_ref, one_ref, two_ref, rows_ref, cols_ref, stack):
     length = rows_ref.shape[1]
     block = 256
-    slot_row_ref[...] = jnp.zeros_like(slot_row_ref)
-    for half, out_ref in enumerate((slot_one_ref, slot_two_ref)):
-        chosen = rows_ref[half : half + 1, :]
-        onehot = jnp.where(iota((8, length), 0) == chosen, 1.0, 0.0)
+    stack[...] = jnp.zeros_like(stack)
+    for half, chosen_ref in enumerate((one_ref, two_ref)):
+        chosen = chosen_ref[...]
+        near = chosen ^ offset_ref[0]
+        onehot = jnp.where(iota((8, length), 0) == near, 1.0, 0.0)
         onehot_low = onehot.astype(bf16)
         for index in range(length // block):
             earlier = iota((length, block), 0) < iota((length, block), 1) + index * block
             counts = dot(onehot_low, jnp.where(earlier, 1.0, 0.0).astype(bf16))
             span = slice(index * block, (index + 1) * block)
-            rank = column_sum(onehot[:, span] * counts).astype(jnp.int32)
-            slot_row_ref[half : half + 1, span] = chosen[:, span] * capacity + rank
-        picks = cols_ref[:, half : half + 1]
-        wide = jnp.where(iota((length, TILE), 1) == picks, 1.0, 0.0)
-        wide_low = wide.astype(bf16)
-        for index in range(length // block):
-            earlier = iota((block, length), 1) < iota((block, length), 0) + index * block
-            counts = dot(jnp.where(earlier, 1.0, 0.0).astype(bf16), wide_low)
-            span = slice(index * block, (index + 1) * block)
-            rank = jnp.sum(wide[span] * counts, axis=1, keepdims=True).astype(jnp.int32)
-            out_ref[span, :] = picks[span] * capacity + rank
-
-
-def find_slots(routes_one, routes_two, experts, capacity):
+            rank = column_sum(onehot[:, span] * counts)
+            stack[half : half + 1, span] = (near[:, span] * capacity).astype(f32) + rank
+        stack[2 + half : 3 + half, :] = chosen.astype(f32)
+    rows_ref[...] = stack[:8, :].astype(jnp.int32)
+    for index in range(length // TILE):
+        span = slice(index * TILE, (index + 1) * TILE)
+        cols_ref[span, :] = jnp.transpose(stack[:, span]).astype(jnp.int32)
+
+
+def find_slots(routes_one, routes_two, offset, capacity):
     length = routes_one.shape[0]
-    rows = jnp.concatenate([routes_one.reshape(1, length), routes_two.reshape(1, length)], axis=0)
-    cols = jnp.concatenate([routes_one, routes_two], axis=1)
     return run(
-        functools.partial(slots_kernel, experts, capacity),
-        (rows, cols),
-        [VMEM, VMEM],
-        [
-            shape_of((8, length), jnp.int32),
-            shape_of((length, 1), jnp.int32),
-            shape_of((length, 1), jnp.int32),
-        ],
+        functools.partial(slots_kernel, capacity),
+        (offset.reshape(1), routes_one.reshape(1, length), routes_two.reshape(1, length)),
+        [SMEM, VMEM, VMEM],
+        [shape_of((8, length), jnp.int32), shape_of((length, TILE), jnp.int32)],
+        [pltpu.VMEM((TILE, length), f32)],
         flops=8 * length * length * 128,
         name="slots",
     )
@@ -174,7 +166,7 @@
 
 
 def front_kernel(
-    experts, hidden_ref, embed_ref, gain_ref, router_ref, picks_ref, slot_row_ref, *refs,
+    experts, hidden_ref, embed_ref, gain_ref, router_ref, cols_ref, slot_row_ref, *refs,
 ):
     out_refs, (probs_ref, gate_ref, low_ref) = refs[:PARTS], refs[PARTS:]
     length = hidden_ref.shape[0]
@@ -184,7 +176,7 @@
         standard, unused = normalize(hidden_ref[at, :].astype(f32))
         low = (standard * gain_ref[0:1, :]).astype(bf16)
         low_ref[at, :] = low
-        probs, gate = route_block(low, embed_ref[at, :], router_ref, picks_ref[at, :], experts)
+        probs, gate = route_block(low, embed_ref[at, :], router_ref, cols_ref[at, 2:3], experts)
         probs_ref[at, :] = probs
         gate_ref[at, :] = gate
 
@@ -213,9 +205,22 @@
     )
 
 
+def forward_in_turn(received, pair):
+    near, far = lax.optimization_barrier((expert_forward(received[:2], *pair), received[2:]))
+    return near + expert_forward(far[:1], *pair) + expert_forward(far[1:], *pair)
+
+
 def expert_backward_kernel(count, in_ref, out_ref, *refs):
-    x_refs, dy_refs, dx_refs = refs[:count], refs[count : 2 * count], refs[2 * count : 3 * count]
-    hidden_refs, dinner_refs = refs[3 * count : 4 * count], refs[4 * count :]
+    x_refs, dy_refs, refs = refs[:count], refs[count : 2 * count], refs[2 * count :]
+    extra, refs = refs[: len(refs) - 3 * count], refs[len(refs) - 3 * count :]
+    if extra:
+        normed_ref, mixed_ref, table_ref, sinus_ref, grad_ref = extra
+        width = normed_ref.shape[1]
+        for part in range(3):
+            lanes = slice(part * width, (part + 1) * width)
+            grad_ref[:, lanes] = t_dot(normed_ref[...], mixed_ref[:, lanes]).astype(bf16)
+        grad_ref[:, 3 * width :] = jnp.transpose(dot(table_ref[...], sinus_ref[...])).astype(bf16)
+    dx_refs, hidden_refs, dinner_refs = refs[:count], refs[count : 2 * count], refs[2 * count :]
     for x_ref, dy_ref, dx_ref, hidden_ref, dinner_ref in zip(
         x_refs, dy_refs, dx_refs, hidden_refs, dinner_refs
     ):
@@ -229,20 +234,34 @@
         dx_ref[...] = dot_t(d_inner, in_ref[...]).astype(bf16)
 
 
-def expert_backward(received, d_result, weight_in, weight_out):
+def expert_backward(received, d_result, weight_in, weight_out, extra=()):
     block, width = received[0].shape
     inner = weight_in.shape[1]
     count = len(received)
+    more = [shape_of((width, 4 * width), bf16)] if extra else []
     outs = run(
         functools.partial(expert_backward_kernel, count),
-        (weight_in, weight_out) + tuple(received) + tuple(d_result),
-        [VMEM] * (2 + 2 * count),
-        [shape_of((block, width), bf16)] * count + [shape_of((block, inner), bf16)] * (2 * count),
+        (weight_in, weight_out) + tuple(received) + tuple(d_result) + tuple(extra),
+        [VMEM] * (2 + 2 * count + len(extra)),
+        more + [shape_of((block, width), bf16)] * count + [shape_of((block, inner), bf16)] * (2 * count),
         flops=6 * count * block * width * inner,
         name="experts_back",
-        limit=40,
-    )
-    return outs[:count], outs[count : 2 * count], outs[2 * count :]
+        limit=48 if extra else 40,
+    )
+    more, outs = outs[: len(more)], outs[len(more) :]
+    return more, outs[:count], outs[count : 2 * count], outs[2 * count :]
+
+
+def backward_in_turn(received, d_result, pair, extra=()):
+    near, far = lax.optimization_barrier(
+        (expert_backward(received[:2], d_result[:2], *pair, extra), d_result[2:])
+    )
+    parts = [
+        near,
+        expert_backward(received[2:3], far[:1], *pair),
+        expert_backward(received[3:], far[1:], *pair),
+    ]
+    return [sum((list(part[k]) for part in parts), []) for k in range(4)]
 
 
 def tile_window(starts_ref, first, length):
@@ -253,7 +272,9 @@
         low = jnp.where(starts_ref[0, k] <= first, starts_ref[0, k], low)
     for k in range(count - 1, 0, -1):
         high = jnp.where(starts_ref[0, k] > first + (TILE - 1), starts_ref[0, k], high)
-    return low // TILE, (high + (TILE - 1)) // TILE
+    low = low // TILE
+    steps = ((high + (TILE - 1)) // TILE - low + 1) // 2
+    return jnp.minimum(low, length // TILE - 2 * steps), steps
 
 
 def numbers_at(starts_ref, positions):
@@ -269,13 +290,16 @@
     return rows == cols
 
 
-def chunk_rows(query_tile, key_tile, extra, length, mirrored=False):
+PAD = 2
+
+
+def chunk_rows(query_tile, key_tile, length, count, mirrored=False):
     tiles = length // TILE
-    index = tiles - 1 - query_tile + key_tile + extra - tiles // 2
-    index = jnp.clip(index, 0, tiles - 1)
+    index = tiles - 1 - query_tile + key_tile - (tiles // 2 - PAD)
     if mirrored:
-        index = tiles - 1 - index
-    return pl.ds(pl.multiple_of(index * TILE, TILE), TILE)
+        index = tiles + 2 * PAD - count - index
+    index = jnp.clip(index, 0, tiles + 2 * PAD - count)
+    return pl.ds(pl.multiple_of(index * TILE, TILE), count * TILE)
 
 
 def halves(values):
@@ -284,6 +308,13 @@
     return jnp.concatenate(
         [jnp.where(left, values, zero), jnp.where(left, zero, values)], axis=0
     )
+
+
+def turned_halves(values):
+    turned = jnp.transpose(values)
+    top = iota(turned.shape, 0) < TILE // 2
+    zero = jnp.zeros_like(turned)
+    return jnp.concatenate([jnp.where(top, turned, zero), jnp.where(top, zero, turned)], axis=1)
 
 
 def skew(values):
@@ -297,7 +328,8 @@
 
 
 def mirror(values):
-    flip = iota((TILE, TILE), 0) + iota((TILE, TILE), 1) == TILE - 1
+    row, col = iota((2 * TILE, 2 * TILE), 0), iota((2 * TILE, 2 * TILE), 1)
+    flip = (row % TILE + col % TILE == TILE - 1) & (row // TILE == col // TILE)
     return dot(values, jnp.where(flip, 1.0, 0.0).astype(bf16))
 
 
@@ -318,8 +350,8 @@
     def query_step(tile):
         first = tile * TILE
         at = rows_at(tile, TILE)
-        low, high = tile_window(starts_ref, first, length)
-        chunk = chunk_rows(tile, low, 0, length)
+        low, steps = tile_window(starts_ref, first, length)
+        chunk = chunk_rows(tile, low, length, 1)
         for p in range(PAIRS):
             lanes = slice(p * TILE, (p + 1) * TILE)
             qum[p] = halves(qu_ref[at, lanes])
@@ -330,37 +362,45 @@
             mixed[p] = jnp.zeros((2 * TILE, TILE), f32)
         lower = twice(iota((TILE, TILE), 1) <= iota((TILE, TILE), 0))
 
-        def score_step(key, carry):
-            keys = rows_at(key, TILE)
-            same = twice(same_tile(starts_ref, first, key * TILE))
-            chunk = chunk_rows(tile, key, 1, length)
+        def score_step(step, carry):
+            key = low + 2 * step
+            keys = pl.ds(pl.multiple_of(key * TILE, TILE), 2 * TILE)
+            same_one = twice(same_tile(starts_ref, first, key * TILE))
+            same_two = twice(same_tile(starts_ref, first, key * TILE + TILE))
+            chunks = chunk_rows(tile, key + 1, length, 2)
             for p in range(PAIRS):
                 lanes = slice(p * TILE, (p + 1) * TILE)
                 content = dot_t(qum[p], k_ref[keys, lanes])
-                fresh = skew(dot_t(qvm[p], t_ref[chunk, lanes]))
-                value = content + jnp.where(lower, rolled[p], fresh)
-                value = jnp.where(same, value, masked_score)
-                rolled[p] = fresh
-                scores[key, p] = value
-                peaks[p] = jnp.maximum(peaks[p], value)
+                fresh = dot_t(qvm[p], t_ref[chunks, lanes])
+                one, two = skew(fresh[:, :TILE]), skew(fresh[:, TILE:])
+                value_one = content[:, :TILE] + jnp.where(lower, rolled[p], one)
+                value_two = content[:, TILE:] + jnp.where(lower, one, two)
+                value_one = jnp.where(same_one, value_one, masked_score)
+                value_two = jnp.where(same_two, value_two, masked_score)
+                rolled[p] = two
+                scores[2 * step, p] = value_one
+                scores[2 * step + 1, p] = value_two
+                peaks[p] = jnp.maximum(peaks[p], jnp.maximum(value_one, value_two))
             return carry
 
-        lax.fori_loop(low, high, score_step, 0)
+        lax.fori_loop(0, steps, score_step, 0)
         for p in range(PAIRS):
             peaks[p] = jnp.broadcast_to(
                 jnp.max(peaks[p], axis=1, keepdims=True), (2 * TILE, TILE)
             )
 
-        def value_step(key, carry):
-            keys = rows_at(key, TILE)
+        def value_step(step, carry):
+            keys = pl.ds(pl.multiple_of((low + 2 * step) * TILE, TILE), 2 * TILE)
             for p in range(PAIRS):
                 lanes = slice(p * TILE, (p + 1) * TILE)
-                raised = jnp.exp(scores[key, p] - peaks[p])
-                sums[p] = sums[p] + raised
-                mixed[p] = mixed[p] + dot(raised.astype(bf16), v_ref[keys, lanes])
+                one = jnp.exp(scores[2 * step, p] - peaks[p])
+                two = jnp.exp(scores[2 * step + 1, p] - peaks[p])
+                sums[p] += one + two
+                raised = jnp.concatenate([one.astype(bf16), two.astype(bf16)], axis=1)
+                mixed[p] += dot(raised, v_ref[keys, lanes])
             return carry
 
-        lax.fori_loop(low, high, value_step, 0)
+        lax.fori_loop(0, steps, value_step, 0)
         left = iota((TILE, TILE), 1) < TILE // 2
         logs = jnp.zeros((TILE, TILE), f32)
         lane = iota((TILE, TILE), 1)
@@ -393,7 +433,7 @@
 def attend_backward(
     starts_ref, qu_ref, qv_ref, k_ref, v_ref, t_ref, mirrored_ref, context_ref, logs_ref, dcontext_ref,
     dm_ref, dk_ref, dv_ref, dt_ref, dbias_ref,
-    qum, qvm, dcm, logs, deltas, rolled, unrolled, dqu, dqv,
+    qum, qvm, dcm, qut, qvt, dct, logs, deltas, rolled, unrolled, dqu, dqv,
 ):
     length, width = qu_ref.shape
     tiles = length // TILE
@@ -406,16 +446,20 @@
     def query_step(tile):
         first = tile * TILE
         at = rows_at(tile, TILE)
-        low, high = tile_window(starts_ref, first, length)
-        chunk = chunk_rows(tile, low, 0, length)
-        lanes_all = iota((TILE, TILE), 1)
+        low, steps = tile_window(starts_ref, first, length)
+        chunk = chunk_rows(tile, low, length, 1)
         logs_tile = logs_ref[at, :]
         for p in range(PAIRS):
             lanes = slice(p * TILE, (p + 1) * TILE)
-            qum[p] = halves(qu_ref[at, lanes])
-            qvm[p] = halves(qv_ref[at, lanes])
+            query_u = halves(qu_ref[at, lanes])
+            query_v = halves(qv_ref[at, lanes])
             upstream = halves(dcontext_ref[at, lanes])
+            qum[p] = query_u
+            qvm[p] = query_v
             dcm[p] = upstream
+            qut[p] = turned_halves(qu_ref[at, lanes])
+            qvt[p] = turned_halves(qv_ref[at, lanes])
+            dct[p] = turned_halves(dcontext_ref[at, lanes])
             delta = jnp.sum(
                 upstream.astype(f32) * twice(context_ref[at, lanes].astype(f32)),
                 axis=1,
@@ -424,47 +468,62 @@
             deltas[p] = jnp.broadcast_to(delta, (2 * TILE, TILE))
             logs[p, :TILE] = jnp.broadcast_to(logs_tile[:, 2 * p : 2 * p + 1], (TILE, TILE))
             logs[p, TILE:] = jnp.broadcast_to(logs_tile[:, 2 * p + 1 : 2 * p + 2], (TILE, TILE))
-            rolled[p] = skew(dot_t(qvm[p], t_ref[chunk, lanes]))
+            rolled[p] = skew(dot_t(query_v, t_ref[chunk, lanes]))
             unrolled[p] = jnp.zeros((2 * TILE, TILE), f32)
             dqu[p] = jnp.zeros((2 * TILE, TILE), f32)
             dqv[p] = jnp.zeros((2 * TILE, TILE), f32)
         lower = twice(iota((TILE, TILE), 1) <= iota((TILE, TILE), 0))
 
-        def step(key, carry):
-            keys = rows_at(key, TILE)
-            same = twice(same_tile(starts_ref, first, key * TILE))
-            before = chunk_rows(tile, key, 0, length, True)
-            after = chunk_rows(tile, key, 1, length)
+        def step_body(step, carry):
+            key = low + 2 * step
+            keys = pl.ds(pl.multiple_of(key * TILE, TILE), 2 * TILE)
+            same_one = twice(same_tile(starts_ref, first, key * TILE))
+            same_two = twice(same_tile(starts_ref, first, key * TILE + TILE))
+            before = chunk_rows(tile, key, length, 2, True)
+            after = chunk_rows(tile, key + 1, length, 2)
             for p in range(PAIRS):
                 lanes = slice(p * TILE, (p + 1) * TILE)
                 content = dot_t(qum[p], k_ref[keys, lanes])
-                fresh = skew(dot_t(qvm[p], t_ref[after, lanes]))
-                value = content + jnp.where(lower, rolled[p], fresh)
-                rolled[p] = fresh
-                probs = jnp.where(same, jnp.exp(value - logs[p]), 0.0)
+                fresh = dot_t(qvm[p], t_ref[after, lanes])
+                one, two = skew(fresh[:, :TILE]), skew(fresh[:, TILE:])
+                value_one = content[:, :TILE] + jnp.where(lower, rolled[p], one)
+                value_two = content[:, TILE:] + jnp.where(lower, one, two)
+                rolled[p] = two
+                probs_one = jnp.where(same_one, jnp.exp(value_one - logs[p]), 0.0)
+                probs_two = jnp.where(same_two, jnp.exp(value_two - logs[p]), 0.0)
+                probs = jnp.concatenate([probs_one.astype(bf16), probs_two.astype(bf16)], axis=1)
                 dprobs = dot_t(dcm[p], v_ref[keys, lanes])
-                dscores = probs * (dprobs - deltas[p])
-                dlow = dscores.astype(bf16)
-                dv_ref[keys, lanes] += t_dot(probs.astype(bf16), dcm[p])
-                dk_ref[keys, lanes] += t_dot(dlow, qum[p])
+                dlow_one = (probs_one * (dprobs[:, :TILE] - deltas[p])).astype(bf16)
+                dlow_two = (probs_two * (dprobs[:, TILE:] - deltas[p])).astype(bf16)
+                dlow = jnp.concatenate([dlow_one, dlow_two], axis=1)
+                dv_ref[lanes, keys] += dot(dct[p], probs)
+                dk_ref[lanes, keys] += dot(qut[p], dlow)
                 dqu[p] += dot(dlow, k_ref[keys, lanes])
-                turned = skew(mirror(dlow))
-                moved = jnp.where(lower, turned, unrolled[p]).astype(bf16)
-                unrolled[p] = turned
+                mirrored = mirror(dlow)
+                one, two = skew(mirrored[:, :TILE]), skew(mirrored[:, TILE:])
+                moved = jnp.concatenate(
+                    [
+                        jnp.where(lower, two, one).astype(bf16),
+                        jnp.where(lower, one, unrolled[p]).astype(bf16),
+                    ],
+                    axis=1,
+                )
+                unrolled[p] = two
+                dt_ref[lanes, before] += dot(qvt[p], moved)
                 dqv[p] += dot(moved, mirrored_ref[before, lanes])
-                dt_ref[before, lanes] += t_dot(moved, qvm[p])
             return carry
 
-        lax.fori_loop(low, high, step, 0)
-        last = chunk_rows(tile, high, 0, length, True)
+        lax.fori_loop(0, steps, step_body, 0)
+        last = chunk_rows(tile, low + 2 * steps, length, 1, True)
         left = iota((TILE, TILE), 1) < TILE // 2
         for p in range(PAIRS):
             lanes = slice(p * TILE, (p + 1) * TILE)
             moved = jnp.where(lower, 0.0, unrolled[p]).astype(bf16)
-            dq = dqv[p] + dot(moved, mirrored_ref[last, lanes])
-            dt_ref[last, lanes] += t_dot(moved, qvm[p])
-            part_u = jnp.where(left, dqu[p, :TILE], dqu[p, TILE:]) * scale
-            part_v = jnp.where(left, dq[:TILE], dq[TILE:]) * scale
+            dt_ref[lanes, last] += dot(qvt[p], moved)
+            full_u = dqu[p]
+            full_v = dqv[p] + dot(moved, mirrored_ref[last, lanes])
+            part_u = jnp.where(left, full_u[:TILE], full_u[TILE:]) * scale
+            part_v = jnp.where(left, full_v[:TILE], full_v[TILE:]) * scale
             dbias_ref[0:1, lanes] += column_sum(part_u)
             dbias_ref[1:2, lanes] += column_sum(part_v)
             dm_ref[at, lanes] = (part_u + part_v).astype(bf16)
@@ -472,16 +531,21 @@
     loop(tiles, query_step)
 
     def finish(index):
-        at = rows_at(index, BLOCK)
-        dm_ref[at, width : 2 * width] = dk_ref[at, :].astype(bf16)
-        dm_ref[at, 2 * width : 3 * width] = dv_ref[at, :].astype(bf16)
-
-    loop(length // BLOCK, finish)
+        at = rows_at(index, TILE)
+        for p in range(PAIRS):
+            lanes = slice(p * TILE, (p + 1) * TILE)
+            key_lanes = slice(width + p * TILE, width + (p + 1) * TILE)
+            value_lanes = slice(2 * width + p * TILE, 2 * width + (p + 1) * TILE)
+            dm_ref[at, key_lanes] = jnp.transpose(dk_ref[lanes, at].astype(bf16))
+            dm_ref[at, value_lanes] = jnp.transpose(dv_ref[lanes, at].astype(bf16))
+
+    loop(tiles, finish)
 
 
 def attend_back_scratch():
     pair = (PAIRS, 2 * TILE, TILE)
-    return [pltpu.VMEM(pair, bf16) for unused in range(3)] + [
+    turned = (PAIRS, TILE, 2 * TILE)
+    return [pltpu.VMEM(dims, bf16) for dims in (pair,) * 3 + (turned,) * 3] + [
         pltpu.VMEM(pair, f32) for unused in range(6)
     ]
 
@@ -495,11 +559,20 @@
     ]
 
 
+def spread_rows(rows_ref, out_ref):
+    width = rows_ref.shape[1]
+    for row in range(out_ref.shape[2] // width):
+        lanes = slice(row * width, (row + 1) * width)
+        out_ref[:, :, lanes] = jnp.broadcast_to(
+            rows_ref[row : row + 1, :][None], (out_ref.shape[0], 1, width)
+        )
+
+
 EDGE = 16
 
 
 def middle_kernel(
-    starts_ref, hidden_ref, slot_ref, gate_ref, gains_ref, dense_ref, bias_ref, taps_ref, sinus_ref,
+    starts_ref, hidden_ref, cols_ref, gate_ref, gains_ref, dense_ref, bias_ref, taps_ref, sinus_ref,
     *refs,
 ):
     returned_refs, refs = refs[:PARTS], refs[PARTS:]
@@ -513,7 +586,7 @@
 
     def queries_step(index):
         at = rows_at(index, BLOCK)
-        picked = collect(slot_ref[at, :], returned_ref)
+        picked = collect(cols_ref[at, 0:1], returned_ref)
         h1 = hidden_ref[at, :].astype(f32) + 0.5 * gate_ref[at, :] * picked
         h1_ref[at, :] = h1
         standard, unused = normalize(h1)
@@ -523,8 +596,12 @@
         qv_ref[at, :] = ((queries + bias_ref[1:2, :]).astype(bf16).astype(f32) * scale).astype(bf16)
         k_ref[at, :] = dot(low, in_ref[:, width : 2 * width]).astype(bf16)
         v_ref[at, :] = dot(low, in_ref[:, 2 * width :]).astype(bf16)
-        t_ref[at, :] = dot(sinus_ref[at, :], place_ref[...]).astype(bf16)
-
+        table_at = pl.ds(pl.multiple_of(index * BLOCK + edge, TILE), BLOCK)
+        t_ref[table_at, :] = dot(sinus_ref[at, :], place_ref[...]).astype(bf16)
+
+    edge = PAD * TILE
+    t_ref[:edge, :] = jnp.zeros((edge, width), bf16)
+    t_ref[edge + length :, :] = jnp.zeros((edge, width), bf16)
     loop(length // BLOCK, queries_step)
     attend_forward(
         starts_ref, qu_ref, qv_ref, k_ref, v_ref, t_ref, context_ref, logs_ref, *attend
@@ -569,14 +646,12 @@
             sums[1:2, lanes] += column_sum(kept * kept)
 
     loop(length // TILE, conv_step)
-    copies = sums_ref.shape[0]
-    sums_ref[:, :width] = jnp.broadcast_to(sums[0:1, :], (copies, width))
-    sums_ref[:, width : 2 * width] = jnp.broadcast_to(sums[1:2, :], (copies, width))
-    sums_ref[:, 2 * width :] = jnp.zeros((copies, width), f32) + frames.astype(f32)
+    sums[2:3, :] = jnp.zeros((1, width), f32) + frames.astype(f32)
+    spread_rows(sums, sums_ref)
 
 
 def batch_totals(totals_ref, width):
-    totals = column_sum(totals_ref[...])
+    totals = jnp.sum(totals_ref[...], axis=0)
     count = totals[:, 2 * width :]
     mean = totals[:, :width] / count
     variance = totals[:, width : 2 * width] / count - mean * mean
@@ -592,7 +667,7 @@
 
 def second_kernel(
     experts, h2_ref, conv_ref, totals_ref, batch_ref, point_ref, embed_ref, gains_ref, router_ref,
-    picks_ref, slot_row_ref, *refs,
+    cols_ref, slot_row_ref, *refs,
 ):
     out_refs, refs = refs[:PARTS], refs[PARTS:]
     h3_ref, active_ref, probs_ref, gate_ref, stats_ref, low_ref = refs
@@ -612,7 +687,7 @@
         standard, unused = normalize(h3)
         low = (standard * gains_ref[3:4, :]).astype(bf16)
         low_ref[at, :] = low
-        probs, gate = route_block(low, embed_ref[at, :], router_ref, picks_ref[at, :], experts)
+        probs, gate = route_block(low, embed_ref[at, :], router_ref, cols_ref[at, 3:4], experts)
         probs_ref[at, :] = probs
         gate_ref[at, :] = gate
 
@@ -627,7 +702,7 @@
 
 
 def turn_kernel(
-    h3_ref, slot_ref, gate_ref, probs_ref, picks_ref, slot_row_ref, gains_ref, cotangent_ref, *refs,
+    h3_ref, cols_ref, gate_ref, probs_ref, slot_row_ref, gains_ref, cotangent_ref, *refs,
 ):
     returned_refs, out_refs, refs = refs[:PARTS], refs[PARTS : 2 * PARTS], refs[2 * PARTS :]
     output_ref, d4_ref, dlogits_ref, dgain_ref, low_ref, returned_ref = refs
@@ -637,7 +712,7 @@
 
     def step(index):
         at = rows_at(index, BLOCK)
-        picked = collect(slot_ref[at, :], returned_ref)
+        picked = collect(cols_ref[at, 1:2], returned_ref)
         gate = gate_ref[at, :]
         h4 = h3_ref[at, :] + 0.5 * gate * picked
         standard, inverse = normalize(h4)
@@ -647,7 +722,7 @@
         dgain_ref[0:1, :] += column_sum(upstream * standard)
         d4 = normalize_back(standard, inverse, gain, upstream)
         d4_ref[at, :] = d4
-        dlogits_ref[at, :] = gate_back(d4, picked, gate, probs_ref[at, :], picks_ref[at, :])
+        dlogits_ref[at, :] = gate_back(d4, picked, gate, probs_ref[at, :], cols_ref[at, 3:4])
         low_ref[at, :] = (0.5 * gate * d4).astype(bf16)
 
     loop(length // BLOCK, step)
@@ -669,7 +744,7 @@
 
 
 def second_back_kernel(
-    slot_ref, dlogits_ref, h3_ref, d4_ref, embed_ref, router_ref, gains_ref, conv_ref, stats_ref,
+    cols_ref, dlogits_ref, h3_ref, d4_ref, embed_ref, router_ref, gains_ref, conv_ref, stats_ref,
     batch_ref, point_ref, *refs,
 ):
     dsent_refs, refs = refs[:PARTS], refs[PARTS:]
@@ -690,7 +765,7 @@
             dlogits_ref[at, :], low, embed_ref[at, :], router_ref, drouter_ref
         )
         dembed_ref[at, :] = d_embed
-        d_norm = collect(slot_ref[at, :], dsent_ref) + d_low
+        d_norm = collect(cols_ref[at, 1:2], dsent_ref) + d_low
         small_ref[0:1, :] += column_sum(d_norm * standard)
         d3 = d4_ref[at, :] + normalize_back(standard, inverse, gain, d_norm)
         d3_ref[at, :] = d3
@@ -707,34 +782,22 @@
         sums[1:2, :] += column_sum(d_z * centred)
 
     loop(length // BLOCK, step)
-    copies = sums_ref.shape[0]
-    sums_ref[:, :width] = jnp.broadcast_to(sums[0:1, :], (copies, width))
-    sums_ref[:, width:] = jnp.broadcast_to(sums[1:2, :], (copies, width))
-
-
-def middle_back_kernel(
-    starts_ref, conv_ref, dz_ref, stats_ref, dsums_ref, batch_ref, d3_ref, h1_ref, h2_ref, gains_ref,
-    dense_ref, taps_ref, sinus_ref, qu_ref, qv_ref, k_ref, v_ref, t_ref, context_ref, logs_ref,
-    slot_ref, gate_ref, probs_ref, picks_ref, slot_row_ref, *refs,
+    spread_rows(sums, sums_ref)
+
+
+def conv_back_kernel(
+    starts_ref, conv_ref, dz_ref, stats_ref, dsums_ref, d3_ref, h2_ref, gains_ref, dense_ref, taps_ref,
+    d2_ref, d2low_ref, dcontext_ref, n3_ref, dg_ref, small_ref, dtaps_ref, padded, linear,
 ):
-    returned_refs, out_refs, refs = refs[:PARTS], refs[PARTS : 2 * PARTS], refs[2 * PARTS :]
-    d1_ref, dlogits_ref, n2_ref, n3_ref, dg_ref, d2low_ref, dm_ref, dtable_ref = refs[:8]
-    small_ref, dtaps_ref, padded, linear, dcontext_ref, low_ref, mirrored_ref, returned_ref = refs[8:16]
-    attend = refs[16:]
-    length, width = h1_ref.shape
-    d2_ref = d1_ref
-    dt_ref = padded.at[pl.ds(0, length)]
-    dk_ref = linear.at[:, pl.ds(0, width)]
-    dv_ref = linear.at[:, pl.ds(width, width)]
-    in_ref, place_ref, mix_ref, unused, point_ref = dense_parts(dense_ref)
+    length, width = h2_ref.shape
+    unused, unused, mix_ref, unused, point_ref = dense_parts(dense_ref)
     taps = taps_ref.shape[0] - 1
     reach = taps // 2
     frames = starts_ref[0, starts_ref.shape[1] - 1]
     small_ref[...] = jnp.zeros_like(small_ref)
     dtaps_ref[...] = jnp.zeros_like(dtaps_ref)
-    join_blocks(returned_refs, returned_ref)
     mean, batch_inverse, count = stats_ref[0:1, :], stats_ref[1:2, :], stats_ref[2:3, :]
-    dsums = column_sum(dsums_ref[...])
+    dsums = jnp.sum(dsums_ref[...], axis=0)
     d_variance = -0.5 * batch_inverse * batch_inverse * batch_inverse * dsums[:, width:]
     padded[:EDGE, :] = jnp.zeros((EDGE, width), f32)
     padded[EDGE + length :, :] = jnp.zeros((EDGE, width), f32)
@@ -792,9 +855,32 @@
         low = d2.astype(bf16)
         d2low_ref[at, :] = low
         dcontext_ref[at, :] = dot_t(low, mix_ref[...]).astype(bf16)
-        mirrored_ref[at, :] = dot(sinus_ref[at, :], place_ref[...]).astype(bf16)
 
     loop(length // BLOCK, gates_step)
+
+
+def attend_back_kernel(
+    starts_ref, d2_ref, dcontext_ref, h1_ref, gains_ref, dense_ref, sinus_ref, qu_ref, qv_ref, k_ref, v_ref,
+    t_ref, context_ref, logs_ref, cols_ref, gate_ref, probs_ref, slot_row_ref, *refs,
+):
+    returned_refs, out_refs, refs = refs[:PARTS], refs[PARTS : 2 * PARTS], refs[2 * PARTS :]
+    d1_ref, dlogits_ref, n2_ref, dm_ref, dtable_ref, small_ref = refs[:6]
+    low_ref, mirrored_ref, returned_ref, dk_ref, dv_ref, dt_ref = refs[6:12]
+    attend = refs[12:]
+    length, width = h1_ref.shape
+    in_ref, place_ref, unused, unused, unused = dense_parts(dense_ref)
+    small_ref[...] = jnp.zeros_like(small_ref)
+    join_blocks(returned_refs, returned_ref)
+
+    def table_step(index):
+        at = rows_at(index, BLOCK)
+        table_at = pl.ds(pl.multiple_of(index * BLOCK + edge, TILE), BLOCK)
+        mirrored_ref[table_at, :] = dot(sinus_ref[at, :], place_ref[...]).astype(bf16)
+
+    edge = PAD * TILE
+    mirrored_ref[:edge, :] = jnp.zeros((edge, width), bf16)
+    mirrored_ref[edge + length :, :] = jnp.zeros((edge, width), bf16)
+    loop(length // BLOCK, table_step)
     attend_backward(
         starts_ref, qu_ref, qv_ref, k_ref, v_ref, t_ref, mirrored_ref, context_ref, logs_ref, dcontext_ref,
         dm_ref, dk_ref, dv_ref, dt_ref, small_ref.at[pl.ds(8, 8)], *attend
@@ -802,7 +888,6 @@
 
     def queries_step(index):
         at = rows_at(index, BLOCK)
-        dtable_ref[at, :] = dt_ref[at, :].astype(bf16)
         d_norm = dot_t(dm_ref[at, :], in_ref[...])
         standard, inverse = normalize(h1_ref[at, :])
         gain = gains_ref[1:2, :]
@@ -810,24 +895,36 @@
         small_ref[1:2, :] += column_sum(d_norm * standard)
         d1 = d2_ref[at, :] + normalize_back(standard, inverse, gain, d_norm)
         d1_ref[at, :] = d1
-        picked = collect(slot_ref[at, :], returned_ref)
+        picked = collect(cols_ref[at, 0:1], returned_ref)
         gate = gate_ref[at, :]
-        dlogits_ref[at, :] = gate_back(d1, picked, gate, probs_ref[at, :], picks_ref[at, :])
+        dlogits_ref[at, :] = gate_back(d1, picked, gate, probs_ref[at, :], cols_ref[at, 2:3])
         low_ref[at, :] = (0.5 * gate * d1).astype(bf16)
 
     loop(length // BLOCK, queries_step)
+    dtable_ref[...] = dt_ref[:, PAD * TILE : PAD * TILE + length].astype(bf16)
     dispatch(low_ref, slot_row_ref[0:1, :], out_refs)
 
 
 def last_kernel(
-    slot_ref, dlogits_ref, hidden_ref, d1_ref, embed_ref, router_ref, gains_ref, dembed_two_ref, *refs,
+    cols_ref, dlogits_ref, hidden_ref, d1_ref, embed_ref, router_ref, gains_ref, dembed_two_ref,
+    drouter_two_ref, mid_ref, conv_ref, two_ref, five_ref, taps_ref, *refs,
 ):
     dsent_refs, refs = refs[:PARTS], refs[PARTS:]
-    d0_ref, dembed_ref, drouter_ref, small_ref, dsent_ref = refs
+    d0_ref, dembed_ref, routers_ref, small_ref, dsent_ref = refs
     length = hidden_ref.shape[0]
+    taps = small_ref.shape[0] - 9
     join_blocks(dsent_refs, dsent_ref)
+    drouter_ref = routers_ref.at[pl.ds(0, 8)]
     drouter_ref[...] = jnp.zeros_like(drouter_ref)
-    small_ref[...] = jnp.zeros_like(small_ref)
+    routers_ref[8:, :] = drouter_two_ref[...]
+    small_ref[0:1, :] = jnp.zeros_like(small_ref[0:1, :])
+    small_ref[1:2, :] = mid_ref[1:2, :]
+    small_ref[2:3, :] = conv_ref[0:1, :]
+    small_ref[3:4, :] = two_ref[0:1, :]
+    small_ref[4:5, :] = five_ref[0:1, :]
+    small_ref[5:7, :] = mid_ref[8:10, :]
+    small_ref[7 : 7 + taps, :] = taps_ref[:taps, :]
+    small_ref[7 + taps :, :] = two_ref[1:3, :]
 
     def step(index):
         at = rows_at(index, BLOCK)
@@ -838,26 +935,20 @@
             dlogits_ref[at, :], low, embed_ref[at, :], router_ref, drouter_ref
         )
         dembed_ref[at, :] = d_embed + dembed_two_ref[at, :]
-        d_norm = collect(slot_ref[at, :], dsent_ref) + d_low
+        d_norm = collect(cols_ref[at, 0:1], dsent_ref) + d_low
         small_ref[0:1, :] += column_sum(d_norm * standard)
         d0_ref[at, :] = d1_ref[at, :] + normalize_back(standard, inverse, gain, d_norm)
 
     loop(length // BLOCK, step)
 
 
-def backward_parts(received, d_result, pair):
-    parts = [
-        expert_backward(received[start:stop], d_result[start:stop], *pair)
-        for start, stop in ((0, 2), (2, 3), (3, PARTS))
-    ]
-    return [sum((part[k] for part in parts), []) for k in range(3)]
-
-
 def gather_small(values):
     return lax.all_to_all(values, BOTH, split_axis=0, concat_axis=0, tiled=True)
 
 
 def across(values, axis, size, offset):
+    if not offset:
+        return values
     return lax.ppermute(values, axis, [(i, i ^ offset) for i in range(size)])
 
 
@@ -869,7 +960,7 @@
         pieces = []
         for k in range(index * per, (index + 1) * per):
             piece = block[(k - index * per) * rows : (k - index * per + 1) * rows]
-            pieces.append(across(piece, "expert", experts, k) if k else piece)
+            pieces.append(across(piece, "expert", experts, k))
         moved.append(pieces[0] if per == 1 else jnp.concatenate(pieces, axis=0))
     return moved
 
@@ -951,42 +1042,46 @@
     return (mine.astype(f32) + arrived.astype(f32)).astype(bf16)
 
 
-def keep_one(values, place, size, stride, mesh_axis):
-    total = lax.dynamic_index_in_dim(values, place, 0, keepdims=False).astype(f32)
+def own_parts(values, place, size, stride, mesh_axis):
+    parts = [lax.dynamic_index_in_dim(values, place, 0, keepdims=False)]
     for k in range(1, values.shape[0]):
         theirs = lax.dynamic_index_in_dim(values, place ^ k, 0, keepdims=False)
-        total = total + across(theirs, mesh_axis, size, k * stride).astype(f32)
+        parts.append(across(theirs, mesh_axis, size, k * stride))
+    return parts
+
+
+def add_up(parts):
+    total = parts[0].astype(f32)
+    for part in parts[1:]:
+        total = total + part.astype(f32)
     return total
 
 
-def scatter_groups(values, size):
-    me = lax.axis_index("dp")
-    rows, width = values.shape
-    values = values.reshape(size // 2, 2, rows // size, width)
-    values = keep_half(values, 1, me % 2, size, 1, "dp")
-    return keep_one(values, me // 2, size, 2, "dp")
-
-
-def scatter_dense(grad, groups, experts):
-    rows, width = grad.shape
-    me, group = lax.axis_index("expert"), lax.axis_index("dp")
-    rows = rows // (groups * experts)
-    values = grad.reshape(groups // 2, 2, experts // 2, 2, rows, width)
-    values = keep_half(values, 3, me % 2, experts, 1, "expert")
-    values = keep_half(values, 1, group % 2, groups, 1, "dp")
-    values = keep_one(values, group // 2, groups, 2, "dp").astype(bf16)
-    return keep_one(values, me // 2, experts, 2, "expert")
+def keep_one(values, place, size, stride, mesh_axis):
+    return add_up(own_parts(values, place, size, stride, mesh_axis))
+
+
+def near_half(values):
+    groups = values.shape[0]
+    values = values.reshape((groups // 2, 2) + values.shape[1:])
+    return keep_half(values, 1, lax.axis_index("dp") % 2, groups, 1, "dp")
+
+
+def expert_parts(values, experts):
+    me = lax.axis_index("expert")
+    return [
+        across(lax.dynamic_index_in_dim(values, me ^ k, 1, keepdims=False), "expert", experts, k)
+        for k in range(experts)
+    ]
 
 
 def rows_product(left, right):
     return lax.dot_general(left, right, (((0,), (0,)), ((), ())), preferred_element_type=f32)
 
 
-def expert_grads(received, d_result, hidden, d_inner):
-    received, d_result, hidden, d_inner = (
-        jnp.concatenate(blocks, axis=0) for blocks in (received, d_result, hidden, d_inner)
-    )
-    return rows_product(received, d_inner).astype(bf16), rows_product(hidden, d_result).astype(bf16)
+def blocks_product(left, right):
+    left, right = jnp.concatenate(left, axis=0), jnp.concatenate(right, axis=0)
+    return rows_product(left, right).astype(bf16)
 
 
 def scatter_offloaded(grad_in, grad_out):
@@ -996,18 +1091,9 @@
     )
 
 
-def scatter_direct(grad_in, grad_out, size):
-    half_in, half_out = grad_in.shape[1] // 2, grad_out.shape[1] // 2
-    sums = [
-        scatter_groups(part, size)
-        for part in (
-            grad_out[:, :half_out], grad_out[:, half_out:], grad_in[:, :half_in], grad_in[:, half_in:],
-        )
-    ]
-    return (
-        jnp.concatenate(sums[2:], axis=1)[None],
-        jnp.concatenate(sums[:2], axis=1)[None],
-    )
+def split_columns(values):
+    middle = values.shape[1] // 2
+    return [values[:, :middle], values[:, middle:]]
 
 
 def sinus_rows(length, width, upward):
@@ -1088,14 +1174,13 @@
     )
 
     me = lax.axis_index("expert")
-    slot_rows, slot_one, slot_two = find_slots(
-        first_routes ^ me, second_routes ^ me, experts, capacity
-    )
+    slot_rows, slot_cols = find_slots(first_routes, second_routes, me, capacity)
     sinus = sinus_rows(length, width, False)
     mirrored = sinus_rows(length, width, True)
     row_low = shape_of((length, width), bf16)
     row_full = shape_of((length, width), f32)
     lane_full = shape_of((length, TILE), f32)
+    table_low = shape_of((length + 2 * PAD * TILE, width), bf16)
     block_low = shape_of((slots // PARTS, width), bf16)
     slots_scratch = pltpu.VMEM((slots, width), bf16)
     sums_scratch = pltpu.VMEM((8, width), f32)
@@ -1105,7 +1190,7 @@
 
     *sent_one, probs_one, gate_one = run(
         functools.partial(front_kernel, experts),
-        (inputs, embedding, gains, routers[0], first_routes, slot_rows),
+        (inputs, embedding, gains, routers[0], slot_cols, slot_rows),
         [VMEM] * 6,
         [block_low] * PARTS + [lane_full, column],
         [low_scratch],
@@ -1113,11 +1198,7 @@
         name="front",
     )
     received_one = exchange(sent_one, experts)
-    result_one = (
-        expert_forward(received_one[:2], *first_pair)
-        + expert_forward(received_one[2:3], *first_pair)
-        + expert_forward(received_one[3:], *first_pair)
-    )
+    result_one = forward_in_turn(received_one, first_pair)
     returned_one = exchange(result_one, experts)
 
     edge_scratch = pltpu.VMEM((length + 2 * EDGE, width), f32)
@@ -1126,11 +1207,13 @@
     ) = run(
         middle_kernel,
         (
-            segment_starts, inputs, slot_one, gate_one, gains, dense, bias, kernel_taps, sinus,
+            segment_starts, inputs, slot_cols, gate_one, gains, dense, bias, kernel_taps, sinus,
             *returned_one,
         ),
         [SMEM] + [VMEM] * (8 + PARTS),
-        [row_full, row_full] + [row_low] * 6 + [lane_full, row_full, shape_of((devices, 3 * width), f32)],
+        [row_full, row_full]
+        + [row_low] * 4
+        + [table_low, row_low, lane_full, row_full, shape_of((devices, 1, 3 * width), f32)],
         [edge_scratch, sums_scratch, slots_scratch] + attend_scratch(length),
         flops=16 * length * length * width,
         name="middle",
@@ -1140,7 +1223,7 @@
     *sent_two, h3, active, probs_two, gate_two, stats = run(
         functools.partial(second_kernel, experts),
         (
-            h2, convolved, totals, batch, point_out, embedding, gains, routers[1], second_routes, slot_rows,
+            h2, convolved, totals, batch, point_out, embedding, gains, routers[1], slot_cols, slot_rows,
         ),
         [VMEM] * 10,
         [block_low] * PARTS + [row_full, row_low, lane_full, column, eight],
@@ -1149,40 +1232,41 @@
         name="second",
     )
     received_two = exchange(sent_two, experts)
-    result_two = (
-        expert_forward(received_two[:2], *second_pair)
-        + expert_forward(received_two[2:3], *second_pair)
-        + expert_forward(received_two[3:], *second_pair)
-    )
+    result_two = forward_in_turn(received_two, second_pair)
     returned_two = exchange(result_two, experts)
 
     *d_sent_two, output, d4, dlogits_two, dgain_five = run(
         turn_kernel,
         (
-            h3, slot_two, gate_two, probs_two, second_routes, slot_rows, gains, cotangent, *returned_two,
+            h3, slot_cols, gate_two, probs_two, slot_rows, gains, cotangent, *returned_two,
         ),
-        [VMEM] * (8 + PARTS),
+        [VMEM] * (7 + PARTS),
         [block_low] * PARTS + [row_low, row_full, lane_full, eight],
         [low_scratch, slots_scratch],
         flops=4 * slots * length * width,
         name="turn",
     )
     d_result_two = exchange(d_sent_two, experts)
-    d_received_two, hidden_two, d_inner_two = backward_parts(received_two, d_result_two, second_pair)
+    unused, d_received_two, hidden_two, d_inner_two = backward_in_turn(
+        received_two, d_result_two, second_pair
+    )
     d_back_two = exchange(d_received_two, experts)
-    d_second_in, d_second_out = scatter_offloaded(
-        *expert_grads(received_two, d_result_two, hidden_two, d_inner_two)
-    )
+    grad_in_two, grad_out_two, *d_back_two = lax.optimization_barrier(
+        (
+            blocks_product(received_two, d_inner_two), blocks_product(hidden_two, d_result_two), *d_back_two,
+        )
+    )
+    d_second_in, d_second_out = scatter_offloaded(grad_in_two, grad_out_two)
 
     router_shape = shape_of((8, 2 * width), f32)
     d3, d3_low, d_z, dembed_two, drouter_two, small_two, dsums_part = run(
         second_back_kernel,
         (
-            slot_two, dlogits_two, h3, d4, embedding, routers[1], gains, convolved, stats, batch, point_out,
+            slot_cols, dlogits_two, h3, d4, embedding, routers[1], gains, convolved, stats, batch, point_out,
             *d_back_two,
         ),
         [VMEM] * (11 + PARTS),
-        [row_full, row_low, row_full, row_full, router_shape, eight, shape_of((devices, 2 * width), f32)],
+        [row_full, row_low, row_full, row_full, router_shape, eight, shape_of((devices, 1, 2 * width), f32)],
         [sums_scratch, slots_scratch],
         flops=4 * slots * length * width,
         name="second_back",
@@ -1190,71 +1274,91 @@
     dsums = gather_small(dsums_part)
     d_pointwise_out = rows_product(active, d3_low)
 
-    (
-        *d_sent_one, d1, dlogits_one, normed_two, normed_three, d_gates, d2_low, d_mixed, d_table, small_mid,
-        d_taps,
-    ) = run(
-        middle_back_kernel,
+    d2, d2_low, d_context, normed_three, d_gates, small_conv, d_taps = run(
+        conv_back_kernel,
+        (segment_starts, convolved, d_z, stats, dsums, d3, h2, gains, dense, kernel_taps),
+        [SMEM] + [VMEM] * 9,
+        [
+            row_full, row_low, row_low, row_low, shape_of((length, 2 * width), bf16), eight,
+            shape_of((16, width), f32),
+        ],
+        [edge_scratch, pltpu.VMEM((length, 2 * width), f32)],
+        flops=6 * length * width * width,
+        name="conv_back",
+    )
+    value_grad, gates_grad = split_columns(rows_product(normed_three, d_gates))
+    early = jnp.stack(
+        [
+            part.astype(bf16).reshape(groups, experts, width // devices, width)
+            for part in (rows_product(context, d2_low), d_pointwise_out, value_grad, gates_grad)
+        ],
+        axis=2,
+    )
+    early = expert_parts(early, experts)
+    *d_sent_one, d1, dlogits_one, normed_two, d_mixed, d_table, small_mid = run(
+        attend_back_kernel,
         (
-            segment_starts, convolved, d_z, stats, dsums, batch, d3, h1, h2, gains, dense, kernel_taps, mirrored, query_u, query_v, keys, values, table, context, logs, slot_one, gate_one, probs_one,
-            first_routes, slot_rows, *returned_one,
+            segment_starts, d2, d_context, h1, gains, dense, mirrored, query_u, query_v, keys, values, table,
+            context, logs, slot_cols, gate_one, probs_one, slot_rows, *returned_one,
         ),
-        [SMEM] + [VMEM] * (24 + PARTS),
+        [SMEM] + [VMEM] * (17 + PARTS),
         [block_low] * PARTS
         + [
-            row_full, lane_full, row_low, row_low, shape_of((length, 2 * width), bf16), row_low,
-            shape_of((length, 3 * width), bf16), row_low, shape_of((16, width), f32),
-            shape_of((16, width), f32),
+            row_full, lane_full, row_low, shape_of((length, 3 * width), bf16),
+            shape_of((width, length), bf16), shape_of((16, width), f32),
         ],
         [
-            edge_scratch, pltpu.VMEM((length, 2 * width), f32), low_scratch, low_scratch, low_scratch,
-            slots_scratch,
+            low_scratch, pltpu.VMEM(table_low.shape, bf16), slots_scratch,
+            pltpu.VMEM((width, length), f32), pltpu.VMEM((width, length), f32),
+            pltpu.VMEM((width, length + 2 * PAD * TILE), f32),
         ]
         + attend_back_scratch(),
         flops=32 * length * length * width,
-        name="middle_back",
-    )
+        name="attend_back",
+    )
+    early, *d_sent_one = lax.optimization_barrier((early, *d_sent_one))
     d_result_one = exchange(d_sent_one, experts)
-    d_received_one, hidden_one, d_inner_one = backward_parts(received_one, d_result_one, first_pair)
+    (late,), d_received_one, hidden_one, d_inner_one = backward_in_turn(
+        received_one, d_result_one, first_pair, (normed_two, d_mixed, d_table, mirrored)
+    )
+    late = expert_parts(late.reshape(groups, experts, width // devices, 4 * width), experts)
     d_back_one = exchange(d_received_one, experts)
-    d_first_in, d_first_out = scatter_direct(
-        *expert_grads(received_one, d_result_one, hidden_one, d_inner_one), groups
-    )
-
-    d_start, d_embed, drouter_one, small_one = run(
+    early = add_up(early).astype(bf16).reshape(groups, -1, width)
+    grad_out = blocks_product(hidden_one, d_result_one).reshape(groups, -1, width)
+    near_out = near_half(jnp.concatenate([grad_out, early], axis=1))
+    grad_in = blocks_product(received_one, d_inner_one).reshape(groups, -1, inner)
+    near_out, grad_in, late, d_second_in, d_second_out, d_back_one = lax.optimization_barrier(
+        (near_out, grad_in, late, d_second_in, d_second_out, d_back_one)
+    )
+    far_out = own_parts(near_out, lax.axis_index("dp") // 2, groups, 2, "dp")
+    late = add_up(late).astype(bf16)
+    near_in = near_half(jnp.concatenate([grad_in, late], axis=1))
+    d_start, d_embed, routers_grad, rows_grad = run(
         last_kernel,
         (
-            slot_one, dlogits_one, inputs, d1, embedding, routers[0], gains, dembed_two, *d_back_one,
+            slot_cols, dlogits_one, inputs, d1, embedding, routers[0], gains, dembed_two,
+            drouter_two, small_mid, small_conv, small_two, dgain_five, d_taps, *d_back_one,
         ),
-        [VMEM] * (8 + PARTS),
-        [row_full, row_full, router_shape, eight],
+        [VMEM] * (14 + PARTS),
+        [row_full, row_full, shape_of((16, 2 * width), f32), shape_of((count, width), f32)],
         [slots_scratch],
         flops=4 * slots * length * width,
         name="last",
     )
 
-    dense_grad = jnp.concatenate(
-        [
-            rows_product(normed_two, d_mixed),
-            rows_product(mirrored, d_table),
-            rows_product(context, d2_low),
-            d_pointwise_out,
-            rows_product(normed_three, d_gates),
-        ],
-        axis=1,
-    ).astype(bf16)
-    dense_share = scatter_dense(dense_grad, groups, experts)
-
-    rows_grad = jnp.concatenate(
-        [
-            small_one[0:1], small_mid[1:2], small_mid[0:1], small_two[0:1], dgain_five[0:1],
-            small_mid[8:10], d_taps[:taps], small_two[1:3],
-        ],
-        axis=0,
-    )
+    near_in, far_out, routers_grad, rows_grad = lax.optimization_barrier(
+        (near_in, far_out, routers_grad, rows_grad)
+    )
+    out_sum = add_up(far_out)
+    in_sum = add_up(own_parts(near_in, lax.axis_index("dp") // 2, groups, 2, "dp"))
+    d_first_out = out_sum[None, : first_out.shape[1]]
+    d_first_in = in_sum[None, : first_in.shape[1]]
+    late_share = in_sum[first_in.shape[1] :]
+    early_share = out_sum[first_out.shape[1] :].reshape(4, width // devices, width)
+    early_share = jnp.concatenate([early_share[k] for k in range(4)], axis=1)
     rows_grad = rows_grad.reshape(count, devices, share).transpose(1, 0, 2).reshape(devices, -1)
-    routers_grad = jnp.stack([drouter_one[:experts], drouter_two[:experts]])
-    routers_grad = routers_grad.reshape(2 * experts, devices, feats).transpose(1, 0, 2).reshape(devices, -1)
+    routers_grad = routers_grad.reshape(2, 8, devices, feats)[:, :experts]
+    routers_grad = routers_grad.transpose(2, 0, 1, 3).reshape(devices, -1)
     small_grad = jnp.concatenate([rows_grad, routers_grad], axis=1)
     small_share = jnp.sum(
         lax.all_to_all(small_grad, BOTH, split_axis=0, concat_axis=0, tiled=True), axis=0
@@ -1273,15 +1377,15 @@
         d_first_out,
         d_second_in,
         d_second_out,
-        dense_share[:, : 3 * width],
-        dense_share[:, 3 * width : 4 * width],
+        late_share[:, : 3 * width],
+        late_share[:, 3 * width :],
         rows_share[5:7],
-        dense_share[:, 4 * width : 5 * width],
-        dense_share[:, 6 * width : 8 * width],
+        early_share[:, :width],
+        early_share[:, 2 * width :],
         rows_share[7 : 7 + taps],
         rows_share[7 + taps],
         rows_share[8 + taps],
-        dense_share[:, 5 * width : 6 * width],
+        early_share[:, width : 2 * width],
     )
 
 

time: 593 us -> 553 us (0.933)
  starting transfers between devices: 98.7 us -> 69.7 us
  local copies, waits for them, and re-layouts: 72.3 us -> 50 us
  waiting for transfers between devices: 114 us -> 134 us
  Pallas kernels: 246 us -> 234 us
    ppermute x46 -> x38, starting transfers between devices: 60.2 us -> 34.6 us  [across(): return lax.ppermute(values, axis, [(i, i ^ offset) for i in range(size)])]
    pallas_call x20 -> x21, Pallas kernels: 241 us -> 229 us  [run(): pl.pallas_call(kernel, out_shape=outs, in_specs=in_specs, out_specs=[VMEM...]
    ppermute x7, waiting for transfers between devices: 6.11 us -> 15.4 us  [ring_gather(): lax.ppermute(pieces[-step + 1 or 0], 'dp', ring_pairs(size, True))]
    all_to_all x3, waiting for transfers between devices: 9.17 us -> 18.1 us  [gather_small(): return lax.all_to_all(values, BOTH, split_axis=0, concat_axis=0, tiled=True)]
    unnamed x141 -> x145, local copies, waits for them, and re-layouts: 32.5 us -> 23.7 us
    ppermute x7, waiting for transfers between devices: 12.8 us -> 4.24 us  [ring_gather(): pieces[step] = lax.ppermute(pieces[step - 1], 'dp', ring_pairs(size, False))]
    ppermute x46 -> x38, waiting for transfers between devices: 77.4 us -> 80.9 us  [across(): return lax.ppermute(values, axis, [(i, i ^ offset) for i in range(size)])]
    dot_general x9 -> x7, matrix products: 25.1 us -> 24.2 us  [rows_product(): lax.dot_general(left, right, (((0,), (0,)), ((), ())), preferred_element_...]
  transfers between devices with their start and end apart: 69 -> 61, of which waited for: 28 -> 22; matrix products, arithmetic and copies ran while one was open for 13% -> 10% of each run, Pallas kernels for 39% -> 41%
where the time goes in v3:
time: 553 us; the launch traced here: 543 us
  Pallas kernels  234 us (42%)
  waiting for transfers between devices  134 us (24%)
  starting transfers between devices  69.7 us (13%)
  local copies, waits for them, and re-layouts  50 us (9%)
  matrix products  24.2 us (4%)
  other arithmetic  16.5 us (3%)
  between operations  15 us (3%)
    pallas_call x21, Pallas kernels, run(): pl.pallas_call(kernel, out_shape=outs, in_specs=in_specs, out_specs=[VMEM...  229 us
    ppermute x38, waiting for transfers between devices, across(): return lax.ppermute(values, axis, [(i, i ^ offset) for i in range(size)])  80.9 us
    ppermute x38, starting transfers between devices, across(): return lax.ppermute(values, axis, [(i, i ^ offset) for i in range(size)])  34.6 us
    dot_general x7, matrix products, rows_product(): lax.dot_general(left, right, (((0,), (0,)), ((), ())), preferred_element_...  24.2 us
    unnamed x145, local copies, waits for them, and re-layouts  23.7 us
    all_to_all x3, waiting for transfers between devices, gather_small(): return lax.all_to_all(values, BOTH, split_axis=0, concat_axis=0, tiled=True)  18.1 us
    ppermute x7, waiting for transfers between devices, ring_gather(): lax.ppermute(pieces[-step + 1 or 0], 'dp', ring_pairs(size, True))  15.4 us
    all_to_all x3, starting transfers between devices, gather_small(): return lax.all_to_all(values, BOTH, split_axis=0, concat_axis=0, tiled=True)  14.6 us
  transfers between devices with their start and end apart: 61, of which 22 were waited for; matrix products, arithmetic and copies ran while one was open for 10% of the time, Pallas kernels for 41%

profile of v3, /device:TPU:0, one launch (start us, length us, event | category | flops | bytes accessed | tf_op | source)
XLA Modules:
  0.0 543.4 jit_solution(9070751689890394483)
XLA Ops:
  22.7 6.3 %all-to-all-start = ((f32[32,1,640]{2,1,0:T(1,128)}), f32[32,1,640]{2,1,0:T(1,128)S(1)}, u32[]{:S(2)}, u32[]{:S(2)}) async-start(f32[32,1,640]{2,1,0:T(1,128)} %broadcast_in_dim.32), calls=%async_computation | async-start | bytes 163840 | tf_op jit(solution)/shard_map/all_to_all | solution.py:946
  33.3 4.1 all-to-all-done
  44.2 6.9 %collective-permute-done.5.refs_6_ = bf16[64,2048]{1,0:T(8,128)(2,1)S(1)} collective-permute-done((bf16[64,2048]{1,0:T(8,128)(2,1)S(1)}, bf16[64,2048]{1,0:T(8,128)(2,1)S(1)}, u32[]{:S(2)}, u32[]{:S(2)}) %collective-permute-start.5) | collective-permute-done | bytes 262176 | tf_op jit(solution)/shard_map/ppermute | solution.py:995
  53.1 6.8 %front.1 = (bf16[272,512]{1,0:T(8,128)(2,1)}, bf16[272,512]{1,0:T(8,128)(2,1)}, bf16[272,512]{1,0:T(8,128)(2,1)}, bf16[272,512]{1,0:T(8,128)(2,1)}, f32[1024,128]{1,0:T(8,128)}, /*index=5*/f32[1024,1]{1,0:T(8,128)}) custom-call(bf16[1024,512]{1,0:T(8,128)(2,1)} %hidden_ref.5, bf16[1024,512]{1,0:T(8,128)(2,1)} %embed_ref.7, f32[8,512]{1,0:T(8,128)} %pad.20.gain_ref.gains_ref, ...), custom_call_target="tpu_custom_call" | custom-call | flops 2281701376 | bytes 4575232 | tf_op jit(solution)/shard_map/front/pallas_call | solution.py:30
  65.5 8.6 %collective-permute-done.13.refs_12_ = bf16[256,512]{1,0:T(8,128)(2,1)S(1)} collective-permute-done((bf16[256,512]{1,0:T(8,128)(2,1)S(1)}, bf16[256,512]{1,0:T(8,128)(2,1)S(1)}, u32[]{:S(2)}, u32[]{:S(2)}) %collective-permute-start.13) | collective-permute-done | bytes 262176 | tf_op jit(solution)/shard_map/ppermute | solution.py:995
  77.2 5.0 assemble.1
  99.3 5.7 %collective-permute-done.18.refs_2_ = bf16[272,512]{1,0:T(8,128)(2,1)S(1)} collective-permute-done((bf16[272,512]{1,0:T(8,128)(2,1)S(1)}, bf16[272,512]{1,0:T(8,128)(2,1)S(1)}, u32[]{:S(2)}, u32[]{:S(2)}) %collective-permute-start.18) | collective-permute-done | bytes 278560 | tf_op jit(solution)/shard_map/ppermute | solution.py:952
  105.8 46.1 %middle.1 = (f32[1024,512]{1,0:T(8,128)}, f32[1024,512]{1,0:T(8,128)}, bf16[1024,512]{1,0:T(8,128)(2,1)}, bf16[1024,512]{1,0:T(8,128)(2,1)}, bf16[1024,512]{1,0:...) custom-call(s32[1,5]{1,0:T(1,128)} %starts_ref.5, ...), custom_call_target="tpu_custom_call" | custom-call | flops 8589934592 | bytes 21827604 | tf_op jit(solution)/shard_map/middle/pallas_call | solution.py:30
  152.0 4.1 all-to-all-start.1
  159.0 6.3 %all-to-all-done.1.totals_ref = f32[32,1,1536]{2,1,0:T(1,128)S(1)} async-done(((f32[32,1,1536]{2,1,0:T(1,128)}), f32[32,1,1536]{2,1,0:T(1,128)S(1)}, u32[]{:S(2)}, u32[]{:S(2)}) %all-to-all-start.1) | async-done | bytes 196640 | tf_op jit(solution)/shard_map/all_to_all | solution.py:946
  165.9 9.9 %second.1 = (bf16[272,512]{1,0:T(8,128)(2,1)}, bf16[272,512]{1,0:T(8,128)(2,1)}, bf16[272,512]{1,0:T(8,128)(2,1)}, bf16[272,512]{1,0:T(8,128)(2,1)}, f32[1024,51...) custom-call(f32[1024,512]{1,0:T(8,128)} %get-tuple-element.187.h2_ref, ...), custom_call_target="tpu_custom_call" | custom-call | flops 2281701376 | bytes 11620352 | tf_op jit(solution)/shard_map/second/pallas_call | solution.py:30
  177.7 11.3 %all-gather.10.cloned.1.call-done = bf16[1,2048,512]{2,1,0:T(8,128)(2,1)} async-done(((bf16[1,256,512]{2,1,0:T(8,128)(2,1)}), bf16[1,2048,512]{2,1,0:T(8,128)(2,1)}) %all-gather.10.cloned.1.call-update) | async-done | bytes 2097168 | tf_op jit(solution)/shard_map/all_gather | solution.py:1173
  200.8 5.1 collective-permute-done.24.refs_2_
  210.4 10.1 %turn.1 = (bf16[272,512]{1,0:T(8,128)(2,1)}, bf16[272,512]{1,0:T(8,128)(2,1)}, bf16[272,512]{1,0:T(8,128)(2,1)}, bf16[272,512]{1,0:T(8,128)(2,1)}, bf16[1024,512...) custom-call(f32[1024,512]{1,0:T(8,128)} %get-tuple-element.190.h3_ref, ...), custom_call_target="tpu_custom_call" | custom-call | flops 2281701376 | bytes 10162176 | tf_op jit(solution)/shard_map/turn/pallas_call | solution.py:30
  223.7 4.1 experts_back.6
  231.0 4.2 collective-permute-done.28.refs_1_
  243.5 4.2 fusion.38
  247.8 6.7 %fusion.41 = bf16[512,2048]{1,0:T(8,128)(2,1)} fusion(bf16[272,2048]{1,0:T(8,128)(2,1)} %copy-done.18, bf16[272,2048]{1,0:T(8,128)(2,1)} %copy-done.17, bf16[272,2048]{1,0:T(8,128)(2,1)} %copy-done.26, bf16[272,2048]{1,0:T(8,128)(2,1)} %copy-done.25, bf16[272,512]{1,0:T(8,128)(2,1)S(1)} %collective-permute-done.22.refs_0_, ...), kind=kOutput, calls=%fused_computation.37 | convolution fusion | flops 2305032192 | bytes 7667712 | tf_op jit(solution)/shard_map/dot_general | solution.py:1079
  255.2 12.2 %second_back.1 = (f32[1024,512]{1,0:T(8,128)}, bf16[1024,512]{1,0:T(8,128)(2,1)}, f32[1024,512]{1,0:T(8,128)}, f32[1024,512]{1,0:T(8,128)}, f32[8,1024]{1,0:T(8,...) custom-call(s32[1024,128]{1,0:T(8,128)} %get-tuple-element.172.cols_ref, f32[1024,128]{1,0:T(8,128)} %get-tuple-element.204.dlogits_ref, ...), custom_call_target="tpu_custom_call" | custom-call | flops 2281701376 | bytes 17858560 | tf_op jit(solution)/shard_map/second_back/pallas_call | solution.py:30
  267.4 4.2 all-to-all-start.2
  274.2 7.7 %all-to-all-done.2.dsums_ref = f32[32,1,1024]{2,1,0:T(1,128)S(1)} async-done(((f32[32,1,1024]{2,1,0:T(1,128)}), f32[32,1,1024]{2,1,0:T(1,128)S(1)}, u32[]{:S(2)}, u32[]{:S(2)}) %all-to-all-start.2) | async-done | bytes 131104 | tf_op jit(solution)/shard_map/all_to_all | solution.py:946
  282.5 28.0 %conv_back.1 = (f32[1024,512]{1,0:T(8,128)}, bf16[1024,512]{1,0:T(8,128)(2,1)}, bf16[1024,512]{1,0:T(8,128)(2,1)}, bf16[1024,512]{1,0:T(8,128)(2,1)}, bf16[1024,...) custom-call(s32[1,5]{1,0:T(1,128)} %starts_ref.5, f32[1024,512]{1,0:T(8,128)} %get-tuple-element.188.conv_ref, ...), custom_call_target="tpu_custom_call" | custom-call | flops 1610612736 | bytes 20168724 | tf_op jit(solution)/shard_map/conv_back/pallas_call | solution.py:30
  318.6 68.7 %attend_back.1 = (bf16[272,512]{1,0:T(8,128)(2,1)}, bf16[272,512]{1,0:T(8,128)(2,1)}, bf16[272,512]{1,0:T(8,128)(2,1)}, bf16[272,512]{1,0:T(8,128)(2,1)}, f32[10...) custom-call(s32[1,5]{1,0:T(1,128)} %starts_ref.5, ...), custom_call_target="tpu_custom_call" | custom-call | flops 17179869184 | bytes 29052948 | tf_op jit(solution)/shard_map/attend_back/pallas_call | solution.py:30
  392.6 11.5 %experts_back.9 = (bf16[512,2048]{1,0:T(8,128)(2,1)}, bf16[272,512]{1,0:T(8,128)(2,1)S(1)}, bf16[272,512]{1,0:T(8,128)(2,1)S(1)}, bf16[272,2048]{1,0:T(8,128)(2,...) custom-call(bf16[512,2048]{1,0:T(8,128)(2,1)} %get-tuple-element.175.in_ref, ...), custom_call_target="tpu_custom_call" | custom-call | flops 3422552064 | bytes 18710528 | tf_op jit(solution)/shard_map/experts_back/pallas_call | solution.py:30
  422.7 4.3 fusion.32
  427.0 18.5 %collective-permute-done.38 = bf16[4,320,512]{2,1,0:T(8,128)(2,1)} collective-permute-done((bf16[4,320,512]{2,1,0:T(8,128)(2,1)}, bf16[4,320,512]{2,1,0:T(8,128)(2,1)}, u32[]{:S(2)}, u32[]{:S(2)}) %collective-permute-start.38) | collective-permute-done | bytes 1310752 | tf_op jit(solution)/shard_map/ppermute | solution.py:952
  453.7 5.9 %collective-permute-done.41 = bf16[8,16,2048]{2,1,0:T(8,128)(2,1)S(1)} collective-permute-done((bf16[8,16,2048]{2,1,0:T(8,128)(2,1)}, bf16[8,16,2048]{2,1,0:T(8,128)(2,1)S(1)}, u32[]{:S(2)}, u32[]{:S(2)}) %collective-permute-start.41) | collective-permute-done | bytes 524320 | tf_op jit(solution)/shard_map/ppermute | solution.py:952
  471.5 9.4 %last.1 = (f32[1024,512]{1,0:T(8,128)}, f32[1024,512]{1,0:T(8,128)}, f32[16,1024]{1,0:T(8,128)}, f32[24,512]{1,0:T(8,128)}) custom-call(s32[1024,128]{1,0:T(8,128)} %get-tuple-element.172.cols_ref, f32[1024,128]{1,0:T(8,128)} %get-tuple-element.249.dlogits_ref, bf16[1024,512]{1,0:T(8,128)(2,1)} %hidden_ref.5, f32[1024,512]{1,0:T(8,128)} %get-tuple-element.250.d1_ref, ...), custom_call_target="tpu_custom_call" | custom-call | flops 2281701376 | bytes 13189120 | tf_op jit(solution)/shard_map/last/pallas_call | solution.py:30
  480.9 14.4 %collective-permute-done.45 = bf16[4,80,2048]{2,1,0:T(8,128)(2,1)} collective-permute-done((bf16[4,80,2048]{2,1,0:T(8,128)(2,1)}, bf16[4,80,2048]{2,1,0:T(8,128)(2,1)}, u32[]{:S(2)}, u32[]{:S(2)}) %collective-permute-start.45) | collective-permute-done | bytes 1310752 | tf_op jit(solution)/shard_map/ppermute | solution.py:952
  499.9 5.6 %all-to-all-start.3 = ((f32[32,1,640]{2,1,0:T(1,128)}), f32[32,1,640]{2,1,0:T(1,128)S(1)}, u32[]{:S(2)}, u32[]{:S(2)}) async-start(f32[32,1,640]{2,1,0:T(1,128)} %all_to_all.22), calls=%async_computation.5 | async-start | bytes 163840 | tf_op jit(solution)/shard_map/all_to_all | solution.py:1364
  516.8 6.9 %collective-permute-done.49 = bf16[80,2048]{1,0:T(8,128)(2,1)S(1)} collective-permute-done((bf16[80,2048]{1,0:T(8,128)(2,1)S(1)}, bf16[80,2048]{1,0:T(8,128)(2,1)S(1)}, u32[]{:S(2)}, u32[]{:S(2)}) %collective-permute-start.49) | collective-permute-done | bytes 327712 | tf_op jit(solution)/shard_map/ppermute | solution.py:952
  523.7 9.8 %collective-permute-done.50 = bf16[80,2048]{1,0:T(8,128)(2,1)S(1)} collective-permute-done((bf16[80,2048]{1,0:T(8,128)(2,1)S(1)}, bf16[80,2048]{1,0:T(8,128)(2,1)S(1)}, u32[]{:S(2)}, u32[]{:S(2)}) %collective-permute-start.50) | collective-permute-done | bytes 327712 | tf_op jit(solution)/shard_map/ppermute | solution.py:952
  (342 shorter events, 165.8 us)
Async XLA Ops:
  7.2 97.9 %all-gather.6.cloned.1.call-start = ((), (), s32[]{:S(2)}) async-start(), calls=%async_computation.6 | async-start | bytes 4325376 | tf_op jit(solution)/shard_map/all_gather | solution.py:1167
  11.6 166.0 %all-gather.8.cloned.1.call-start = ((), (), s32[]{:S(2)}) async-start(), calls=%async_computation.9 | async-start | bytes 2359296 | tf_op jit(solution)/shard_map/all_gather | solution.py:1172
  12.4 176.6 %all-gather.10.cloned.1.call-start = ((), (), s32[]{:S(2)}) async-start(), calls=%async_computation.10 | async-start | bytes 2359296 | tf_op jit(solution)/shard_map/all_gather | solution.py:1173
  13.1 15.9 %collective-permute-start.10 = (bf16[256,512]{1,0:T(8,128)(2,1)}, bf16[256,512]{1,0:T(8,128)(2,1)S(1)}, u32[]{:S(2)}, u32[]{:S(2)}) collective-permute-start(bf16[256,512]{1,0:T(8,128)(2,1)} %bitcast.148), channel_id=1, source_target_pairs={{0,8},{8,16},{16,24},{24,28},{28,20},{20,12},{12,4},{4,0},{1,9},{9... | collective-permute-start | bytes 786440 | tf_op jit(solution)/shard_map/ppermute | solution.py:995
  16.2 22.0 %collective-permute-start.4 = (bf16[64,2048]{1,0:T(8,128)(2,1)}, bf16[64,2048]{1,0:T(8,128)(2,1)S(1)}, u32[]{:S(2)}, u32[]{:S(2)}) collective-permute-start(bf16[64,2048]{1,0:T(8,128)(2,1)} %bitcast.146), channel_id=1, source_target_pairs={{0,8},{8,16},{16,24},{24,28},{28,20},{20,12},{12,4},{4,0},{1,9},{9... | collective-permute-start | bytes 786440 | tf_op jit(solution)/shard_map/ppermute | solution.py:995
  18.2 20.8 %collective-permute-start.7 = (bf16[256,512]{1,0:T(8,128)(2,1)}, bf16[256,512]{1,0:T(8,128)(2,1)S(1)}, u32[]{:S(2)}, u32[]{:S(2)}) collective-permute-start(bf16[256,512]{1,0:T(8,128)(2,1)} %bitcast.149), channel_id=1, source_target_pairs={{0,4},{8,0},{16,8},{24,16},{28,24},{20,28},{12,20},{4,12},{1,5},{9... | collective-permute-start | bytes 786440 | tf_op jit(solution)/shard_map/ppermute | solution.py:993
  40.4 19.6 %collective-permute-start.12 = (bf16[256,512]{1,0:T(8,128)(2,1)S(1)}, bf16[256,512]{1,0:T(8,128)(2,1)S(1)}, u32[]{:S(2)}, u32[]{:S(2)}) collective-permute-start(bf16[256,512]{1,0:T(8,128)(2,1)S(1)} %collective-permute-done.11.refs_14_), channel_id=1, source_target_pairs={{0,8},{8,16},{16,24},{24,28},{28,20},{20,12},{12,4},{4,0},{1,9},{9... | collective-permute-start | bytes 786440 | tf_op jit(solution)/shard_map/ppermute | solution.py:995
  41.2 20.5 %collective-permute-start.2 = (bf16[64,2048]{1,0:T(8,128)(2,1)S(1)}, bf16[64,2048]{1,0:T(8,128)(2,1)S(1)}, u32[]{:S(2)}, u32[]{:S(2)}) collective-permute-start(bf16[64,2048]{1,0:T(8,128)(2,1)S(1)} %collective-permute-done.1.refs_2_), channel_id=1, source_target_pairs={{0,4},{8,0},{16,8},{24,16},{28,24},{20,28},{12,20},{4,12},{1,5},{9... | collective-permute-start | bytes 786440 | tf_op jit(solution)/shard_map/ppermute | solution.py:993
  60.0 22.3 %collective-permute-start.14 = (bf16[272,512]{1,0:T(8,128)(2,1)}, bf16[272,512]{1,0:T(8,128)(2,1)S(1)}, u32[]{:S(2)}, u32[]{:S(2)}) collective-permute-start(bf16[272,512]{1,0:T(8,128)(2,1)} %get-tuple-element.178), channel_id=1, source_target_pairs={{0,1},{1,0},{2,3},{3,2},{4,5},{5,4},{6,7},{7,6},{8,9},{9,8},{10,11... | collective-permute-start | bytes 835592 | tf_op jit(solution)/shard_map/ppermute | solution.py:952
  63.0 25.9 %collective-permute-start.15 = (bf16[272,512]{1,0:T(8,128)(2,1)}, bf16[272,512]{1,0:T(8,128)(2,1)S(1)}, u32[]{:S(2)}, u32[]{:S(2)}) collective-permute-start(bf16[272,512]{1,0:T(8,128)(2,1)} %get-tuple-element.181), channel_id=1, source_target_pairs={{0,2},{1,3},{2,0},{3,1},{4,6},{5,7},{6,4},{7,5},{8,10},{9,11},{10,... | collective-permute-start | bytes 835592 | tf_op jit(solution)/shard_map/ppermute | solution.py:952
  64.6 24.3 %collective-permute-start.16 = (bf16[272,512]{1,0:T(8,128)(2,1)}, bf16[272,512]{1,0:T(8,128)(2,1)S(1)}, u32[]{:S(2)}, u32[]{:S(2)}) collective-permute-start(bf16[272,512]{1,0:T(8,128)(2,1)} %get-tuple-element.182), channel_id=1, source_target_pairs={{0,3},{1,2},{2,1},{3,0},{4,7},{5,6},{6,5},{7,4},{8,11},{9,10},{10,... | collective-permute-start | bytes 835592 | tf_op jit(solution)/shard_map/ppermute | solution.py:952
  156.1 294.0 %reduce-scatter.3.cloned.1.call-start = ((), (), s32[]{:S(2)}) async-start(), calls=%async_computation.7 | async-start | bytes 2359296 | tf_op jit(solution)/shard_map/reduce_scatter | solution.py:1089
  176.2 19.7 %collective-permute-start.21 = (bf16[272,512]{1,0:T(8,128)(2,1)}, bf16[272,512]{1,0:T(8,128)(2,1)S(1)}, u32[]{:S(2)}, u32[]{:S(2)}) collective-permute-start(bf16[272,512]{1,0:T(8,128)(2,1)} %get-tuple-element.197), channel_id=1, source_target_pairs={{0,2},{1,3},{2,0},{3,1},{4,6},{5,7},{6,4},{7,5},{8,10},{9,11},{10,... | collective-permute-start | bytes 835592 | tf_op jit(solution)/shard_map/ppermute | solution.py:952
  177.0 18.9 %collective-permute-start.22 = (bf16[272,512]{1,0:T(8,128)(2,1)}, bf16[272,512]{1,0:T(8,128)(2,1)S(1)}, u32[]{:S(2)}, u32[]{:S(2)}) collective-permute-start(bf16[272,512]{1,0:T(8,128)(2,1)} %get-tuple-element.198), channel_id=1, source_target_pairs={{0,3},{1,2},{2,1},{3,0},{4,7},{5,6},{6,5},{7,4},{8,11},{9,10},{10,... | collective-permute-start | bytes 835592 | tf_op jit(solution)/shard_map/ppermute | solution.py:952
  238.3 16.2 %collective-permute-start.30 = (bf16[272,512]{1,0:T(8,128)(2,1)S(1)}, bf16[272,512]{1,0:T(8,128)(2,1)S(1)}, u32[]{:S(2)}, u32[]{:S(2)}) collective-permute-start(bf16[272,512]{1,0:T(8,128)(2,1)S(1)} %get-tuple-element.229), channel_id=1, source_target_pairs={{0,2},{1,3},{2,0},{3,1},{4,6},{5,7},{6,4},{7,5},{8,10},{9,11},{10,... | collective-permute-start | bytes 835592 | tf_op jit(solution)/shard_map/ppermute | solution.py:952
  271.6 180.3 %reduce-scatter.5.cloned.1.call-start = ((), (), s32[]{:S(2)}) async-start(), calls=%async_computation.8 | async-start | bytes 2359296 | tf_op jit(solution)/shard_map/reduce_scatter | solution.py:1090
  316.5 71.0 %collective-permute-start.32 = (bf16[8,4,16,512]{3,2,1,0:T(8,128)(2,1)S(1)}, bf16[8,4,16,512]{3,2,1,0:T(8,128)(2,1)S(1)}, u32[]{:S(2)}, u32[]{:S(2)}) collective-permute-start(bf16[8,4,16,512]{3,2,1,0:T(8,128)(2,1)S(1)} %bitcast.140), channel_id=1, source_target_pairs={{0,1},{1,0},{2,3},{3,2},{4,5},{5,4},{6,7},{7,6},{8,9},{9,8},{10,11... | collective-permute-start | bytes 1572872 | tf_op jit(solution)/shard_map/ppermute | solution.py:952
  316.8 70.7 %collective-permute-start.33 = (bf16[8,4,16,512]{3,2,1,0:T(8,128)(2,1)S(1)}, bf16[8,4,16,512]{3,2,1,0:T(8,128)(2,1)S(1)}, u32[]{:S(2)}, u32[]{:S(2)}) collective-permute-start(bf16[8,4,16,512]{3,2,1,0:T(8,128)(2,1)S(1)} %bitcast.141), channel_id=1, source_target_pairs={{0,2},{1,3},{2,0},{3,1},{4,6},{5,7},{6,4},{7,5},{8,10},{9,11},{10,... | collective-permute-start | bytes 1572872 | tf_op jit(solution)/shard_map/ppermute | solution.py:952
  318.1 69.4 %collective-permute-start.34 = (bf16[8,4,16,512]{3,2,1,0:T(8,128)(2,1)S(1)}, bf16[8,4,16,512]{3,2,1,0:T(8,128)(2,1)S(1)}, u32[]{:S(2)}, u32[]{:S(2)}) collective-permute-start(bf16[8,4,16,512]{3,2,1,0:T(8,128)(2,1)S(1)} %bitcast.142), channel_id=1, source_target_pairs={{0,3},{1,2},{2,1},{3,0},{4,7},{5,6},{6,5},{7,4},{8,11},{9,10},{10,... | collective-permute-start | bytes 1572872 | tf_op jit(solution)/shard_map/ppermute | solution.py:952
  387.6 16.5 %collective-permute-start.36 = (bf16[272,512]{1,0:T(8,128)(2,1)}, bf16[272,512]{1,0:T(8,128)(2,1)S(1)}, u32[]{:S(2)}, u32[]{:S(2)}) collective-permute-start(bf16[272,512]{1,0:T(8,128)(2,1)} %get-tuple-element.279), channel_id=1, source_target_pairs={{0,2},{1,3},{2,0},{3,1},{4,6},{5,7},{6,4},{7,5},{8,10},{9,11},{10,... | collective-permute-start | bytes 835592 | tf_op jit(solution)/shard_map/ppermute | solution.py:952
  414.4 31.1 %collective-permute-start.38 = (bf16[4,320,512]{2,1,0:T(8,128)(2,1)}, bf16[4,320,512]{2,1,0:T(8,128)(2,1)}, u32[]{:S(2)}, u32[]{:S(2)}) collective-permute-start(bf16[4,320,512]{2,1,0:T(8,128)(2,1)} %fusion.47), channel_id=1, source_target_pairs={{0,4},{4,0},{8,12},{12,8},{16,20},{20,16},{24,28},{28,24},{1,5},{5... | collective-permute-start | bytes 3932168 | tf_op jit(solution)/shard_map/ppermute | solution.py:952
  415.9 33.1 %collective-permute-start.43 = (bf16[272,512]{1,0:T(8,128)(2,1)S(1)}, bf16[272,512]{1,0:T(8,128)(2,1)S(1)}, u32[]{:S(2)}, u32[]{:S(2)}) collective-permute-start(bf16[272,512]{1,0:T(8,128)(2,1)S(1)} %get-tuple-element.300), channel_id=1, source_target_pairs={{0,2},{1,3},{2,0},{3,1},{4,6},{5,7},{6,4},{7,5},{8,10},{9,11},{10,... | collective-permute-start | bytes 835592 | tf_op jit(solution)/shard_map/ppermute | solution.py:952
  417.5 36.2 %collective-permute-start.44 = (bf16[272,512]{1,0:T(8,128)(2,1)S(1)}, bf16[272,512]{1,0:T(8,128)(2,1)}, u32[]{:S(2)}, u32[]{:S(2)}) collective-permute-start(bf16[272,512]{1,0:T(8,128)(2,1)S(1)} %get-tuple-element.301), channel_id=1, source_target_pairs={{0,3},{1,2},{2,1},{3,0},{4,7},{5,6},{6,5},{7,4},{8,11},{9,10},{10,... | collective-permute-start | bytes 835592 | tf_op jit(solution)/shard_map/ppermute | solution.py:952
  420.5 33.2 %collective-permute-start.39 = (bf16[8,16,2048]{2,1,0:T(8,128)(2,1)}, bf16[8,16,2048]{2,1,0:T(8,128)(2,1)}, u32[]{:S(2)}, u32[]{:S(2)}) collective-permute-start(bf16[8,16,2048]{2,1,0:T(8,128)(2,1)} %get-tuple-element.327), channel_id=1, source_target_pairs={{0,1},{1,0},{2,3},{3,2},{4,5},{5,4},{6,7},{7,6},{8,9},{9,8},{10,11... | collective-permute-start | bytes 1572872 | tf_op jit(solution)/shard_map/ppermute | solution.py:952
  421.1 32.6 %collective-permute-start.40 = (bf16[8,16,2048]{2,1,0:T(8,128)(2,1)}, bf16[8,16,2048]{2,1,0:T(8,128)(2,1)}, u32[]{:S(2)}, u32[]{:S(2)}) collective-permute-start(bf16[8,16,2048]{2,1,0:T(8,128)(2,1)} %get-tuple-element.326), channel_id=1, source_target_pairs={{0,2},{1,3},{2,0},{3,1},{4,6},{5,7},{6,4},{7,5},{8,10},{9,11},{10,... | collective-permute-start | bytes 1572872 | tf_op jit(solution)/shard_map/ppermute | solution.py:952
  464.1 31.1 %collective-permute-start.45 = (bf16[4,80,2048]{2,1,0:T(8,128)(2,1)}, bf16[4,80,2048]{2,1,0:T(8,128)(2,1)}, u32[]{:S(2)}, u32[]{:S(2)}) collective-permute-start(bf16[4,80,2048]{2,1,0:T(8,128)(2,1)} %dynamic-slice_bitcast_fusion), channel_id=1, source_target_pairs={{0,4},{4,0},{8,12},{12,8},{16,20},{20,16},{24,28},{28,24},{1,5},{5... | collective-permute-start | bytes 3932168 | tf_op jit(solution)/shard_map/ppermute | solution.py:952
  467.0 30.0 %collective-permute-start.46 = (bf16[320,512]{1,0:T(8,128)(2,1)S(1)}, bf16[320,512]{1,0:T(8,128)(2,1)S(1)}, u32[]{:S(2)}, u32[]{:S(2)}) collective-permute-start(bf16[320,512]{1,0:T(8,128)(2,1)S(1)} %get-tuple-element.338), channel_id=1, source_target_pairs={{0,8},{4,12},{8,0},{12,4},{16,24},{20,28},{24,16},{28,20},{1,9},{5... | collective-permute-start | bytes 983048 | tf_op jit(solution)/shard_map/ppermute | solution.py:952
  467.1 30.0 %collective-permute-start.47 = (bf16[320,512]{1,0:T(8,128)(2,1)S(1)}, bf16[320,512]{1,0:T(8,128)(2,1)S(1)}, u32[]{:S(2)}, u32[]{:S(2)}) collective-permute-start(bf16[320,512]{1,0:T(8,128)(2,1)S(1)} %get-tuple-element.337), channel_id=1, source_target_pairs={{0,16},{4,20},{8,24},{12,28},{16,0},{20,4},{24,8},{28,12},{1,17},{... | collective-permute-start | bytes 983048 | tf_op jit(solution)/shard_map/ppermute | solution.py:952
  470.5 26.6 %collective-permute-start.48 = (bf16[320,512]{1,0:T(8,128)(2,1)S(1)}, bf16[320,512]{1,0:T(8,128)(2,1)S(1)}, u32[]{:S(2)}, u32[]{:S(2)}) collective-permute-start(bf16[320,512]{1,0:T(8,128)(2,1)S(1)} %get-tuple-element.336), channel_id=1, source_target_pairs={{0,24},{4,28},{8,16},{12,20},{16,8},{20,12},{24,0},{28,4},{1,25},{... | collective-permute-start | bytes 983048 | tf_op jit(solution)/shard_map/ppermute | solution.py:952
  506.1 17.5 %collective-permute-start.49 = (bf16[80,2048]{1,0:T(8,128)(2,1)S(1)}, bf16[80,2048]{1,0:T(8,128)(2,1)S(1)}, u32[]{:S(2)}, u32[]{:S(2)}) collective-permute-start(bf16[80,2048]{1,0:T(8,128)(2,1)S(1)} %get-tuple-element.333), channel_id=1, source_target_pairs={{0,8},{4,12},{8,0},{12,4},{16,24},{20,28},{24,16},{28,20},{1,9},{5... | collective-permute-start | bytes 983048 | tf_op jit(solution)/shard_map/ppermute | solution.py:952
  507.9 25.5 %collective-permute-start.50 = (bf16[80,2048]{1,0:T(8,128)(2,1)S(1)}, bf16[80,2048]{1,0:T(8,128)(2,1)S(1)}, u32[]{:S(2)}, u32[]{:S(2)}) collective-permute-start(bf16[80,2048]{1,0:T(8,128)(2,1)S(1)} %get-tuple-element.335), channel_id=1, source_target_pairs={{0,16},{4,20},{8,24},{12,28},{16,0},{20,4},{24,8},{28,12},{1,17},{... | collective-permute-start | bytes 983048 | tf_op jit(solution)/shard_map/ppermute | solution.py:952
  510.3 23.1 %collective-permute-start.51 = (bf16[80,2048]{1,0:T(8,128)(2,1)S(1)}, bf16[80,2048]{1,0:T(8,128)(2,1)S(1)}, u32[]{:S(2)}, u32[]{:S(2)}) collective-permute-start(bf16[80,2048]{1,0:T(8,128)(2,1)S(1)} %get-tuple-element.334), channel_id=1, source_target_pairs={{0,24},{4,28},{8,16},{12,20},{16,8},{20,12},{24,0},{28,4},{1,25},{... | collective-permute-start | bytes 983048 | tf_op jit(solution)/shard_map/ppermute | solution.py:952
  (97 other events, 733.1 us)
Sparse Core Ops, SparseCore 0:
  11.8 74.0 all-gather.5
  88.0 49.4 all-gather.7
  139.6 49.3 all-gather.9
  254.6 69.3 reduce-scatter.2
  327.4 66.8 reduce-scatter.4

commit v4 on v3

--- a/solution.py
+++ b/solution.py
@@ -559,6 +559,28 @@
     ]
 
 
+def shifted(values, reach, taps):
+    rows = values.shape[0]
+    found = {}
+    for rest in range(8):
+        starts = [EDGE - reach + k for k in range(taps) if (EDGE - reach + k) % 8 == rest]
+        turned = pltpu.roll(values, (rows - rest) % rows, 0) if rest else values
+        for start in starts:
+            found[start - EDGE + reach] = turned[start - rest : start - rest + rows - 2 * EDGE]
+    return [found[k] for k in range(taps)]
+
+
+def at_edges(starts_ref, length, step):
+    for k in range(1, starts_ref.shape[1]):
+        edge = starts_ref[0, k]
+
+        @pl.when(edge < length)
+        def unused():
+            start = jnp.minimum((edge - 8) // 8 * 8, length - 2 * EDGE)
+            start = pl.multiple_of(start, 8)
+            step(start, iota((2 * EDGE, TILE), 0) + start)
+
+
 def spread_rows(rows_ref, out_ref):
     width = rows_ref.shape[1]
     for row in range(out_ref.shape[2] // width):
@@ -627,25 +649,37 @@
 
     def conv_step(index):
         first = index * TILE
-        place = iota((TILE, TILE), 0) + first
-        here = numbers_at(starts_ref, place)
-        valid = place < frames
-        totals = [jnp.zeros((TILE, TILE), f32) for unused in range(width // TILE)]
         around = pl.ds(pl.multiple_of(first, TILE), TILE + 2 * EDGE)
-        for tap in range(taps):
-            same = numbers_at(starts_ref, place + (tap - reach)) == here
-            for part in range(width // TILE):
-                lanes = slice(part * TILE, (part + 1) * TILE)
-                near = padded[around, lanes][EDGE + tap - reach : EDGE + tap - reach + TILE]
-                totals[part] = totals[part] + jnp.where(same, near, 0.0) * taps_ref[tap : tap + 1, lanes]
         for part in range(width // TILE):
             lanes = slice(part * TILE, (part + 1) * TILE)
-            conv_ref[rows_at(index, TILE), lanes] = totals[part]
-            kept = jnp.where(valid, totals[part], 0.0)
-            sums[0:1, lanes] += column_sum(kept)
-            sums[1:2, lanes] += column_sum(kept * kept)
+            total = jnp.zeros((TILE, TILE), f32)
+            for tap, near in enumerate(shifted(padded[around, lanes], reach, taps)):
+                total = total + near * taps_ref[tap : tap + 1, lanes]
+            conv_ref[rows_at(index, TILE), lanes] = total
 
     loop(length // TILE, conv_step)
+
+    def edge_step(start, place):
+        here = numbers_at(starts_ref, place)
+        masks = [numbers_at(starts_ref, place + (tap - reach)) == here for tap in range(taps)]
+        around = pl.ds(start, 2 * EDGE + 2 * EDGE)
+        for part in range(width // TILE):
+            lanes = slice(part * TILE, (part + 1) * TILE)
+            total = jnp.zeros(place.shape, f32)
+            for tap, near in enumerate(shifted(padded[around, lanes], reach, taps)):
+                total = total + jnp.where(masks[tap], near, 0.0) * taps_ref[tap : tap + 1, lanes]
+            conv_ref[pl.ds(start, 2 * EDGE), lanes] = total
+
+    at_edges(starts_ref, length, edge_step)
+
+    def sums_step(index):
+        at = rows_at(index, BLOCK)
+        inside = (iota((BLOCK, 1), 0) + index * BLOCK) < frames
+        kept = jnp.where(inside, conv_ref[at, :], 0.0)
+        sums[0:1, :] += column_sum(kept)
+        sums[1:2, :] += column_sum(kept * kept)
+
+    loop(length // BLOCK, sums_step)
     sums[2:3, :] = jnp.zeros((1, width), f32) + frames.astype(f32)
     spread_rows(sums, sums_ref)
 
@@ -787,7 +821,7 @@
 
 def conv_back_kernel(
     starts_ref, conv_ref, dz_ref, stats_ref, dsums_ref, d3_ref, h2_ref, gains_ref, dense_ref, taps_ref,
-    d2_ref, d2low_ref, dcontext_ref, n3_ref, dg_ref, small_ref, dtaps_ref, padded, linear,
+    d2_ref, d2low_ref, dcontext_ref, n3_ref, dg_ref, small_ref, dtaps_ref, padded, linear, dtaps, edge_grad,
 ):
     length, width = h2_ref.shape
     unused, unused, mix_ref, unused, point_ref = dense_parts(dense_ref)
@@ -795,7 +829,7 @@
     reach = taps // 2
     frames = starts_ref[0, starts_ref.shape[1] - 1]
     small_ref[...] = jnp.zeros_like(small_ref)
-    dtaps_ref[...] = jnp.zeros_like(dtaps_ref)
+    dtaps[...] = jnp.zeros_like(dtaps)
     mean, batch_inverse, count = stats_ref[0:1, :], stats_ref[1:2, :], stats_ref[2:3, :]
     dsums = jnp.sum(dsums_ref[...], axis=0)
     d_variance = -0.5 * batch_inverse * batch_inverse * batch_inverse * dsums[:, width:]
@@ -819,31 +853,57 @@
     loop(length // BLOCK, conv_step)
 
     def turn_step(index):
-        first = index * TILE
         at = rows_at(index, TILE)
-        place = iota((TILE, TILE), 0) + first
-        here = numbers_at(starts_ref, place)
-        parts = width // TILE
-        totals = [jnp.zeros((TILE, TILE), f32) for unused in range(parts)]
-        values = [linear[at, part * TILE : (part + 1) * TILE] for part in range(parts)]
-        gates = [linear[at, width + part * TILE : width + (part + 1) * TILE] for part in range(parts)]
-        around = pl.ds(pl.multiple_of(first, TILE), TILE + 2 * EDGE)
-        for tap in range(taps):
-            same = numbers_at(starts_ref, place - (tap - reach)) == here
-            for part in range(parts):
-                lanes = slice(part * TILE, (part + 1) * TILE)
-                near = padded[around, lanes][EDGE - tap + reach : EDGE - tap + reach + TILE]
-                near = jnp.where(same, near, 0.0)
-                totals[part] = totals[part] + near * taps_ref[tap : tap + 1, lanes]
-                dtaps_ref[tap : tap + 1, lanes] += column_sum(near * (values[part] * gates[part]))
-        for part in range(parts):
+        around = pl.ds(pl.multiple_of(index * TILE, TILE), TILE + 2 * EDGE)
+        for part in range(width // TILE):
             lanes = slice(part * TILE, (part + 1) * TILE)
             other = slice(width + part * TILE, width + (part + 1) * TILE)
-            gate = gates[part]
-            dg_ref[at, lanes] = (totals[part] * gate).astype(bf16)
-            dg_ref[at, other] = (totals[part] * values[part] * gate * (1.0 - gate)).astype(bf16)
+            value, gate = linear[at, lanes], linear[at, other]
+            passed = value * gate
+            total = jnp.zeros((TILE, TILE), f32)
+            for step, near in enumerate(shifted(padded[around, lanes], reach, taps)):
+                tap = taps - 1 - step
+                total = total + near * taps_ref[tap : tap + 1, lanes]
+                dtaps[tap, :, lanes] += jnp.sum((near * passed).reshape(TILE // 8, 8, TILE), axis=0)
+            dg_ref[at, lanes] = (total * gate).astype(bf16)
+            dg_ref[at, other] = (total * passed * (1.0 - gate)).astype(bf16)
+
+    def edge_step(start, place):
+        rows = 2 * EDGE
+        at = pl.ds(start, rows)
+        here = numbers_at(starts_ref, place)
+        masks = [numbers_at(starts_ref, place - (reach - tap)) == here for tap in range(taps)]
+        around = pl.ds(start, rows + 2 * EDGE)
+        for part in range(width // TILE):
+            lanes = slice(part * TILE, (part + 1) * TILE)
+            other = slice(width + part * TILE, width + (part + 1) * TILE)
+            value, gate = linear[at, lanes], linear[at, other]
+            passed = value * gate
+            total = jnp.zeros((rows, TILE), f32)
+            for step, near in enumerate(shifted(padded[around, lanes], reach, taps)):
+                tap = taps - 1 - step
+                total = total + jnp.where(masks[step], near, 0.0) * taps_ref[tap : tap + 1, lanes]
+                extra = jnp.where(masks[step], 0.0, near) * passed
+                dtaps[tap, :, lanes] -= jnp.sum(extra.reshape(rows // 8, 8, TILE), axis=0)
+            edge_grad[:, lanes] = total * gate
+            edge_grad[:, other] = total * passed * (1.0 - gate)
+        low = pl.multiple_of(jnp.minimum(start // 16 * 16, length - rows - 16), 16)
+        wide = pl.ds(low, rows + 16)
+        shift = start - low
+        whole = dg_ref[wide, :].astype(f32)
+        grad = edge_grad[...]
+        zero = jnp.zeros((16, 2 * width), f32)
+        head = jnp.concatenate([grad, zero], axis=0)
+        middle = jnp.concatenate([zero[:8], grad, zero[:8]], axis=0)
+        tail = jnp.concatenate([zero, grad], axis=0)
+        place = iota((rows + 16, 1), 0) - shift
+        moved = jnp.where(shift == 0, head, jnp.where(shift == 8, middle, tail))
+        inside = (place >= 0) & (place < rows)
+        dg_ref[wide, :] = jnp.where(inside, moved, whole).astype(bf16)
 
     loop(length // TILE, turn_step)
+    at_edges(starts_ref, length, edge_step)
+    dtaps_ref[...] = jnp.sum(dtaps[...], axis=1)
 
     def gates_step(index):
         at = rows_at(index, BLOCK)
@@ -1198,7 +1258,10 @@
         name="front",
     )
     received_one = exchange(sent_one, experts)
-    result_one = forward_in_turn(received_one, first_pair)
+    result_one = (
+        expert_forward(received_one[2:3], *first_pair) + expert_forward(received_one[3:], *first_pair)
+    )
+    result_one = expert_forward(received_one[:2], *first_pair) + result_one
     returned_one = exchange(result_one, experts)
 
     edge_scratch = pltpu.VMEM((length + 2 * EDGE, width), f32)
@@ -1282,7 +1345,10 @@
             row_full, row_low, row_low, row_low, shape_of((length, 2 * width), bf16), eight,
             shape_of((16, width), f32),
         ],
-        [edge_scratch, pltpu.VMEM((length, 2 * width), f32)],
+        [
+            edge_scratch, pltpu.VMEM((length, 2 * width), f32), pltpu.VMEM((16, 8, width), f32),
+            pltpu.VMEM((2 * EDGE, 2 * width), f32),
+        ],
         flops=6 * length * width * width,
         name="conv_back",
     )
@@ -1327,12 +1393,11 @@
     grad_out = blocks_product(hidden_one, d_result_one).reshape(groups, -1, width)
     near_out = near_half(jnp.concatenate([grad_out, early], axis=1))
     grad_in = blocks_product(received_one, d_inner_one).reshape(groups, -1, inner)
-    near_out, grad_in, late, d_second_in, d_second_out, d_back_one = lax.optimization_barrier(
-        (near_out, grad_in, late, d_second_in, d_second_out, d_back_one)
-    )
+    near_out, grad_in, d_back_one = lax.optimization_barrier((near_out, grad_in, d_back_one))
     far_out = own_parts(near_out, lax.axis_index("dp") // 2, groups, 2, "dp")
-    late = add_up(late).astype(bf16)
-    near_in = near_half(jnp.concatenate([grad_in, late], axis=1))
+    near_in = near_half(grad_in)
+    near_late = near_half(add_up(late).astype(bf16))
+    d1, d_second_in, d_second_out = lax.optimization_barrier((d1, d_second_in, d_second_out))
     d_start, d_embed, routers_grad, rows_grad = run(
         last_kernel,
         (
@@ -1346,11 +1411,16 @@
         name="last",
     )
 
-    near_in, far_out, routers_grad, rows_grad = lax.optimization_barrier(
-        (near_in, far_out, routers_grad, rows_grad)
-    )
+    near_in, near_late, far_out, routers_grad, rows_grad = lax.optimization_barrier(
+        (near_in, near_late, far_out, routers_grad, rows_grad)
+    )
+    near_in = jnp.concatenate([near_in, near_late], axis=1)
     out_sum = add_up(far_out)
-    in_sum = add_up(own_parts(near_in, lax.axis_index("dp") // 2, groups, 2, "dp"))
+    far_in = own_parts(near_in, lax.axis_index("dp") // 2, groups, 2, "dp")
+    far_in[1], routers_grad, rows_grad = lax.optimization_barrier(
+        (far_in[1], routers_grad, rows_grad)
+    )
+    in_sum = add_up(far_in)
     d_first_out = out_sum[None, : first_out.shape[1]]
     d_first_in = in_sum[None, : first_in.shape[1]]
     late_share = in_sum[first_in.shape[1] :]

time: 553 us -> 564 us (1.020)
  waiting for transfers between devices: 134 us -> 169 us
  other arithmetic: 16.5 us -> 9.26 us
  local copies, waits for them, and re-layouts: 50 us -> 44.3 us
    ppermute x38 -> x39, waiting for transfers between devices: 80.9 us -> 103 us  [across(): return lax.ppermute(values, axis, [(i, i ^ offset) for i in range(size)])]
    all_gather x1, waiting for transfers between devices: 11.3 us -> 17.7 us  [body(): lax.all_gather(second_out[0], 'dp', axis=0, tiled=True)]
    unnamed x145 -> x132, local copies, waits for them, and re-layouts: 23.7 us -> 22.3 us
    ppermute x38 -> x39, starting transfers between devices: 34.6 us -> 35.9 us  [across(): return lax.ppermute(values, axis, [(i, i ^ offset) for i in range(size)])]
  transfers between devices with their start and end apart: 61 -> 62, of which waited for: 22 -> 26; matrix products, arithmetic and copies ran while one was open for 10% -> 9% of each run, Pallas kernels for 41% -> 39%
where the time goes in v4:
time: 564 us; the launch traced here: 558 us
  Pallas kernels  229 us (41%)
  waiting for transfers between devices  169 us (30%)
  starting transfers between devices  67.9 us (12%)
  local copies, waits for them, and re-layouts  44.3 us (8%)
  matrix products  23.1 us (4%)
  between operations  15.1 us (3%)
  other arithmetic  9.26 us (2%)
    pallas_call x21, Pallas kernels, run(): pl.pallas_call(kernel, out_shape=outs, in_specs=in_specs, out_specs=[VMEM...  224 us
    ppermute x39, waiting for transfers between devices, across(): return lax.ppermute(values, axis, [(i, i ^ offset) for i in range(size)])  103 us
    ppermute x39, starting transfers between devices, across(): return lax.ppermute(values, axis, [(i, i ^ offset) for i in range(size)])  35.9 us
    dot_general x7, matrix products, rows_product(): lax.dot_general(left, right, (((0,), (0,)), ((), ())), preferred_element_...  23.1 us
    unnamed x132, local copies, waits for them, and re-layouts  22.3 us
    all_to_all x3, waiting for transfers between devices, gather_small(): return lax.all_to_all(values, BOTH, split_axis=0, concat_axis=0, tiled=True)  21.7 us
    all_gather x1, waiting for transfers between devices, body(): lax.all_gather(second_out[0], 'dp', axis=0, tiled=True)  17.7 us
    ppermute x7, waiting for transfers between devices, ring_gather(): lax.ppermute(pieces[-step + 1 or 0], 'dp', ring_pairs(size, True))  16.1 us
  transfers between devices with their start and end apart: 62, of which 26 were waited for; matrix products, arithmetic and copies ran while one was open for 9% of the time, Pallas kernels for 39%

profile of v4, /device:TPU:0, one launch (start us, length us, event | category | flops | bytes accessed | tf_op | source)
XLA Modules:
  0.0 557.6 jit_solution(14209053570038598728)
XLA Ops:
  22.7 6.3 %all-to-all-start = ((f32[32,1,640]{2,1,0:T(1,128)}), f32[32,1,640]{2,1,0:T(1,128)S(1)}, u32[]{:S(2)}, u32[]{:S(2)}) async-start(f32[32,1,640]{2,1,0:T(1,128)} %broadcast_in_dim.32), calls=%async_computation | async-start | bytes 163840 | tf_op jit(solution)/shard_map/all_to_all | solution.py:1006
  44.2 7.0 %collective-permute-done.5.refs_6_ = bf16[64,2048]{1,0:T(8,128)(2,1)} collective-permute-done((bf16[64,2048]{1,0:T(8,128)(2,1)S(1)}, bf16[64,2048]{1,0:T(8,128)(2,1)}, u32[]{:S(2)}, u32[]{:S(2)}) %collective-permute-start.5) | collective-permute-done | bytes 262176 | tf_op jit(solution)/shard_map/ppermute | solution.py:1055
  53.2 6.8 %front.1 = (bf16[272,512]{1,0:T(8,128)(2,1)}, bf16[272,512]{1,0:T(8,128)(2,1)}, bf16[272,512]{1,0:T(8,128)(2,1)}, bf16[272,512]{1,0:T(8,128)(2,1)}, f32[1024,128]{1,0:T(8,128)}, /*index=5*/f32[1024,1]{1,0:T(8,128)}) custom-call(bf16[1024,512]{1,0:T(8,128)(2,1)} %hidden_ref.5, bf16[1024,512]{1,0:T(8,128)(2,1)} %embed_ref.7, f32[8,512]{1,0:T(8,128)} %pad.20.gain_ref.gains_ref, ...), custom_call_target="tpu_custom_call" | custom-call | flops 2281701376 | bytes 4575232 | tf_op jit(solution)/shard_map/front/pallas_call | solution.py:30
  65.2 8.8 %collective-permute-done.13.refs_12_ = bf16[256,512]{1,0:T(8,128)(2,1)S(1)} collective-permute-done((bf16[256,512]{1,0:T(8,128)(2,1)S(1)}, bf16[256,512]{1,0:T(8,128)(2,1)S(1)}, u32[]{:S(2)}, u32[]{:S(2)}) %collective-permute-start.13) | collective-permute-done | bytes 262176 | tf_op jit(solution)/shard_map/ppermute | solution.py:1055
  77.0 5.0 assemble.1
  95.7 5.1 collective-permute-done.17.refs_2_
  101.6 43.7 %middle.1 = (f32[1024,512]{1,0:T(8,128)}, f32[1024,512]{1,0:T(8,128)}, bf16[1024,512]{1,0:T(8,128)(2,1)}, bf16[1024,512]{1,0:T(8,128)(2,1)}, bf16[1024,512]{1,0:...) custom-call(s32[1,5]{1,0:T(1,128)} %starts_ref.5, ...), custom_call_target="tpu_custom_call" | custom-call | flops 8589934592 | bytes 21827604 | tf_op jit(solution)/shard_map/middle/pallas_call | solution.py:30
  151.2 9.8 %all-to-all-done.1.totals_ref = f32[32,1,1536]{2,1,0:T(1,128)S(1)} async-done(((f32[32,1,1536]{2,1,0:T(1,128)}), f32[32,1,1536]{2,1,0:T(1,128)S(1)}, u32[]{:S(2)}, u32[]{:S(2)}) %all-to-all-start.1) | async-done | bytes 196640 | tf_op jit(solution)/shard_map/all_to_all | solution.py:1006
  161.7 9.8 %second.1 = (bf16[272,512]{1,0:T(8,128)(2,1)}, bf16[272,512]{1,0:T(8,128)(2,1)}, bf16[272,512]{1,0:T(8,128)(2,1)}, bf16[272,512]{1,0:T(8,128)(2,1)}, f32[1024,51...) custom-call(f32[1024,512]{1,0:T(8,128)} %get-tuple-element.180.h2_ref, ...), custom_call_target="tpu_custom_call" | custom-call | flops 2281701376 | bytes 11620352 | tf_op jit(solution)/shard_map/second/pallas_call | solution.py:30
  173.3 17.7 %all-gather.10.cloned.1.call-done = bf16[1,2048,512]{2,1,0:T(8,128)(2,1)} async-done(((bf16[1,256,512]{2,1,0:T(8,128)(2,1)}), bf16[1,2048,512]{2,1,0:T(8,128)(2,1)}) %all-gather.10.cloned.1.call-update) | async-done | bytes 2097168 | tf_op jit(solution)/shard_map/all_gather | solution.py:1233
  202.9 5.1 collective-permute-done.24.refs_2_
  212.4 9.8 %turn.1 = (bf16[272,512]{1,0:T(8,128)(2,1)}, bf16[272,512]{1,0:T(8,128)(2,1)}, bf16[272,512]{1,0:T(8,128)(2,1)}, bf16[272,512]{1,0:T(8,128)(2,1)}, bf16[1024,512...) custom-call(f32[1024,512]{1,0:T(8,128)} %get-tuple-element.183.h3_ref, ...), custom_call_target="tpu_custom_call" | custom-call | flops 2281701376 | bytes 10162176 | tf_op jit(solution)/shard_map/turn/pallas_call | solution.py:30
  225.5 4.1 experts_back.6
  232.8 4.2 collective-permute-done.28.refs_1_
  245.4 4.3 fusion.38
  249.8 6.8 %fusion.41 = bf16[512,2048]{1,0:T(8,128)(2,1)} fusion(bf16[272,2048]{1,0:T(8,128)(2,1)} %copy-done.15, bf16[272,2048]{1,0:T(8,128)(2,1)} %copy-done.14, bf16[272,2048]{1,0:T(8,128)(2,1)} %copy-done.23, bf16[272,2048]{1,0:T(8,128)(2,1)} %copy-done.22, bf16[272,512]{1,0:T(8,128)(2,1)S(1)} %collective-permute-done.22.refs_0_, ...), kind=kOutput, calls=%fused_computation.37 | convolution fusion | flops 2305032192 | bytes 7667712 | tf_op jit(solution)/shard_map/dot_general | solution.py:1139
  257.2 12.2 %second_back.1 = (f32[1024,512]{1,0:T(8,128)}, bf16[1024,512]{1,0:T(8,128)(2,1)}, f32[1024,512]{1,0:T(8,128)}, f32[1024,512]{1,0:T(8,128)}, f32[8,1024]{1,0:T(8,...) custom-call(s32[1024,128]{1,0:T(8,128)} %get-tuple-element.169.cols_ref, f32[1024,128]{1,0:T(8,128)} %get-tuple-element.197.dlogits_ref, ...), custom_call_target="tpu_custom_call" | custom-call | flops 2281701376 | bytes 17858560 | tf_op jit(solution)/shard_map/second_back/pallas_call | solution.py:30
  269.4 4.2 all-to-all-start.2
  276.2 7.8 %all-to-all-done.2.dsums_ref = f32[32,1,1024]{2,1,0:T(1,128)S(1)} async-done(((f32[32,1,1024]{2,1,0:T(1,128)}), f32[32,1,1024]{2,1,0:T(1,128)S(1)}, u32[]{:S(2)}, u32[]{:S(2)}) %all-to-all-start.2) | async-done | bytes 131104 | tf_op jit(solution)/shard_map/all_to_all | solution.py:1006
  284.6 23.4 %conv_back.1 = (f32[1024,512]{1,0:T(8,128)}, bf16[1024,512]{1,0:T(8,128)(2,1)}, bf16[1024,512]{1,0:T(8,128)(2,1)}, bf16[1024,512]{1,0:T(8,128)(2,1)}, bf16[1024,...) custom-call(s32[1,5]{1,0:T(1,128)} %starts_ref.5, f32[1024,512]{1,0:T(8,128)} %get-tuple-element.181.conv_ref, ...), custom_call_target="tpu_custom_call" | custom-call | flops 1610612736 | bytes 20168724 | tf_op jit(solution)/shard_map/conv_back/pallas_call | solution.py:30
  316.2 71.3 %attend_back.1 = (bf16[272,512]{1,0:T(8,128)(2,1)}, bf16[272,512]{1,0:T(8,128)(2,1)}, bf16[272,512]{1,0:T(8,128)(2,1)}, bf16[272,512]{1,0:T(8,128)(2,1)}, f32[10...) custom-call(s32[1,5]{1,0:T(1,128)} %starts_ref.5, ...), custom_call_target="tpu_custom_call" | custom-call | flops 17179869184 | bytes 29052948 | tf_op jit(solution)/shard_map/attend_back/pallas_call | solution.py:30
  390.0 11.5 %experts_back.9 = (bf16[512,2048]{1,0:T(8,128)(2,1)}, bf16[272,512]{1,0:T(8,128)(2,1)S(1)}, bf16[272,512]{1,0:T(8,128)(2,1)S(1)}, bf16[272,2048]{1,0:T(8,128)(2,...) custom-call(bf16[512,2048]{1,0:T(8,128)(2,1)} %get-tuple-element.172.in_ref, ...), custom_call_target="tpu_custom_call" | custom-call | flops 3422552064 | bytes 18710528 | tf_op jit(solution)/shard_map/experts_back/pallas_call | solution.py:30
  418.5 8.2 %collective-permute-done.44 = bf16[8,16,2048]{2,1,0:T(8,128)(2,1)S(1)} collective-permute-done((bf16[8,16,2048]{2,1,0:T(8,128)(2,1)S(1)}, bf16[8,16,2048]{2,1,0:T(8,128)(2,1)S(1)}, u32[]{:S(2)}, u32[]{:S(2)}) %collective-permute-start.44) | collective-permute-done | bytes 524320 | tf_op jit(solution)/shard_map/ppermute | solution.py:1012
  426.8 9.8 %collective-permute-done.45 = bf16[8,16,2048]{2,1,0:T(8,128)(2,1)S(1)} collective-permute-done((bf16[8,16,2048]{2,1,0:T(8,128)(2,1)S(1)}, bf16[8,16,2048]{2,1,0:T(8,128)(2,1)S(1)}, u32[]{:S(2)}, u32[]{:S(2)}) %collective-permute-start.45) | collective-permute-done | bytes 524320 | tf_op jit(solution)/shard_map/ppermute | solution.py:1012
  436.9 4.2 collective-permute-done.38
  444.0 4.6 collective-permute-done.41.refs_3_
  450.8 29.1 %collective-permute-done.46 = bf16[4,16,2048]{2,1,0:T(8,128)(2,1)S(1)} collective-permute-done((bf16[4,16,2048]{2,1,0:T(8,128)(2,1)S(1)}, bf16[4,16,2048]{2,1,0:T(8,128)(2,1)S(1)}, u32[]{:S(2)}, u32[]{:S(2)}) %collective-permute-start.46) | collective-permute-done | bytes 262176 | tf_op jit(solution)/shard_map/ppermute | solution.py:1012
  490.6 9.4 %last.1 = (f32[1024,512]{1,0:T(8,128)}, f32[1024,512]{1,0:T(8,128)}, f32[16,1024]{1,0:T(8,128)}, f32[24,512]{1,0:T(8,128)}) custom-call(s32[1024,128]{1,0:T(8,128)} %get-tuple-element.169.cols_ref, f32[1024,128]{1,0:T(8,128)} %get-tuple-element.242.dlogits_ref, bf16[1024,512]{1,0:T(8,128)(2,1)} %hidden_ref.5, f32[1024,512]{1,0:T(8,128)} %get-tuple-element.246.d1_ref, ...), custom_call_target="tpu_custom_call" | custom-call | flops 2281701376 | bytes 13189120 | tf_op jit(solution)/shard_map/last/pallas_call | solution.py:30
  500.0 6.7 %collective-permute-done.48 = bf16[320,512]{1,0:T(8,128)(2,1)S(1)} collective-permute-done((bf16[320,512]{1,0:T(8,128)(2,1)}, bf16[320,512]{1,0:T(8,128)(2,1)S(1)}, u32[]{:S(2)}, u32[]{:S(2)}) %collective-permute-start.48) | collective-permute-done | bytes 327712 | tf_op jit(solution)/shard_map/ppermute | solution.py:1012
  507.8 6.6 %collective-permute-start.50 = (bf16[80,2048]{1,0:T(8,128)(2,1)S(1)}, bf16[80,2048]{1,0:T(8,128)(2,1)S(1)}, u32[]{:S(2)}, u32[]{:S(2)}) collective-permute-start(bf16[80,2048]{1,0:T(8,128)(2,1)S(1)} %get-tuple-element.328), channel_id=1, source_target_pairs={{0,8},{4,12},{8,0},{12,4},{16,24},{20,28},{24,16},{28,20},{1,9},{5... | collective-permute-start | bytes 983048 | tf_op jit(solution)/shard_map/ppermute | solution.py:1012
  519.2 7.8 %collective-permute-done.50 = bf16[80,2048]{1,0:T(8,128)(2,1)S(1)} collective-permute-done((bf16[80,2048]{1,0:T(8,128)(2,1)S(1)}, bf16[80,2048]{1,0:T(8,128)(2,1)S(1)}, u32[]{:S(2)}, u32[]{:S(2)}) %collective-permute-start.50) | collective-permute-done | bytes 327712 | tf_op jit(solution)/shard_map/ppermute | solution.py:1012
  532.0 8.9 %collective-permute-done.51 = bf16[80,2048]{1,0:T(8,128)(2,1)S(1)} collective-permute-done((bf16[80,2048]{1,0:T(8,128)(2,1)S(1)}, bf16[80,2048]{1,0:T(8,128)(2,1)S(1)}, u32[]{:S(2)}, u32[]{:S(2)}) %collective-permute-start.51) | collective-permute-done | bytes 327712 | tf_op jit(solution)/shard_map/ppermute | solution.py:1012
  (333 shorter events, 162.6 us)
Async XLA Ops:
  7.2 93.6 %all-gather.6.cloned.1.call-start = ((), (), s32[]{:S(2)}) async-start(), calls=%async_computation.6 | async-start | bytes 4325376 | tf_op jit(solution)/shard_map/all_gather | solution.py:1227
  11.6 161.7 %all-gather.8.cloned.1.call-start = ((), (), s32[]{:S(2)}) async-start(), calls=%async_computation.9 | async-start | bytes 2359296 | tf_op jit(solution)/shard_map/all_gather | solution.py:1232
  12.4 178.6 %all-gather.10.cloned.1.call-start = ((), (), s32[]{:S(2)}) async-start(), calls=%async_computation.10 | async-start | bytes 2359296 | tf_op jit(solution)/shard_map/all_gather | solution.py:1233
  16.2 22.0 %collective-permute-start.4 = (bf16[64,2048]{1,0:T(8,128)(2,1)}, bf16[64,2048]{1,0:T(8,128)(2,1)S(1)}, u32[]{:S(2)}, u32[]{:S(2)}) collective-permute-start(bf16[64,2048]{1,0:T(8,128)(2,1)} %bitcast.159), channel_id=1, source_target_pairs={{0,8},{8,16},{16,24},{24,28},{28,20},{20,12},{12,4},{4,0},{1,9},{9... | collective-permute-start | bytes 786440 | tf_op jit(solution)/shard_map/ppermute | solution.py:1055
  18.2 20.8 %collective-permute-start.7 = (bf16[256,512]{1,0:T(8,128)(2,1)}, bf16[256,512]{1,0:T(8,128)(2,1)S(1)}, u32[]{:S(2)}, u32[]{:S(2)}) collective-permute-start(bf16[256,512]{1,0:T(8,128)(2,1)} %bitcast.162), channel_id=1, source_target_pairs={{0,4},{8,0},{16,8},{24,16},{28,24},{20,28},{12,20},{4,12},{1,5},{9... | collective-permute-start | bytes 786440 | tf_op jit(solution)/shard_map/ppermute | solution.py:1053
  40.4 19.7 %collective-permute-start.12 = (bf16[256,512]{1,0:T(8,128)(2,1)S(1)}, bf16[256,512]{1,0:T(8,128)(2,1)S(1)}, u32[]{:S(2)}, u32[]{:S(2)}) collective-permute-start(bf16[256,512]{1,0:T(8,128)(2,1)S(1)} %collective-permute-done.11.refs_14_), channel_id=1, source_target_pairs={{0,8},{8,16},{16,24},{24,28},{28,20},{20,12},{12,4},{4,0},{1,9},{9... | collective-permute-start | bytes 786440 | tf_op jit(solution)/shard_map/ppermute | solution.py:1055
  41.2 20.6 %collective-permute-start.2 = (bf16[64,2048]{1,0:T(8,128)(2,1)S(1)}, bf16[64,2048]{1,0:T(8,128)(2,1)S(1)}, u32[]{:S(2)}, u32[]{:S(2)}) collective-permute-start(bf16[64,2048]{1,0:T(8,128)(2,1)S(1)} %collective-permute-done.1.refs_2_), channel_id=1, source_target_pairs={{0,4},{8,0},{16,8},{24,16},{28,24},{20,28},{12,20},{4,12},{1,5},{9... | collective-permute-start | bytes 786440 | tf_op jit(solution)/shard_map/ppermute | solution.py:1053
  60.0 21.9 %collective-permute-start.18 = (bf16[272,512]{1,0:T(8,128)(2,1)}, bf16[272,512]{1,0:T(8,128)(2,1)S(1)}, u32[]{:S(2)}, u32[]{:S(2)}) collective-permute-start(bf16[272,512]{1,0:T(8,128)(2,1)} %get-tuple-element.179), channel_id=1, source_target_pairs={{0,3},{1,2},{2,1},{3,0},{4,7},{5,6},{6,5},{7,4},{8,11},{9,10},{10,... | collective-permute-start | bytes 835592 | tf_op jit(solution)/shard_map/ppermute | solution.py:1012
  62.8 24.1 %collective-permute-start.16 = (bf16[272,512]{1,0:T(8,128)(2,1)}, bf16[272,512]{1,0:T(8,128)(2,1)S(1)}, u32[]{:S(2)}, u32[]{:S(2)}) collective-permute-start(bf16[272,512]{1,0:T(8,128)(2,1)} %get-tuple-element.178), channel_id=1, source_target_pairs={{0,2},{1,3},{2,0},{3,1},{4,6},{5,7},{6,4},{7,5},{8,10},{9,11},{10,... | collective-permute-start | bytes 835592 | tf_op jit(solution)/shard_map/ppermute | solution.py:1012
  64.6 24.4 %collective-permute-start.14 = (bf16[272,512]{1,0:T(8,128)(2,1)}, bf16[272,512]{1,0:T(8,128)(2,1)S(1)}, u32[]{:S(2)}, u32[]{:S(2)}) collective-permute-start(bf16[272,512]{1,0:T(8,128)(2,1)} %get-tuple-element.175), channel_id=1, source_target_pairs={{0,1},{1,0},{2,3},{3,2},{4,5},{5,4},{6,7},{7,6},{8,9},{9,8},{10,11... | collective-permute-start | bytes 835592 | tf_op jit(solution)/shard_map/ppermute | solution.py:1012
  148.0 339.0 %reduce-scatter.3.cloned.1.call-start = ((), (), s32[]{:S(2)}) async-start(), calls=%async_computation.7 | async-start | bytes 2359296 | tf_op jit(solution)/shard_map/reduce_scatter | solution.py:1149
  171.5 19.6 %collective-permute-start.20 = (bf16[272,512]{1,0:T(8,128)(2,1)}, bf16[272,512]{1,0:T(8,128)(2,1)S(1)}, u32[]{:S(2)}, u32[]{:S(2)}) collective-permute-start(bf16[272,512]{1,0:T(8,128)(2,1)} %get-tuple-element.187), channel_id=1, source_target_pairs={{0,1},{1,0},{2,3},{3,2},{4,5},{5,4},{6,7},{7,6},{8,9},{9,8},{10,11... | collective-permute-start | bytes 835592 | tf_op jit(solution)/shard_map/ppermute | solution.py:1012
  171.5 26.4 %collective-permute-start.21 = (bf16[272,512]{1,0:T(8,128)(2,1)}, bf16[272,512]{1,0:T(8,128)(2,1)S(1)}, u32[]{:S(2)}, u32[]{:S(2)}) collective-permute-start(bf16[272,512]{1,0:T(8,128)(2,1)} %get-tuple-element.190), channel_id=1, source_target_pairs={{0,2},{1,3},{2,0},{3,1},{4,6},{5,7},{6,4},{7,5},{8,10},{9,11},{10,... | collective-permute-start | bytes 835592 | tf_op jit(solution)/shard_map/ppermute | solution.py:1012
  173.2 24.6 %collective-permute-start.22 = (bf16[272,512]{1,0:T(8,128)(2,1)}, bf16[272,512]{1,0:T(8,128)(2,1)S(1)}, u32[]{:S(2)}, u32[]{:S(2)}) collective-permute-start(bf16[272,512]{1,0:T(8,128)(2,1)} %get-tuple-element.191), channel_id=1, source_target_pairs={{0,3},{1,2},{2,1},{3,0},{4,7},{5,6},{6,5},{7,4},{8,11},{9,10},{10,... | collective-permute-start | bytes 835592 | tf_op jit(solution)/shard_map/ppermute | solution.py:1012
  273.6 215.2 %reduce-scatter.5.cloned.1.call-start = ((), (), s32[]{:S(2)}) async-start(), calls=%async_computation.8 | async-start | bytes 2359296 | tf_op jit(solution)/shard_map/reduce_scatter | solution.py:1150
  314.1 73.5 %collective-permute-start.32 = (bf16[8,4,16,512]{3,2,1,0:T(8,128)(2,1)S(1)}, bf16[8,4,16,512]{3,2,1,0:T(8,128)(2,1)S(1)}, u32[]{:S(2)}, u32[]{:S(2)}) collective-permute-start(bf16[8,4,16,512]{3,2,1,0:T(8,128)(2,1)S(1)} %bitcast.153), channel_id=1, source_target_pairs={{0,1},{1,0},{2,3},{3,2},{4,5},{5,4},{6,7},{7,6},{8,9},{9,8},{10,11... | collective-permute-start | bytes 1572872 | tf_op jit(solution)/shard_map/ppermute | solution.py:1012
  314.3 73.3 %collective-permute-start.33 = (bf16[8,4,16,512]{3,2,1,0:T(8,128)(2,1)S(1)}, bf16[8,4,16,512]{3,2,1,0:T(8,128)(2,1)S(1)}, u32[]{:S(2)}, u32[]{:S(2)}) collective-permute-start(bf16[8,4,16,512]{3,2,1,0:T(8,128)(2,1)S(1)} %bitcast.154), channel_id=1, source_target_pairs={{0,2},{1,3},{2,0},{3,1},{4,6},{5,7},{6,4},{7,5},{8,10},{9,11},{10,... | collective-permute-start | bytes 1572872 | tf_op jit(solution)/shard_map/ppermute | solution.py:1012
  315.8 71.8 %collective-permute-start.34 = (bf16[8,4,16,512]{3,2,1,0:T(8,128)(2,1)S(1)}, bf16[8,4,16,512]{3,2,1,0:T(8,128)(2,1)S(1)}, u32[]{:S(2)}, u32[]{:S(2)}) collective-permute-start(bf16[8,4,16,512]{3,2,1,0:T(8,128)(2,1)S(1)} %bitcast.155), channel_id=1, source_target_pairs={{0,3},{1,2},{2,1},{3,0},{4,7},{5,6},{6,5},{7,4},{8,11},{9,10},{10,... | collective-permute-start | bytes 1572872 | tf_op jit(solution)/shard_map/ppermute | solution.py:1012
  410.1 31.0 %collective-permute-start.38 = (bf16[4,320,512]{2,1,0:T(8,128)(2,1)S(1)}, bf16[4,320,512]{2,1,0:T(8,128)(2,1)S(1)}, u32[]{:S(2)}, u32[]{:S(2)}) collective-permute-start(bf16[4,320,512]{2,1,0:T(8,128)(2,1)S(1)} %fusion.47), channel_id=1, source_target_pairs={{0,4},{4,0},{8,12},{12,8},{16,20},{20,16},{24,28},{28,24},{1,5},{5... | collective-permute-start | bytes 3932168 | tf_op jit(solution)/shard_map/ppermute | solution.py:1012
  412.6 24.0 %collective-permute-start.45 = (bf16[8,16,2048]{2,1,0:T(8,128)(2,1)S(1)}, bf16[8,16,2048]{2,1,0:T(8,128)(2,1)S(1)}, u32[]{:S(2)}, u32[]{:S(2)}) collective-permute-start(bf16[8,16,2048]{2,1,0:T(8,128)(2,1)S(1)} %get-tuple-element.320), channel_id=1, source_target_pairs={{0,3},{1,2},{2,1},{3,0},{4,7},{5,6},{6,5},{7,4},{8,11},{9,10},{10,... | collective-permute-start | bytes 1572872 | tf_op jit(solution)/shard_map/ppermute | solution.py:1012
  413.6 30.4 %collective-permute-start.40 = (bf16[272,512]{1,0:T(8,128)(2,1)S(1)}, bf16[272,512]{1,0:T(8,128)(2,1)S(1)}, u32[]{:S(2)}, u32[]{:S(2)}) collective-permute-start(bf16[272,512]{1,0:T(8,128)(2,1)S(1)} %get-tuple-element.293), channel_id=1, source_target_pairs={{0,2},{1,3},{2,0},{3,1},{4,6},{5,7},{6,4},{7,5},{8,10},{9,11},{10,... | collective-permute-start | bytes 835592 | tf_op jit(solution)/shard_map/ppermute | solution.py:1012
  417.0 31.5 %collective-permute-start.41 = (bf16[272,512]{1,0:T(8,128)(2,1)S(1)}, bf16[272,512]{1,0:T(8,128)(2,1)S(1)}, u32[]{:S(2)}, u32[]{:S(2)}) collective-permute-start(bf16[272,512]{1,0:T(8,128)(2,1)S(1)} %get-tuple-element.294), channel_id=1, source_target_pairs={{0,3},{1,2},{2,1},{3,0},{4,7},{5,6},{6,5},{7,4},{8,11},{9,10},{10,... | collective-permute-start | bytes 835592 | tf_op jit(solution)/shard_map/ppermute | solution.py:1012
  426.8 21.8 %collective-permute-start.39 = (bf16[272,512]{1,0:T(8,128)(2,1)S(1)}, bf16[272,512]{1,0:T(8,128)(2,1)S(1)}, u32[]{:S(2)}, u32[]{:S(2)}) collective-permute-start(bf16[272,512]{1,0:T(8,128)(2,1)S(1)} %get-tuple-element.292), channel_id=1, source_target_pairs={{0,1},{1,0},{2,3},{3,2},{4,5},{5,4},{6,7},{7,6},{8,9},{9,8},{10,11... | collective-permute-start | bytes 835592 | tf_op jit(solution)/shard_map/ppermute | solution.py:1012
  448.6 36.7 %collective-permute-start.42 = (bf16[4,64,2048]{2,1,0:T(8,128)(2,1)S(1)}, bf16[4,64,2048]{2,1,0:T(8,128)(2,1)}, u32[]{:S(2)}, u32[]{:S(2)}) collective-permute-start(bf16[4,64,2048]{2,1,0:T(8,128)(2,1)S(1)} %dynamic-slice_bitcast_fusion), channel_id=1, source_target_pairs={{0,4},{4,0},{8,12},{12,8},{16,20},{20,16},{24,28},{28,24},{1,5},{5... | collective-permute-start | bytes 3145736 | tf_op jit(solution)/shard_map/ppermute | solution.py:1012
  449.4 30.5 %collective-permute-start.46 = (bf16[4,16,2048]{2,1,0:T(8,128)(2,1)S(1)}, bf16[4,16,2048]{2,1,0:T(8,128)(2,1)S(1)}, u32[]{:S(2)}, u32[]{:S(2)}) collective-permute-start(bf16[4,16,2048]{2,1,0:T(8,128)(2,1)S(1)} %dynamic-slice_bitcast_fusion.11), channel_id=1, source_target_pairs={{0,4},{4,0},{8,12},{12,8},{16,20},{20,16},{24,28},{28,24},{1,5},{5... | collective-permute-start | bytes 786440 | tf_op jit(solution)/shard_map/ppermute | solution.py:1012
  481.0 19.0 %collective-permute-start.47 = (bf16[320,512]{1,0:T(8,128)(2,1)}, bf16[320,512]{1,0:T(8,128)(2,1)S(1)}, u32[]{:S(2)}, u32[]{:S(2)}) collective-permute-start(bf16[320,512]{1,0:T(8,128)(2,1)} %get-tuple-element.331), channel_id=1, source_target_pairs={{0,8},{4,12},{8,0},{12,4},{16,24},{20,28},{24,16},{28,20},{1,9},{5... | collective-permute-start | bytes 983048 | tf_op jit(solution)/shard_map/ppermute | solution.py:1012
  481.0 25.8 %collective-permute-start.48 = (bf16[320,512]{1,0:T(8,128)(2,1)}, bf16[320,512]{1,0:T(8,128)(2,1)S(1)}, u32[]{:S(2)}, u32[]{:S(2)}) collective-permute-start(bf16[320,512]{1,0:T(8,128)(2,1)} %get-tuple-element.330), channel_id=1, source_target_pairs={{0,16},{4,20},{8,24},{12,28},{16,0},{20,4},{24,8},{28,12},{1,17},{... | collective-permute-start | bytes 983048 | tf_op jit(solution)/shard_map/ppermute | solution.py:1012
  483.5 23.2 %collective-permute-start.49 = (bf16[320,512]{1,0:T(8,128)(2,1)S(1)}, bf16[320,512]{1,0:T(8,128)(2,1)S(1)}, u32[]{:S(2)}, u32[]{:S(2)}) collective-permute-start(bf16[320,512]{1,0:T(8,128)(2,1)S(1)} %get-tuple-element.329), channel_id=1, source_target_pairs={{0,24},{4,28},{8,16},{12,20},{16,8},{20,12},{24,0},{28,4},{1,25},{... | collective-permute-start | bytes 983048 | tf_op jit(solution)/shard_map/ppermute | solution.py:1012
  507.8 19.2 %collective-permute-start.50 = (bf16[80,2048]{1,0:T(8,128)(2,1)S(1)}, bf16[80,2048]{1,0:T(8,128)(2,1)S(1)}, u32[]{:S(2)}, u32[]{:S(2)}) collective-permute-start(bf16[80,2048]{1,0:T(8,128)(2,1)S(1)} %get-tuple-element.328), channel_id=1, source_target_pairs={{0,8},{4,12},{8,0},{12,4},{16,24},{20,28},{24,16},{28,20},{1,9},{5... | collective-permute-start | bytes 983048 | tf_op jit(solution)/shard_map/ppermute | solution.py:1012
  514.4 26.5 %collective-permute-start.51 = (bf16[80,2048]{1,0:T(8,128)(2,1)S(1)}, bf16[80,2048]{1,0:T(8,128)(2,1)S(1)}, u32[]{:S(2)}, u32[]{:S(2)}) collective-permute-start(bf16[80,2048]{1,0:T(8,128)(2,1)S(1)} %get-tuple-element.326), channel_id=1, source_target_pairs={{0,16},{4,20},{8,24},{12,28},{16,0},{20,4},{24,8},{28,12},{1,17},{... | collective-permute-start | bytes 983048 | tf_op jit(solution)/shard_map/ppermute | solution.py:1012
  516.3 24.5 %collective-permute-start.52 = (bf16[80,2048]{1,0:T(8,128)(2,1)S(1)}, bf16[80,2048]{1,0:T(8,128)(2,1)}, u32[]{:S(2)}, u32[]{:S(2)}) collective-permute-start(bf16[80,2048]{1,0:T(8,128)(2,1)S(1)} %get-tuple-element.327), channel_id=1, source_target_pairs={{0,24},{4,28},{8,16},{12,20},{16,8},{20,12},{24,0},{28,4},{1,25},{... | collective-permute-start | bytes 983048 | tf_op jit(solution)/shard_map/ppermute | solution.py:1012
  528.4 18.9 %all-to-all-start.3 = ((f32[32,1,640]{2,1,0:T(1,128)}), f32[32,1,640]{2,1,0:T(1,128)S(1)}, u32[]{:S(2)}, u32[]{:S(2)}) async-start(f32[32,1,640]{2,1,0:T(1,128)} %all_to_all.22), calls=%async_computation.5 | async-start | bytes 163840 | tf_op jit(solution)/shard_map/all_to_all | solution.py:1434
  (91 other events, 739.5 us)
Sparse Core Ops, SparseCore 0:
  11.8 74.6 all-gather.5
  88.6 49.3 all-gather.7
  140.1 50.9 all-gather.9
  256.7 69.2 reduce-scatter.2
  329.3 66.7 reduce-scatter.4

commit v5 on v4

--- a/solution.py
+++ b/solution.py
@@ -430,10 +430,26 @@
     ]
 
 
+STRIP = 32
+
+
+def strips():
+    return [
+        (slice(head * TILE + row, head * TILE + row + STRIP), row)
+        for head in range(2)
+        for row in range(0, TILE, STRIP)
+    ]
+
+
+def skew_strip(values, row):
+    return pltpu.roll(values, 1 + row, 1, stride=1, stride_axis=0)
+
+
 def attend_backward(
     starts_ref, qu_ref, qv_ref, k_ref, v_ref, t_ref, mirrored_ref, context_ref, logs_ref, dcontext_ref,
     dm_ref, dk_ref, dv_ref, dt_ref, dbias_ref,
-    qum, qvm, dcm, qut, qvt, dct, logs, deltas, rolled, unrolled, dqu, dqv,
+    qum, qvm, dcm, qut, qvt, dct, logs, deltas, rolled, unrolled, dqu, dqv, first_s, second_s, third_s,
+    probs_s, dlow_s, moved_s,
 ):
     length, width = qu_ref.shape
     tiles = length // TILE
@@ -477,40 +493,49 @@
         def step_body(step, carry):
             key = low + 2 * step
             keys = pl.ds(pl.multiple_of(key * TILE, TILE), 2 * TILE)
-            same_one = twice(same_tile(starts_ref, first, key * TILE))
-            same_two = twice(same_tile(starts_ref, first, key * TILE + TILE))
+            same_one = same_tile(starts_ref, first, key * TILE)
+            same_two = same_tile(starts_ref, first, key * TILE + TILE)
             before = chunk_rows(tile, key, length, 2, True)
             after = chunk_rows(tile, key + 1, length, 2)
             for p in range(PAIRS):
                 lanes = slice(p * TILE, (p + 1) * TILE)
-                content = dot_t(qum[p], k_ref[keys, lanes])
-                fresh = dot_t(qvm[p], t_ref[after, lanes])
-                one, two = skew(fresh[:, :TILE]), skew(fresh[:, TILE:])
-                value_one = content[:, :TILE] + jnp.where(lower, rolled[p], one)
-                value_two = content[:, TILE:] + jnp.where(lower, one, two)
-                rolled[p] = two
-                probs_one = jnp.where(same_one, jnp.exp(value_one - logs[p]), 0.0)
-                probs_two = jnp.where(same_two, jnp.exp(value_two - logs[p]), 0.0)
-                probs = jnp.concatenate([probs_one.astype(bf16), probs_two.astype(bf16)], axis=1)
-                dprobs = dot_t(dcm[p], v_ref[keys, lanes])
-                dlow_one = (probs_one * (dprobs[:, :TILE] - deltas[p])).astype(bf16)
-                dlow_two = (probs_two * (dprobs[:, TILE:] - deltas[p])).astype(bf16)
-                dlow = jnp.concatenate([dlow_one, dlow_two], axis=1)
-                dv_ref[lanes, keys] += dot(dct[p], probs)
-                dk_ref[lanes, keys] += dot(qut[p], dlow)
-                dqu[p] += dot(dlow, k_ref[keys, lanes])
-                mirrored = mirror(dlow)
-                one, two = skew(mirrored[:, :TILE]), skew(mirrored[:, TILE:])
-                moved = jnp.concatenate(
-                    [
-                        jnp.where(lower, two, one).astype(bf16),
-                        jnp.where(lower, one, unrolled[p]).astype(bf16),
-                    ],
-                    axis=1,
-                )
-                unrolled[p] = two
-                dt_ref[lanes, before] += dot(qvt[p], moved)
-                dqv[p] += dot(moved, mirrored_ref[before, lanes])
+                first_s[p] = dot_t(qum[p], k_ref[keys, lanes])
+                second_s[p] = dot_t(qvm[p], t_ref[after, lanes])
+                third_s[p] = dot_t(dcm[p], v_ref[keys, lanes])
+            for p in range(PAIRS):
+                for rows, row in strips():
+                    near = iota((STRIP, TILE), 1) <= iota((STRIP, TILE), 0) + row
+                    span = slice(row, row + STRIP)
+                    one = skew_strip(second_s[p, rows, :TILE], row)
+                    two = skew_strip(second_s[p, rows, TILE:], row)
+                    value_one = first_s[p, rows, :TILE] + jnp.where(near, rolled[p, rows], one)
+                    value_two = first_s[p, rows, TILE:] + jnp.where(near, one, two)
+                    rolled[p, rows] = two
+                    log, delta = logs[p, rows], deltas[p, rows]
+                    probs_one = jnp.where(same_one[span], jnp.exp(value_one - log), 0.0)
+                    probs_two = jnp.where(same_two[span], jnp.exp(value_two - log), 0.0)
+                    probs_s[p, rows, :TILE] = probs_one.astype(bf16)
+                    probs_s[p, rows, TILE:] = probs_two.astype(bf16)
+                    dlow_s[p, rows, :TILE] = (probs_one * (third_s[p, rows, :TILE] - delta)).astype(bf16)
+                    dlow_s[p, rows, TILE:] = (probs_two * (third_s[p, rows, TILE:] - delta)).astype(bf16)
+            for p in range(PAIRS):
+                lanes = slice(p * TILE, (p + 1) * TILE)
+                second_s[p] = mirror(dlow_s[p])
+                dv_ref[lanes, keys] += dot(dct[p], probs_s[p])
+                dk_ref[lanes, keys] += dot(qut[p], dlow_s[p])
+                dqu[p] += dot(dlow_s[p], k_ref[keys, lanes])
+            for p in range(PAIRS):
+                for rows, row in strips():
+                    near = iota((STRIP, TILE), 1) <= iota((STRIP, TILE), 0) + row
+                    one = skew_strip(second_s[p, rows, :TILE], row)
+                    two = skew_strip(second_s[p, rows, TILE:], row)
+                    moved_s[p, rows, :TILE] = jnp.where(near, two, one).astype(bf16)
+                    moved_s[p, rows, TILE:] = jnp.where(near, one, unrolled[p, rows]).astype(bf16)
+                    unrolled[p, rows] = two
+            for p in range(PAIRS):
+                lanes = slice(p * TILE, (p + 1) * TILE)
+                dt_ref[lanes, before] += dot(qvt[p], moved_s[p])
+                dqv[p] += dot(moved_s[p], mirrored_ref[before, lanes])
             return carry
 
         lax.fori_loop(0, steps, step_body, 0)
@@ -545,9 +570,12 @@
 def attend_back_scratch():
     pair = (PAIRS, 2 * TILE, TILE)
     turned = (PAIRS, TILE, 2 * TILE)
-    return [pltpu.VMEM(dims, bf16) for dims in (pair,) * 3 + (turned,) * 3] + [
-        pltpu.VMEM(pair, f32) for unused in range(6)
-    ]
+    square = (PAIRS, 2 * TILE, 2 * TILE)
+    return (
+        [pltpu.VMEM(dims, bf16) for dims in (pair,) * 3 + (turned,) * 3]
+        + [pltpu.VMEM(dims, f32) for dims in (pair,) * 6 + (square,) * 3]
+        + [pltpu.VMEM(square, bf16) for unused in range(3)]
+    )
 
 
 def dense_parts(dense_ref):
@@ -967,10 +995,12 @@
 
 def last_kernel(
     cols_ref, dlogits_ref, hidden_ref, d1_ref, embed_ref, router_ref, gains_ref, dembed_two_ref,
-    drouter_two_ref, mid_ref, conv_ref, two_ref, five_ref, taps_ref, *refs,
+    drouter_two_ref, mid_ref, conv_ref, two_ref, five_ref, taps_ref, in_low_ref, out_low_ref, *refs,
 ):
     dsent_refs, refs = refs[:PARTS], refs[PARTS:]
-    d0_ref, dembed_ref, routers_ref, small_ref, dsent_ref = refs
+    d0_ref, dembed_ref, routers_ref, small_ref, in_ref, out_ref, dsent_ref = refs
+    in_ref[...] = in_low_ref[...].astype(f32)
+    out_ref[...] = out_low_ref[...].astype(f32)
     length = hidden_ref.shape[0]
     taps = small_ref.shape[0] - 9
     join_blocks(dsent_refs, dsent_ref)
@@ -1095,13 +1125,6 @@
     )(order, *[piece for pieces in groups for piece in pieces])
 
 
-def keep_half(values, axis, bit, size, offset, mesh_axis):
-    mine = lax.dynamic_index_in_dim(values, bit, axis, keepdims=False)
-    theirs = lax.dynamic_index_in_dim(values, 1 - bit, axis, keepdims=False)
-    arrived = across(theirs, mesh_axis, size, offset)
-    return (mine.astype(f32) + arrived.astype(f32)).astype(bf16)
-
-
 def own_parts(values, place, size, stride, mesh_axis):
     parts = [lax.dynamic_index_in_dim(values, place, 0, keepdims=False)]
     for k in range(1, values.shape[0]):
@@ -1121,10 +1144,17 @@
     return add_up(own_parts(values, place, size, stride, mesh_axis))
 
 
-def near_half(values):
+def near_parts(values):
     groups = values.shape[0]
     values = values.reshape((groups // 2, 2) + values.shape[1:])
-    return keep_half(values, 1, lax.axis_index("dp") % 2, groups, 1, "dp")
+    bit = lax.axis_index("dp") % 2
+    mine = lax.dynamic_index_in_dim(values, bit, 1, keepdims=False)
+    theirs = lax.dynamic_index_in_dim(values, 1 - bit, 1, keepdims=False)
+    return [mine, across(theirs, "dp", groups, 1)]
+
+
+def near_half(values):
+    return add_up(near_parts(values)).astype(bf16)
 
 
 def expert_parts(values, experts):
@@ -1146,8 +1176,8 @@
 
 def scatter_offloaded(grad_in, grad_out):
     return (
-        lax.psum_scatter(grad_in, "dp", scatter_dimension=0, tiled=True).astype(f32)[None],
-        lax.psum_scatter(grad_out, "dp", scatter_dimension=0, tiled=True).astype(f32)[None],
+        lax.psum_scatter(grad_in, "dp", scatter_dimension=0, tiled=True),
+        lax.psum_scatter(grad_out, "dp", scatter_dimension=0, tiled=True),
     )
 
 
@@ -1393,28 +1423,34 @@
     grad_out = blocks_product(hidden_one, d_result_one).reshape(groups, -1, width)
     near_out = near_half(jnp.concatenate([grad_out, early], axis=1))
     grad_in = blocks_product(received_one, d_inner_one).reshape(groups, -1, inner)
-    near_out, grad_in, d_back_one = lax.optimization_barrier((near_out, grad_in, d_back_one))
+    near_out, grad_in, late, d_back_one = lax.optimization_barrier(
+        (near_out, grad_in, late, d_back_one)
+    )
     far_out = own_parts(near_out, lax.axis_index("dp") // 2, groups, 2, "dp")
-    near_in = near_half(grad_in)
-    near_late = near_half(add_up(late).astype(bf16))
-    d1, d_second_in, d_second_out = lax.optimization_barrier((d1, d_second_in, d_second_out))
-    d_start, d_embed, routers_grad, rows_grad = run(
+    near_in = near_parts(grad_in)
+    d_start, d_embed, routers_grad, rows_grad, d_second_in, d_second_out = run(
         last_kernel,
         (
             slot_cols, dlogits_one, inputs, d1, embedding, routers[0], gains, dembed_two,
-            drouter_two, small_mid, small_conv, small_two, dgain_five, d_taps, *d_back_one,
+            drouter_two, small_mid, small_conv, small_two, dgain_five, d_taps, d_second_in, d_second_out,
+            *d_back_one,
         ),
-        [VMEM] * (14 + PARTS),
-        [row_full, row_full, shape_of((16, 2 * width), f32), shape_of((count, width), f32)],
+        [VMEM] * (16 + PARTS),
+        [
+            row_full, row_full, shape_of((16, 2 * width), f32), shape_of((count, width), f32),
+            shape_of(first_in.shape[1:], f32), shape_of(first_out.shape[1:], f32),
+        ],
         [slots_scratch],
         flops=4 * slots * length * width,
         name="last",
     )
 
-    near_in, near_late, far_out, routers_grad, rows_grad = lax.optimization_barrier(
-        (near_in, near_late, far_out, routers_grad, rows_grad)
-    )
-    near_in = jnp.concatenate([near_in, near_late], axis=1)
+    near_in, late, far_out, routers_grad, rows_grad = lax.optimization_barrier(
+        (near_in, late, far_out, routers_grad, rows_grad)
+    )
+    near_in = add_up(near_in).astype(bf16)
+    near_late = near_half(add_up(late).astype(bf16))
+    late_share = add_up(own_parts(near_late, lax.axis_index("dp") // 2, groups, 2, "dp"))
     out_sum = add_up(far_out)
     far_in = own_parts(near_in, lax.axis_index("dp") // 2, groups, 2, "dp")
     far_in[1], routers_grad, rows_grad = lax.optimization_barrier(
@@ -1422,8 +1458,7 @@
     )
     in_sum = add_up(far_in)
     d_first_out = out_sum[None, : first_out.shape[1]]
-    d_first_in = in_sum[None, : first_in.shape[1]]
-    late_share = in_sum[first_in.shape[1] :]
+    d_first_in = in_sum[None]
     early_share = out_sum[first_out.shape[1] :].reshape(4, width // devices, width)
     early_share = jnp.concatenate([early_share[k] for k in range(4)], axis=1)
     rows_grad = rows_grad.reshape(count, devices, share).transpose(1, 0, 2).reshape(devices, -1)
@@ -1445,8 +1480,8 @@
         routers_share[1],
         d_first_in,
         d_first_out,
-        d_second_in,
-        d_second_out,
+        d_second_in[None],
+        d_second_out[None],
         late_share[:, : 3 * width],
         late_share[:, 3 * width :],
         rows_share[5:7],

time: 564 us -> 519 us (0.920)
  waiting for transfers between devices: 169 us -> 136 us
  Pallas kernels: 229 us -> 204 us
  starting transfers between devices: 67.9 us -> 76.5 us
    ppermute x39 -> x42, waiting for transfers between devices: 103 us -> 75 us  [across(): return lax.ppermute(values, axis, [(i, i ^ offset) for i in range(size)])]
    pallas_call x21, Pallas kernels: 224 us -> 199 us  [run(): pl.pallas_call(kernel, out_shape=outs, in_specs=in_specs, out_specs=[VMEM...]
    ppermute x39 -> x42, starting transfers between devices: 35.9 us -> 40.9 us  [across(): return lax.ppermute(values, axis, [(i, i ^ offset) for i in range(size)])]
    unnamed x132 -> x151, local copies, waits for them, and re-layouts: 22.3 us -> 23 us
  transfers between devices with their start and end apart: 62 -> 65, of which waited for: 26 -> 23; matrix products, arithmetic and copies ran while one was open for 9% -> 10% of each run, Pallas kernels for 39% -> 37%
where the time goes in v5:
time: 519 us; the launch traced here: 513 us
  Pallas kernels  204 us (39%)
  waiting for transfers between devices  136 us (26%)
  starting transfers between devices  76.5 us (15%)
  local copies, waits for them, and re-layouts  48.9 us (9%)
  matrix products  23.2 us (4%)
  between operations  15.1 us (3%)
  other arithmetic  9.56 us (2%)
    pallas_call x21, Pallas kernels, run(): pl.pallas_call(kernel, out_shape=outs, in_specs=in_specs, out_specs=[VMEM...  199 us
    ppermute x42, waiting for transfers between devices, across(): return lax.ppermute(values, axis, [(i, i ^ offset) for i in range(size)])  75 us
    ppermute x42, starting transfers between devices, across(): return lax.ppermute(values, axis, [(i, i ^ offset) for i in range(size)])  40.9 us
    dot_general x7, matrix products, rows_product(): lax.dot_general(left, right, (((0,), (0,)), ((), ())), preferred_element_...  23.2 us
    unnamed x151, local copies, waits for them, and re-layouts  23 us
    all_to_all x3, waiting for transfers between devices, gather_small(): return lax.all_to_all(values, BOTH, split_axis=0, concat_axis=0, tiled=True)  21.3 us
    all_to_all x3, starting transfers between devices, gather_small(): return lax.all_to_all(values, BOTH, split_axis=0, concat_axis=0, tiled=True)  16.5 us
    all_gather x1, waiting for transfers between devices, body(): lax.all_gather(second_out[0], 'dp', axis=0, tiled=True)  16.2 us
  transfers between devices with their start and end apart: 65, of which 23 were waited for; matrix products, arithmetic and copies ran while one was open for 10% of the time, Pallas kernels for 37%

profile of v5, /device:TPU:0, one launch (start us, length us, event | category | flops | bytes accessed | tf_op | source)
XLA Modules:
  0.0 513.2 jit_solution(15385286441818741479)
XLA Ops:
  22.7 6.3 %all-to-all-start = ((f32[32,1,640]{2,1,0:T(1,128)}), f32[32,1,640]{2,1,0:T(1,128)S(1)}, u32[]{:S(2)}, u32[]{:S(2)}) async-start(f32[32,1,640]{2,1,0:T(1,128)} %broadcast_in_dim.26), calls=%async_computation | async-start | bytes 163840 | tf_op jit(solution)/shard_map/all_to_all | solution.py:1036
  33.3 4.1 all-to-all-done
  44.2 6.9 %collective-permute-done.5.refs_6_ = bf16[64,2048]{1,0:T(8,128)(2,1)} collective-permute-done((bf16[64,2048]{1,0:T(8,128)(2,1)S(1)}, bf16[64,2048]{1,0:T(8,128)(2,1)}, u32[]{:S(2)}, u32[]{:S(2)}) %collective-permute-start.5) | collective-permute-done | bytes 262176 | tf_op jit(solution)/shard_map/ppermute | solution.py:1085
  53.2 6.8 %front.1 = (bf16[272,512]{1,0:T(8,128)(2,1)}, bf16[272,512]{1,0:T(8,128)(2,1)}, bf16[272,512]{1,0:T(8,128)(2,1)}, bf16[272,512]{1,0:T(8,128)(2,1)}, f32[1024,128]{1,0:T(8,128)}, /*index=5*/f32[1024,1]{1,0:T(8,128)}) custom-call(bf16[1024,512]{1,0:T(8,128)(2,1)} %hidden_ref.5, bf16[1024,512]{1,0:T(8,128)(2,1)} %embed_ref.7, f32[8,512]{1,0:T(8,128)} %pad.20.gain_ref.gains_ref, ...), custom_call_target="tpu_custom_call" | custom-call | flops 2281701376 | bytes 4575232 | tf_op jit(solution)/shard_map/front/pallas_call | solution.py:30
  65.2 8.8 %collective-permute-done.13.refs_12_ = bf16[256,512]{1,0:T(8,128)(2,1)S(1)} collective-permute-done((bf16[256,512]{1,0:T(8,128)(2,1)S(1)}, bf16[256,512]{1,0:T(8,128)(2,1)S(1)}, u32[]{:S(2)}, u32[]{:S(2)}) %collective-permute-start.13) | collective-permute-done | bytes 262176 | tf_op jit(solution)/shard_map/ppermute | solution.py:1085
  76.9 5.0 assemble.1
  95.7 5.1 collective-permute-done.17.refs_2_
  101.5 42.0 %middle.1 = (f32[1024,512]{1,0:T(8,128)}, f32[1024,512]{1,0:T(8,128)}, bf16[1024,512]{1,0:T(8,128)(2,1)}, bf16[1024,512]{1,0:T(8,128)(2,1)}, bf16[1024,512]{1,0:...) custom-call(s32[1,5]{1,0:T(1,128)} %starts_ref.5, ...), custom_call_target="tpu_custom_call" | custom-call | flops 8589934592 | bytes 21827604 | tf_op jit(solution)/shard_map/middle/pallas_call | solution.py:30
  143.6 6.0 %all-to-all-start.1 = ((f32[32,1,1536]{2,1,0:T(1,128)}), f32[32,1,1536]{2,1,0:T(1,128)S(1)}, u32[]{:S(2)}, u32[]{:S(2)}) async-start(f32[32,1,1536]{2,1,0:T(1,128)} %get-tuple-element.189), calls=%async_computation.1 | async-start | bytes 393216 | tf_op jit(solution)/shard_map/all_to_all | solution.py:1036
  152.9 9.4 %all-to-all-done.1.totals_ref = f32[32,1,1536]{2,1,0:T(1,128)S(1)} async-done(((f32[32,1,1536]{2,1,0:T(1,128)}), f32[32,1,1536]{2,1,0:T(1,128)S(1)}, u32[]{:S(2)}, u32[]{:S(2)}) %all-to-all-start.1) | async-done | bytes 196640 | tf_op jit(solution)/shard_map/all_to_all | solution.py:1036
  163.0 9.8 %second.1 = (bf16[272,512]{1,0:T(8,128)(2,1)}, bf16[272,512]{1,0:T(8,128)(2,1)}, bf16[272,512]{1,0:T(8,128)(2,1)}, bf16[272,512]{1,0:T(8,128)(2,1)}, f32[1024,51...) custom-call(f32[1024,512]{1,0:T(8,128)} %get-tuple-element.187.h2_ref, ...), custom_call_target="tpu_custom_call" | custom-call | flops 2281701376 | bytes 11620352 | tf_op jit(solution)/shard_map/second/pallas_call | solution.py:30
  174.6 16.2 %all-gather.10.cloned.1.call-done = bf16[1,2048,512]{2,1,0:T(8,128)(2,1)} async-done(((bf16[1,256,512]{2,1,0:T(8,128)(2,1)}), bf16[1,2048,512]{2,1,0:T(8,128)(2,1)}) %all-gather.10.cloned.1.call-update) | async-done | bytes 2097168 | tf_op jit(solution)/shard_map/all_gather | solution.py:1263
  202.7 5.1 collective-permute-done.24.refs_2_
  212.2 9.8 %turn.1 = (bf16[272,512]{1,0:T(8,128)(2,1)}, bf16[272,512]{1,0:T(8,128)(2,1)}, bf16[272,512]{1,0:T(8,128)(2,1)}, bf16[272,512]{1,0:T(8,128)(2,1)}, bf16[1024,512...) custom-call(f32[1024,512]{1,0:T(8,128)} %get-tuple-element.190.h3_ref, ...), custom_call_target="tpu_custom_call" | custom-call | flops 2281701376 | bytes 10162176 | tf_op jit(solution)/shard_map/turn/pallas_call | solution.py:30
  225.3 4.1 experts_back.6
  232.6 4.2 collective-permute-done.28.refs_1_
  245.1 4.3 fusion.38
  249.4 6.9 %fusion.41 = bf16[512,2048]{1,0:T(8,128)(2,1)} fusion(bf16[272,2048]{1,0:T(8,128)(2,1)} %copy-done.17, bf16[272,2048]{1,0:T(8,128)(2,1)} %copy-done.16, bf16[272,2048]{1,0:T(8,128)(2,1)} %copy-done.25, bf16[272,2048]{1,0:T(8,128)(2,1)} %copy-done.24, bf16[272,512]{1,0:T(8,128)(2,1)S(1)} %collective-permute-done.22.refs_0_, ...), kind=kOutput, calls=%fused_computation.37 | convolution fusion | flops 2305032192 | bytes 7667712 | tf_op jit(solution)/shard_map/dot_general | solution.py:1169
  257.0 12.2 %second_back.1 = (f32[1024,512]{1,0:T(8,128)}, bf16[1024,512]{1,0:T(8,128)(2,1)}, f32[1024,512]{1,0:T(8,128)}, f32[1024,512]{1,0:T(8,128)}, f32[8,1024]{1,0:T(8,...) custom-call(s32[1024,128]{1,0:T(8,128)} %get-tuple-element.176.cols_ref, f32[1024,128]{1,0:T(8,128)} %get-tuple-element.204.dlogits_ref, ...), custom_call_target="tpu_custom_call" | custom-call | flops 2281701376 | bytes 17858560 | tf_op jit(solution)/shard_map/second_back/pallas_call | solution.py:30
  269.3 4.2 all-to-all-start.2
  276.0 7.8 %all-to-all-done.2.dsums_ref = f32[32,1,1024]{2,1,0:T(1,128)S(1)} async-done(((f32[32,1,1024]{2,1,0:T(1,128)}), f32[32,1,1024]{2,1,0:T(1,128)S(1)}, u32[]{:S(2)}, u32[]{:S(2)}) %all-to-all-start.2) | async-done | bytes 131104 | tf_op jit(solution)/shard_map/all_to_all | solution.py:1036
  284.4 22.9 %conv_back.1 = (f32[1024,512]{1,0:T(8,128)}, bf16[1024,512]{1,0:T(8,128)(2,1)}, bf16[1024,512]{1,0:T(8,128)(2,1)}, bf16[1024,512]{1,0:T(8,128)(2,1)}, bf16[1024,...) custom-call(s32[1,5]{1,0:T(1,128)} %starts_ref.5, f32[1024,512]{1,0:T(8,128)} %get-tuple-element.188.conv_ref, ...), custom_call_target="tpu_custom_call" | custom-call | flops 1610612736 | bytes 20168724 | tf_op jit(solution)/shard_map/conv_back/pallas_call | solution.py:30
  315.7 48.4 %attend_back.1 = (bf16[272,512]{1,0:T(8,128)(2,1)}, bf16[272,512]{1,0:T(8,128)(2,1)}, bf16[272,512]{1,0:T(8,128)(2,1)}, bf16[272,512]{1,0:T(8,128)(2,1)}, f32[10...) custom-call(s32[1,5]{1,0:T(1,128)} %starts_ref.5, ...), custom_call_target="tpu_custom_call" | custom-call | flops 17179869184 | bytes 29052948 | tf_op jit(solution)/shard_map/attend_back/pallas_call | solution.py:30
  368.7 11.5 %experts_back.9 = (bf16[512,2048]{1,0:T(8,128)(2,1)}, bf16[272,512]{1,0:T(8,128)(2,1)S(1)}, bf16[272,512]{1,0:T(8,128)(2,1)S(1)}, bf16[272,2048]{1,0:T(8,128)(2,...) custom-call(bf16[512,2048]{1,0:T(8,128)(2,1)} %get-tuple-element.179.in_ref, ...), custom_call_target="tpu_custom_call" | custom-call | flops 3422552064 | bytes 18710528 | tf_op jit(solution)/shard_map/experts_back/pallas_call | solution.py:30
  402.4 19.9 %collective-permute-done.38 = bf16[4,320,512]{2,1,0:T(8,128)(2,1)} collective-permute-done((bf16[4,320,512]{2,1,0:T(8,128)(2,1)}, bf16[4,320,512]{2,1,0:T(8,128)(2,1)}, u32[]{:S(2)}, u32[]{:S(2)}) %collective-permute-start.38) | collective-permute-done | bytes 1310752 | tf_op jit(solution)/shard_map/ppermute | solution.py:1042
  424.0 4.8 collective-permute-done.44.refs_3_
  436.5 9.9 %last.1 = (f32[1024,512]{1,0:T(8,128)}, f32[1024,512]{1,0:T(8,128)}, f32[16,1024]{1,0:T(8,128)}, f32[24,512]{1,0:T(8,128)}, f32[64,2048]{1,0:T(8,128)}, /*index=5*/f32[256,512]{1,0:T(8,128)}) custom-call(s32[1024,128]{1,0:T(8,128)} %get-tuple-element.176.cols_ref, f32[1024,128]{1,0:T(8,128)} %get-tuple-element.249.dlogits_ref, bf16[1024,512]{1,0:T(8,128)(2,1)} %hidden_ref.5, ...), custom_call_target="tpu_custom_call" | custom-call | flops 2281701376 | bytes 14761984 | tf_op jit(solution)/shard_map/last/pallas_call | solution.py:30
  447.5 11.8 %collective-permute-done.47 = bf16[320,512]{1,0:T(8,128)(2,1)S(1)} collective-permute-done((bf16[320,512]{1,0:T(8,128)(2,1)}, bf16[320,512]{1,0:T(8,128)(2,1)S(1)}, u32[]{:S(2)}, u32[]{:S(2)}) %collective-permute-start.47) | collective-permute-done | bytes 327712 | tf_op jit(solution)/shard_map/ppermute | solution.py:1042
  462.9 6.6 %collective-permute-start.49 = (bf16[64,2048]{1,0:T(8,128)(2,1)S(1)}, bf16[64,2048]{1,0:T(8,128)(2,1)S(1)}, u32[]{:S(2)}, u32[]{:S(2)}) collective-permute-start(bf16[64,2048]{1,0:T(8,128)(2,1)S(1)} %get-tuple-element.349), channel_id=1, source_target_pairs={{0,8},{4,12},{8,0},{12,4},{16,24},{20,28},{24,16},{28,20},{1,9},{5... | collective-permute-start | bytes 786440 | tf_op jit(solution)/shard_map/ppermute | solution.py:1042
  483.8 3.9 all-to-all-start.3
  487.6 7.0 %collective-permute-done.50 = bf16[64,2048]{1,0:T(8,128)(2,1)S(1)} collective-permute-done((bf16[64,2048]{1,0:T(8,128)(2,1)S(1)}, bf16[64,2048]{1,0:T(8,128)(2,1)S(1)}, u32[]{:S(2)}, u32[]{:S(2)}) %collective-permute-start.50) | collective-permute-done | bytes 262176 | tf_op jit(solution)/shard_map/ppermute | solution.py:1042
  495.5 5.2 %collective-permute-done.54 = bf16[16,2048]{1,0:T(8,128)(2,1)} collective-permute-done((bf16[16,2048]{1,0:T(8,128)(2,1)}, bf16[16,2048]{1,0:T(8,128)(2,1)}, u32[]{:S(2)}, u32[]{:S(2)}) %collective-permute-start.54) | collective-permute-done | bytes 65568 | tf_op jit(solution)/shard_map/ppermute | solution.py:1042
  (356 shorter events, 161.1 us)
Async XLA Ops:
  7.2 93.6 %all-gather.6.cloned.1.call-start = ((), (), s32[]{:S(2)}) async-start(), calls=%async_computation.6 | async-start | bytes 4325376 | tf_op jit(solution)/shard_map/all_gather | solution.py:1257
  11.6 163.0 %all-gather.8.cloned.1.call-start = ((), (), s32[]{:S(2)}) async-start(), calls=%async_computation.9 | async-start | bytes 2359296 | tf_op jit(solution)/shard_map/all_gather | solution.py:1262
  12.4 178.5 %all-gather.10.cloned.1.call-start = ((), (), s32[]{:S(2)}) async-start(), calls=%async_computation.10 | async-start | bytes 2359296 | tf_op jit(solution)/shard_map/all_gather | solution.py:1263
  16.2 22.0 %collective-permute-start.4 = (bf16[64,2048]{1,0:T(8,128)(2,1)}, bf16[64,2048]{1,0:T(8,128)(2,1)S(1)}, u32[]{:S(2)}, u32[]{:S(2)}) collective-permute-start(bf16[64,2048]{1,0:T(8,128)(2,1)} %bitcast.160), channel_id=1, source_target_pairs={{0,8},{8,16},{16,24},{24,28},{28,20},{20,12},{12,4},{4,0},{1,9},{9... | collective-permute-start | bytes 786440 | tf_op jit(solution)/shard_map/ppermute | solution.py:1085
  18.2 20.8 %collective-permute-start.7 = (bf16[256,512]{1,0:T(8,128)(2,1)}, bf16[256,512]{1,0:T(8,128)(2,1)S(1)}, u32[]{:S(2)}, u32[]{:S(2)}) collective-permute-start(bf16[256,512]{1,0:T(8,128)(2,1)} %bitcast.163), channel_id=1, source_target_pairs={{0,4},{8,0},{16,8},{24,16},{28,24},{20,28},{12,20},{4,12},{1,5},{9... | collective-permute-start | bytes 786440 | tf_op jit(solution)/shard_map/ppermute | solution.py:1083
  40.4 19.7 %collective-permute-start.12 = (bf16[256,512]{1,0:T(8,128)(2,1)S(1)}, bf16[256,512]{1,0:T(8,128)(2,1)S(1)}, u32[]{:S(2)}, u32[]{:S(2)}) collective-permute-start(bf16[256,512]{1,0:T(8,128)(2,1)S(1)} %collective-permute-done.11.refs_14_), channel_id=1, source_target_pairs={{0,8},{8,16},{16,24},{24,28},{28,20},{20,12},{12,4},{4,0},{1,9},{9... | collective-permute-start | bytes 786440 | tf_op jit(solution)/shard_map/ppermute | solution.py:1085
  41.2 20.6 %collective-permute-start.2 = (bf16[64,2048]{1,0:T(8,128)(2,1)S(1)}, bf16[64,2048]{1,0:T(8,128)(2,1)S(1)}, u32[]{:S(2)}, u32[]{:S(2)}) collective-permute-start(bf16[64,2048]{1,0:T(8,128)(2,1)S(1)} %collective-permute-done.1.refs_2_), channel_id=1, source_target_pairs={{0,4},{8,0},{16,8},{24,16},{28,24},{20,28},{12,20},{4,12},{1,5},{9... | collective-permute-start | bytes 786440 | tf_op jit(solution)/shard_map/ppermute | solution.py:1083
  60.0 21.9 %collective-permute-start.18 = (bf16[272,512]{1,0:T(8,128)(2,1)}, bf16[272,512]{1,0:T(8,128)(2,1)S(1)}, u32[]{:S(2)}, u32[]{:S(2)}) collective-permute-start(bf16[272,512]{1,0:T(8,128)(2,1)} %get-tuple-element.186), channel_id=1, source_target_pairs={{0,3},{1,2},{2,1},{3,0},{4,7},{5,6},{6,5},{7,4},{8,11},{9,10},{10,... | collective-permute-start | bytes 835592 | tf_op jit(solution)/shard_map/ppermute | solution.py:1042
  62.8 24.1 %collective-permute-start.16 = (bf16[272,512]{1,0:T(8,128)(2,1)}, bf16[272,512]{1,0:T(8,128)(2,1)S(1)}, u32[]{:S(2)}, u32[]{:S(2)}) collective-permute-start(bf16[272,512]{1,0:T(8,128)(2,1)} %get-tuple-element.185), channel_id=1, source_target_pairs={{0,2},{1,3},{2,0},{3,1},{4,6},{5,7},{6,4},{7,5},{8,10},{9,11},{10,... | collective-permute-start | bytes 835592 | tf_op jit(solution)/shard_map/ppermute | solution.py:1042
  64.6 24.4 %collective-permute-start.14 = (bf16[272,512]{1,0:T(8,128)(2,1)}, bf16[272,512]{1,0:T(8,128)(2,1)S(1)}, u32[]{:S(2)}, u32[]{:S(2)}) collective-permute-start(bf16[272,512]{1,0:T(8,128)(2,1)} %get-tuple-element.182), channel_id=1, source_target_pairs={{0,1},{1,0},{2,3},{3,2},{4,5},{5,4},{6,7},{7,6},{8,9},{9,8},{10,11... | collective-permute-start | bytes 835592 | tf_op jit(solution)/shard_map/ppermute | solution.py:1042
  143.6 18.7 %all-to-all-start.1 = ((f32[32,1,1536]{2,1,0:T(1,128)}), f32[32,1,1536]{2,1,0:T(1,128)S(1)}, u32[]{:S(2)}, u32[]{:S(2)}) async-start(f32[32,1,1536]{2,1,0:T(1,128)} %get-tuple-element.189), calls=%async_computation.1 | async-start | bytes 393216 | tf_op jit(solution)/shard_map/all_to_all | solution.py:1036
  149.6 286.8 %reduce-scatter.3.cloned.1.call-start = ((), (), s32[]{:S(2)}) async-start(), calls=%async_computation.7 | async-start | bytes 2359296 | tf_op jit(solution)/shard_map/reduce_scatter | solution.py:1179
  172.8 24.9 %collective-permute-start.21 = (bf16[272,512]{1,0:T(8,128)(2,1)}, bf16[272,512]{1,0:T(8,128)(2,1)S(1)}, u32[]{:S(2)}, u32[]{:S(2)}) collective-permute-start(bf16[272,512]{1,0:T(8,128)(2,1)} %get-tuple-element.197), channel_id=1, source_target_pairs={{0,2},{1,3},{2,0},{3,1},{4,6},{5,7},{6,4},{7,5},{8,10},{9,11},{10,... | collective-permute-start | bytes 835592 | tf_op jit(solution)/shard_map/ppermute | solution.py:1042
  174.3 23.4 %collective-permute-start.22 = (bf16[272,512]{1,0:T(8,128)(2,1)}, bf16[272,512]{1,0:T(8,128)(2,1)S(1)}, u32[]{:S(2)}, u32[]{:S(2)}) collective-permute-start(bf16[272,512]{1,0:T(8,128)(2,1)} %get-tuple-element.198), channel_id=1, source_target_pairs={{0,3},{1,2},{2,1},{3,0},{4,7},{5,6},{6,5},{7,4},{8,11},{9,10},{10,... | collective-permute-start | bytes 835592 | tf_op jit(solution)/shard_map/ppermute | solution.py:1042
  273.4 163.0 %reduce-scatter.5.cloned.1.call-start = ((), (), s32[]{:S(2)}) async-start(), calls=%async_computation.8 | async-start | bytes 2359296 | tf_op jit(solution)/shard_map/reduce_scatter | solution.py:1180
  313.5 50.6 %collective-permute-start.32 = (bf16[8,4,16,512]{3,2,1,0:T(8,128)(2,1)S(1)}, bf16[8,4,16,512]{3,2,1,0:T(8,128)(2,1)S(1)}, u32[]{:S(2)}, u32[]{:S(2)}) collective-permute-start(bf16[8,4,16,512]{3,2,1,0:T(8,128)(2,1)S(1)} %bitcast.154), channel_id=1, source_target_pairs={{0,1},{1,0},{2,3},{3,2},{4,5},{5,4},{6,7},{7,6},{8,9},{9,8},{10,11... | collective-permute-start | bytes 1572872 | tf_op jit(solution)/shard_map/ppermute | solution.py:1042
  313.7 50.4 %collective-permute-start.33 = (bf16[8,4,16,512]{3,2,1,0:T(8,128)(2,1)S(1)}, bf16[8,4,16,512]{3,2,1,0:T(8,128)(2,1)S(1)}, u32[]{:S(2)}, u32[]{:S(2)}) collective-permute-start(bf16[8,4,16,512]{3,2,1,0:T(8,128)(2,1)S(1)} %bitcast.155), channel_id=1, source_target_pairs={{0,2},{1,3},{2,0},{3,1},{4,6},{5,7},{6,4},{7,5},{8,10},{9,11},{10,... | collective-permute-start | bytes 1572872 | tf_op jit(solution)/shard_map/ppermute | solution.py:1042
  314.9 49.3 %collective-permute-start.34 = (bf16[8,4,16,512]{3,2,1,0:T(8,128)(2,1)S(1)}, bf16[8,4,16,512]{3,2,1,0:T(8,128)(2,1)S(1)}, u32[]{:S(2)}, u32[]{:S(2)}) collective-permute-start(bf16[8,4,16,512]{3,2,1,0:T(8,128)(2,1)S(1)} %bitcast.156), channel_id=1, source_target_pairs={{0,3},{1,2},{2,1},{3,0},{4,7},{5,6},{6,5},{7,4},{8,11},{9,10},{10,... | collective-permute-start | bytes 1572872 | tf_op jit(solution)/shard_map/ppermute | solution.py:1042
  390.1 32.2 %collective-permute-start.38 = (bf16[4,320,512]{2,1,0:T(8,128)(2,1)}, bf16[4,320,512]{2,1,0:T(8,128)(2,1)}, u32[]{:S(2)}, u32[]{:S(2)}) collective-permute-start(bf16[4,320,512]{2,1,0:T(8,128)(2,1)} %fusion.46), channel_id=1, source_target_pairs={{0,4},{4,0},{8,12},{12,8},{16,20},{20,16},{24,28},{28,24},{1,5},{5... | collective-permute-start | bytes 3932168 | tf_op jit(solution)/shard_map/ppermute | solution.py:1042
  395.9 32.9 %collective-permute-start.39 = (bf16[8,16,2048]{2,1,0:T(8,128)(2,1)S(1)}, bf16[8,16,2048]{2,1,0:T(8,128)(2,1)S(1)}, u32[]{:S(2)}, u32[]{:S(2)}) collective-permute-start(bf16[8,16,2048]{2,1,0:T(8,128)(2,1)S(1)} %get-tuple-element.337), channel_id=1, source_target_pairs={{0,1},{1,0},{2,3},{3,2},{4,5},{5,4},{6,7},{7,6},{8,9},{9,8},{10,11... | collective-permute-start | bytes 1572872 | tf_op jit(solution)/shard_map/ppermute | solution.py:1042
  395.9 32.9 %collective-permute-start.40 = (bf16[8,16,2048]{2,1,0:T(8,128)(2,1)S(1)}, bf16[8,16,2048]{2,1,0:T(8,128)(2,1)S(1)}, u32[]{:S(2)}, u32[]{:S(2)}) collective-permute-start(bf16[8,16,2048]{2,1,0:T(8,128)(2,1)S(1)} %get-tuple-element.336), channel_id=1, source_target_pairs={{0,2},{1,3},{2,0},{3,1},{4,6},{5,7},{6,4},{7,5},{8,10},{9,11},{10,... | collective-permute-start | bytes 1572872 | tf_op jit(solution)/shard_map/ppermute | solution.py:1042
  397.5 31.3 %collective-permute-start.41 = (bf16[8,16,2048]{2,1,0:T(8,128)(2,1)S(1)}, bf16[8,16,2048]{2,1,0:T(8,128)(2,1)S(1)}, u32[]{:S(2)}, u32[]{:S(2)}) collective-permute-start(bf16[8,16,2048]{2,1,0:T(8,128)(2,1)S(1)} %get-tuple-element.335), channel_id=1, source_target_pairs={{0,3},{1,2},{2,1},{3,0},{4,7},{5,6},{6,5},{7,4},{8,11},{9,10},{10,... | collective-permute-start | bytes 1572872 | tf_op jit(solution)/shard_map/ppermute | solution.py:1042
  402.3 26.5 %collective-permute-start.44 = (bf16[272,512]{1,0:T(8,128)(2,1)S(1)}, bf16[272,512]{1,0:T(8,128)(2,1)S(1)}, u32[]{:S(2)}, u32[]{:S(2)}) collective-permute-start(bf16[272,512]{1,0:T(8,128)(2,1)S(1)} %get-tuple-element.301), channel_id=1, source_target_pairs={{0,3},{1,2},{2,1},{3,0},{4,7},{5,6},{6,5},{7,4},{8,11},{9,10},{10,... | collective-permute-start | bytes 835592 | tf_op jit(solution)/shard_map/ppermute | solution.py:1042
  430.5 28.8 %collective-permute-start.45 = (bf16[4,64,2048]{2,1,0:T(8,128)(2,1)}, bf16[4,64,2048]{2,1,0:T(8,128)(2,1)}, u32[]{:S(2)}, u32[]{:S(2)}) collective-permute-start(bf16[4,64,2048]{2,1,0:T(8,128)(2,1)} %get-tuple-element.333), channel_id=1, source_target_pairs={{0,4},{4,0},{8,12},{12,8},{16,20},{20,16},{24,28},{28,24},{1,5},{5... | collective-permute-start | bytes 3145736 | tf_op jit(solution)/shard_map/ppermute | solution.py:1042
  433.6 25.7 %collective-permute-start.47 = (bf16[320,512]{1,0:T(8,128)(2,1)}, bf16[320,512]{1,0:T(8,128)(2,1)S(1)}, u32[]{:S(2)}, u32[]{:S(2)}) collective-permute-start(bf16[320,512]{1,0:T(8,128)(2,1)} %get-tuple-element.344), channel_id=1, source_target_pairs={{0,16},{4,20},{8,24},{12,28},{16,0},{20,4},{24,8},{28,12},{1,17},{... | collective-permute-start | bytes 983048 | tf_op jit(solution)/shard_map/ppermute | solution.py:1042
  435.0 24.3 %collective-permute-start.48 = (bf16[320,512]{1,0:T(8,128)(2,1)S(1)}, bf16[320,512]{1,0:T(8,128)(2,1)S(1)}, u32[]{:S(2)}, u32[]{:S(2)}) collective-permute-start(bf16[320,512]{1,0:T(8,128)(2,1)S(1)} %get-tuple-element.343), channel_id=1, source_target_pairs={{0,24},{4,28},{8,16},{12,20},{16,8},{20,12},{24,0},{28,4},{1,25},{... | collective-permute-start | bytes 983048 | tf_op jit(solution)/shard_map/ppermute | solution.py:1042
  469.5 25.1 %collective-permute-start.50 = (bf16[64,2048]{1,0:T(8,128)(2,1)S(1)}, bf16[64,2048]{1,0:T(8,128)(2,1)S(1)}, u32[]{:S(2)}, u32[]{:S(2)}) collective-permute-start(bf16[64,2048]{1,0:T(8,128)(2,1)S(1)} %get-tuple-element.347), channel_id=1, source_target_pairs={{0,16},{4,20},{8,24},{12,28},{16,0},{20,4},{24,8},{28,12},{1,17},{... | collective-permute-start | bytes 786440 | tf_op jit(solution)/shard_map/ppermute | solution.py:1042
  470.5 24.1 %collective-permute-start.51 = (bf16[64,2048]{1,0:T(8,128)(2,1)S(1)}, bf16[64,2048]{1,0:T(8,128)(2,1)S(1)}, u32[]{:S(2)}, u32[]{:S(2)}) collective-permute-start(bf16[64,2048]{1,0:T(8,128)(2,1)S(1)} %get-tuple-element.348), channel_id=1, source_target_pairs={{0,24},{4,28},{8,16},{12,20},{16,8},{20,12},{24,0},{28,4},{1,25},{... | collective-permute-start | bytes 786440 | tf_op jit(solution)/shard_map/ppermute | solution.py:1042
  474.2 21.3 %collective-permute-start.53 = (bf16[16,2048]{1,0:T(8,128)(2,1)}, bf16[16,2048]{1,0:T(8,128)(2,1)S(1)}, u32[]{:S(2)}, u32[]{:S(2)}) collective-permute-start(bf16[16,2048]{1,0:T(8,128)(2,1)} %get-tuple-element.358), channel_id=1, source_target_pairs={{0,8},{4,12},{8,0},{12,4},{16,24},{20,28},{24,16},{28,20},{1,9},{5... | collective-permute-start | bytes 196616 | tf_op jit(solution)/shard_map/ppermute | solution.py:1042
  475.8 24.9 %collective-permute-start.54 = (bf16[16,2048]{1,0:T(8,128)(2,1)}, bf16[16,2048]{1,0:T(8,128)(2,1)}, u32[]{:S(2)}, u32[]{:S(2)}) collective-permute-start(bf16[16,2048]{1,0:T(8,128)(2,1)} %get-tuple-element.360), channel_id=1, source_target_pairs={{0,16},{4,20},{8,24},{12,28},{16,0},{20,4},{24,8},{28,12},{1,17},{... | collective-permute-start | bytes 196616 | tf_op jit(solution)/shard_map/ppermute | solution.py:1042
  480.3 20.4 %collective-permute-start.55 = (bf16[16,2048]{1,0:T(8,128)(2,1)S(1)}, bf16[16,2048]{1,0:T(8,128)(2,1)}, u32[]{:S(2)}, u32[]{:S(2)}) collective-permute-start(bf16[16,2048]{1,0:T(8,128)(2,1)S(1)} %get-tuple-element.359), channel_id=1, source_target_pairs={{0,24},{4,28},{8,16},{12,20},{16,8},{20,12},{24,0},{28,4},{1,25},{... | collective-permute-start | bytes 196616 | tf_op jit(solution)/shard_map/ppermute | solution.py:1042
  483.8 19.2 %all-to-all-start.3 = ((f32[32,1,640]{2,1,0:T(1,128)}), f32[32,1,640]{2,1,0:T(1,128)S(1)}, u32[]{:S(2)}, u32[]{:S(2)}) async-start(f32[32,1,640]{2,1,0:T(1,128)} %all_to_all.22), calls=%async_computation.5 | async-start | bytes 163840 | tf_op jit(solution)/shard_map/all_to_all | solution.py:1469
  (104 other events, 863.7 us)
Sparse Core Ops, SparseCore 0:
  11.7 74.6 all-gather.5
  88.6 49.2 all-gather.7
  140.0 50.7 all-gather.9
  256.5 69.4 reduce-scatter.2
  329.3 66.6 reduce-scatter.4

commit v6 on v5

--- a/solution.py
+++ b/solution.py
@@ -79,6 +79,11 @@
 
 
 def loop(count, body):
+    if count <= 4:
+        for index in range(count):
+            body(index)
+        return
+
     def step(index, carry):
         body(index)
         return carry
@@ -86,7 +91,15 @@
     lax.fori_loop(0, count, step, 0)
 
 
+def span_at(start, size, step):
+    if isinstance(start, int):
+        return slice(start, start + size)
+    return pl.ds(pl.multiple_of(start, step), size)
+
+
 def rows_at(index, size):
+    if isinstance(index, int):
+        return slice(index * size, (index + 1) * size)
     return pl.ds(pl.multiple_of(index * size, size), size)
 
 
@@ -646,7 +659,7 @@
         qv_ref[at, :] = ((queries + bias_ref[1:2, :]).astype(bf16).astype(f32) * scale).astype(bf16)
         k_ref[at, :] = dot(low, in_ref[:, width : 2 * width]).astype(bf16)
         v_ref[at, :] = dot(low, in_ref[:, 2 * width :]).astype(bf16)
-        table_at = pl.ds(pl.multiple_of(index * BLOCK + edge, TILE), BLOCK)
+        table_at = span_at(index * BLOCK + edge, BLOCK, TILE)
         t_ref[table_at, :] = dot(sinus_ref[at, :], place_ref[...]).astype(bf16)
 
     edge = PAD * TILE
@@ -667,7 +680,7 @@
         low = (standard * gains_ref[2:3, :]).astype(bf16)
         value = dot(low, point_ref[:, :width])
         gates = dot(low, point_ref[:, width:])
-        padded[pl.ds(pl.multiple_of(index * BLOCK + EDGE, EDGE), BLOCK), :] = value * sigmoid(gates)
+        padded[span_at(index * BLOCK + EDGE, BLOCK, EDGE), :] = value * sigmoid(gates)
 
     loop(length // BLOCK, gates_step)
     sums[...] = jnp.zeros_like(sums)
@@ -870,7 +883,7 @@
         inside = (iota((BLOCK, 1), 0) + index * BLOCK) < frames
         shared = (2.0 * d_variance * centred - batch_inverse * dsums[:, :width]) / count
         d_conv = batch_inverse * dz_ref[at, :] + jnp.where(inside, shared, 0.0)
-        padded[pl.ds(pl.multiple_of(index * BLOCK + EDGE, EDGE), BLOCK), :] = d_conv
+        padded[span_at(index * BLOCK + EDGE, BLOCK, EDGE), :] = d_conv
         standard, unused = normalize(h2_ref[at, :])
         low = (standard * gains_ref[2:3, :]).astype(bf16)
         n3_ref[at, :] = low
@@ -962,7 +975,7 @@
 
     def table_step(index):
         at = rows_at(index, BLOCK)
-        table_at = pl.ds(pl.multiple_of(index * BLOCK + edge, TILE), BLOCK)
+        table_at = span_at(index * BLOCK + edge, BLOCK, TILE)
         mirrored_ref[table_at, :] = dot(sinus_ref[at, :], place_ref[...]).astype(bf16)
 
     edge = PAD * TILE

time: 519 us -> 513 us (0.988)
  Pallas kernels: 204 us -> 193 us
  waiting for transfers between devices: 136 us -> 143 us
    pallas_call x21, Pallas kernels: 199 us -> 188 us  [run(): pl.pallas_call(kernel, out_shape=outs, in_specs=in_specs, out_specs=[VMEM...]
    all_gather x1, waiting for transfers between devices: 16.2 us -> 22.5 us  [body(): lax.all_gather(second_out[0], 'dp', axis=0, tiled=True)]
  transfers between devices with their start and end apart: 65 -> 65, of which waited for: 23 -> 23; matrix products, arithmetic and copies ran while one was open for 10% -> 10% of each run, Pallas kernels for 37% -> 36%
where the time goes in v6:
time: 513 us; the launch traced here: 507 us
  Pallas kernels  193 us (38%)
  waiting for transfers between devices  143 us (28%)
  starting transfers between devices  75 us (15%)
  local copies, waits for them, and re-layouts  48.7 us (9%)
  matrix products  22.9 us (4%)
  between operations  15.2 us (3%)
  other arithmetic  9.55 us (2%)
    pallas_call x21, Pallas kernels, run(): pl.pallas_call(kernel, out_shape=outs, in_specs=in_specs, out_specs=[VMEM...  188 us
    ppermute x42, waiting for transfers between devices, across(): return lax.ppermute(values, axis, [(i, i ^ offset) for i in range(size)])  75.7 us
    ppermute x42, starting transfers between devices, across(): return lax.ppermute(values, axis, [(i, i ^ offset) for i in range(size)])  41.1 us
    unnamed x151, local copies, waits for them, and re-layouts  22.9 us
    dot_general x7, matrix products, rows_product(): lax.dot_general(left, right, (((0,), (0,)), ((), ())), preferred_element_...  22.9 us
    all_gather x1, waiting for transfers between devices, body(): lax.all_gather(second_out[0], 'dp', axis=0, tiled=True)  22.5 us
    all_to_all x3, waiting for transfers between devices, gather_small(): return lax.all_to_all(values, BOTH, split_axis=0, concat_axis=0, tiled=True)  19.9 us
    all_to_all x3, starting transfers between devices, gather_small(): return lax.all_to_all(values, BOTH, split_axis=0, concat_axis=0, tiled=True)  15.8 us
  transfers between devices with their start and end apart: 65, of which 23 were waited for; matrix products, arithmetic and copies ran while one was open for 10% of the time, Pallas kernels for 36%

profile of v6, /device:TPU:0, one launch (start us, length us, event | category | flops | bytes accessed | tf_op | source)
XLA Modules:
  0.0 507.1 jit_solution(18026546751456816322)
XLA Ops:
  22.7 6.3 %all-to-all-start = ((f32[32,1,640]{2,1,0:T(1,128)}), f32[32,1,640]{2,1,0:T(1,128)S(1)}, u32[]{:S(2)}, u32[]{:S(2)}) async-start(f32[32,1,640]{2,1,0:T(1,128)} %broadcast_in_dim.26), calls=%async_computation | async-start | bytes 163840 | tf_op jit(solution)/shard_map/all_to_all | solution.py:1049
  33.3 4.1 all-to-all-done
  44.2 6.9 %collective-permute-done.5.refs_6_ = bf16[64,2048]{1,0:T(8,128)(2,1)} collective-permute-done((bf16[64,2048]{1,0:T(8,128)(2,1)S(1)}, bf16[64,2048]{1,0:T(8,128)(2,1)}, u32[]{:S(2)}, u32[]{:S(2)}) %collective-permute-start.5) | collective-permute-done | bytes 262176 | tf_op jit(solution)/shard_map/ppermute | solution.py:1098
  53.2 5.4 %front.1 = (bf16[272,512]{1,0:T(8,128)(2,1)}, bf16[272,512]{1,0:T(8,128)(2,1)}, bf16[272,512]{1,0:T(8,128)(2,1)}, bf16[272,512]{1,0:T(8,128)(2,1)}, f32[1024,128]{1,0:T(8,128)}, /*index=5*/f32[1024,1]{1,0:T(8,128)}) custom-call(bf16[1024,512]{1,0:T(8,128)(2,1)} %hidden_ref.5, bf16[1024,512]{1,0:T(8,128)(2,1)} %embed_ref.7, f32[8,512]{1,0:T(8,128)} %pad.20.gain_ref.gains_ref, ...), custom_call_target="tpu_custom_call" | custom-call | flops 2281701376 | bytes 4575232 | tf_op jit(solution)/shard_map/front/pallas_call | solution.py:30
  67.2 5.9 %collective-permute-done.13.refs_12_ = bf16[256,512]{1,0:T(8,128)(2,1)S(1)} collective-permute-done((bf16[256,512]{1,0:T(8,128)(2,1)S(1)}, bf16[256,512]{1,0:T(8,128)(2,1)S(1)}, u32[]{:S(2)}, u32[]{:S(2)}) %collective-permute-start.13) | collective-permute-done | bytes 262176 | tf_op jit(solution)/shard_map/ppermute | solution.py:1098
  76.9 5.0 assemble.1
  95.6 3.6 collective-permute-done.17.refs_2_
  100.1 40.5 %middle.1 = (f32[1024,512]{1,0:T(8,128)}, f32[1024,512]{1,0:T(8,128)}, bf16[1024,512]{1,0:T(8,128)(2,1)}, bf16[1024,512]{1,0:T(8,128)(2,1)}, bf16[1024,512]{1,0:...) custom-call(s32[1,5]{1,0:T(1,128)} %starts_ref.5, ...), custom_call_target="tpu_custom_call" | custom-call | flops 8589934592 | bytes 21827604 | tf_op jit(solution)/shard_map/middle/pallas_call | solution.py:30
  140.5 5.3 %all-to-all-start.1 = ((f32[32,1,1536]{2,1,0:T(1,128)}), f32[32,1,1536]{2,1,0:T(1,128)S(1)}, u32[]{:S(2)}, u32[]{:S(2)}) async-start(f32[32,1,1536]{2,1,0:T(1,128)} %get-tuple-element.189), calls=%async_computation.1 | async-start | bytes 393216 | tf_op jit(solution)/shard_map/all_to_all | solution.py:1049
  148.9 8.7 %all-to-all-done.1.totals_ref = f32[32,1,1536]{2,1,0:T(1,128)S(1)} async-done(((f32[32,1,1536]{2,1,0:T(1,128)}), f32[32,1,1536]{2,1,0:T(1,128)S(1)}, u32[]{:S(2)}, u32[]{:S(2)}) %all-to-all-start.1) | async-done | bytes 196640 | tf_op jit(solution)/shard_map/all_to_all | solution.py:1049
  158.3 8.2 %second.1 = (bf16[272,512]{1,0:T(8,128)(2,1)}, bf16[272,512]{1,0:T(8,128)(2,1)}, bf16[272,512]{1,0:T(8,128)(2,1)}, bf16[272,512]{1,0:T(8,128)(2,1)}, f32[1024,51...) custom-call(f32[1024,512]{1,0:T(8,128)} %get-tuple-element.187.h2_ref, ...), custom_call_target="tpu_custom_call" | custom-call | flops 2281701376 | bytes 11620352 | tf_op jit(solution)/shard_map/second/pallas_call | solution.py:30
  168.4 22.5 %all-gather.10.cloned.1.call-done = bf16[1,2048,512]{2,1,0:T(8,128)(2,1)} async-done(((bf16[1,256,512]{2,1,0:T(8,128)(2,1)}), bf16[1,2048,512]{2,1,0:T(8,128)(2,1)}) %all-gather.10.cloned.1.call-update) | async-done | bytes 2097168 | tf_op jit(solution)/shard_map/all_gather | solution.py:1276
  202.7 5.1 %collective-permute-done.24.refs_2_ = bf16[272,512]{1,0:T(8,128)(2,1)S(1)} collective-permute-done((bf16[272,512]{1,0:T(8,128)(2,1)S(1)}, bf16[272,512]{1,0:T(8,128)(2,1)S(1)}, u32[]{:S(2)}, u32[]{:S(2)}) %collective-permute-start.24) | collective-permute-done | bytes 278560 | tf_op jit(solution)/shard_map/ppermute | solution.py:1055
  212.3 7.6 %turn.1 = (bf16[272,512]{1,0:T(8,128)(2,1)}, bf16[272,512]{1,0:T(8,128)(2,1)}, bf16[272,512]{1,0:T(8,128)(2,1)}, bf16[272,512]{1,0:T(8,128)(2,1)}, bf16[1024,512...) custom-call(f32[1024,512]{1,0:T(8,128)} %get-tuple-element.190.h3_ref, ...), custom_call_target="tpu_custom_call" | custom-call | flops 2281701376 | bytes 10162176 | tf_op jit(solution)/shard_map/turn/pallas_call | solution.py:30
  223.3 4.1 experts_back.6
  230.6 4.2 collective-permute-done.28.refs_1_
  243.1 4.3 fusion.38
  247.4 6.8 %fusion.41 = bf16[512,2048]{1,0:T(8,128)(2,1)} fusion(bf16[272,2048]{1,0:T(8,128)(2,1)} %copy-done.17, bf16[272,2048]{1,0:T(8,128)(2,1)} %copy-done.16, bf16[272,2048]{1,0:T(8,128)(2,1)} %copy-done.25, bf16[272,2048]{1,0:T(8,128)(2,1)} %copy-done.24, bf16[272,512]{1,0:T(8,128)(2,1)S(1)} %collective-permute-done.22.refs_0_, ...), kind=kOutput, calls=%fused_computation.37 | convolution fusion | flops 2305032192 | bytes 7667712 | tf_op jit(solution)/shard_map/dot_general | solution.py:1182
  254.8 11.7 %second_back.1 = (f32[1024,512]{1,0:T(8,128)}, bf16[1024,512]{1,0:T(8,128)(2,1)}, f32[1024,512]{1,0:T(8,128)}, f32[1024,512]{1,0:T(8,128)}, f32[8,1024]{1,0:T(8,...) custom-call(s32[1024,128]{1,0:T(8,128)} %get-tuple-element.176.cols_ref, f32[1024,128]{1,0:T(8,128)} %get-tuple-element.204.dlogits_ref, ...), custom_call_target="tpu_custom_call" | custom-call | flops 2281701376 | bytes 17858560 | tf_op jit(solution)/shard_map/second_back/pallas_call | solution.py:30
  266.5 4.2 all-to-all-start.2
  273.3 7.1 %all-to-all-done.2.dsums_ref = f32[32,1,1024]{2,1,0:T(1,128)S(1)} async-done(((f32[32,1,1024]{2,1,0:T(1,128)}), f32[32,1,1024]{2,1,0:T(1,128)S(1)}, u32[]{:S(2)}, u32[]{:S(2)}) %all-to-all-start.2) | async-done | bytes 131104 | tf_op jit(solution)/shard_map/all_to_all | solution.py:1049
  281.1 20.8 %conv_back.1 = (f32[1024,512]{1,0:T(8,128)}, bf16[1024,512]{1,0:T(8,128)(2,1)}, bf16[1024,512]{1,0:T(8,128)(2,1)}, bf16[1024,512]{1,0:T(8,128)(2,1)}, bf16[1024,...) custom-call(s32[1,5]{1,0:T(1,128)} %starts_ref.5, f32[1024,512]{1,0:T(8,128)} %get-tuple-element.188.conv_ref, ...), custom_call_target="tpu_custom_call" | custom-call | flops 1610612736 | bytes 20168724 | tf_op jit(solution)/shard_map/conv_back/pallas_call | solution.py:30
  310.5 46.7 %attend_back.1 = (bf16[272,512]{1,0:T(8,128)(2,1)}, bf16[272,512]{1,0:T(8,128)(2,1)}, bf16[272,512]{1,0:T(8,128)(2,1)}, bf16[272,512]{1,0:T(8,128)(2,1)}, f32[10...) custom-call(s32[1,5]{1,0:T(1,128)} %starts_ref.5, ...), custom_call_target="tpu_custom_call" | custom-call | flops 17179869184 | bytes 29052948 | tf_op jit(solution)/shard_map/attend_back/pallas_call | solution.py:30
  357.3 3.9 collective-permute-start.35
  363.8 11.5 %experts_back.9 = (bf16[512,2048]{1,0:T(8,128)(2,1)}, bf16[272,512]{1,0:T(8,128)(2,1)S(1)}, bf16[272,512]{1,0:T(8,128)(2,1)S(1)}, bf16[272,2048]{1,0:T(8,128)(2,...) custom-call(bf16[512,2048]{1,0:T(8,128)(2,1)} %get-tuple-element.179.in_ref, ...), custom_call_target="tpu_custom_call" | custom-call | flops 3422552064 | bytes 18710528 | tf_op jit(solution)/shard_map/experts_back/pallas_call | solution.py:30
  395.3 21.7 %collective-permute-done.38 = bf16[4,320,512]{2,1,0:T(8,128)(2,1)} collective-permute-done((bf16[4,320,512]{2,1,0:T(8,128)(2,1)}, bf16[4,320,512]{2,1,0:T(8,128)(2,1)}, u32[]{:S(2)}, u32[]{:S(2)}) %collective-permute-start.38) | collective-permute-done | bytes 1310752 | tf_op jit(solution)/shard_map/ppermute | solution.py:1055
  418.7 4.0 collective-permute-done.44.refs_3_
  431.3 9.5 %last.1 = (f32[1024,512]{1,0:T(8,128)}, f32[1024,512]{1,0:T(8,128)}, f32[16,1024]{1,0:T(8,128)}, f32[24,512]{1,0:T(8,128)}, f32[64,2048]{1,0:T(8,128)}, /*index=5*/f32[256,512]{1,0:T(8,128)}) custom-call(s32[1024,128]{1,0:T(8,128)} %get-tuple-element.176.cols_ref, f32[1024,128]{1,0:T(8,128)} %get-tuple-element.249.dlogits_ref, bf16[1024,512]{1,0:T(8,128)(2,1)} %hidden_ref.5, ...), custom_call_target="tpu_custom_call" | custom-call | flops 2281701376 | bytes 14761984 | tf_op jit(solution)/shard_map/last/pallas_call | solution.py:30
  442.7 11.6 %collective-permute-done.47 = bf16[320,512]{1,0:T(8,128)(2,1)S(1)} collective-permute-done((bf16[320,512]{1,0:T(8,128)(2,1)}, bf16[320,512]{1,0:T(8,128)(2,1)S(1)}, u32[]{:S(2)}, u32[]{:S(2)}) %collective-permute-start.47) | collective-permute-done | bytes 327712 | tf_op jit(solution)/shard_map/ppermute | solution.py:1055
  457.7 6.2 %collective-permute-start.49 = (bf16[64,2048]{1,0:T(8,128)(2,1)S(1)}, bf16[64,2048]{1,0:T(8,128)(2,1)S(1)}, u32[]{:S(2)}, u32[]{:S(2)}) collective-permute-start(bf16[64,2048]{1,0:T(8,128)(2,1)S(1)} %get-tuple-element.349), channel_id=1, source_target_pairs={{0,8},{4,12},{8,0},{12,4},{16,24},{20,28},{24,16},{28,20},{1,9},{5... | collective-permute-start | bytes 786440 | tf_op jit(solution)/shard_map/ppermute | solution.py:1055
  480.7 8.4 %collective-permute-done.50 = bf16[64,2048]{1,0:T(8,128)(2,1)S(1)} collective-permute-done((bf16[64,2048]{1,0:T(8,128)(2,1)S(1)}, bf16[64,2048]{1,0:T(8,128)(2,1)S(1)}, u32[]{:S(2)}, u32[]{:S(2)}) %collective-permute-start.50) | collective-permute-done | bytes 262176 | tf_op jit(solution)/shard_map/ppermute | solution.py:1055
  490.0 4.7 collective-permute-done.54
  (356 shorter events, 165.8 us)
Async XLA Ops:
  7.2 92.1 %all-gather.6.cloned.1.call-start = ((), (), s32[]{:S(2)}) async-start(), calls=%async_computation.6 | async-start | bytes 4325376 | tf_op jit(solution)/shard_map/all_gather | solution.py:1270
  11.6 156.8 %all-gather.8.cloned.1.call-start = ((), (), s32[]{:S(2)}) async-start(), calls=%async_computation.9 | async-start | bytes 2359296 | tf_op jit(solution)/shard_map/all_gather | solution.py:1275
  12.4 178.5 %all-gather.10.cloned.1.call-start = ((), (), s32[]{:S(2)}) async-start(), calls=%async_computation.10 | async-start | bytes 2359296 | tf_op jit(solution)/shard_map/all_gather | solution.py:1276
  16.2 22.0 %collective-permute-start.4 = (bf16[64,2048]{1,0:T(8,128)(2,1)}, bf16[64,2048]{1,0:T(8,128)(2,1)S(1)}, u32[]{:S(2)}, u32[]{:S(2)}) collective-permute-start(bf16[64,2048]{1,0:T(8,128)(2,1)} %bitcast.160), channel_id=1, source_target_pairs={{0,8},{8,16},{16,24},{24,28},{28,20},{20,12},{12,4},{4,0},{1,9},{9... | collective-permute-start | bytes 786440 | tf_op jit(solution)/shard_map/ppermute | solution.py:1098
  18.2 20.8 %collective-permute-start.7 = (bf16[256,512]{1,0:T(8,128)(2,1)}, bf16[256,512]{1,0:T(8,128)(2,1)S(1)}, u32[]{:S(2)}, u32[]{:S(2)}) collective-permute-start(bf16[256,512]{1,0:T(8,128)(2,1)} %bitcast.163), channel_id=1, source_target_pairs={{0,4},{8,0},{16,8},{24,16},{28,24},{20,28},{12,20},{4,12},{1,5},{9... | collective-permute-start | bytes 786440 | tf_op jit(solution)/shard_map/ppermute | solution.py:1096
  40.4 18.2 %collective-permute-start.12 = (bf16[256,512]{1,0:T(8,128)(2,1)S(1)}, bf16[256,512]{1,0:T(8,128)(2,1)S(1)}, u32[]{:S(2)}, u32[]{:S(2)}) collective-permute-start(bf16[256,512]{1,0:T(8,128)(2,1)S(1)} %collective-permute-done.11.refs_14_), channel_id=1, source_target_pairs={{0,8},{8,16},{16,24},{24,28},{28,20},{20,12},{12,4},{4,0},{1,9},{9... | collective-permute-start | bytes 786440 | tf_op jit(solution)/shard_map/ppermute | solution.py:1098
  41.2 19.2 %collective-permute-start.2 = (bf16[64,2048]{1,0:T(8,128)(2,1)S(1)}, bf16[64,2048]{1,0:T(8,128)(2,1)S(1)}, u32[]{:S(2)}, u32[]{:S(2)}) collective-permute-start(bf16[64,2048]{1,0:T(8,128)(2,1)S(1)} %collective-permute-done.1.refs_2_), channel_id=1, source_target_pairs={{0,4},{8,0},{16,8},{24,16},{28,24},{20,28},{12,20},{4,12},{1,5},{9... | collective-permute-start | bytes 786440 | tf_op jit(solution)/shard_map/ppermute | solution.py:1096
  58.6 23.3 %collective-permute-start.18 = (bf16[272,512]{1,0:T(8,128)(2,1)}, bf16[272,512]{1,0:T(8,128)(2,1)S(1)}, u32[]{:S(2)}, u32[]{:S(2)}) collective-permute-start(bf16[272,512]{1,0:T(8,128)(2,1)} %get-tuple-element.186), channel_id=1, source_target_pairs={{0,3},{1,2},{2,1},{3,0},{4,7},{5,6},{6,5},{7,4},{8,11},{9,10},{10,... | collective-permute-start | bytes 835592 | tf_op jit(solution)/shard_map/ppermute | solution.py:1055
  63.3 23.3 %collective-permute-start.16 = (bf16[272,512]{1,0:T(8,128)(2,1)}, bf16[272,512]{1,0:T(8,128)(2,1)S(1)}, u32[]{:S(2)}, u32[]{:S(2)}) collective-permute-start(bf16[272,512]{1,0:T(8,128)(2,1)} %get-tuple-element.185), channel_id=1, source_target_pairs={{0,2},{1,3},{2,0},{3,1},{4,6},{5,7},{6,4},{7,5},{8,10},{9,11},{10,... | collective-permute-start | bytes 835592 | tf_op jit(solution)/shard_map/ppermute | solution.py:1055
  66.6 21.7 %collective-permute-start.14 = (bf16[272,512]{1,0:T(8,128)(2,1)}, bf16[272,512]{1,0:T(8,128)(2,1)S(1)}, u32[]{:S(2)}, u32[]{:S(2)}) collective-permute-start(bf16[272,512]{1,0:T(8,128)(2,1)} %get-tuple-element.182), channel_id=1, source_target_pairs={{0,1},{1,0},{2,3},{3,2},{4,5},{5,4},{6,7},{7,6},{8,9},{9,8},{10,11... | collective-permute-start | bytes 835592 | tf_op jit(solution)/shard_map/ppermute | solution.py:1055
  145.8 285.5 %reduce-scatter.3.cloned.1.call-start = ((), (), s32[]{:S(2)}) async-start(), calls=%async_computation.7 | async-start | bytes 2359296 | tf_op jit(solution)/shard_map/reduce_scatter | solution.py:1192
  166.5 24.4 %collective-permute-start.20 = (bf16[272,512]{1,0:T(8,128)(2,1)}, bf16[272,512]{1,0:T(8,128)(2,1)S(1)}, u32[]{:S(2)}, u32[]{:S(2)}) collective-permute-start(bf16[272,512]{1,0:T(8,128)(2,1)} %get-tuple-element.194), channel_id=1, source_target_pairs={{0,1},{1,0},{2,3},{3,2},{4,5},{5,4},{6,7},{7,6},{8,9},{9,8},{10,11... | collective-permute-start | bytes 835592 | tf_op jit(solution)/shard_map/ppermute | solution.py:1055
  167.0 30.8 %collective-permute-start.21 = (bf16[272,512]{1,0:T(8,128)(2,1)}, bf16[272,512]{1,0:T(8,128)(2,1)S(1)}, u32[]{:S(2)}, u32[]{:S(2)}) collective-permute-start(bf16[272,512]{1,0:T(8,128)(2,1)} %get-tuple-element.197), channel_id=1, source_target_pairs={{0,2},{1,3},{2,0},{3,1},{4,6},{5,7},{6,4},{7,5},{8,10},{9,11},{10,... | collective-permute-start | bytes 835592 | tf_op jit(solution)/shard_map/ppermute | solution.py:1055
  168.1 29.7 %collective-permute-start.22 = (bf16[272,512]{1,0:T(8,128)(2,1)}, bf16[272,512]{1,0:T(8,128)(2,1)S(1)}, u32[]{:S(2)}, u32[]{:S(2)}) collective-permute-start(bf16[272,512]{1,0:T(8,128)(2,1)} %get-tuple-element.198), channel_id=1, source_target_pairs={{0,3},{1,2},{2,1},{3,0},{4,7},{5,6},{6,5},{7,4},{8,11},{9,10},{10,... | collective-permute-start | bytes 835592 | tf_op jit(solution)/shard_map/ppermute | solution.py:1055
  270.7 160.6 %reduce-scatter.5.cloned.1.call-start = ((), (), s32[]{:S(2)}) async-start(), calls=%async_computation.8 | async-start | bytes 2359296 | tf_op jit(solution)/shard_map/reduce_scatter | solution.py:1193
  307.9 49.4 %collective-permute-start.32 = (bf16[8,4,16,512]{3,2,1,0:T(8,128)(2,1)S(1)}, bf16[8,4,16,512]{3,2,1,0:T(8,128)(2,1)S(1)}, u32[]{:S(2)}, u32[]{:S(2)}) collective-permute-start(bf16[8,4,16,512]{3,2,1,0:T(8,128)(2,1)S(1)} %bitcast.154), channel_id=1, source_target_pairs={{0,1},{1,0},{2,3},{3,2},{4,5},{5,4},{6,7},{7,6},{8,9},{9,8},{10,11... | collective-permute-start | bytes 1572872 | tf_op jit(solution)/shard_map/ppermute | solution.py:1055
  309.0 48.3 %collective-permute-start.33 = (bf16[8,4,16,512]{3,2,1,0:T(8,128)(2,1)S(1)}, bf16[8,4,16,512]{3,2,1,0:T(8,128)(2,1)S(1)}, u32[]{:S(2)}, u32[]{:S(2)}) collective-permute-start(bf16[8,4,16,512]{3,2,1,0:T(8,128)(2,1)S(1)} %bitcast.155), channel_id=1, source_target_pairs={{0,2},{1,3},{2,0},{3,1},{4,6},{5,7},{6,4},{7,5},{8,10},{9,11},{10,... | collective-permute-start | bytes 1572872 | tf_op jit(solution)/shard_map/ppermute | solution.py:1055
  309.6 47.8 %collective-permute-start.34 = (bf16[8,4,16,512]{3,2,1,0:T(8,128)(2,1)S(1)}, bf16[8,4,16,512]{3,2,1,0:T(8,128)(2,1)S(1)}, u32[]{:S(2)}, u32[]{:S(2)}) collective-permute-start(bf16[8,4,16,512]{3,2,1,0:T(8,128)(2,1)S(1)} %bitcast.156), channel_id=1, source_target_pairs={{0,3},{1,2},{2,1},{3,0},{4,7},{5,6},{6,5},{7,4},{8,11},{9,10},{10,... | collective-permute-start | bytes 1572872 | tf_op jit(solution)/shard_map/ppermute | solution.py:1055
  385.3 31.7 %collective-permute-start.38 = (bf16[4,320,512]{2,1,0:T(8,128)(2,1)}, bf16[4,320,512]{2,1,0:T(8,128)(2,1)}, u32[]{:S(2)}, u32[]{:S(2)}) collective-permute-start(bf16[4,320,512]{2,1,0:T(8,128)(2,1)} %fusion.46), channel_id=1, source_target_pairs={{0,4},{4,0},{8,12},{12,8},{16,20},{20,16},{24,28},{28,24},{1,5},{5... | collective-permute-start | bytes 3932168 | tf_op jit(solution)/shard_map/ppermute | solution.py:1055
  388.6 34.1 %collective-permute-start.39 = (bf16[8,16,2048]{2,1,0:T(8,128)(2,1)S(1)}, bf16[8,16,2048]{2,1,0:T(8,128)(2,1)S(1)}, u32[]{:S(2)}, u32[]{:S(2)}) collective-permute-start(bf16[8,16,2048]{2,1,0:T(8,128)(2,1)S(1)} %get-tuple-element.337), channel_id=1, source_target_pairs={{0,1},{1,0},{2,3},{3,2},{4,5},{5,4},{6,7},{7,6},{8,9},{9,8},{10,11... | collective-permute-start | bytes 1572872 | tf_op jit(solution)/shard_map/ppermute | solution.py:1055
  388.8 33.9 %collective-permute-start.40 = (bf16[8,16,2048]{2,1,0:T(8,128)(2,1)S(1)}, bf16[8,16,2048]{2,1,0:T(8,128)(2,1)S(1)}, u32[]{:S(2)}, u32[]{:S(2)}) collective-permute-start(bf16[8,16,2048]{2,1,0:T(8,128)(2,1)S(1)} %get-tuple-element.336), channel_id=1, source_target_pairs={{0,2},{1,3},{2,0},{3,1},{4,6},{5,7},{6,4},{7,5},{8,10},{9,11},{10,... | collective-permute-start | bytes 1572872 | tf_op jit(solution)/shard_map/ppermute | solution.py:1055
  390.4 32.3 %collective-permute-start.41 = (bf16[8,16,2048]{2,1,0:T(8,128)(2,1)S(1)}, bf16[8,16,2048]{2,1,0:T(8,128)(2,1)S(1)}, u32[]{:S(2)}, u32[]{:S(2)}) collective-permute-start(bf16[8,16,2048]{2,1,0:T(8,128)(2,1)S(1)} %get-tuple-element.335), channel_id=1, source_target_pairs={{0,3},{1,2},{2,1},{3,0},{4,7},{5,6},{6,5},{7,4},{8,11},{9,10},{10,... | collective-permute-start | bytes 1572872 | tf_op jit(solution)/shard_map/ppermute | solution.py:1055
  394.8 27.9 %collective-permute-start.44 = (bf16[272,512]{1,0:T(8,128)(2,1)S(1)}, bf16[272,512]{1,0:T(8,128)(2,1)S(1)}, u32[]{:S(2)}, u32[]{:S(2)}) collective-permute-start(bf16[272,512]{1,0:T(8,128)(2,1)S(1)} %get-tuple-element.301), channel_id=1, source_target_pairs={{0,3},{1,2},{2,1},{3,0},{4,7},{5,6},{6,5},{7,4},{8,11},{9,10},{10,... | collective-permute-start | bytes 835592 | tf_op jit(solution)/shard_map/ppermute | solution.py:1055
  424.4 29.9 %collective-permute-start.45 = (bf16[4,64,2048]{2,1,0:T(8,128)(2,1)}, bf16[4,64,2048]{2,1,0:T(8,128)(2,1)}, u32[]{:S(2)}, u32[]{:S(2)}) collective-permute-start(bf16[4,64,2048]{2,1,0:T(8,128)(2,1)} %get-tuple-element.333), channel_id=1, source_target_pairs={{0,4},{4,0},{8,12},{12,8},{16,20},{20,16},{24,28},{28,24},{1,5},{5... | collective-permute-start | bytes 3145736 | tf_op jit(solution)/shard_map/ppermute | solution.py:1055
  428.5 25.8 %collective-permute-start.47 = (bf16[320,512]{1,0:T(8,128)(2,1)}, bf16[320,512]{1,0:T(8,128)(2,1)S(1)}, u32[]{:S(2)}, u32[]{:S(2)}) collective-permute-start(bf16[320,512]{1,0:T(8,128)(2,1)} %get-tuple-element.344), channel_id=1, source_target_pairs={{0,16},{4,20},{8,24},{12,28},{16,0},{20,4},{24,8},{28,12},{1,17},{... | collective-permute-start | bytes 983048 | tf_op jit(solution)/shard_map/ppermute | solution.py:1055
  428.5 25.8 %collective-permute-start.48 = (bf16[320,512]{1,0:T(8,128)(2,1)S(1)}, bf16[320,512]{1,0:T(8,128)(2,1)S(1)}, u32[]{:S(2)}, u32[]{:S(2)}) collective-permute-start(bf16[320,512]{1,0:T(8,128)(2,1)S(1)} %get-tuple-element.343), channel_id=1, source_target_pairs={{0,24},{4,28},{8,16},{12,20},{16,8},{20,12},{24,0},{28,4},{1,25},{... | collective-permute-start | bytes 983048 | tf_op jit(solution)/shard_map/ppermute | solution.py:1055
  464.0 25.1 %collective-permute-start.50 = (bf16[64,2048]{1,0:T(8,128)(2,1)S(1)}, bf16[64,2048]{1,0:T(8,128)(2,1)S(1)}, u32[]{:S(2)}, u32[]{:S(2)}) collective-permute-start(bf16[64,2048]{1,0:T(8,128)(2,1)S(1)} %get-tuple-element.347), channel_id=1, source_target_pairs={{0,16},{4,20},{8,24},{12,28},{16,0},{20,4},{24,8},{28,12},{1,17},{... | collective-permute-start | bytes 786440 | tf_op jit(solution)/shard_map/ppermute | solution.py:1055
  464.1 24.9 %collective-permute-start.51 = (bf16[64,2048]{1,0:T(8,128)(2,1)S(1)}, bf16[64,2048]{1,0:T(8,128)(2,1)S(1)}, u32[]{:S(2)}, u32[]{:S(2)}) collective-permute-start(bf16[64,2048]{1,0:T(8,128)(2,1)S(1)} %get-tuple-element.348), channel_id=1, source_target_pairs={{0,24},{4,28},{8,16},{12,20},{16,8},{20,12},{24,0},{28,4},{1,25},{... | collective-permute-start | bytes 786440 | tf_op jit(solution)/shard_map/ppermute | solution.py:1055
  468.6 21.3 %collective-permute-start.53 = (bf16[16,2048]{1,0:T(8,128)(2,1)}, bf16[16,2048]{1,0:T(8,128)(2,1)S(1)}, u32[]{:S(2)}, u32[]{:S(2)}) collective-permute-start(bf16[16,2048]{1,0:T(8,128)(2,1)} %get-tuple-element.358), channel_id=1, source_target_pairs={{0,8},{4,12},{8,0},{12,4},{16,24},{20,28},{24,16},{28,20},{1,9},{5... | collective-permute-start | bytes 196616 | tf_op jit(solution)/shard_map/ppermute | solution.py:1055
  469.7 24.9 %collective-permute-start.54 = (bf16[16,2048]{1,0:T(8,128)(2,1)}, bf16[16,2048]{1,0:T(8,128)(2,1)}, u32[]{:S(2)}, u32[]{:S(2)}) collective-permute-start(bf16[16,2048]{1,0:T(8,128)(2,1)} %get-tuple-element.360), channel_id=1, source_target_pairs={{0,16},{4,20},{8,24},{12,28},{16,0},{20,4},{24,8},{28,12},{1,17},{... | collective-permute-start | bytes 196616 | tf_op jit(solution)/shard_map/ppermute | solution.py:1055
  473.8 20.9 %collective-permute-start.55 = (bf16[16,2048]{1,0:T(8,128)(2,1)S(1)}, bf16[16,2048]{1,0:T(8,128)(2,1)}, u32[]{:S(2)}, u32[]{:S(2)}) collective-permute-start(bf16[16,2048]{1,0:T(8,128)(2,1)S(1)} %get-tuple-element.359), channel_id=1, source_target_pairs={{0,24},{4,28},{8,16},{12,20},{16,8},{20,12},{24,0},{28,4},{1,25},{... | collective-permute-start | bytes 196616 | tf_op jit(solution)/shard_map/ppermute | solution.py:1055
  477.5 19.3 %all-to-all-start.3 = ((f32[32,1,640]{2,1,0:T(1,128)}), f32[32,1,640]{2,1,0:T(1,128)S(1)}, u32[]{:S(2)}, u32[]{:S(2)}) async-start(f32[32,1,640]{2,1,0:T(1,128)} %all_to_all.22), calls=%async_computation.5 | async-start | bytes 163840 | tf_op jit(solution)/shard_map/all_to_all | solution.py:1482
  (104 other events, 869.2 us)
Sparse Core Ops, SparseCore 0:
  11.7 74.7 all-gather.5
  88.7 49.0 all-gather.7
  139.9 50.9 all-gather.9
  254.3 69.1 reduce-scatter.2
  326.9 66.6 reduce-scatter.4

commit v7 on v6

--- a/solution.py
+++ b/solution.py
@@ -216,11 +216,6 @@
         name="experts",
         limit=32,
     )
-
-
-def forward_in_turn(received, pair):
-    near, far = lax.optimization_barrier((expert_forward(received[:2], *pair), received[2:]))
-    return near + expert_forward(far[:1], *pair) + expert_forward(far[1:], *pair)
 
 
 def expert_backward_kernel(count, in_ref, out_ref, *refs):
@@ -1338,7 +1333,10 @@
         name="second",
     )
     received_two = exchange(sent_two, experts)
-    result_two = forward_in_turn(received_two, second_pair)
+    result_two = (
+        expert_forward(received_two[2:3], *second_pair) + expert_forward(received_two[3:], *second_pair)
+    )
+    result_two = expert_forward(received_two[:2], *second_pair) + result_two
     returned_two = exchange(result_two, experts)
 
     *d_sent_two, output, d4, dlogits_two, dgain_five = run(

time: 513 us -> 515 us (level)
  no operation moved by 1% of the time
where the time goes in v7:
time: 515 us; the launch traced here: 509 us
  Pallas kernels  193 us (37%)
  waiting for transfers between devices  144 us (28%)
  starting transfers between devices  75.1 us (15%)
  local copies, waits for them, and re-layouts  48.6 us (9%)
  matrix products  22.8 us (4%)
  between operations  15.2 us (3%)
  other arithmetic  9.55 us (2%)
    pallas_call x21, Pallas kernels, run(): pl.pallas_call(kernel, out_shape=outs, in_specs=in_specs, out_specs=[VMEM...  188 us
    ppermute x42, waiting for transfers between devices, across(): return lax.ppermute(values, axis, [(i, i ^ offset) for i in range(size)])  77.2 us
    ppermute x42, starting transfers between devices, across(): return lax.ppermute(values, axis, [(i, i ^ offset) for i in range(size)])  42.6 us
    dot_general x7, matrix products, rows_product(): lax.dot_general(left, right, (((0,), (0,)), ((), ())), preferred_element_...  22.8 us
    unnamed x151, local copies, waits for them, and re-layouts  22.8 us
    all_gather x1, waiting for transfers between devices, body(): lax.all_gather(second_out[0], 'dp', axis=0, tiled=True)  21.8 us
    all_to_all x3, waiting for transfers between devices, gather_small(): return lax.all_to_all(values, BOTH, split_axis=0, concat_axis=0, tiled=True)  20.6 us
    ppermute x7, waiting for transfers between devices, ring_gather(): lax.ppermute(pieces[-step + 1 or 0], 'dp', ring_pairs(size, True))  15.2 us
  transfers between devices with their start and end apart: 65, of which 23 were waited for; matrix products, arithmetic and copies ran while one was open for 10% of the time, Pallas kernels for 36%

profile of v7, /device:TPU:0, one launch (start us, length us, event | category | flops | bytes accessed | tf_op | source)
XLA Modules:
  0.0 508.6 jit_solution(6346637464430099022)
XLA Ops:
  22.7 6.3 %all-to-all-start = ((f32[32,1,640]{2,1,0:T(1,128)}), f32[32,1,640]{2,1,0:T(1,128)S(1)}, u32[]{:S(2)}, u32[]{:S(2)}) async-start(f32[32,1,640]{2,1,0:T(1,128)} %broadcast_in_dim.26), calls=%async_computation | async-start | bytes 163840 | tf_op jit(solution)/shard_map/all_to_all | solution.py:1044
  33.3 4.1 all-to-all-done
  44.2 6.9 %collective-permute-done.5.refs_6_ = bf16[64,2048]{1,0:T(8,128)(2,1)} collective-permute-done((bf16[64,2048]{1,0:T(8,128)(2,1)S(1)}, bf16[64,2048]{1,0:T(8,128)(2,1)}, u32[]{:S(2)}, u32[]{:S(2)}) %collective-permute-start.5) | collective-permute-done | bytes 262176 | tf_op jit(solution)/shard_map/ppermute | solution.py:1093
  53.2 5.4 %front.1 = (bf16[272,512]{1,0:T(8,128)(2,1)}, bf16[272,512]{1,0:T(8,128)(2,1)}, bf16[272,512]{1,0:T(8,128)(2,1)}, bf16[272,512]{1,0:T(8,128)(2,1)}, f32[1024,128]{1,0:T(8,128)}, /*index=5*/f32[1024,1]{1,0:T(8,128)}) custom-call(bf16[1024,512]{1,0:T(8,128)(2,1)} %hidden_ref.5, bf16[1024,512]{1,0:T(8,128)(2,1)} %embed_ref.7, f32[8,512]{1,0:T(8,128)} %pad.20.gain_ref.gains_ref, ...), custom_call_target="tpu_custom_call" | custom-call | flops 2281701376 | bytes 4575232 | tf_op jit(solution)/shard_map/front/pallas_call | solution.py:30
  67.2 5.9 %collective-permute-done.13.refs_12_ = bf16[256,512]{1,0:T(8,128)(2,1)S(1)} collective-permute-done((bf16[256,512]{1,0:T(8,128)(2,1)S(1)}, bf16[256,512]{1,0:T(8,128)(2,1)S(1)}, u32[]{:S(2)}, u32[]{:S(2)}) %collective-permute-start.13) | collective-permute-done | bytes 262176 | tf_op jit(solution)/shard_map/ppermute | solution.py:1093
  76.9 5.0 assemble.1
  95.6 3.6 collective-permute-done.17.refs_2_
  100.1 40.5 %middle.1 = (f32[1024,512]{1,0:T(8,128)}, f32[1024,512]{1,0:T(8,128)}, bf16[1024,512]{1,0:T(8,128)(2,1)}, bf16[1024,512]{1,0:T(8,128)(2,1)}, bf16[1024,512]{1,0:...) custom-call(s32[1,5]{1,0:T(1,128)} %starts_ref.5, ...), custom_call_target="tpu_custom_call" | custom-call | flops 8589934592 | bytes 21827604 | tf_op jit(solution)/shard_map/middle/pallas_call | solution.py:30
  140.5 5.5 %all-to-all-start.1 = ((f32[32,1,1536]{2,1,0:T(1,128)}), f32[32,1,1536]{2,1,0:T(1,128)S(1)}, u32[]{:S(2)}, u32[]{:S(2)}) async-start(f32[32,1,1536]{2,1,0:T(1,128)} %get-tuple-element.185), calls=%async_computation.1 | async-start | bytes 393216 | tf_op jit(solution)/shard_map/all_to_all | solution.py:1044
  149.2 9.3 %all-to-all-done.1.totals_ref = f32[32,1,1536]{2,1,0:T(1,128)S(1)} async-done(((f32[32,1,1536]{2,1,0:T(1,128)}), f32[32,1,1536]{2,1,0:T(1,128)S(1)}, u32[]{:S(2)}, u32[]{:S(2)}) %all-to-all-start.1) | async-done | bytes 196640 | tf_op jit(solution)/shard_map/all_to_all | solution.py:1044
  159.2 8.2 %second.1 = (bf16[272,512]{1,0:T(8,128)(2,1)}, bf16[272,512]{1,0:T(8,128)(2,1)}, bf16[272,512]{1,0:T(8,128)(2,1)}, bf16[272,512]{1,0:T(8,128)(2,1)}, f32[1024,51...) custom-call(f32[1024,512]{1,0:T(8,128)} %get-tuple-element.183.h2_ref, ...), custom_call_target="tpu_custom_call" | custom-call | flops 2281701376 | bytes 11620352 | tf_op jit(solution)/shard_map/second/pallas_call | solution.py:30
  169.3 21.8 %all-gather.10.cloned.1.call-done = bf16[1,2048,512]{2,1,0:T(8,128)(2,1)} async-done(((bf16[1,256,512]{2,1,0:T(8,128)(2,1)}), bf16[1,2048,512]{2,1,0:T(8,128)(2,1)}) %all-gather.10.cloned.1.call-update) | async-done | bytes 2097168 | tf_op jit(solution)/shard_map/all_gather | solution.py:1271
  202.7 6.2 %collective-permute-done.23.refs_2_ = bf16[272,512]{1,0:T(8,128)(2,1)S(1)} collective-permute-done((bf16[272,512]{1,0:T(8,128)(2,1)S(1)}, bf16[272,512]{1,0:T(8,128)(2,1)S(1)}, u32[]{:S(2)}, u32[]{:S(2)}) %collective-permute-start.23) | collective-permute-done | bytes 278560 | tf_op jit(solution)/shard_map/ppermute | solution.py:1050
  208.9 5.1 %collective-permute-done.25.refs_3_ = bf16[272,512]{1,0:T(8,128)(2,1)S(1)} collective-permute-done((bf16[272,512]{1,0:T(8,128)(2,1)S(1)}, bf16[272,512]{1,0:T(8,128)(2,1)S(1)}, u32[]{:S(2)}, u32[]{:S(2)}) %collective-permute-start.25) | collective-permute-done | bytes 278560 | tf_op jit(solution)/shard_map/ppermute | solution.py:1050
  214.7 7.6 %turn.1 = (bf16[272,512]{1,0:T(8,128)(2,1)}, bf16[272,512]{1,0:T(8,128)(2,1)}, bf16[272,512]{1,0:T(8,128)(2,1)}, bf16[272,512]{1,0:T(8,128)(2,1)}, bf16[1024,512...) custom-call(f32[1024,512]{1,0:T(8,128)} %get-tuple-element.186.h3_ref, ...), custom_call_target="tpu_custom_call" | custom-call | flops 2281701376 | bytes 10162176 | tf_op jit(solution)/shard_map/turn/pallas_call | solution.py:30
  225.3 4.1 experts_back.6
  232.4 4.6 collective-permute-done.28.refs_1_
  245.4 4.3 fusion.38
  249.6 6.7 %fusion.41 = bf16[512,2048]{1,0:T(8,128)(2,1)} fusion(bf16[272,2048]{1,0:T(8,128)(2,1)} %copy-done.17, bf16[272,2048]{1,0:T(8,128)(2,1)} %copy-done.16, bf16[272,2048]{1,0:T(8,128)(2,1)} %copy-done.25, bf16[272,2048]{1,0:T(8,128)(2,1)} %copy-done.24, bf16[272,512]{1,0:T(8,128)(2,1)S(1)} %collective-permute-done.24.refs_0_, ...), kind=kOutput, calls=%fused_computation.37 | convolution fusion | flops 2305032192 | bytes 7667712 | tf_op jit(solution)/shard_map/dot_general | solution.py:1177
  257.1 11.7 %second_back.1 = (f32[1024,512]{1,0:T(8,128)}, bf16[1024,512]{1,0:T(8,128)(2,1)}, f32[1024,512]{1,0:T(8,128)}, f32[1024,512]{1,0:T(8,128)}, f32[8,1024]{1,0:T(8,...) custom-call(s32[1024,128]{1,0:T(8,128)} %get-tuple-element.172.cols_ref, f32[1024,128]{1,0:T(8,128)} %get-tuple-element.196.dlogits_ref, ...), custom_call_target="tpu_custom_call" | custom-call | flops 2281701376 | bytes 17858560 | tf_op jit(solution)/shard_map/second_back/pallas_call | solution.py:30
  274.5 7.1 %all-to-all-done.2.dsums_ref = f32[32,1,1024]{2,1,0:T(1,128)S(1)} async-done(((f32[32,1,1024]{2,1,0:T(1,128)}), f32[32,1,1024]{2,1,0:T(1,128)S(1)}, u32[]{:S(2)}, u32[]{:S(2)}) %all-to-all-start.2) | async-done | bytes 131104 | tf_op jit(solution)/shard_map/all_to_all | solution.py:1044
  282.3 20.8 %conv_back.1 = (f32[1024,512]{1,0:T(8,128)}, bf16[1024,512]{1,0:T(8,128)(2,1)}, bf16[1024,512]{1,0:T(8,128)(2,1)}, bf16[1024,512]{1,0:T(8,128)(2,1)}, bf16[1024,...) custom-call(s32[1,5]{1,0:T(1,128)} %starts_ref.5, f32[1024,512]{1,0:T(8,128)} %get-tuple-element.184.conv_ref, ...), custom_call_target="tpu_custom_call" | custom-call | flops 1610612736 | bytes 20168724 | tf_op jit(solution)/shard_map/conv_back/pallas_call | solution.py:30
  311.6 46.7 %attend_back.1 = (bf16[272,512]{1,0:T(8,128)(2,1)}, bf16[272,512]{1,0:T(8,128)(2,1)}, bf16[272,512]{1,0:T(8,128)(2,1)}, bf16[272,512]{1,0:T(8,128)(2,1)}, f32[10...) custom-call(s32[1,5]{1,0:T(1,128)} %starts_ref.5, ...), custom_call_target="tpu_custom_call" | custom-call | flops 17179869184 | bytes 29052948 | tf_op jit(solution)/shard_map/attend_back/pallas_call | solution.py:30
  362.6 11.5 %experts_back.9 = (bf16[512,2048]{1,0:T(8,128)(2,1)}, bf16[272,512]{1,0:T(8,128)(2,1)S(1)}, bf16[272,512]{1,0:T(8,128)(2,1)S(1)}, bf16[272,2048]{1,0:T(8,128)(2,...) custom-call(bf16[512,2048]{1,0:T(8,128)(2,1)} %get-tuple-element.175.in_ref, ...), custom_call_target="tpu_custom_call" | custom-call | flops 3422552064 | bytes 18710528 | tf_op jit(solution)/shard_map/experts_back/pallas_call | solution.py:30
  396.9 19.6 %collective-permute-done.38 = bf16[4,320,512]{2,1,0:T(8,128)(2,1)} collective-permute-done((bf16[4,320,512]{2,1,0:T(8,128)(2,1)}, bf16[4,320,512]{2,1,0:T(8,128)(2,1)}, u32[]{:S(2)}, u32[]{:S(2)}) %collective-permute-start.38) | collective-permute-done | bytes 1310752 | tf_op jit(solution)/shard_map/ppermute | solution.py:1050
  418.2 5.2 %collective-permute-done.44.refs_3_ = bf16[272,512]{1,0:T(8,128)(2,1)S(1)} collective-permute-done((bf16[272,512]{1,0:T(8,128)(2,1)S(1)}, bf16[272,512]{1,0:T(8,128)(2,1)S(1)}, u32[]{:S(2)}, u32[]{:S(2)}) %collective-permute-start.44) | collective-permute-done | bytes 278560 | tf_op jit(solution)/shard_map/ppermute | solution.py:1050
  427.5 3.5 collective-permute-start.47
  431.0 9.5 %last.1 = (f32[1024,512]{1,0:T(8,128)}, f32[1024,512]{1,0:T(8,128)}, f32[16,1024]{1,0:T(8,128)}, f32[24,512]{1,0:T(8,128)}, f32[64,2048]{1,0:T(8,128)}, /*index=5*/f32[256,512]{1,0:T(8,128)}) custom-call(s32[1024,128]{1,0:T(8,128)} %get-tuple-element.172.cols_ref, f32[1024,128]{1,0:T(8,128)} %get-tuple-element.241.dlogits_ref, bf16[1024,512]{1,0:T(8,128)(2,1)} %hidden_ref.5, ...), custom_call_target="tpu_custom_call" | custom-call | flops 2281701376 | bytes 14761984 | tf_op jit(solution)/shard_map/last/pallas_call | solution.py:30
  442.9 11.0 %collective-permute-done.47 = bf16[320,512]{1,0:T(8,128)(2,1)S(1)} collective-permute-done((bf16[320,512]{1,0:T(8,128)(2,1)}, bf16[320,512]{1,0:T(8,128)(2,1)S(1)}, u32[]{:S(2)}, u32[]{:S(2)}) %collective-permute-start.47) | collective-permute-done | bytes 327712 | tf_op jit(solution)/shard_map/ppermute | solution.py:1050
  458.5 6.7 %collective-permute-start.49 = (bf16[64,2048]{1,0:T(8,128)(2,1)S(1)}, bf16[64,2048]{1,0:T(8,128)(2,1)S(1)}, u32[]{:S(2)}, u32[]{:S(2)}) collective-permute-start(bf16[64,2048]{1,0:T(8,128)(2,1)S(1)} %get-tuple-element.341), channel_id=1, source_target_pairs={{0,8},{4,12},{8,0},{12,4},{16,24},{20,28},{24,16},{28,20},{1,9},{5... | collective-permute-start | bytes 786440 | tf_op jit(solution)/shard_map/ppermute | solution.py:1050
  481.5 8.7 %collective-permute-done.50 = bf16[64,2048]{1,0:T(8,128)(2,1)S(1)} collective-permute-done((bf16[64,2048]{1,0:T(8,128)(2,1)S(1)}, bf16[64,2048]{1,0:T(8,128)(2,1)S(1)}, u32[]{:S(2)}, u32[]{:S(2)}) %collective-permute-start.50) | collective-permute-done | bytes 262176 | tf_op jit(solution)/shard_map/ppermute | solution.py:1050
  491.2 5.0 collective-permute-done.54
  (356 shorter events, 165.4 us)
Async XLA Ops:
  7.2 92.1 %all-gather.6.cloned.1.call-start = ((), (), s32[]{:S(2)}) async-start(), calls=%async_computation.6 | async-start | bytes 4325376 | tf_op jit(solution)/shard_map/all_gather | solution.py:1265
  11.6 157.6 %all-gather.8.cloned.1.call-start = ((), (), s32[]{:S(2)}) async-start(), calls=%async_computation.9 | async-start | bytes 2359296 | tf_op jit(solution)/shard_map/all_gather | solution.py:1270
  12.4 178.7 %all-gather.10.cloned.1.call-start = ((), (), s32[]{:S(2)}) async-start(), calls=%async_computation.10 | async-start | bytes 2359296 | tf_op jit(solution)/shard_map/all_gather | solution.py:1271
  16.2 22.0 %collective-permute-start.4 = (bf16[64,2048]{1,0:T(8,128)(2,1)}, bf16[64,2048]{1,0:T(8,128)(2,1)S(1)}, u32[]{:S(2)}, u32[]{:S(2)}) collective-permute-start(bf16[64,2048]{1,0:T(8,128)(2,1)} %bitcast.160), channel_id=1, source_target_pairs={{0,8},{8,16},{16,24},{24,28},{28,20},{20,12},{12,4},{4,0},{1,9},{9... | collective-permute-start | bytes 786440 | tf_op jit(solution)/shard_map/ppermute | solution.py:1093
  18.2 20.8 %collective-permute-start.7 = (bf16[256,512]{1,0:T(8,128)(2,1)}, bf16[256,512]{1,0:T(8,128)(2,1)S(1)}, u32[]{:S(2)}, u32[]{:S(2)}) collective-permute-start(bf16[256,512]{1,0:T(8,128)(2,1)} %bitcast.163), channel_id=1, source_target_pairs={{0,4},{8,0},{16,8},{24,16},{28,24},{20,28},{12,20},{4,12},{1,5},{9... | collective-permute-start | bytes 786440 | tf_op jit(solution)/shard_map/ppermute | solution.py:1091
  40.4 18.2 %collective-permute-start.12 = (bf16[256,512]{1,0:T(8,128)(2,1)S(1)}, bf16[256,512]{1,0:T(8,128)(2,1)S(1)}, u32[]{:S(2)}, u32[]{:S(2)}) collective-permute-start(bf16[256,512]{1,0:T(8,128)(2,1)S(1)} %collective-permute-done.11.refs_14_), channel_id=1, source_target_pairs={{0,8},{8,16},{16,24},{24,28},{28,20},{20,12},{12,4},{4,0},{1,9},{9... | collective-permute-start | bytes 786440 | tf_op jit(solution)/shard_map/ppermute | solution.py:1093
  41.2 19.2 %collective-permute-start.2 = (bf16[64,2048]{1,0:T(8,128)(2,1)S(1)}, bf16[64,2048]{1,0:T(8,128)(2,1)S(1)}, u32[]{:S(2)}, u32[]{:S(2)}) collective-permute-start(bf16[64,2048]{1,0:T(8,128)(2,1)S(1)} %collective-permute-done.1.refs_2_), channel_id=1, source_target_pairs={{0,4},{8,0},{16,8},{24,16},{28,24},{20,28},{12,20},{4,12},{1,5},{9... | collective-permute-start | bytes 786440 | tf_op jit(solution)/shard_map/ppermute | solution.py:1091
  58.6 23.3 %collective-permute-start.18 = (bf16[272,512]{1,0:T(8,128)(2,1)}, bf16[272,512]{1,0:T(8,128)(2,1)S(1)}, u32[]{:S(2)}, u32[]{:S(2)}) collective-permute-start(bf16[272,512]{1,0:T(8,128)(2,1)} %get-tuple-element.182), channel_id=1, source_target_pairs={{0,3},{1,2},{2,1},{3,0},{4,7},{5,6},{6,5},{7,4},{8,11},{9,10},{10,... | collective-permute-start | bytes 835592 | tf_op jit(solution)/shard_map/ppermute | solution.py:1050
  63.3 23.3 %collective-permute-start.16 = (bf16[272,512]{1,0:T(8,128)(2,1)}, bf16[272,512]{1,0:T(8,128)(2,1)S(1)}, u32[]{:S(2)}, u32[]{:S(2)}) collective-permute-start(bf16[272,512]{1,0:T(8,128)(2,1)} %get-tuple-element.181), channel_id=1, source_target_pairs={{0,2},{1,3},{2,0},{3,1},{4,6},{5,7},{6,4},{7,5},{8,10},{9,11},{10,... | collective-permute-start | bytes 835592 | tf_op jit(solution)/shard_map/ppermute | solution.py:1050
  66.6 21.7 %collective-permute-start.14 = (bf16[272,512]{1,0:T(8,128)(2,1)}, bf16[272,512]{1,0:T(8,128)(2,1)S(1)}, u32[]{:S(2)}, u32[]{:S(2)}) collective-permute-start(bf16[272,512]{1,0:T(8,128)(2,1)} %get-tuple-element.178), channel_id=1, source_target_pairs={{0,1},{1,0},{2,3},{3,2},{4,5},{5,4},{6,7},{7,6},{8,9},{9,8},{10,11... | collective-permute-start | bytes 835592 | tf_op jit(solution)/shard_map/ppermute | solution.py:1050
  146.0 285.0 %reduce-scatter.3.cloned.1.call-start = ((), (), s32[]{:S(2)}) async-start(), calls=%async_computation.7 | async-start | bytes 2359296 | tf_op jit(solution)/shard_map/reduce_scatter | solution.py:1187
  167.4 23.7 %collective-permute-start.20 = (bf16[272,512]{1,0:T(8,128)(2,1)}, bf16[272,512]{1,0:T(8,128)(2,1)S(1)}, u32[]{:S(2)}, u32[]{:S(2)}) collective-permute-start(bf16[272,512]{1,0:T(8,128)(2,1)} %get-tuple-element.190), channel_id=1, source_target_pairs={{0,1},{1,0},{2,3},{3,2},{4,5},{5,4},{6,7},{7,6},{8,9},{9,8},{10,11... | collective-permute-start | bytes 835592 | tf_op jit(solution)/shard_map/ppermute | solution.py:1050
  167.4 30.6 %collective-permute-start.22 = (bf16[272,512]{1,0:T(8,128)(2,1)}, bf16[272,512]{1,0:T(8,128)(2,1)S(1)}, u32[]{:S(2)}, u32[]{:S(2)}) collective-permute-start(bf16[272,512]{1,0:T(8,128)(2,1)} %get-tuple-element.193), channel_id=1, source_target_pairs={{0,2},{1,3},{2,0},{3,1},{4,6},{5,7},{6,4},{7,5},{8,10},{9,11},{10,... | collective-permute-start | bytes 835592 | tf_op jit(solution)/shard_map/ppermute | solution.py:1050
  168.9 32.0 %collective-permute-start.24 = (bf16[272,512]{1,0:T(8,128)(2,1)}, bf16[272,512]{1,0:T(8,128)(2,1)S(1)}, u32[]{:S(2)}, u32[]{:S(2)}) collective-permute-start(bf16[272,512]{1,0:T(8,128)(2,1)} %get-tuple-element.194), channel_id=1, source_target_pairs={{0,3},{1,2},{2,1},{3,0},{4,7},{5,6},{6,5},{7,4},{8,11},{9,10},{10,... | collective-permute-start | bytes 835592 | tf_op jit(solution)/shard_map/ppermute | solution.py:1050
  271.9 159.1 %reduce-scatter.5.cloned.1.call-start = ((), (), s32[]{:S(2)}) async-start(), calls=%async_computation.8 | async-start | bytes 2359296 | tf_op jit(solution)/shard_map/reduce_scatter | solution.py:1188
  309.1 49.3 %collective-permute-start.32 = (bf16[8,4,16,512]{3,2,1,0:T(8,128)(2,1)S(1)}, bf16[8,4,16,512]{3,2,1,0:T(8,128)(2,1)S(1)}, u32[]{:S(2)}, u32[]{:S(2)}) collective-permute-start(bf16[8,4,16,512]{3,2,1,0:T(8,128)(2,1)S(1)} %bitcast.154), channel_id=1, source_target_pairs={{0,1},{1,0},{2,3},{3,2},{4,5},{5,4},{6,7},{7,6},{8,9},{9,8},{10,11... | collective-permute-start | bytes 1572872 | tf_op jit(solution)/shard_map/ppermute | solution.py:1050
  310.1 48.3 %collective-permute-start.33 = (bf16[8,4,16,512]{3,2,1,0:T(8,128)(2,1)S(1)}, bf16[8,4,16,512]{3,2,1,0:T(8,128)(2,1)S(1)}, u32[]{:S(2)}, u32[]{:S(2)}) collective-permute-start(bf16[8,4,16,512]{3,2,1,0:T(8,128)(2,1)S(1)} %bitcast.155), channel_id=1, source_target_pairs={{0,2},{1,3},{2,0},{3,1},{4,6},{5,7},{6,4},{7,5},{8,10},{9,11},{10,... | collective-permute-start | bytes 1572872 | tf_op jit(solution)/shard_map/ppermute | solution.py:1050
  310.7 47.7 %collective-permute-start.34 = (bf16[8,4,16,512]{3,2,1,0:T(8,128)(2,1)S(1)}, bf16[8,4,16,512]{3,2,1,0:T(8,128)(2,1)S(1)}, u32[]{:S(2)}, u32[]{:S(2)}) collective-permute-start(bf16[8,4,16,512]{3,2,1,0:T(8,128)(2,1)S(1)} %bitcast.156), channel_id=1, source_target_pairs={{0,3},{1,2},{2,1},{3,0},{4,7},{5,6},{6,5},{7,4},{8,11},{9,10},{10,... | collective-permute-start | bytes 1572872 | tf_op jit(solution)/shard_map/ppermute | solution.py:1050
  384.0 32.5 %collective-permute-start.38 = (bf16[4,320,512]{2,1,0:T(8,128)(2,1)}, bf16[4,320,512]{2,1,0:T(8,128)(2,1)}, u32[]{:S(2)}, u32[]{:S(2)}) collective-permute-start(bf16[4,320,512]{2,1,0:T(8,128)(2,1)} %fusion.46), channel_id=1, source_target_pairs={{0,4},{4,0},{8,12},{12,8},{16,20},{20,16},{24,28},{28,24},{1,5},{5... | collective-permute-start | bytes 3932168 | tf_op jit(solution)/shard_map/ppermute | solution.py:1050
  391.2 32.2 %collective-permute-start.39 = (bf16[8,16,2048]{2,1,0:T(8,128)(2,1)S(1)}, bf16[8,16,2048]{2,1,0:T(8,128)(2,1)S(1)}, u32[]{:S(2)}, u32[]{:S(2)}) collective-permute-start(bf16[8,16,2048]{2,1,0:T(8,128)(2,1)S(1)} %get-tuple-element.329), channel_id=1, source_target_pairs={{0,1},{1,0},{2,3},{3,2},{4,5},{5,4},{6,7},{7,6},{8,9},{9,8},{10,11... | collective-permute-start | bytes 1572872 | tf_op jit(solution)/shard_map/ppermute | solution.py:1050
  391.4 32.1 %collective-permute-start.40 = (bf16[8,16,2048]{2,1,0:T(8,128)(2,1)S(1)}, bf16[8,16,2048]{2,1,0:T(8,128)(2,1)S(1)}, u32[]{:S(2)}, u32[]{:S(2)}) collective-permute-start(bf16[8,16,2048]{2,1,0:T(8,128)(2,1)S(1)} %get-tuple-element.328), channel_id=1, source_target_pairs={{0,2},{1,3},{2,0},{3,1},{4,6},{5,7},{6,4},{7,5},{8,10},{9,11},{10,... | collective-permute-start | bytes 1572872 | tf_op jit(solution)/shard_map/ppermute | solution.py:1050
  391.8 31.7 %collective-permute-start.41 = (bf16[8,16,2048]{2,1,0:T(8,128)(2,1)S(1)}, bf16[8,16,2048]{2,1,0:T(8,128)(2,1)S(1)}, u32[]{:S(2)}, u32[]{:S(2)}) collective-permute-start(bf16[8,16,2048]{2,1,0:T(8,128)(2,1)S(1)} %get-tuple-element.327), channel_id=1, source_target_pairs={{0,3},{1,2},{2,1},{3,0},{4,7},{5,6},{6,5},{7,4},{8,11},{9,10},{10,... | collective-permute-start | bytes 1572872 | tf_op jit(solution)/shard_map/ppermute | solution.py:1050
  396.6 26.8 %collective-permute-start.44 = (bf16[272,512]{1,0:T(8,128)(2,1)S(1)}, bf16[272,512]{1,0:T(8,128)(2,1)S(1)}, u32[]{:S(2)}, u32[]{:S(2)}) collective-permute-start(bf16[272,512]{1,0:T(8,128)(2,1)S(1)} %get-tuple-element.293), channel_id=1, source_target_pairs={{0,3},{1,2},{2,1},{3,0},{4,7},{5,6},{6,5},{7,4},{8,11},{9,10},{10,... | collective-permute-start | bytes 835592 | tf_op jit(solution)/shard_map/ppermute | solution.py:1050
  425.1 28.7 %collective-permute-start.45 = (bf16[4,64,2048]{2,1,0:T(8,128)(2,1)}, bf16[4,64,2048]{2,1,0:T(8,128)(2,1)}, u32[]{:S(2)}, u32[]{:S(2)}) collective-permute-start(bf16[4,64,2048]{2,1,0:T(8,128)(2,1)} %get-tuple-element.325), channel_id=1, source_target_pairs={{0,4},{4,0},{8,12},{12,8},{16,20},{20,16},{24,28},{28,24},{1,5},{5... | collective-permute-start | bytes 3145736 | tf_op jit(solution)/shard_map/ppermute | solution.py:1050
  427.5 26.3 %collective-permute-start.47 = (bf16[320,512]{1,0:T(8,128)(2,1)}, bf16[320,512]{1,0:T(8,128)(2,1)S(1)}, u32[]{:S(2)}, u32[]{:S(2)}) collective-permute-start(bf16[320,512]{1,0:T(8,128)(2,1)} %get-tuple-element.336), channel_id=1, source_target_pairs={{0,16},{4,20},{8,24},{12,28},{16,0},{20,4},{24,8},{28,12},{1,17},{... | collective-permute-start | bytes 983048 | tf_op jit(solution)/shard_map/ppermute | solution.py:1050
  431.0 22.8 %collective-permute-start.48 = (bf16[320,512]{1,0:T(8,128)(2,1)S(1)}, bf16[320,512]{1,0:T(8,128)(2,1)S(1)}, u32[]{:S(2)}, u32[]{:S(2)}) collective-permute-start(bf16[320,512]{1,0:T(8,128)(2,1)S(1)} %get-tuple-element.335), channel_id=1, source_target_pairs={{0,24},{4,28},{8,16},{12,20},{16,8},{20,12},{24,0},{28,4},{1,25},{... | collective-permute-start | bytes 983048 | tf_op jit(solution)/shard_map/ppermute | solution.py:1050
  465.2 25.1 %collective-permute-start.50 = (bf16[64,2048]{1,0:T(8,128)(2,1)S(1)}, bf16[64,2048]{1,0:T(8,128)(2,1)S(1)}, u32[]{:S(2)}, u32[]{:S(2)}) collective-permute-start(bf16[64,2048]{1,0:T(8,128)(2,1)S(1)} %get-tuple-element.339), channel_id=1, source_target_pairs={{0,16},{4,20},{8,24},{12,28},{16,0},{20,4},{24,8},{28,12},{1,17},{... | collective-permute-start | bytes 786440 | tf_op jit(solution)/shard_map/ppermute | solution.py:1050
  466.1 24.1 %collective-permute-start.51 = (bf16[64,2048]{1,0:T(8,128)(2,1)S(1)}, bf16[64,2048]{1,0:T(8,128)(2,1)S(1)}, u32[]{:S(2)}, u32[]{:S(2)}) collective-permute-start(bf16[64,2048]{1,0:T(8,128)(2,1)S(1)} %get-tuple-element.340), channel_id=1, source_target_pairs={{0,24},{4,28},{8,16},{12,20},{16,8},{20,12},{24,0},{28,4},{1,25},{... | collective-permute-start | bytes 786440 | tf_op jit(solution)/shard_map/ppermute | solution.py:1050
  469.8 21.4 %collective-permute-start.53 = (bf16[16,2048]{1,0:T(8,128)(2,1)}, bf16[16,2048]{1,0:T(8,128)(2,1)S(1)}, u32[]{:S(2)}, u32[]{:S(2)}) collective-permute-start(bf16[16,2048]{1,0:T(8,128)(2,1)} %get-tuple-element.350), channel_id=1, source_target_pairs={{0,8},{4,12},{8,0},{12,4},{16,24},{20,28},{24,16},{28,20},{1,9},{5... | collective-permute-start | bytes 196616 | tf_op jit(solution)/shard_map/ppermute | solution.py:1050
  470.9 25.3 %collective-permute-start.54 = (bf16[16,2048]{1,0:T(8,128)(2,1)}, bf16[16,2048]{1,0:T(8,128)(2,1)}, u32[]{:S(2)}, u32[]{:S(2)}) collective-permute-start(bf16[16,2048]{1,0:T(8,128)(2,1)} %get-tuple-element.352), channel_id=1, source_target_pairs={{0,16},{4,20},{8,24},{12,28},{16,0},{20,4},{24,8},{28,12},{1,17},{... | collective-permute-start | bytes 196616 | tf_op jit(solution)/shard_map/ppermute | solution.py:1050
  475.5 20.6 %collective-permute-start.55 = (bf16[16,2048]{1,0:T(8,128)(2,1)S(1)}, bf16[16,2048]{1,0:T(8,128)(2,1)}, u32[]{:S(2)}, u32[]{:S(2)}) collective-permute-start(bf16[16,2048]{1,0:T(8,128)(2,1)S(1)} %get-tuple-element.351), channel_id=1, source_target_pairs={{0,24},{4,28},{8,16},{12,20},{16,8},{20,12},{24,0},{28,4},{1,25},{... | collective-permute-start | bytes 196616 | tf_op jit(solution)/shard_map/ppermute | solution.py:1050
  479.0 19.4 %all-to-all-start.3 = ((f32[32,1,640]{2,1,0:T(1,128)}), f32[32,1,640]{2,1,0:T(1,128)S(1)}, u32[]{:S(2)}, u32[]{:S(2)}) async-start(f32[32,1,640]{2,1,0:T(1,128)} %all_to_all.22), calls=%async_computation.5 | async-start | bytes 163840 | tf_op jit(solution)/shard_map/all_to_all | solution.py:1480
  (104 other events, 864.6 us)
Sparse Core Ops, SparseCore 0:
  11.7 74.7 all-gather.5
  88.7 49.0 all-gather.7
  139.9 51.0 all-gather.9
  256.6 68.1 reduce-scatter.2
  328.1 67.0 reduce-scatter.4
